TPU v7x, 128 devices: a whole 4x4x4 slice. The times are simulated.
128 devices in a mesh: row: 8 (over z, y_hi), col: 16 (over y_lo, x, core).
Axes of the slice: x: 4, y: 4 (y_hi: 2, y_lo: 2; y = y_hi * 2 + y_lo), z: 4, core: 2. Of those that a mesh axis runs over, the one named last changes fastest.
Arguments:
- features: bfloat16 [131072, 128], P(('row', 'col')), may hold values from -6 to 6
- weight_self: bfloat16 [128, 256], replicated, may hold values from -0.5 to 0.5
- weight_neigh: bfloat16 [128, 256], replicated, may hold values from -0.5 to 0.5
- bias_term: float32 [256], replicated, may hold values from -3 to 3
- upstream: bfloat16 [131072, 256], P(('row', 'col')), may hold values from -6 to 6
- tile_values: bfloat16 [8, 16, 128, 256, 256], P('row', 'col'), may hold values from -0.1875 to 0.1875
- block_pairs: int32 [8, 16, 128, 2], P('row', 'col'), may hold values from 0 to 63, as said below
- tile_counts: int32 [8, 16], P('row', 'col'), may hold values from 16 to 128, as said below
Outputs:
- hidden_out: bfloat16 [131072, 256], P(('row', 'col'))
- grad_features: bfloat16 [131072, 128], P(('row', 'col'))
- grad_self_weight: float32 [128, 256], replicated
- grad_neigh_weight: float32 [128, 256], replicated
Inputs may be any that keep to these rules, and one draw needn't show every extreme that they name: `block_pairs`: within one grid cell all 128 slots name distinct block pairs; destination indices are below 8 * 4 and source indices below 16 * 4. Slots from tile_counts on are ignored. `tile_counts`: some grid cell uses all 128 slots in every draw.
All inputs are finite; a program needn't handle non-finite values.
Results may differ from a plain program's by a relative error of at most 0.0061.
Values may be sent and summed in bfloat16 or wider, within the bound.
No kernel may reach another device: no remote copies, remote signals or barrier semaphores. Data moves between devices by JAX's collectives and lax.ppermute only.
A program may use at most 192 MiB of HBM per device.

v0:
```python
import jax
import jax.numpy as jnp
from jax import lax
from jax.sharding import PartitionSpec as P


def silu_slope(pre_act):
    sig_value = jax.nn.sigmoid(pre_act)
    return sig_value * (1.0 + pre_act * (1.0 - sig_value))


def shards(
    features, weight_self, weight_neigh, bias_term, upstream, tile_values, block_pairs, tile_counts
):
    rows_dev = features.shape[0]
    width = features.shape[1]
    tile_size = tile_values.shape[-1]
    block_local = rows_dev // tile_size
    row_count = lax.axis_size("row")
    col_count = lax.axis_size("col")
    tile_stack = tile_values[0, 0]
    pair_list = block_pairs[0, 0]
    live_count = tile_counts[0, 0]
    slot_count = tile_stack.shape[0]
    slot_valid = (jnp.arange(slot_count, dtype=jnp.int32) < live_count).astype(jnp.float32)
    gathered = lax.all_gather(features, "col", axis=0, tiled=True).reshape(
        col_count * block_local, tile_size, width
    )
    source_blocks = gathered[pair_list[:, 1]]
    products = jnp.einsum(
        "stu,suf->stf", tile_stack, source_blocks, preferred_element_type=jnp.float32
    )
    products = products * slot_valid[:, None, None]
    partial_sums = jnp.zeros((row_count * block_local, tile_size, width), jnp.float32)
    partial_sums = (
        partial_sums.at[pair_list[:, 0]].add(products).reshape(row_count * rows_dev, width)
    )
    own_sums = lax.psum_scatter(partial_sums, "row", scatter_dimension=0, tiled=True)
    aggregated = own_sums.astype(jnp.bfloat16)
    pre_act = (
        jnp.dot(features, weight_self, preferred_element_type=jnp.float32)
        + jnp.dot(aggregated, weight_neigh, preferred_element_type=jnp.float32)
        + bias_term
    )
    hidden_out = jax.nn.silu(pre_act).astype(jnp.bfloat16)
    dpre = (upstream.astype(jnp.float32) * silu_slope(pre_act)).astype(jnp.bfloat16)
    dz_local = jnp.dot(dpre, weight_neigh.T, preferred_element_type=jnp.float32).astype(
        jnp.bfloat16
    )
    dz_target = lax.all_gather(dz_local, "row", axis=0, tiled=True)
    grad_self = jnp.dot(features.T, dpre, preferred_element_type=jnp.float32)
    grad_neigh = jnp.dot(aggregated.T, dpre, preferred_element_type=jnp.float32)
    grad_self, grad_neigh = lax.psum((grad_self, grad_neigh), ("row", "col"))
    grad_scale = float(rows_dev * row_count * col_count) ** (-0.5)
    self_grad = jnp.dot(dpre, weight_self.T, preferred_element_type=jnp.float32)
    dz_blocks = dz_target.reshape(row_count * block_local, tile_size, width)[pair_list[:, 0]]
    back_products = jnp.einsum(
        "stu,stf->suf", tile_stack, dz_blocks, preferred_element_type=jnp.float32
    )
    back_products = back_products * slot_valid[:, None, None]
    source_index = pair_list[:, 1]
    back_partial = jnp.zeros((col_count * block_local, tile_size, width), jnp.float32)
    back_partial = (
        back_partial.at[source_index].add(back_products).reshape(col_count * rows_dev, width)
    )
    back_sums = lax.psum_scatter(back_partial, "col", scatter_dimension=0, tiled=True)
    grad_features = (self_grad + back_sums).astype(jnp.bfloat16)
    return (hidden_out, grad_features, grad_self * grad_scale, grad_neigh * grad_scale)


def solution(mesh):
    placed = (
        P(("row", "col"), None),
        P(),
        P(),
        P(),
        P(("row", "col"), None),
        P("row", "col", None, None, None),
        P("row", "col", None, None),
        P("row", "col"),
    )
    return jax.shard_map(
        shards,
        mesh=mesh,
        in_specs=placed,
        out_specs=(P(("row", "col"), None), P(("row", "col"), None), P(), P()),
        check_vma=False,
    )
```

profile of v0, /device:TPU:0, one launch (start us, length us, event | category | flops | bytes accessed | tf_op | source)
XLA Modules:
  0.0 503.9 jit_solution(15717007249425223824)
XLA Ops:
  7.2 0.0 all-gather.3.cloned.1.call-start
  7.2 0.7 all-gather.3.cloned.1.call-update
  7.9 0.0 reduce-scatter.3.cloned.1.call-start
  8.6 0.8 fusion.14
  9.4 40.2 %all-gather.3.cloned.1.call-done = bf16[16384,128]{1,0:T(8,128)(2,1)} async-done(((bf16[1024,128]{1,0:T(8,128)(2,1)}), bf16[16384,128]{1,0:T(8,128)(2,1)}) %all-gather.3.cloned.1.call-update) | async-done | bytes 4194320 | tf_op jit(solution)/shard_map/all_gather | solution.py:26
  49.5 8.8 %gather_fusion = bf16[128,256,128]{2,1,0:T(8,128)(2,1)} fusion(bf16[64,256,128]{2,1,0:T(8,128)(2,1)} %bitcast.41, s32[1024]{0:T(1024)S(1)} %pad_clamp_fusion.1), kind=kCustom, calls=%fused_computation | custom fusion | bytes 16777728 | tf_op jit(solution)/shard_map/gather | solution.py:29
  58.3 17.3 %multiply_bitcast_fusion.1 = f32[128,256,128]{1,2,0:T(8,128)} fusion(bf16[128,256,128]{2,1,0:T(8,128)(2,1)} %gather_fusion, bf16[1,1,128,256,256]{4,3,2,1,0:T(8,128)(2,1)} %param.13, f32[128]{0:T(128)S(1)} %compare_convert_fusion), kind=kOutput, calls=%fused_computation.9 | convolution fusion | flops 2151677952 | bytes 41943552 | tf_op jit(solution)/shard_map/stu,suf->stf/dot_general | solution.py:30
  75.6 17.4 %copy.18 = f32[128,256,128]{2,1,0:T(8,128)} copy(f32[128,256,128]{1,2,0:T(8,128)} %multiply_bitcast_fusion.1) | data formatting | bytes 33554432 | tf_op jit(solution)/shard_map/mul | solution.py:33
  93.0 2.4 broadcast_in_dim.4
  95.4 38.2 %scatter_fusion = f32[32,256,128]{2,1,0:T(8,128)} fusion(f32[32,256,128]{2,1,0:T(8,128)} %broadcast_in_dim.4, s32[128]{0:T(128)S(1)} %get-tuple-element.17, f32[128,256,128]{2,1,0:T(8,128)} %copy.18), kind=kCustom, calls=%fused_computation.2 | custom fusion | flops 4194304 | bytes 50332160 | tf_op jit(solution)/shard_map/scatter-add | solution.py:36
  133.6 0.0 reduce-scatter.3.cloned.1.call-update
  133.6 0.0 all-gather.5.cloned.1.call-start
  133.7 0.3 fusion.15
  133.9 84.3 %reduce-scatter.3.cloned.1.call-done = f32[1024,128]{1,0:T(8,128)} async-done(((f32[8192,128]{1,0:T(8,128)}), f32[1024,128]{1,0:T(8,128)}) %reduce-scatter.3.cloned.1.call-update) | async-done | bytes 524304 | tf_op jit(solution)/shard_map/reduce_scatter | solution.py:38
  218.2 2.6 multiply_convert_fusion
  220.8 1.0 convolution_convert_fusion
  221.8 0.0 all-reduce.3.cloned.1.call-start
  221.9 1.0 convolution_bitcast_fusion
  222.9 1.0 fusion.10
  223.9 0.2 reduce-scatter.5.cloned.1.call-start
  224.1 50.7 %all-gather.5.cloned.1.call-done = bf16[8192,128]{1,0:T(8,128)(2,1)} async-done(((bf16[1024,128]{1,0:T(8,128)(2,1)}), bf16[8192,128]{1,0:T(8,128)(2,1)}) %all-gather.5.cloned.1.call-update) | async-done | bytes 2097168 | tf_op jit(solution)/shard_map/all_gather | solution.py:50
  274.9 8.1 %gather_fusion.1 = bf16[128,256,128]{2,1,0:T(8,128)(2,1)} fusion(bf16[32,256,128]{2,1,0:T(8,128)(2,1)} %bitcast.40, s32[1024]{0:T(1024)S(1)} %pad_clamp_fusion), kind=kCustom, calls=%fused_computation.1 | custom fusion | bytes 16777728 | tf_op jit(solution)/shard_map/gather | solution.py:56
  283.0 14.8 %multiply_bitcast_fusion = f32[128,256,128]{1,2,0:T(8,128)} fusion(bf16[128,256,128]{2,1,0:T(8,128)(2,1)} %gather_fusion.1, bf16[1,1,128,256,256]{4,3,2,1,0:T(8,128)(2,1)} %param.13, f32[128]{0:T(128)S(1)} %compare_convert_fusion), kind=kOutput, calls=%fused_computation.8 | convolution fusion | flops 2151677952 | bytes 41943552 | tf_op jit(solution)/shard_map/stu,stf->suf/dot_general | solution.py:57
  297.8 17.4 %copy.20 = f32[128,256,128]{2,1,0:T(8,128)} copy(f32[128,256,128]{1,2,0:T(8,128)} %multiply_bitcast_fusion) | data formatting | bytes 33554432 | tf_op jit(solution)/shard_map/mul | solution.py:60
  315.2 4.2 broadcast_in_dim.5
  319.5 38.3 %scatter_fusion.1 = f32[64,256,128]{2,1,0:T(8,128)} fusion(f32[64,256,128]{2,1,0:T(8,128)} %broadcast_in_dim.5, s32[128]{0:T(128)S(1)} %get-tuple-element.16, f32[128,256,128]{2,1,0:T(8,128)} %copy.20), kind=kCustom, calls=%fused_computation.3 | custom fusion | flops 4194304 | bytes 50332160 | tf_op jit(solution)/shard_map/scatter-add | solution.py:64
  357.8 63.4 %all-reduce.3.cloned.1.call-done = (f32[128,256]{0,1:T(8,128)}, f32[128,256]{0,1:T(8,128)}) async-done(((f32[128,256]{0,1:T(8,128)}, f32[128,256]{0,1:T(8,128)}), (f32[128,256]{0,1:T(8,128)}, f32[128,256]{0,1:T(8,128)})) %all-reduce.3.cloned.1.call-update) | async-done | bytes 262160 | tf_op jit(solution)/shard_map/psum | solution.py:53
  421.3 1.0 broadcast_multiply_fusion
  422.3 0.8 copy.22
  423.0 0.8 copy.23
  423.8 71.5 %reduce-scatter.5.cloned.1.call-done = f32[1024,128]{1,0:T(8,128)} async-done(((f32[16384,128]{1,0:T(8,128)}), f32[1024,128]{1,0:T(8,128)}) %reduce-scatter.5.cloned.1.call-update) | async-done | bytes 524304 | tf_op jit(solution)/shard_map/reduce_scatter | solution.py:66
  495.3 2.0 fusion.9
  (20 shorter events, 0.1 us)
Async XLA Ops:
  7.2 211.1 %copy-start = (bf16[128,256]{1,0:T(8,128)(2,1)S(1)}, bf16[128,256]{1,0:T(8,128)(2,1)}, u32[]{:S(2)}) copy-start(bf16[128,256]{1,0:T(8,128)(2,1)} %param.10) | copy-start | bytes 196612
  7.2 42.4 %all-gather.3.cloned.1.call-start = ((), (), s32[]{:S(2)}) async-start(), calls=%async_computation.2 | async-start | bytes 4456448 | tf_op jit(solution)/shard_map/all_gather | solution.py:26
  7.9 210.3 %reduce-scatter.3.cloned.1.call-start = ((), (), s32[]{:S(2)}) async-start(), calls=%async_computation.3 | async-start | bytes 4718592 | tf_op jit(solution)/shard_map/reduce_scatter | solution.py:38
  95.4 38.3 %copy-start.2 = (bf16[1024,128]{1,0:T(8,128)(2,1)S(1)}, bf16[1024,128]{1,0:T(8,128)(2,1)}, u32[]{:S(2)}) copy-start(bf16[1024,128]{1,0:T(8,128)(2,1)} %param.8) | copy-start | bytes 786436
  95.4 38.3 %copy-start.4 = (bf16[128,256]{1,0:T(8,128)(2,1)S(1)}, bf16[128,256]{1,0:T(8,128)(2,1)}, u32[]{:S(2)}) copy-start(bf16[128,256]{1,0:T(8,128)(2,1)} %param.9) | copy-start | bytes 196612
  95.4 122.8 %copy-start.5 = (bf16[1024,256]{1,0:T(8,128)(2,1)S(1)}, bf16[1024,256]{1,0:T(8,128)(2,1)}, u32[]{:S(2)}) copy-start(bf16[1024,256]{1,0:T(8,128)(2,1)} %param.12) | copy-start | bytes 1572868
  95.4 122.8 %copy-start.6 = (f32[256]{0:T(256)S(1)}, f32[256]{0:T(256)}, u32[]{:S(2)}) copy-start(f32[256]{0:T(256)} %param.11) | copy-start | bytes 3076
  133.6 141.3 %all-gather.5.cloned.1.call-start = ((), (), s32[]{:S(2)}) async-start(), calls=%async_computation.4 | async-start | bytes 2359296 | tf_op jit(solution)/shard_map/all_gather | solution.py:50
  218.2 4.6 copy-start.3
  221.8 199.4 %all-reduce.3.cloned.1.call-start = ((), (), s32[]{:S(2)}) async-start(), calls=%async_computation.6 | async-start | bytes 524288 | tf_op jit(solution)/shard_map/psum | solution.py:53
  223.9 271.4 %reduce-scatter.5.cloned.1.call-start = ((), (), s32[]{:S(2)}) async-start(), calls=%async_computation.5 | async-start | bytes 8912896 | tf_op jit(solution)/shard_map/reduce_scatter | solution.py:66
  319.5 177.9 %copy-start.1 = (bf16[128,256]{1,0:T(8,128)(2,1)S(1)}, bf16[128,256]{1,0:T(8,128)(2,1)}, u32[]{:S(2)}) copy-start(bf16[128,256]{1,0:T(8,128)(2,1)} %param.10) | copy-start | bytes 196612
Sparse Core Ops, SparseCore 0:
  9.7 39.7 all-gather.2
  133.7 84.4 reduce-scatter.2
  221.9 52.8 all-gather.4
  281.0 140.2 all-reduce.2
  423.6 71.6 reduce-scatter.4
where the time goes:
time: 505 us; the launch traced here: 504 us
  waiting for transfers between devices  311 us (62%)
  other arithmetic  78.3 us (16%)
  local copies, waits for them, and re-layouts  59.9 us (12%)
  matrix products  40 us (8%)
  between operations  14.5 us (3%)
    reduce_scatter x1, waiting for transfers between devices, shards(): lax.psum_scatter(partial_sums, 'row', scatter_dimension=0, tiled=True)  84.3 us
    reduce_scatter x1, waiting for transfers between devices, shards(): lax.psum_scatter(back_partial, 'col', scatter_dimension=0, tiled=True)  71.5 us
    psum x1, waiting for transfers between devices, shards(): grad_self, grad_neigh = lax.psum((grad_self, grad_neigh), ('row', 'col'))  63.4 us
    all_gather x1, waiting for transfers between devices, shards(): dz_target = lax.all_gather(dz_local, 'row', axis=0, tiled=True)  50.7 us
    all_gather x1, waiting for transfers between devices, shards(): lax.all_gather(features, 'col', axis=0, tiled=True)  40.2 us
    scatter-add x1, other arithmetic, shards(): back_partial.at[source_index].add(back_products)  38.3 us
    scatter-add x1, other arithmetic, shards(): partial_sums.at[pair_list[:, 0]].add(products)  38.2 us
    mul x1, local copies, waits for them, and re-layouts, shards(): back_products = back_products * slot_valid[:, None, None]  17.4 us
  transfers between devices with their start and end apart: 5, of which 5 were waited for; matrix products, arithmetic and copies ran while one was open for 18% of the time, Pallas kernels for 0%

commit v1 on v0

v1 whole, which is shorter than its diff:
```python
import functools

import jax
import jax.numpy as jnp
from jax import lax
from jax.experimental import pallas as pl
from jax.experimental.pallas import tpu as pltpu
from jax.sharding import PartitionSpec as P

TILE = 256
VMEM = pltpu.VMEM
BF16 = jnp.bfloat16
F32 = jnp.float32
LIMIT = 28 * 1024 * 1024


def hop_col(value, dy, dx, dc=0):
    pairs = []
    for y in range(2):
        for x in range(4):
            for c in range(2):
                to = (((y + dy) % 2) * 4 + (x + dx) % 4) * 2 + (c + dc) % 2
                pairs.append(((y * 4 + x) * 2 + c, to))
    return lax.ppermute(value, "col", pairs)


def hop_row(value, dy, dz):
    pairs = []
    for z in range(4):
        for y in range(2):
            pairs.append((z * 2 + y, ((z + dz) % 4) * 2 + (y + dy) % 2))
    return lax.ppermute(value, "row", pairs)


def hop_diag(value):
    pairs = []
    for r in range(8):
        for c in range(16):
            pairs.append((r * 16 + c, (r ^ 1) * 16 + (c ^ 8)))
    return lax.ppermute(value, ("row", "col"), pairs)


def in_vmem(*values):
    return [pltpu.with_memory_space_constraint(v, VMEM) for v in values]


def vmem_specs(n):
    return [pl.BlockSpec(memory_space=VMEM)] * n


def call(body, outs, vmem_args, smem_args=(), scratch=(), flops=0, nbytes=0, limit=LIMIT):
    single = not isinstance(outs, (list, tuple))
    specs = [pl.BlockSpec(memory_space=pltpu.SMEM)] * len(smem_args) + vmem_specs(len(vmem_args))
    return pl.pallas_call(
        body,
        out_shape=outs,
        in_specs=specs,
        out_specs=pl.BlockSpec(memory_space=VMEM) if single else vmem_specs(len(outs)),
        scratch_shapes=list(scratch),
        compiler_params=pltpu.CompilerParams(vmem_limit_bytes=limit),
        cost_estimate=pl.CostEstimate(flops=flops, bytes_accessed=nbytes, transcendentals=0),
    )(*smem_args, *in_vmem(*vmem_args))


def gather_halves(lo, hi, whole, step, swap):
    l_lo = step(lo, 1)
    r_hi = step(hi, -1)
    other = swap(whole)
    l_hi = step(hi, 1)
    r_lo = step(lo, -1)
    o_lo = step(l_lo, 1)
    o_hi = step(r_hi, -1)
    y_l = step(other, 1)
    y_r = step(other, -1)
    yo_lo = swap(o_lo)
    yo_hi = swap(o_hi)
    return {
        (0, 0): [whole],
        (0, 3): [l_lo, l_hi],
        (0, 1): [r_lo, r_hi],
        (0, 2): [o_lo, o_hi],
        (1, 0): [other],
        (1, 3): [y_l],
        (1, 1): [y_r],
        (1, 2): [yo_lo, yo_hi],
    }


def places():
    col = lax.axis_index("col")
    row = lax.axis_index("row")
    return col, row


def source_slot(s, col):
    c = s >> 2
    away = (c ^ col) & 9
    dx = ((c >> 1) - (col >> 1)) & 3
    return ((away & 1) << 5) | ((away >> 3) << 4) | (dx << 2) | (s & 3)


def target_slot(d, row):
    q = d >> 2
    dz = ((q >> 1) - (row >> 1)) & 3
    return (((q ^ row) & 1) << 4) | (dz << 2) | (d & 3)


def over_slots(count, step):
    group = 4

    def many(i, carry):
        step([i * group + k for k in range(group)])
        return carry

    def one(i, carry):
        step([i])
        return carry

    full = count // group
    lax.fori_loop(0, full, many, 0)
    lax.fori_loop(full * group, count, one, 0)


def forward_body(places_in, pairs, count, tiles, *rest):
    parts = rest[: len(places_in)]
    outs = rest[len(places_in) : len(places_in) + 8]
    held, total = rest[len(places_in) + 8 :]
    col, row = places()
    for ref, (start, size) in zip(parts, places_in):
        held[start : start + size] = ref[...].reshape(size, TILE, 128)
    total[...] = jnp.zeros_like(total)

    def step(slots):
        news = []
        for i in slots:
            d = target_slot(pairs[2 * i], row)
            s = source_slot(pairs[2 * i + 1], col)
            news.append((d, jnp.dot(tiles[i], held[s], preferred_element_type=F32)))
        for d, new in news:
            total[d] += new

    over_slots(count[0], step)
    for k in range(8):
        outs[k][...] = total[4 * k : 4 * k + 4].reshape(1024, 128).astype(BF16)


def backward_body(widths, pairs, count, tiles, *rest):
    n = len(widths)
    parts = rest[:n]
    sib = rest[n]
    outs = rest[n + 1 : n + 9]
    held, total = rest[n + 9 :]
    col, row = places()
    at = 0
    for ref, blocks in zip(parts, widths):
        for b in range(blocks):
            held[at] = ref[:, b * TILE : (b + 1) * TILE]
            at += 1
    total[...] = jnp.zeros_like(total)

    def step(slots):
        news = []
        for i in slots:
            d = target_slot(pairs[2 * i], row)
            s = source_slot(pairs[2 * i + 1], col)
            news.append((s, jnp.dot(held[d], tiles[i], preferred_element_type=F32)))
        for s, new in news:
            total[s] += new

    over_slots(count[0], step)
    for k in range(8):
        for b in range(4):
            outs[k][:, b * TILE : (b + 1) * TILE] = total[4 * k + b].astype(BF16)
            sib[k, :, b * TILE : (b + 1) * TILE] = total[32 + 4 * k + b].astype(BF16)


def add_body(sib, *rest):
    for k in range(8):
        rest[8 + k][...] = (rest[k][...].astype(F32) + sib[k].astype(F32)).astype(BF16)


def dense_body(bias, feats, upstream, w_self, w_neigh, *rest):
    sums = rest[:8]
    hidden, dpre_out, agg_out, dz_whole, dz_lo, dz_hi = rest[8:]
    for b in range(4):
        rows = slice(b * TILE, (b + 1) * TILE)
        agg = sums[0][rows].astype(F32)
        for k in range(1, 8):
            agg = agg + sums[k][rows].astype(F32)
        agg = agg.astype(BF16)
        agg_out[rows] = agg
        pre = jnp.dot(feats[rows], w_self[...], preferred_element_type=F32)
        pre = pre + jnp.dot(agg, w_neigh[...], preferred_element_type=F32) + bias[...]
        sig = jax.nn.sigmoid(pre)
        hidden[rows] = (pre * sig).astype(BF16)
        slope = sig * (1.0 + pre * (1.0 - sig))
        dpre = (upstream[rows].astype(F32) * slope).astype(BF16)
        dpre_out[rows] = dpre
        dz = lax.dot_general(
            w_neigh[...], dpre, (((1,), (1,)), ((), ())), preferred_element_type=F32
        ).astype(BF16)
        dz_whole[:, rows] = dz
        half = slice((b % 2) * TILE, (b % 2 + 1) * TILE)
        if b < 2:
            dz_lo[:, half] = dz
        else:
            dz_hi[:, half] = dz


def weights_body(feats, agg, dpre, w_self, keep, send, own_grad):
    over_nodes = (((0,), (0,)), ((), ()))
    grad_self = lax.dot_general(feats[...], dpre[...], over_nodes, preferred_element_type=F32)
    grad_neigh = lax.dot_general(agg[...], dpre[...], over_nodes, preferred_element_type=F32)
    first = lax.axis_index("col") % 2 == 0

    @pl.when(first)
    def _():
        keep[...] = grad_self
        send[...] = grad_neigh

    @pl.when(jnp.logical_not(first))
    def _():
        keep[...] = grad_neigh
        send[...] = grad_self

    own_grad[...] = lax.dot_general(
        w_self[...], dpre[...], (((1,), (1,)), ((), ())), preferred_element_type=F32
    )


def finish_body(own_grad, *rest):
    out = rest[-1]
    for b in range(4):
        nodes = slice(b * TILE, (b + 1) * TILE)
        total = own_grad[:, nodes]
        for k in range(8):
            total = total + rest[k][:, nodes].astype(F32)
        out[nodes] = total.T.astype(BF16)


def ring_place(axis):
    col, row = places()
    return (col >> 1) & 3 if axis == "x" else row >> 1


def sum_split_body(axis, n_in, *rest):
    ins, outs = rest[:n_in], rest[n_in : n_in + 4]
    held = rest[n_in + 4]
    total = ins[0][...]
    for ref in ins[1:]:
        total = total + ref[...]
    held[...] = total
    me = ring_place(axis)
    size = outs[0].shape[0]
    for k in range(4):
        at = pl.multiple_of(((me + k) & 3) * size, size)
        outs[k][...] = held[pl.ds(at, size), :]


def sum_body(*rest):
    total = rest[0][...]
    for ref in rest[1:-1]:
        total = total + ref[...]
    rest[-1][...] = total


def pair_sum_body(a, b, c, d, out):
    out[...] = (a[...] + b[...]) + (c[...] + d[...])


def join_body(axis, *rest):
    me = ring_place(axis)
    out = rest[4]
    size = rest[0].shape[0]
    for k in range(4):
        at = pl.multiple_of(((me + k) & 3) * size, size)
        out[pl.ds(at, size), :] = rest[k][...]


def place_body(scale, mine, other, grad_self, grad_neigh):
    first = lax.axis_index("col") % 2 == 0
    a = mine[...] * scale
    b = other[...] * scale
    grad_self[...] = jnp.where(first, a, b)
    grad_neigh[...] = jnp.where(first, b, a)


def sum_weights(keep, send, scale):
    def f32(rows):
        return VMEM((rows, 256), F32)

    got = hop_col(send, 0, 0, 1)
    pieces = call(
        functools.partial(sum_split_body, "x", 2), [f32(32)] * 4, [keep, got], scratch=[f32(128)]
    )
    got = [pieces[0]] + [hop_col(pieces[k], 0, k) for k in (1, 2, 3)]
    pieces = call(
        functools.partial(sum_split_body, "z", 4), [f32(8)] * 4, got, scratch=[f32(32)]
    )
    got = [pieces[0]] + [hop_row(pieces[k], 0, k) for k in (1, 2, 3)]
    part = call(sum_body, f32(8), got)
    whole = call(
        pair_sum_body, f32(8), [part, hop_col(part, 1, 0), hop_row(part, 1, 0), hop_diag(part)]
    )
    got = [whole] + [hop_row(whole, 0, -k) for k in (1, 2, 3)]
    quarter = call(functools.partial(join_body, "z"), f32(32), got)
    got = [quarter] + [hop_col(quarter, 0, -k) for k in (1, 2, 3)]
    half = call(functools.partial(join_body, "x"), f32(128), got)
    other = hop_col(half, 0, 0, 1)
    shape = jax.ShapeDtypeStruct((128, 256), F32)
    return call(functools.partial(place_body, scale), [shape, shape], [half, other])


def shards(
    features, weight_self, weight_neigh, bias_term, upstream, tile_values, block_pairs, tile_counts
):
    tiles = tile_values.reshape(tile_values.shape[2:])
    pairs = block_pairs.reshape(-1)
    count = tile_counts.reshape(-1)
    nodes = 131072

    with jax.named_scope("gather_features"):
        got = gather_halves(
            features[:512],
            features[512:],
            features,
            lambda v, d: hop_col(v, 0, d),
            lambda v: hop_col(v, 1, 0),
        )
        parts, where = [], []
        for core in range(2):
            for (y, x), pieces in got.items():
                at = (core * 8 + y * 4 + x) * 4
                for piece in pieces:
                    size = piece.shape[0] // TILE
                    parts.append(hop_col(piece, 0, 0, 1) if core else piece)
                    where.append((at, size))
                    at += size
    with jax.named_scope("forward_tiles"):
        partial = call(
            functools.partial(forward_body, where),
            [VMEM((1024, 128), BF16)] * 8,
            [tiles, *parts],
            [pairs, count],
            [VMEM((64, TILE, 128), BF16), VMEM((32, TILE, 128), F32)],
            flops=128 * 2 * TILE * TILE * 128,
            nbytes=24 << 20,
        )
    with jax.named_scope("sum_aggregates"):
        sums = [partial[0]]
        for y in range(2):
            for z in range(4):
                if y or z:
                    sums.append(hop_row(partial[y * 4 + z], y, z))
    with jax.named_scope("dense"):
        bias = bias_term.reshape(1, 256)
        hidden, dpre, agg, dz_whole, dz_lo, dz_hi = call(
            dense_body,
            [
                jax.ShapeDtypeStruct((1024, 256), BF16),
                VMEM((1024, 256), BF16),
                VMEM((1024, 128), BF16),
                VMEM((128, 1024), BF16),
                VMEM((128, 512), BF16),
                VMEM((128, 512), BF16),
            ],
            [bias, features, upstream, weight_self, weight_neigh, *sums],
            flops=3 * 2 * 1024 * 128 * 256,
            nbytes=6 << 20,
        )
    with jax.named_scope("gather_dz"):
        got = gather_halves(
            dz_lo, dz_hi, dz_whole, lambda v, d: hop_row(v, 0, d), lambda v: hop_row(v, 1, 0)
        )
        parts, widths = [], []
        for y in range(2):
            for z in range(4):
                for piece in got[y, z]:
                    parts.append(piece)
                    widths.append(piece.shape[1] // TILE)
    with jax.named_scope("weights"):
        keep, send, own_grad = call(
            weights_body,
            [VMEM((128, 256), F32), VMEM((128, 256), F32), VMEM((128, 1024), F32)],
            [features, agg, dpre, weight_self],
            flops=3 * 2 * 1024 * 128 * 256,
            nbytes=2 << 20,
        )
        grad_self, grad_neigh = sum_weights(keep, send, float(nodes) ** -0.5)
    with jax.named_scope("backward_tiles"):
        sib, *mine = call(
            functools.partial(backward_body, widths),
            [VMEM((8, 128, 1024), BF16)] + [VMEM((128, 1024), BF16)] * 8,
            [tiles, *parts],
            [pairs, count],
            [VMEM((32, 128, TILE), BF16), VMEM((64, 128, TILE), F32)],
            flops=128 * 2 * TILE * TILE * 128,
            nbytes=24 << 20,
        )
    with jax.named_scope("sum_grads"):
        sib = hop_col(sib, 0, 0, 1)
        mine = call(add_body, [VMEM((128, 1024), BF16)] * 8, [sib, *mine], nbytes=6 << 20)
        sums = [mine[0]]
        for y in range(2):
            for x in range(4):
                if y or x:
                    sums.append(hop_col(mine[y * 4 + x], y, x))
    with jax.named_scope("finish"):
        grad_features = call(
            finish_body,
            jax.ShapeDtypeStruct((1024, 128), BF16),
            [own_grad, *sums],
            nbytes=4 << 20,
        )
    return hidden, grad_features, grad_self, grad_neigh


def solution(mesh):
    placed = (
        P(("row", "col"), None),
        P(),
        P(),
        P(),
        P(("row", "col"), None),
        P("row", "col", None, None, None),
        P("row", "col", None, None),
        P("row", "col"),
    )
    return jax.shard_map(
        shards,
        mesh=mesh,
        in_specs=placed,
        out_specs=(P(("row", "col"), None), P(("row", "col"), None), P(), P()),
        check_vma=False,
    )
```

time: 505 us -> 210 us (0.42)
  waiting for transfers between devices: 311 us -> 82.8 us
  starting transfers between devices: 0.38 us -> 83.5 us
  other arithmetic: 78.3 us -> 0 us
  local copies, waits for them, and re-layouts: 59.9 us -> 15.9 us
  matrix products: 40 us -> 0 us
  Pallas kernels: 0 us -> 25.2 us
  between operations: 14.5 us -> 1.57 us
    reduce_scatter x2 -> x0, waiting for transfers between devices: 156 us -> none  [the longest x1 84.3 us: shards(): lax.psum_scatter(partial_sums, 'row', scatter_dimension=0, tiled=True)]
    all_gather x2 -> x0, waiting for transfers between devices: 90.9 us -> none  [the longest x1 50.7 us: shards(): dz_target = lax.all_gather(dz_local, 'row', axis=0, tiled=True)]
    ppermute x0 -> x66, starting transfers between devices: none -> 83.5 us  [the longest x25 45.2 us: hop_row(): return lax.ppermute(value, 'row', pairs)]
    ppermute x0 -> x66, waiting for transfers between devices: none -> 82.8 us  [the longest x40 48.4 us: hop_col(): return lax.ppermute(value, 'col', pairs)]
    scatter-add x2 -> x0, other arithmetic: 76.5 us -> none  [the longest x1 38.3 us: shards(): back_partial.at[source_index].add(back_products)]
    psum x1 -> x0, waiting for transfers between devices: 63.4 us -> none  [shards(): grad_self, grad_neigh = lax.psum((grad_self, grad_neigh), ('row', 'col'))]
    dot_general x8 -> x0, matrix products: 40 us -> none  [the longest x1 17.3 us: shards(): jnp.einsum('stu,suf->stf', tile_stack, source_blocks, preferred_element_t...]
    mul x2 -> x0, local copies, waits for them, and re-layouts: 34.8 us -> none  [the longest x1 17.4 us: shards(): back_products = back_products * slot_valid[:, None, None]]
  transfers between devices with their start and end apart: 5 -> 66, of which waited for: 5 -> 29; matrix products, arithmetic and copies ran while one was open for 18% -> 1% of each run, Pallas kernels for 0% -> 1%
where the time goes in v1:
time: 210 us; the launch traced here: 209 us
  starting transfers between devices  83.5 us (40%)
  waiting for transfers between devices  82.8 us (39%)
  Pallas kernels  25.2 us (12%)
  local copies, waits for them, and re-layouts  15.9 us (8%)
    ppermute x40, waiting for transfers between devices, hop_col(): return lax.ppermute(value, 'col', pairs)  48.4 us
    ppermute x25, starting transfers between devices, hop_row(): return lax.ppermute(value, 'row', pairs)  45.2 us
    ppermute x40, starting transfers between devices, hop_col(): return lax.ppermute(value, 'col', pairs)  37.7 us
    ppermute x25, waiting for transfers between devices, hop_row(): return lax.ppermute(value, 'row', pairs)  33.6 us
    pallas_call x13, Pallas kernels, call(): pl.pallas_call(body, out_shape=outs, in_specs=specs, out_specs=pl.BlockSp...  25.2 us
    unnamed x17, local copies, waits for them, and re-layouts  13.9 us
  transfers between devices with their start and end apart: 66, of which 29 were waited for; matrix products, arithmetic and copies ran while one was open for 1% of the time, Pallas kernels for 1%

profile of v1, /device:TPU:0, one launch (start us, length us, event | category | flops | bytes accessed | tf_op | source)
XLA Modules:
  0.0 209.0 jit_solution(2630239360265838733)
XLA Ops:
  1.6 2.9 %collective-permute-start.3 = (bf16[512,128]{1,0:T(8,128)(2,1)S(1)}, bf16[512,128]{1,0:T(8,128)(2,1)S(1)}, u32[]{:S(2)}, u32[]{:S(2)}) collective-permute-start(bf16[512,128]{1,0:T(8,128)(2,1)S(1)} %get-tuple-element.92), channel_id=1, source_target_pairs={{0,6},{1,7},{2,0},{3,1},{4,2},{5,3},{6,4},{7,5},{8,14},{9,15},{10,... | collective-permute-start | bytes 393224 | tf_op jit(solution)/shard_map/gather_features/ppermute | solution.py:24
  4.5 3.2 %collective-permute-start.2 = (bf16[512,128]{1,0:T(8,128)(2,1)S(1)}, bf16[512,128]{1,0:T(8,128)(2,1)S(1)}, u32[]{:S(2)}, u32[]{:S(2)}) collective-permute-start(bf16[512,128]{1,0:T(8,128)(2,1)S(1)} %get-tuple-element.93), channel_id=1, source_target_pairs={{0,6},{1,7},{2,0},{3,1},{4,2},{5,3},{6,4},{7,5},{8,14},{9,15},{10,... | collective-permute-start | bytes 393224 | tf_op jit(solution)/shard_map/gather_features/ppermute | solution.py:24
  12.8 2.7 %collective-permute-done.rest_1_ = bf16[512,128]{1,0:T(8,128)(2,1)S(1)} collective-permute-done((bf16[512,128]{1,0:T(8,128)(2,1)S(1)}, bf16[512,128]{1,0:T(8,128)(2,1)S(1)}, u32[]{:S(2)}, u32[]{:S(2)}) %collective-permute-start) | collective-permute-done | bytes 131104 | tf_op jit(solution)/shard_map/gather_features/ppermute | solution.py:24
  16.1 3.7 %collective-permute-start.8 = (bf16[1024,128]{1,0:T(8,128)(2,1)S(1)}, bf16[1024,128]{1,0:T(8,128)(2,1)S(1)}, u32[]{:S(2)}, u32[]{:S(2)}) collective-permute-start(bf16[1024,128]{1,0:T(8,128)(2,1)S(1)} %collective-permute-done.6.rest_7_), channel_id=1, source_target_pairs={{0,6},{1,7},{2,0},{3,1},{4,2},{5,3},{6,4},{7,5},{8,14},{9,15},{10,... | collective-permute-start | bytes 786440 | tf_op jit(solution)/shard_map/gather_features/ppermute | solution.py:24
  20.1 3.8 %collective-permute-done.4.rest_5_ = bf16[512,128]{1,0:T(8,128)(2,1)S(1)} collective-permute-done((bf16[512,128]{1,0:T(8,128)(2,1)S(1)}, bf16[512,128]{1,0:T(8,128)(2,1)S(1)}, u32[]{:S(2)}, u32[]{:S(2)}) %collective-permute-start.4) | collective-permute-done | bytes 131104 | tf_op jit(solution)/shard_map/gather_features/ppermute | solution.py:24
  26.0 4.3 %collective-permute-done.10.rest_11_ = bf16[512,128]{1,0:T(8,128)(2,1)S(1)} collective-permute-done((bf16[512,128]{1,0:T(8,128)(2,1)S(1)}, bf16[512,128]{1,0:T(8,128)(2,1)S(1)}, u32[]{:S(2)}, u32[]{:S(2)}) %collective-permute-start.10) | collective-permute-done | bytes 131104 | tf_op jit(solution)/shard_map/gather_features/ppermute | solution.py:24
  35.2 5.8 %copy-done = bf16[1,1,128,256,256]{4,3,2,1,0:T(8,128)(2,1)S(1)} copy-done((bf16[1,1,128,256,256]{4,3,2,1,0:T(8,128)(2,1)S(1)}, bf16[1,1,128,256,256]{4,3,2,1,0:T(8,128)(2,1)}, u32[]{:S(2)}) %copy-start) | copy-done | bytes 16777240
  42.0 11.1 %forward_tiles.1 = (bf16[1024,128]{1,0:T(8,128)(2,1)S(1)}, bf16[1024,128]{1,0:T(8,128)(2,1)S(1)}, bf16[1024,128]{1,0:T(8,128)(2,1)S(1)}, bf16[1024,128]{1,0:T(8,...) custom-call(s32[256]{0:T(256)S(1)} %reshape.21.pairs, ...), custom_call_target="tpu_custom_call" | custom-call | flops 2147483648 | bytes 25165824 | tf_op jit(solution)/shard_map/forward_tiles/pallas_call | solution.py:54
  53.2 3.1 %collective-permute-start.25 = (bf16[1024,128]{1,0:T(8,128)(2,1)S(1)}, bf16[1024,128]{1,0:T(8,128)(2,1)S(1)}, u32[]{:S(2)}, u32[]{:S(2)}) collective-permute-start(bf16[1024,128]{1,0:T(8,128)(2,1)S(1)} %get-tuple-element.51), channel_id=1, source_target_pairs={{0,96},{16,112},{32,0},{48,16},{64,32},{80,48},{96,64},{112,80},{1... | collective-permute-start | bytes 786440 | tf_op jit(solution)/shard_map/sum_aggregates/ppermute | solution.py:32
  56.4 5.0 %collective-permute-start.26 = (bf16[1024,128]{1,0:T(8,128)(2,1)S(1)}, bf16[1024,128]{1,0:T(8,128)(2,1)S(1)}, u32[]{:S(2)}, u32[]{:S(2)}) collective-permute-start(bf16[1024,128]{1,0:T(8,128)(2,1)S(1)} %get-tuple-element.52), channel_id=1, source_target_pairs={{0,16},{16,0},{32,48},{48,32},{64,80},{80,64},{96,112},{112,96},{1... | collective-permute-start | bytes 786440 | tf_op jit(solution)/shard_map/sum_aggregates/ppermute | solution.py:32
  62.8 4.4 %collective-permute-done.23.rest_1_ = bf16[1024,128]{1,0:T(8,128)(2,1)S(1)} collective-permute-done((bf16[1024,128]{1,0:T(8,128)(2,1)S(1)}, bf16[1024,128]{1,0:T(8,128)(2,1)S(1)}, u32[]{:S(2)}, u32[]{:S(2)}) %collective-permute-start.23) | collective-permute-done | bytes 262176 | tf_op jit(solution)/shard_map/sum_aggregates/ppermute | solution.py:32
  67.5 2.6 %collective-permute-start.29 = (bf16[1024,128]{1,0:T(8,128)(2,1)S(1)}, bf16[1024,128]{1,0:T(8,128)(2,1)S(1)}, u32[]{:S(2)}, u32[]{:S(2)}) collective-permute-start(bf16[1024,128]{1,0:T(8,128)(2,1)S(1)} %get-tuple-element.55), channel_id=1, source_target_pairs={{0,112},{16,96},{32,16},{48,0},{64,48},{80,32},{96,80},{112,64},{1... | collective-permute-start | bytes 786440 | tf_op jit(solution)/shard_map/sum_aggregates/ppermute | solution.py:32
  70.1 4.0 %collective-permute-done.27.rest_5_ = bf16[1024,128]{1,0:T(8,128)(2,1)S(1)} collective-permute-done((bf16[1024,128]{1,0:T(8,128)(2,1)S(1)}, bf16[1024,128]{1,0:T(8,128)(2,1)S(1)}, u32[]{:S(2)}, u32[]{:S(2)}) %collective-permute-start.27) | collective-permute-done | bytes 262176 | tf_op jit(solution)/shard_map/sum_aggregates/ppermute | solution.py:32
  74.1 5.7 %collective-permute-done.28.rest_6_ = bf16[1024,128]{1,0:T(8,128)(2,1)S(1)} collective-permute-done((bf16[1024,128]{1,0:T(8,128)(2,1)S(1)}, bf16[1024,128]{1,0:T(8,128)(2,1)S(1)}, u32[]{:S(2)}, u32[]{:S(2)}) %collective-permute-start.28) | collective-permute-done | bytes 262176 | tf_op jit(solution)/shard_map/sum_aggregates/ppermute | solution.py:32
  79.8 5.7 %collective-permute-done.29.rest_7_ = bf16[1024,128]{1,0:T(8,128)(2,1)S(1)} collective-permute-done((bf16[1024,128]{1,0:T(8,128)(2,1)S(1)}, bf16[1024,128]{1,0:T(8,128)(2,1)S(1)}, u32[]{:S(2)}, u32[]{:S(2)}) %collective-permute-start.29) | collective-permute-done | bytes 262176 | tf_op jit(solution)/shard_map/sum_aggregates/ppermute | solution.py:32
  87.6 8.5 %collective-permute-start.36 = (bf16[128,1024]{1,0:T(8,128)(2,1)S(1)}, bf16[128,1024]{1,0:T(8,128)(2,1)S(1)}, u32[]{:S(2)}, u32[]{:S(2)}) collective-permute-start(bf16[128,1024]{1,0:T(8,128)(2,1)S(1)} %get-tuple-element.60.rest_0_), channel_id=1, source_target_pairs={{0,16},{16,0},{32,48},{48,32},{64,80},{80,64},{96,112},{112,96},{1... | collective-permute-start | bytes 786440 | tf_op jit(solution)/shard_map/gather_dz/ppermute | solution.py:32
  96.1 3.2 %collective-permute-start.31 = (bf16[128,512]{1,0:T(8,128)(2,1)S(1)}, bf16[128,512]{1,0:T(8,128)(2,1)S(1)}, u32[]{:S(2)}, u32[]{:S(2)}) collective-permute-start(bf16[128,512]{1,0:T(8,128)(2,1)S(1)} %get-tuple-element.62), channel_id=1, source_target_pairs={{0,96},{16,112},{32,0},{48,16},{64,32},{80,48},{96,64},{112,80},{1... | collective-permute-start | bytes 393224 | tf_op jit(solution)/shard_map/gather_dz/ppermute | solution.py:32
  99.4 2.9 %collective-permute-done.32.rest_5_ = bf16[128,512]{1,0:T(8,128)(2,1)S(1)} collective-permute-done((bf16[128,512]{1,0:T(8,128)(2,1)S(1)}, bf16[128,512]{1,0:T(8,128)(2,1)S(1)}, u32[]{:S(2)}, u32[]{:S(2)}) %collective-permute-start.32) | collective-permute-done | bytes 131104 | tf_op jit(solution)/shard_map/gather_dz/ppermute | solution.py:32
  102.3 3.5 %collective-permute-start.34 = (bf16[128,512]{1,0:T(8,128)(2,1)S(1)}, bf16[128,512]{1,0:T(8,128)(2,1)S(1)}, u32[]{:S(2)}, u32[]{:S(2)}) collective-permute-start(bf16[128,512]{1,0:T(8,128)(2,1)S(1)} %collective-permute-done.31.rest_2_), channel_id=1, source_target_pairs={{0,96},{16,112},{32,0},{48,16},{64,32},{80,48},{96,64},{112,80},{1... | collective-permute-start | bytes 393224 | tf_op jit(solution)/shard_map/gather_dz/ppermute | solution.py:32
  105.8 3.2 %collective-permute-start.37 = (bf16[128,1024]{1,0:T(8,128)(2,1)S(1)}, bf16[128,1024]{1,0:T(8,128)(2,1)S(1)}, u32[]{:S(2)}, u32[]{:S(2)}) collective-permute-start(bf16[128,1024]{1,0:T(8,128)(2,1)S(1)} %collective-permute-done.36.rest_7_), channel_id=1, source_target_pairs={{0,96},{16,112},{32,0},{48,16},{64,32},{80,48},{96,64},{112,80},{1... | collective-permute-start | bytes 786440 | tf_op jit(solution)/shard_map/gather_dz/ppermute | solution.py:32
  110.0 3.5 %collective-permute-start.39 = (bf16[128,512]{1,0:T(8,128)(2,1)S(1)}, bf16[128,512]{1,0:T(8,128)(2,1)S(1)}, u32[]{:S(2)}, u32[]{:S(2)}) collective-permute-start(bf16[128,512]{1,0:T(8,128)(2,1)S(1)} %collective-permute-done.34.rest_4_), channel_id=1, source_target_pairs={{0,16},{16,0},{32,48},{48,32},{64,80},{80,64},{96,112},{112,96},{1... | collective-permute-start | bytes 393224 | tf_op jit(solution)/shard_map/gather_dz/ppermute | solution.py:32
  117.8 5.8 %copy-done.1 = bf16[1,1,128,256,256]{4,3,2,1,0:T(8,128)(2,1)S(1)} copy-done((bf16[1,1,128,256,256]{4,3,2,1,0:T(8,128)(2,1)S(1)}, bf16[1,1,128,256,256]{4,3,2,1,0:T(8,128)(2,1)}, u32[]{:S(2)}) %copy-start.1) | copy-done | bytes 16777240
  123.6 9.1 %backward_tiles.1 = (bf16[8,128,1024]{2,1,0:T(8,128)(2,1)S(1)}, bf16[128,1024]{1,0:T(8,128)(2,1)S(1)}, bf16[128,1024]{1,0:T(8,128)(2,1)S(1)}, bf16[128,1024]{1,0...) custom-call(s32[256]{0:T(256)S(1)} %reshape.21.pairs, ...), custom_call_target="tpu_custom_call" | custom-call | flops 2147483648 | bytes 25165824 | tf_op jit(solution)/shard_map/backward_tiles/pallas_call | solution.py:54
  134.0 2.9 %collective-permute-done.41.sib = bf16[8,128,1024]{2,1,0:T(8,128)(2,1)S(1)} collective-permute-done((bf16[8,128,1024]{2,1,0:T(8,128)(2,1)S(1)}, bf16[8,128,1024]{2,1,0:T(8,128)(2,1)S(1)}, u32[]{:S(2)}, u32[]{:S(2)}) %collective-permute-start.41) | collective-permute-done | bytes 2097184 | tf_op jit(solution)/shard_map/sum_grads/ppermute | solution.py:24
  137.6 4.1 %collective-permute-start.50 = (f32[32,256]{1,0:T(8,128)S(1)}, f32[32,256]{1,0:T(8,128)S(1)}, u32[]{:S(2)}, u32[]{:S(2)}) collective-permute-start(f32[32,256]{1,0:T(8,128)S(1)} %get-tuple-element.83), channel_id=1, source_target_pairs={{0,2},{1,3},{2,4},{3,5},{4,6},{5,7},{6,0},{7,1},{8,10},{9,11},{10,... | collective-permute-start | bytes 98312 | tf_op jit(solution)/shard_map/weights/ppermute | solution.py:24
  144.4 9.6 %collective-permute-done.50.rest_1_ = f32[32,256]{1,0:T(8,128)S(1)} collective-permute-done((f32[32,256]{1,0:T(8,128)S(1)}, f32[32,256]{1,0:T(8,128)S(1)}, u32[]{:S(2)}, u32[]{:S(2)}) %collective-permute-start.50) | collective-permute-done | bytes 32800 | tf_op jit(solution)/shard_map/weights/ppermute | solution.py:24
  155.2 2.2 %collective-permute-start.55 = (f32[8,256]{1,0:T(8,128)S(1)}, f32[8,256]{1,0:T(8,128)S(1)}, u32[]{:S(2)}, u32[]{:S(2)}) collective-permute-start(f32[8,256]{1,0:T(8,128)S(1)} %get-tuple-element.89), channel_id=1, source_target_pairs={{0,96},{16,112},{32,0},{48,16},{64,32},{80,48},{96,64},{112,80},{1... | collective-permute-start | bytes 24584 | tf_op jit(solution)/shard_map/weights/ppermute | solution.py:32
  160.5 3.1 %collective-permute-start.57 = (f32[8,256]{1,0:T(8,128)S(1)}, f32[8,256]{1,0:T(8,128)S(1)}, u32[]{:S(2)}, u32[]{:S(2)}) collective-permute-start(f32[8,256]{1,0:T(8,128)S(1)} %weights.11.a), channel_id=1, source_target_pairs={{0,16},{16,0},{32,48},{48,32},{64,80},{80,64},{96,112},{112,96},{1... | collective-permute-start | bytes 24584 | tf_op jit(solution)/shard_map/weights/ppermute | solution.py:32
  167.7 2.3 %collective-permute-start.60 = (f32[8,256]{1,0:T(8,128)S(1)}, f32[8,256]{1,0:T(8,128)S(1)}, u32[]{:S(2)}, u32[]{:S(2)}) collective-permute-start(f32[8,256]{1,0:T(8,128)S(1)} %weights.12.rest_0_), channel_id=1, source_target_pairs={{0,64},{16,80},{32,96},{48,112},{64,0},{80,16},{96,32},{112,48},{1... | collective-permute-start | bytes 24584 | tf_op jit(solution)/shard_map/weights/ppermute | solution.py:32
  180.1 2.5 %collective-permute-start.44 = (bf16[128,1024]{1,0:T(8,128)(2,1)S(1)}, bf16[128,1024]{1,0:T(8,128)(2,1)S(1)}, u32[]{:S(2)}, u32[]{:S(2)}) collective-permute-start(bf16[128,1024]{1,0:T(8,128)(2,1)S(1)} %get-tuple-element.75), channel_id=1, source_target_pairs={{0,6},{1,7},{2,0},{3,1},{4,2},{5,3},{6,4},{7,5},{8,14},{9,15},{10,... | collective-permute-start | bytes 786440 | tf_op jit(solution)/shard_map/sum_grads/ppermute | solution.py:24
  184.4 2.4 %collective-permute-start.47 = (bf16[128,1024]{1,0:T(8,128)(2,1)S(1)}, bf16[128,1024]{1,0:T(8,128)(2,1)S(1)}, u32[]{:S(2)}, u32[]{:S(2)}) collective-permute-start(bf16[128,1024]{1,0:T(8,128)(2,1)S(1)} %get-tuple-element.78), channel_id=1, source_target_pairs={{0,12},{1,13},{2,14},{3,15},{4,8},{5,9},{6,10},{7,11},{8,4},{9,5},... | collective-permute-start | bytes 786440 | tf_op jit(solution)/shard_map/sum_grads/ppermute | solution.py:24
  189.6 18.3 %collective-permute-done.45.rest_4_ = bf16[128,1024]{1,0:T(8,128)(2,1)S(1)} collective-permute-done((bf16[128,1024]{1,0:T(8,128)(2,1)S(1)}, bf16[128,1024]{1,0:T(8,128)(2,1)S(1)}, u32[]{:S(2)}, u32[]{:S(2)}) %collective-permute-start.45) | collective-permute-done | bytes 262176 | tf_op jit(solution)/shard_map/sum_grads/ppermute | solution.py:24
  (132 shorter events, 52.4 us)
Async XLA Ops:
  1.6 7.7 %collective-permute-start.3 = (bf16[512,128]{1,0:T(8,128)(2,1)S(1)}, bf16[512,128]{1,0:T(8,128)(2,1)S(1)}, u32[]{:S(2)}, u32[]{:S(2)}) collective-permute-start(bf16[512,128]{1,0:T(8,128)(2,1)S(1)} %get-tuple-element.92), channel_id=1, source_target_pairs={{0,6},{1,7},{2,0},{3,1},{4,2},{5,3},{6,4},{7,5},{8,14},{9,15},{10,... | collective-permute-start | bytes 393224 | tf_op jit(solution)/shard_map/gather_features/ppermute | solution.py:24
  4.5 8.1 %collective-permute-start.2 = (bf16[512,128]{1,0:T(8,128)(2,1)S(1)}, bf16[512,128]{1,0:T(8,128)(2,1)S(1)}, u32[]{:S(2)}, u32[]{:S(2)}) collective-permute-start(bf16[512,128]{1,0:T(8,128)(2,1)S(1)} %get-tuple-element.93), channel_id=1, source_target_pairs={{0,6},{1,7},{2,0},{3,1},{4,2},{5,3},{6,4},{7,5},{8,14},{9,15},{10,... | collective-permute-start | bytes 393224 | tf_op jit(solution)/shard_map/gather_features/ppermute | solution.py:24
  7.8 8.4 %collective-permute-start.6 = (bf16[1024,128]{1,0:T(8,128)(2,1)}, bf16[1024,128]{1,0:T(8,128)(2,1)S(1)}, u32[]{:S(2)}, u32[]{:S(2)}) collective-permute-start(bf16[1024,128]{1,0:T(8,128)(2,1)} %feats.3), channel_id=1, source_target_pairs={{0,8},{1,9},{2,10},{3,11},{4,12},{5,13},{6,14},{7,15},{8,0},{9,1},... | collective-permute-start | bytes 786440 | tf_op jit(solution)/shard_map/gather_features/ppermute | solution.py:24
  15.5 8.9 %collective-permute-start.11 = (bf16[1024,128]{1,0:T(8,128)(2,1)}, bf16[1024,128]{1,0:T(8,128)(2,1)S(1)}, u32[]{:S(2)}, u32[]{:S(2)}) collective-permute-start(bf16[1024,128]{1,0:T(8,128)(2,1)} %feats.3), channel_id=1, source_target_pairs={{0,1},{1,0},{2,3},{3,2},{4,5},{5,4},{6,7},{7,6},{8,9},{9,8},{10,11... | collective-permute-start | bytes 786440 | tf_op jit(solution)/shard_map/gather_features/ppermute | solution.py:24
  16.1 7.8 %collective-permute-start.4 = (bf16[512,128]{1,0:T(8,128)(2,1)S(1)}, bf16[512,128]{1,0:T(8,128)(2,1)S(1)}, u32[]{:S(2)}, u32[]{:S(2)}) collective-permute-start(bf16[512,128]{1,0:T(8,128)(2,1)S(1)} %collective-permute-done.rest_1_), channel_id=1, source_target_pairs={{0,2},{1,3},{2,4},{3,5},{4,6},{5,7},{6,0},{7,1},{8,10},{9,11},{10,... | collective-permute-start | bytes 393224 | tf_op jit(solution)/shard_map/gather_features/ppermute | solution.py:24
  16.1 14.1 %collective-permute-start.8 = (bf16[1024,128]{1,0:T(8,128)(2,1)S(1)}, bf16[1024,128]{1,0:T(8,128)(2,1)S(1)}, u32[]{:S(2)}, u32[]{:S(2)}) collective-permute-start(bf16[1024,128]{1,0:T(8,128)(2,1)S(1)} %collective-permute-done.6.rest_7_), channel_id=1, source_target_pairs={{0,6},{1,7},{2,0},{3,1},{4,2},{5,3},{6,4},{7,5},{8,14},{9,15},{10,... | collective-permute-start | bytes 786440 | tf_op jit(solution)/shard_map/gather_features/ppermute | solution.py:24
  19.8 11.0 %collective-permute-start.7 = (bf16[1024,128]{1,0:T(8,128)(2,1)S(1)}, bf16[1024,128]{1,0:T(8,128)(2,1)S(1)}, u32[]{:S(2)}, u32[]{:S(2)}) collective-permute-start(bf16[1024,128]{1,0:T(8,128)(2,1)S(1)} %collective-permute-done.6.rest_7_), channel_id=1, source_target_pairs={{0,2},{1,3},{2,4},{3,5},{4,6},{5,7},{6,0},{7,1},{8,10},{9,11},{10,... | collective-permute-start | bytes 786440 | tf_op jit(solution)/shard_map/gather_features/ppermute | solution.py:24
  24.4 7.7 %collective-permute-start.9 = (bf16[512,128]{1,0:T(8,128)(2,1)S(1)}, bf16[512,128]{1,0:T(8,128)(2,1)}, u32[]{:S(2)}, u32[]{:S(2)}) collective-permute-start(bf16[512,128]{1,0:T(8,128)(2,1)S(1)} %collective-permute-done.4.rest_5_), channel_id=1, source_target_pairs={{0,8},{1,9},{2,10},{3,11},{4,12},{5,13},{6,14},{7,15},{8,0},{9,1},... | collective-permute-start | bytes 393224 | tf_op jit(solution)/shard_map/gather_features/ppermute | solution.py:24
  53.1 14.2 %collective-permute-start.23 = (bf16[1024,128]{1,0:T(8,128)(2,1)S(1)}, bf16[1024,128]{1,0:T(8,128)(2,1)S(1)}, u32[]{:S(2)}, u32[]{:S(2)}) collective-permute-start(bf16[1024,128]{1,0:T(8,128)(2,1)S(1)} %get-tuple-element.49), channel_id=1, source_target_pairs={{0,32},{16,48},{32,64},{48,80},{64,96},{80,112},{96,0},{112,16},{1... | collective-permute-start | bytes 786440 | tf_op jit(solution)/shard_map/sum_aggregates/ppermute | solution.py:32
  53.1 14.3 %collective-permute-start.24 = (bf16[1024,128]{1,0:T(8,128)(2,1)S(1)}, bf16[1024,128]{1,0:T(8,128)(2,1)S(1)}, u32[]{:S(2)}, u32[]{:S(2)}) collective-permute-start(bf16[1024,128]{1,0:T(8,128)(2,1)S(1)} %get-tuple-element.50), channel_id=1, source_target_pairs={{0,64},{16,80},{32,96},{48,112},{64,0},{80,16},{96,32},{112,48},{1... | collective-permute-start | bytes 786440 | tf_op jit(solution)/shard_map/sum_aggregates/ppermute | solution.py:32
  53.2 16.9 %collective-permute-start.25 = (bf16[1024,128]{1,0:T(8,128)(2,1)S(1)}, bf16[1024,128]{1,0:T(8,128)(2,1)S(1)}, u32[]{:S(2)}, u32[]{:S(2)}) collective-permute-start(bf16[1024,128]{1,0:T(8,128)(2,1)S(1)} %get-tuple-element.51), channel_id=1, source_target_pairs={{0,96},{16,112},{32,0},{48,16},{64,32},{80,48},{96,64},{112,80},{1... | collective-permute-start | bytes 786440 | tf_op jit(solution)/shard_map/sum_aggregates/ppermute | solution.py:32
  56.4 13.7 %collective-permute-start.26 = (bf16[1024,128]{1,0:T(8,128)(2,1)S(1)}, bf16[1024,128]{1,0:T(8,128)(2,1)S(1)}, u32[]{:S(2)}, u32[]{:S(2)}) collective-permute-start(bf16[1024,128]{1,0:T(8,128)(2,1)S(1)} %get-tuple-element.52), channel_id=1, source_target_pairs={{0,16},{16,0},{32,48},{48,32},{64,80},{80,64},{96,112},{112,96},{1... | collective-permute-start | bytes 786440 | tf_op jit(solution)/shard_map/sum_aggregates/ppermute | solution.py:32
  61.4 12.8 %collective-permute-start.27 = (bf16[1024,128]{1,0:T(8,128)(2,1)S(1)}, bf16[1024,128]{1,0:T(8,128)(2,1)S(1)}, u32[]{:S(2)}, u32[]{:S(2)}) collective-permute-start(bf16[1024,128]{1,0:T(8,128)(2,1)S(1)} %get-tuple-element.53), channel_id=1, source_target_pairs={{0,48},{16,32},{32,80},{48,64},{64,112},{80,96},{96,16},{112,0},{1... | collective-permute-start | bytes 786440 | tf_op jit(solution)/shard_map/sum_aggregates/ppermute | solution.py:32
  67.3 12.6 %collective-permute-start.28 = (bf16[1024,128]{1,0:T(8,128)(2,1)S(1)}, bf16[1024,128]{1,0:T(8,128)(2,1)S(1)}, u32[]{:S(2)}, u32[]{:S(2)}) collective-permute-start(bf16[1024,128]{1,0:T(8,128)(2,1)S(1)} %get-tuple-element.54), channel_id=1, source_target_pairs={{0,80},{16,64},{32,112},{48,96},{64,16},{80,0},{96,48},{112,32},{1... | collective-permute-start | bytes 786440 | tf_op jit(solution)/shard_map/sum_aggregates/ppermute | solution.py:32
  67.5 18.0 %collective-permute-start.29 = (bf16[1024,128]{1,0:T(8,128)(2,1)S(1)}, bf16[1024,128]{1,0:T(8,128)(2,1)S(1)}, u32[]{:S(2)}, u32[]{:S(2)}) collective-permute-start(bf16[1024,128]{1,0:T(8,128)(2,1)S(1)} %get-tuple-element.55), channel_id=1, source_target_pairs={{0,112},{16,96},{32,16},{48,0},{64,48},{80,32},{96,80},{112,64},{1... | collective-permute-start | bytes 786440 | tf_op jit(solution)/shard_map/sum_aggregates/ppermute | solution.py:32
  87.6 18.2 %collective-permute-start.36 = (bf16[128,1024]{1,0:T(8,128)(2,1)S(1)}, bf16[128,1024]{1,0:T(8,128)(2,1)S(1)}, u32[]{:S(2)}, u32[]{:S(2)}) collective-permute-start(bf16[128,1024]{1,0:T(8,128)(2,1)S(1)} %get-tuple-element.60.rest_0_), channel_id=1, source_target_pairs={{0,16},{16,0},{32,48},{48,32},{64,80},{80,64},{96,112},{112,96},{1... | collective-permute-start | bytes 786440 | tf_op jit(solution)/shard_map/gather_dz/ppermute | solution.py:32
  99.4 9.7 %collective-permute-start.30 = (bf16[128,512]{1,0:T(8,128)(2,1)S(1)}, bf16[128,512]{1,0:T(8,128)(2,1)S(1)}, u32[]{:S(2)}, u32[]{:S(2)}) collective-permute-start(bf16[128,512]{1,0:T(8,128)(2,1)S(1)} %get-tuple-element.61), channel_id=1, source_target_pairs={{0,96},{16,112},{32,0},{48,16},{64,32},{80,48},{96,64},{112,80},{1... | collective-permute-start | bytes 393224 | tf_op jit(solution)/shard_map/gather_dz/ppermute | solution.py:32
  102.3 7.6 %collective-permute-start.33 = (bf16[128,512]{1,0:T(8,128)(2,1)S(1)}, bf16[128,512]{1,0:T(8,128)(2,1)S(1)}, u32[]{:S(2)}, u32[]{:S(2)}) collective-permute-start(bf16[128,512]{1,0:T(8,128)(2,1)S(1)} %collective-permute-done.32.rest_5_), channel_id=1, source_target_pairs={{0,32},{16,48},{32,64},{48,80},{64,96},{80,112},{96,0},{112,16},{1... | collective-permute-start | bytes 393224 | tf_op jit(solution)/shard_map/gather_dz/ppermute | solution.py:32
  102.3 7.6 %collective-permute-start.34 = (bf16[128,512]{1,0:T(8,128)(2,1)S(1)}, bf16[128,512]{1,0:T(8,128)(2,1)S(1)}, u32[]{:S(2)}, u32[]{:S(2)}) collective-permute-start(bf16[128,512]{1,0:T(8,128)(2,1)S(1)} %collective-permute-done.31.rest_2_), channel_id=1, source_target_pairs={{0,96},{16,112},{32,0},{48,16},{64,32},{80,48},{96,64},{112,80},{1... | collective-permute-start | bytes 393224 | tf_op jit(solution)/shard_map/gather_dz/ppermute | solution.py:32
  105.8 12.0 %collective-permute-start.40 = (bf16[128,1024]{1,0:T(8,128)(2,1)S(1)}, bf16[128,1024]{1,0:T(8,128)(2,1)S(1)}, u32[]{:S(2)}, u32[]{:S(2)}) collective-permute-start(bf16[128,1024]{1,0:T(8,128)(2,1)S(1)} %collective-permute-done.36.rest_7_), channel_id=1, source_target_pairs={{0,32},{16,48},{32,64},{48,80},{64,96},{80,112},{96,0},{112,16},{1... | collective-permute-start | bytes 786440 | tf_op jit(solution)/shard_map/gather_dz/ppermute | solution.py:32
  105.8 12.0 %collective-permute-start.37 = (bf16[128,1024]{1,0:T(8,128)(2,1)S(1)}, bf16[128,1024]{1,0:T(8,128)(2,1)S(1)}, u32[]{:S(2)}, u32[]{:S(2)}) collective-permute-start(bf16[128,1024]{1,0:T(8,128)(2,1)S(1)} %collective-permute-done.36.rest_7_), channel_id=1, source_target_pairs={{0,96},{16,112},{32,0},{48,16},{64,32},{80,48},{96,64},{112,80},{1... | collective-permute-start | bytes 786440 | tf_op jit(solution)/shard_map/gather_dz/ppermute | solution.py:32
  110.0 7.9 %collective-permute-start.39 = (bf16[128,512]{1,0:T(8,128)(2,1)S(1)}, bf16[128,512]{1,0:T(8,128)(2,1)S(1)}, u32[]{:S(2)}, u32[]{:S(2)}) collective-permute-start(bf16[128,512]{1,0:T(8,128)(2,1)S(1)} %collective-permute-done.34.rest_4_), channel_id=1, source_target_pairs={{0,16},{16,0},{32,48},{48,32},{64,80},{80,64},{96,112},{112,96},{1... | collective-permute-start | bytes 393224 | tf_op jit(solution)/shard_map/gather_dz/ppermute | solution.py:32
  137.4 47.0 %collective-permute-start.42 = (bf16[128,1024]{1,0:T(8,128)(2,1)S(1)}, bf16[128,1024]{1,0:T(8,128)(2,1)S(1)}, u32[]{:S(2)}, u32[]{:S(2)}) collective-permute-start(bf16[128,1024]{1,0:T(8,128)(2,1)S(1)} %get-tuple-element.73), channel_id=1, source_target_pairs={{0,2},{1,3},{2,4},{3,5},{4,6},{5,7},{6,0},{7,1},{8,10},{9,11},{10,... | collective-permute-start | bytes 786440 | tf_op jit(solution)/shard_map/sum_grads/ppermute | solution.py:24
  137.5 49.4 %collective-permute-start.43 = (bf16[128,1024]{1,0:T(8,128)(2,1)S(1)}, bf16[128,1024]{1,0:T(8,128)(2,1)S(1)}, u32[]{:S(2)}, u32[]{:S(2)}) collective-permute-start(bf16[128,1024]{1,0:T(8,128)(2,1)S(1)} %get-tuple-element.74), channel_id=1, source_target_pairs={{0,4},{1,5},{2,6},{3,7},{4,0},{5,1},{6,2},{7,3},{8,12},{9,13},{10,... | collective-permute-start | bytes 786440 | tf_op jit(solution)/shard_map/sum_grads/ppermute | solution.py:24
  137.6 16.4 %collective-permute-start.50 = (f32[32,256]{1,0:T(8,128)S(1)}, f32[32,256]{1,0:T(8,128)S(1)}, u32[]{:S(2)}, u32[]{:S(2)}) collective-permute-start(f32[32,256]{1,0:T(8,128)S(1)} %get-tuple-element.83), channel_id=1, source_target_pairs={{0,2},{1,3},{2,4},{3,5},{4,6},{5,7},{6,0},{7,1},{8,10},{9,11},{10,... | collective-permute-start | bytes 98312 | tf_op jit(solution)/shard_map/weights/ppermute | solution.py:24
  141.7 12.4 %collective-permute-start.51 = (f32[32,256]{1,0:T(8,128)S(1)}, f32[32,256]{1,0:T(8,128)S(1)}, u32[]{:S(2)}, u32[]{:S(2)}) collective-permute-start(f32[32,256]{1,0:T(8,128)S(1)} %get-tuple-element.84), channel_id=1, source_target_pairs={{0,4},{1,5},{2,6},{3,7},{4,0},{5,1},{6,2},{7,3},{8,12},{9,13},{10,... | collective-permute-start | bytes 98312 | tf_op jit(solution)/shard_map/weights/ppermute | solution.py:24
  142.3 11.8 %collective-permute-start.52 = (f32[32,256]{1,0:T(8,128)S(1)}, f32[32,256]{1,0:T(8,128)S(1)}, u32[]{:S(2)}, u32[]{:S(2)}) collective-permute-start(f32[32,256]{1,0:T(8,128)S(1)} %get-tuple-element.85), channel_id=1, source_target_pairs={{0,6},{1,7},{2,0},{3,1},{4,2},{5,3},{6,4},{7,5},{8,14},{9,15},{10,... | collective-permute-start | bytes 98312 | tf_op jit(solution)/shard_map/weights/ppermute | solution.py:24
  180.1 9.6 %collective-permute-start.44 = (bf16[128,1024]{1,0:T(8,128)(2,1)S(1)}, bf16[128,1024]{1,0:T(8,128)(2,1)S(1)}, u32[]{:S(2)}, u32[]{:S(2)}) collective-permute-start(bf16[128,1024]{1,0:T(8,128)(2,1)S(1)} %get-tuple-element.75), channel_id=1, source_target_pairs={{0,6},{1,7},{2,0},{3,1},{4,2},{5,3},{6,4},{7,5},{8,14},{9,15},{10,... | collective-permute-start | bytes 786440 | tf_op jit(solution)/shard_map/sum_grads/ppermute | solution.py:24
  182.5 25.4 %collective-permute-start.45 = (bf16[128,1024]{1,0:T(8,128)(2,1)S(1)}, bf16[128,1024]{1,0:T(8,128)(2,1)S(1)}, u32[]{:S(2)}, u32[]{:S(2)}) collective-permute-start(bf16[128,1024]{1,0:T(8,128)(2,1)S(1)} %get-tuple-element.76), channel_id=1, source_target_pairs={{0,8},{1,9},{2,10},{3,11},{4,12},{5,13},{6,14},{7,15},{8,0},{9,1},... | collective-permute-start | bytes 786440 | tf_op jit(solution)/shard_map/sum_grads/ppermute | solution.py:24
  184.4 23.5 %collective-permute-start.46 = (bf16[128,1024]{1,0:T(8,128)(2,1)S(1)}, bf16[128,1024]{1,0:T(8,128)(2,1)S(1)}, u32[]{:S(2)}, u32[]{:S(2)}) collective-permute-start(bf16[128,1024]{1,0:T(8,128)(2,1)S(1)} %get-tuple-element.77), channel_id=1, source_target_pairs={{0,10},{1,11},{2,12},{3,13},{4,14},{5,15},{6,8},{7,9},{8,2},{9,3},... | collective-permute-start | bytes 786440 | tf_op jit(solution)/shard_map/sum_grads/ppermute | solution.py:24
  184.4 23.5 %collective-permute-start.47 = (bf16[128,1024]{1,0:T(8,128)(2,1)S(1)}, bf16[128,1024]{1,0:T(8,128)(2,1)S(1)}, u32[]{:S(2)}, u32[]{:S(2)}) collective-permute-start(bf16[128,1024]{1,0:T(8,128)(2,1)S(1)} %get-tuple-element.78), channel_id=1, source_target_pairs={{0,12},{1,13},{2,14},{3,15},{4,8},{5,9},{6,10},{7,11},{8,4},{9,5},... | collective-permute-start | bytes 786440 | tf_op jit(solution)/shard_map/sum_grads/ppermute | solution.py:24
  186.9 21.0 %collective-permute-start.48 = (bf16[128,1024]{1,0:T(8,128)(2,1)S(1)}, bf16[128,1024]{1,0:T(8,128)(2,1)S(1)}, u32[]{:S(2)}, u32[]{:S(2)}) collective-permute-start(bf16[128,1024]{1,0:T(8,128)(2,1)S(1)} %get-tuple-element.79), channel_id=1, source_target_pairs={{0,14},{1,15},{2,8},{3,9},{4,10},{5,11},{6,12},{7,13},{8,6},{9,7},... | collective-permute-start | bytes 786440 | tf_op jit(solution)/shard_map/sum_grads/ppermute | solution.py:24
  (42 other events, 366.4 us)

commit v2 on v1

v2 whole, which is shorter than its diff:
```python
import functools

import jax
import jax.numpy as jnp
from jax import lax
from jax.experimental import pallas as pl
from jax.experimental.pallas import tpu as pltpu
from jax.sharding import PartitionSpec as P

TILE = 256
VMEM = pltpu.VMEM
BF16 = jnp.bfloat16
F32 = jnp.float32
LIMIT = 12 * 1024 * 1024
GROUP = 16
ROOM = 144

ORDER = [(0, 0), (0, 3), (0, 1), (1, 0), (0, 2), (1, 3), (1, 1), (1, 2)]
OWN, LEFT, RIGHT, PAIR, OPPOSITE, PAIR_LEFT, PAIR_RIGHT, PAIR_OPPOSITE = range(8)
PLACE = sum(ORDER.index((k // 4, k % 4)) << (4 * k) for k in range(8))


def hop_col(value, dy, dx, dc=0):
    pairs = []
    for y in range(2):
        for x in range(4):
            for c in range(2):
                to = (((y + dy) % 2) * 4 + (x + dx) % 4) * 2 + (c + dc) % 2
                pairs.append(((y * 4 + x) * 2 + c, to))
    return lax.ppermute(value, "col", pairs)


def hop_row(value, dy, dz):
    pairs = []
    for z in range(4):
        for y in range(2):
            pairs.append((z * 2 + y, ((z + dz) % 4) * 2 + (y + dy) % 2))
    return lax.ppermute(value, "row", pairs)


def hop_diag(value):
    pairs = []
    for r in range(8):
        for c in range(16):
            pairs.append((r * 16 + c, (r ^ 1) * 16 + (c ^ 8)))
    return lax.ppermute(value, ("row", "col"), pairs)


def in_vmem(*values):
    return [pltpu.with_memory_space_constraint(v, VMEM) for v in values]


def vmem_specs(n):
    return [pl.BlockSpec(memory_space=VMEM)] * n


def call(body, outs, vmem_args, smem_args=(), after=(), scratch=(), alias=None, flops=0, nbytes=0):
    single = not isinstance(outs, (list, tuple))
    skip = len(smem_args) + len(vmem_args)

    def run(*refs):
        body(*refs[:skip], *refs[skip + len(after) :])

    return pl.pallas_call(
        run,
        out_shape=outs,
        in_specs=[pl.BlockSpec(memory_space=pltpu.SMEM)] * len(smem_args)
        + vmem_specs(len(vmem_args))
        + [pl.BlockSpec(memory_space=pl.ANY)] * len(after),
        out_specs=pl.BlockSpec(memory_space=VMEM) if single else vmem_specs(len(outs)),
        scratch_shapes=list(scratch),
        input_output_aliases=alias or {},
        compiler_params=pltpu.CompilerParams(vmem_limit_bytes=LIMIT),
        cost_estimate=pl.CostEstimate(flops=flops, bytes_accessed=nbytes, transcendentals=0),
    )(*smem_args, *in_vmem(*vmem_args), *after)


def places():
    return lax.axis_index("col"), lax.axis_index("row")


def first_round(value, step, swap):
    return [value, step(value, 1), step(value, -1), swap(value), step(value, 2)]


def second_round(near, step, swap):
    return [step(near[PAIR], 1), step(near[PAIR], -1), swap(near[OPPOSITE])]


def place_of(index, me, other_bit, ring_shift):
    other = ((index ^ me) >> other_bit) & 1
    offset = ((index >> ring_shift) - (me >> ring_shift)) & 3
    return (PLACE >> ((other * 4 + offset) * 4)) & 15


def plan_body(pairs, count, tiles, held, lists, sizes, sems):
    copies = []
    for k in range(8):
        part = pl.ds(16 * k, 16)
        copies.append(pltpu.make_async_copy(tiles.at[part], held.at[part], sems.at[k]))
        copies[-1].start()
    col, row = places()
    for k in range(8):
        sizes[k] = 0

    def put(which, entry):
        at = sizes[which]
        lists[which * ROOM + at] = entry
        sizes[which] = at + 1

    def sort(i, carry):
        d = pairs[2 * i]
        s = pairs[2 * i + 1]
        c = s >> 2
        q = d >> 2
        sib = (c ^ col) & 1
        source = place_of(c, col, 3, 1) * 4 + (s & 3)
        target = place_of(q, row, 0, 1) * 4 + (d & 3)
        put((source >> 4) * 2 + sib, i | (target << 8) | ((source & 15) << 16))
        put(4 + (target >> 4) * 2 + sib, i | ((target & 15) << 8) | (source << 16))
        return carry

    lax.fori_loop(0, count[0], sort, 0)
    for k in range(8):
        at = sizes[k]
        for j in range(GROUP - 1):
            lists[k * ROOM + at + j] = 32 << 8 if k < 4 else 32 << 16
    for copy in copies:
        copy.wait()


def over_list(which, lists, sizes, product, total, to_target):
    def step(g, carry):
        news = []
        for j in range(GROUP):
            entry = lists[which * ROOM + g * GROUP + j]
            i = entry & 255
            d = (entry >> 8) & 255
            s = entry >> 16
            news.append((d if to_target else s, product(i, d, s)))
        for at, new in news:
            total[at] += new
        return carry

    lax.fori_loop(0, (sizes[which] + GROUP - 1) // GROUP, step, 0)


def pack_body(*rest):
    for k in range(4):
        rest[4][4 * k : 4 * k + 4] = rest[k][...].reshape(4, TILE, 128)
    for out in rest[5:]:
        out[...] = rest[PAIR][...]


def forward_step(lists, sizes, tiles, which, blocks, total):
    def product(i, d, s):
        return jnp.dot(tiles[i], blocks[s], preferred_element_type=F32)

    over_list(which, lists, sizes, product, total, True)


def forward_near_body(lists, sizes, tiles, mine, sib, total):
    total[...] = jnp.zeros_like(total)
    forward_step(lists, sizes, tiles, 0, mine, total)
    forward_step(lists, sizes, tiles, 1, sib, total)


def forward_far_body(lists, sizes, tiles, mine, before, total):
    forward_step(lists, sizes, tiles, 2, mine, total)


def forward_last_body(lists, sizes, tiles, sib, before, total, *outs):
    forward_step(lists, sizes, tiles, 3, sib, total)
    for k in range(8):
        outs[k][...] = total[4 * k : 4 * k + 4].reshape(1024, 128).astype(outs[k].dtype)


def hold_dz(parts, held):
    for k, ref in enumerate(parts):
        for b in range(4):
            held[4 * k + b] = ref[:, b * TILE : (b + 1) * TILE]


def backward_step(lists, sizes, tiles, which, held, total):
    def product(i, d, s):
        return jnp.dot(held[d], tiles[i], preferred_element_type=F32)

    over_list(which, lists, sizes, product, total, False)


def backward_near_body(lists, sizes, tiles, *rest):
    parts, (mine, sib, held) = rest[:4], rest[4:]
    hold_dz(parts, held)
    mine[...] = jnp.zeros_like(mine)
    sib[...] = jnp.zeros_like(sib)
    backward_step(lists, sizes, tiles, 5, held, sib)
    backward_step(lists, sizes, tiles, 4, held, mine)


def write_places(total, first, outs):
    for k, ref in enumerate(outs):
        for b in range(4):
            ref[:, b * TILE : (b + 1) * TILE] = total[4 * (first + k) + b].astype(ref.dtype)


def backward_sib_body(lists, sizes, tiles, *rest):
    parts, (before, sib, far, near, held) = rest[:4], rest[4:]
    hold_dz(parts, held)
    backward_step(lists, sizes, tiles, 7, held, sib)
    write_places(sib, PAIR_LEFT, [far.at[k] for k in range(3)])
    write_places(sib, OWN, [near.at[k] for k in range(5)])


def backward_mine_body(lists, sizes, tiles, *rest):
    parts, (before, mine, held) = rest[:4], rest[4:]
    hold_dz(parts, held)
    backward_step(lists, sizes, tiles, 6, held, mine)


def add_sib_body(first, mine, got, *outs):
    for k, ref in enumerate(outs):
        for b in range(4):
            nodes = slice(b * TILE, (b + 1) * TILE)
            new = mine[4 * (first + k) + b] + got[k, :, nodes].astype(F32)
            ref[:, nodes] = new.astype(ref.dtype)


def add_round_body(pair, opposite, a, b, c, pair_out, opposite_out):
    new = pair[...] + (a[...].astype(F32) + b[...].astype(F32))
    pair_out[...] = new.astype(BF16)
    opposite_out[...] = (opposite[...] + c[...].astype(F32)).astype(BF16)


def reduce_places(parts, step, swap, after=()):
    shape = parts[OWN].shape
    for_pair = [step(parts[PAIR_LEFT], -1), step(parts[PAIR_RIGHT], 1)]
    for_opposite = swap(parts[PAIR_OPPOSITE])
    left = step(parts[LEFT], -1)
    right = step(parts[RIGHT], 1)
    pair, opposite = call(
        add_round_body,
        [VMEM(shape, BF16)] * 2,
        [parts[PAIR], parts[OPPOSITE], *for_pair, for_opposite],
        after=after,
        nbytes=4 << 20,
    )
    return [parts[OWN], left, right, step(opposite, 2), swap(pair)]


def dense_body(bias, feats, upstream, w_self, w_neigh, *rest):
    sums = rest[:5]
    hidden, dpre_out, agg_out, dz_out = rest[5:]
    for b in range(4):
        rows = slice(b * TILE, (b + 1) * TILE)
        agg = sums[0][rows]
        for ref in sums[1:]:
            agg = agg + ref[rows].astype(F32)
        agg = agg.astype(BF16)
        agg_out[rows] = agg
        pre = jnp.dot(feats[rows], w_self[...], preferred_element_type=F32)
        pre = pre + jnp.dot(agg, w_neigh[...], preferred_element_type=F32) + bias[...]
        sig = jax.nn.sigmoid(pre)
        hidden[rows] = (pre * sig).astype(BF16)
        slope = sig * (1.0 + pre * (1.0 - sig))
        dpre = (upstream[rows].astype(F32) * slope).astype(BF16)
        dpre_out[rows] = dpre
        dz = lax.dot_general(
            w_neigh[...], dpre, (((1,), (1,)), ((), ())), preferred_element_type=F32
        ).astype(BF16)
        dz_out[:, rows] = dz


def weights_body(feats, agg, dpre, w_self, keep, send, own_grad):
    over_nodes = (((0,), (0,)), ((), ()))
    grad_self = lax.dot_general(feats[...], dpre[...], over_nodes, preferred_element_type=F32)
    grad_neigh = lax.dot_general(agg[...], dpre[...], over_nodes, preferred_element_type=F32)
    first = lax.axis_index("col") % 2 == 0

    @pl.when(first)
    def _():
        keep[...] = grad_self
        send[...] = grad_neigh

    @pl.when(jnp.logical_not(first))
    def _():
        keep[...] = grad_neigh
        send[...] = grad_self

    own_grad[...] = lax.dot_general(
        w_self[...], dpre[...], (((1,), (1,)), ((), ())), preferred_element_type=F32
    )


def finish_body(own_grad, *rest):
    out = rest[-1]
    for b in range(4):
        nodes = slice(b * TILE, (b + 1) * TILE)
        total = own_grad[:, nodes]
        for ref in rest[:-1]:
            total = total + ref[:, nodes].astype(F32)
        out[nodes] = total.T.astype(BF16)


def ring_place(axis):
    col, row = places()
    return (col >> 1) & 3 if axis == "x" else row >> 1


def sum_split_body(axis, n_in, *rest):
    ins, outs = rest[:n_in], rest[n_in : n_in + 4]
    held = rest[n_in + 4]
    total = ins[0][...]
    for ref in ins[1:]:
        total = total + ref[...]
    held[...] = total
    me = ring_place(axis)
    size = outs[0].shape[0]
    for k in range(4):
        at = pl.multiple_of(((me + k) & 3) * size, size)
        outs[k][...] = held[pl.ds(at, size), :]


def sum_body(*rest):
    total = rest[0][...]
    for ref in rest[1:-1]:
        total = total + ref[...]
    rest[-1][...] = total


def pair_sum_body(a, b, c, d, out):
    out[...] = (a[...] + b[...]) + (c[...] + d[...])


def join_body(axis, *rest):
    me = ring_place(axis)
    out = rest[4]
    size = rest[0].shape[0]
    for k in range(4):
        at = pl.multiple_of(((me + k) & 3) * size, size)
        out[pl.ds(at, size), :] = rest[k][...]


def place_body(scale, mine, other, grad_self, grad_neigh):
    first = lax.axis_index("col") % 2 == 0
    a = mine[...] * scale
    b = other[...] * scale
    grad_self[...] = jnp.where(first, a, b)
    grad_neigh[...] = jnp.where(first, b, a)


def sum_weights_down(keep, send, first):
    def f32(rows):
        return VMEM((rows, 256), F32)

    got = hop_col(send, 0, 0, 1)
    pieces = call(
        functools.partial(sum_split_body, "x", 2), [f32(32)] * 4, [keep, got], scratch=[f32(128)]
    )
    got = [pieces[0]] + [hop_col(pieces[k], 0, k) for k in (1, 2, 3)]
    pieces = call(
        functools.partial(sum_split_body, "z", 4),
        [f32(8)] * 4,
        got,
        after=[first],
        scratch=[f32(32)],
    )
    got = [pieces[0]] + [hop_row(pieces[k], 0, k) for k in (1, 2, 3)]
    part = call(sum_body, f32(8), got)
    whole = call(
        pair_sum_body, f32(8), [part, hop_col(part, 1, 0), hop_row(part, 1, 0), hop_diag(part)]
    )
    return pieces[0], whole


def gather_weights_rings(whole):
    def f32(rows):
        return VMEM((rows, 256), F32)

    got = [whole] + [hop_row(whole, 0, -k) for k in (1, 2, 3)]
    quarter = call(functools.partial(join_body, "z"), f32(32), got)
    got = [quarter] + [hop_col(quarter, 0, -k) for k in (1, 2, 3)]
    return quarter, call(functools.partial(join_body, "x"), f32(128), got)


def gather_weights_cores(half, scale):
    other = hop_col(half, 0, 0, 1)
    shape = jax.ShapeDtypeStruct((128, 256), F32)
    return call(functools.partial(place_body, scale), [shape, shape], [half, other])


def shards(
    features, weight_self, weight_neigh, bias_term, upstream, tile_values, block_pairs, tile_counts
):
    nodes = 131072
    tile_bytes = 128 * TILE * TILE * 2
    share = 32 * 2 * TILE * TILE * 128
    in_hbm = pltpu.with_memory_space_constraint(tile_values.reshape(128, TILE, TILE), pltpu.HBM)
    with jax.named_scope("plan"):
        tiles, lists, sizes = pl.pallas_call(
            plan_body,
            out_shape=[
                VMEM((128, TILE, TILE), BF16),
                pltpu.SMEM((8 * ROOM,), jnp.int32),
                pltpu.SMEM((8,), jnp.int32),
            ],
            in_specs=[pl.BlockSpec(memory_space=pltpu.SMEM)] * 2
            + [pl.BlockSpec(memory_space=pl.ANY)],
            out_specs=[pl.BlockSpec(memory_space=VMEM)]
            + [pl.BlockSpec(memory_space=pltpu.SMEM)] * 2,
            scratch_shapes=[pltpu.SemaphoreType.DMA((8,))],
            compiler_params=pltpu.CompilerParams(vmem_limit_bytes=LIMIT),
            cost_estimate=pl.CostEstimate(flops=0, bytes_accessed=tile_bytes, transcendentals=0),
        )(block_pairs.reshape(-1), tile_counts.reshape(-1), in_hbm)
    by_list = [lists, sizes]

    with jax.named_scope("gather_features"):
        step, swap = (lambda v, d: hop_col(v, 0, d)), (lambda v: hop_col(v, 1, 0))
        packed = VMEM((16, TILE, 128), BF16)
        near = first_round(features, step, swap)
        near_mine, near[PAIR] = call(
            pack_body, [packed, VMEM((1024, 128), BF16)], near[:4], after=[sizes], nbytes=2 << 20
        )
        far = [near[OPPOSITE], *second_round(near, step, swap)]
        near_sib = hop_col(near_mine, 0, 0, 1)
        far_mine = call(pack_body, packed, far, nbytes=2 << 20)
        far_sib = hop_col(far_mine, 0, 0, 1)
    with jax.named_scope("forward_tiles"):
        total = VMEM((33, TILE, 128), F32)
        sums = call(
            forward_near_body,
            total,
            [tiles, near_mine, near_sib],
            by_list,
            flops=2 * share,
            nbytes=tile_bytes // 2,
        )
        sums = call(
            forward_far_body,
            total,
            [tiles, far_mine, sums],
            by_list,
            alias={4: 0},
            flops=share,
            nbytes=tile_bytes // 4,
        )
        f32, bf16 = VMEM((1024, 128), F32), VMEM((1024, 128), BF16)
        _, *partial = call(
            forward_last_body,
            [total, f32, bf16, bf16, f32, f32, bf16, bf16, bf16],
            [tiles, far_sib, sums],
            by_list,
            alias={4: 0},
            flops=share,
            nbytes=tile_bytes // 4,
        )
    with jax.named_scope("sum_aggregates"):
        step, swap = (lambda v, d: hop_row(v, 0, d)), (lambda v: hop_row(v, 1, 0))
        sums = reduce_places(partial, step, swap)
    with jax.named_scope("dense"):
        hidden, dpre, agg, dz = call(
            dense_body,
            [
                jax.ShapeDtypeStruct((1024, 256), BF16),
                VMEM((1024, 256), BF16),
                VMEM((1024, 128), BF16),
                VMEM((128, 1024), BF16),
            ],
            [bias_term.reshape(1, 256), features, upstream, weight_self, weight_neigh, *sums],
            flops=3 * 2 * 1024 * 128 * 256,
            nbytes=6 << 20,
        )
    with jax.named_scope("gather_dz"):
        near = first_round(dz, step, swap)
        far = [near[OPPOSITE], *second_round(near, step, swap)]
    with jax.named_scope("weights"):
        keep, send, own_grad = call(
            weights_body,
            [VMEM((128, 256), F32), VMEM((128, 256), F32), VMEM((128, 1024), F32)],
            [features, agg, dpre, weight_self],
            flops=3 * 2 * 1024 * 128 * 256,
            nbytes=2 << 20,
        )
        early, whole = sum_weights_down(keep, send, near[PAIR])
    with jax.named_scope("backward_tiles"):
        total = VMEM((33, 128, TILE), F32)
        held = [VMEM((16, 128, TILE), BF16)]
        mine, sib = call(
            backward_near_body,
            [total, total],
            [tiles, *near[:4]],
            by_list,
            after=[early],
            scratch=held,
            flops=2 * share,
            nbytes=tile_bytes // 2,
        )
        _, sib_far, sib_near = call(
            backward_sib_body,
            [total, VMEM((3, 128, 1024), BF16), VMEM((5, 128, 1024), BF16)],
            [tiles, *far, sib],
            by_list,
            after=[whole],
            alias={7: 0},
            scratch=held,
            flops=share,
            nbytes=tile_bytes // 4,
        )
        mine = call(
            backward_mine_body,
            total,
            [tiles, *far, mine],
            by_list,
            scratch=held,
            alias={7: 0},
            flops=share,
            nbytes=tile_bytes // 4,
        )
    with jax.named_scope("gather_weights"):
        quarter, half = gather_weights_rings(whole)
        grad_self, grad_neigh = gather_weights_cores(half, float(nodes) ** -0.5)
    with jax.named_scope("sum_grads"):
        step, swap = (lambda v, d: hop_col(v, 0, d)), (lambda v: hop_col(v, 1, 0))
        f32, bf16 = VMEM((128, 1024), F32), VMEM((128, 1024), BF16)
        far = call(
            functools.partial(add_sib_body, PAIR_LEFT),
            [bf16] * 3,
            [mine, hop_col(sib_far, 0, 0, 1)],
            nbytes=3 << 20,
        )
        near = call(
            functools.partial(add_sib_body, OWN),
            [f32, bf16, bf16, f32, f32],
            [mine, hop_col(sib_near, 0, 0, 1)],
            after=[quarter],
            nbytes=5 << 20,
        )
        sums = reduce_places([*near, *far], step, swap, [half])
    with jax.named_scope("finish"):
        grad_features = call(
            finish_body,
            jax.ShapeDtypeStruct((1024, 128), BF16),
            [own_grad, *sums],
            nbytes=4 << 20,
        )
    return hidden, grad_features, grad_self, grad_neigh


def solution(mesh):
    placed = (
        P(("row", "col"), None),
        P(),
        P(),
        P(),
        P(("row", "col"), None),
        P("row", "col", None, None, None),
        P("row", "col", None, None),
        P("row", "col"),
    )
    return jax.shard_map(
        shards,
        mesh=mesh,
        in_specs=placed,
        out_specs=(P(("row", "col"), None), P(("row", "col"), None), P(), P()),
        check_vma=False,
    )
```

time: 210 us -> 154 us (0.73)
  starting transfers between devices: 83.5 us -> 63.4 us
  waiting for transfers between devices: 82.8 us -> 64 us
  local copies, waits for them, and re-layouts: 15.9 us -> 0.95 us
  Pallas kernels: 25.2 us -> 22.4 us
    ppermute x25 -> x21, starting transfers between devices: 45.2 us -> 31.9 us  [hop_row(): return lax.ppermute(value, 'row', pairs)]
    unnamed x17 -> x11, local copies, waits for them, and re-layouts: 13.9 us -> 0.82 us
    ppermute x40 -> x27, waiting for transfers between devices: 48.4 us -> 37.3 us  [hop_col(): return lax.ppermute(value, 'col', pairs)]
    ppermute x40 -> x27, starting transfers between devices: 37.7 us -> 28.7 us  [hop_col(): return lax.ppermute(value, 'col', pairs)]
    ppermute x25 -> x21, waiting for transfers between devices: 33.6 us -> 26.7 us  [hop_row(): return lax.ppermute(value, 'row', pairs)]
    pallas_call x13 -> x23, Pallas kernels: 25.2 us -> 22.4 us  [the longest x22 15.9 us: call(): pl.pallas_call(run, out_shape=outs, in_specs=[pl.BlockSpec(memory_space=p...]
    ppermute x1, starting transfers between devices: 0.58 us -> 2.73 us  [hop_diag(): return lax.ppermute(value, ('row', 'col'), pairs)]
  transfers between devices with their start and end apart: 66 -> 49, of which waited for: 29 -> 22; matrix products, arithmetic and copies ran while one was open for 1% -> 1% of each run, Pallas kernels for 1% -> 11%
where the time goes in v2:
time: 154 us; the launch traced here: 152 us
  waiting for transfers between devices  64 us (42%)
  starting transfers between devices  63.4 us (41%)
  Pallas kernels  22.4 us (15%)
  between operations  1.65 us (1%)
    ppermute x27, waiting for transfers between devices, hop_col(): return lax.ppermute(value, 'col', pairs)  37.3 us
    ppermute x21, starting transfers between devices, hop_row(): return lax.ppermute(value, 'row', pairs)  31.9 us
    ppermute x27, starting transfers between devices, hop_col(): return lax.ppermute(value, 'col', pairs)  28.7 us
    ppermute x21, waiting for transfers between devices, hop_row(): return lax.ppermute(value, 'row', pairs)  26.7 us
    pallas_call x22, Pallas kernels, call(): pl.pallas_call(run, out_shape=outs, in_specs=[pl.BlockSpec(memory_space=p...  15.9 us
    pallas_call x1, Pallas kernels, shards(): pl.pallas_call(plan_body, out_shape=[VMEM((128, TILE, TILE), BF16), pltpu...  6.47 us
  transfers between devices with their start and end apart: 49, of which 22 were waited for; matrix products, arithmetic and copies ran while one was open for 1% of the time, Pallas kernels for 11%

profile of v2, /device:TPU:0, one launch (start us, length us, event | category | flops | bytes accessed | tf_op | source)
XLA Modules:
  0.0 152.3 jit_solution(3661319856874159791)
XLA Ops:
  5.6 1.8 %collective-permute-start = (bf16[1024,128]{1,0:T(8,128)(2,1)}, bf16[1024,128]{1,0:T(8,128)(2,1)S(1)}, u32[]{:S(2)}, u32[]{:S(2)}) collective-permute-start(bf16[1024,128]{1,0:T(8,128)(2,1)} %refs_0_.3), channel_id=1, source_target_pairs={{0,4},{1,5},{2,6},{3,7},{4,0},{5,1},{6,2},{7,3},{8,12},{9,13},{10,... | collective-permute-start | bytes 786440 | tf_op jit(solution)/shard_map/gather_features/ppermute | solution.py:30
  9.0 6.5 %plan.1 = (bf16[128,256,256]{2,1,0:T(8,128)(2,1)S(1)}, s32[1152]{0:T(1024)S(4)}, s32[8]{0:T(128)S(4)}) custom-call(s32[256]{0:T(256)S(1)} %reshape.21.pairs, s32[1]{0:T(128)} %bitcast.5.count, bf16[128,256,256]{2,1,0:T(8,128)(2,1)} %bitcast.7), custom_call_target="tpu_custom_call" | custom-call | bytes 16777216 | tf_op jit(solution)/shard_map/plan/pallas_call | solution.py:399
  16.3 2.7 %collective-permute-start.5 = (bf16[1024,128]{1,0:T(8,128)(2,1)S(1)}, bf16[1024,128]{1,0:T(8,128)(2,1)S(1)}, u32[]{:S(2)}, u32[]{:S(2)}) collective-permute-start(bf16[1024,128]{1,0:T(8,128)(2,1)S(1)} %get-tuple-element.53), channel_id=1, source_target_pairs={{0,6},{1,7},{2,0},{3,1},{4,2},{5,3},{6,4},{7,5},{8,14},{9,15},{10,... | collective-permute-start | bytes 786440 | tf_op jit(solution)/shard_map/gather_features/ppermute | solution.py:30
  20.7 3.2 %collective-permute-done.4.refs_1_ = bf16[1024,128]{1,0:T(8,128)(2,1)S(1)} collective-permute-done((bf16[1024,128]{1,0:T(8,128)(2,1)S(1)}, bf16[1024,128]{1,0:T(8,128)(2,1)S(1)}, u32[]{:S(2)}, u32[]{:S(2)}) %collective-permute-start.4) | collective-permute-done | bytes 262176 | tf_op jit(solution)/shard_map/gather_features/ppermute | solution.py:30
  25.5 2.5 %forward_tiles.3.refs_4_ = f32[33,256,128]{2,1,0:T(8,128)S(1)} custom-call(s32[1152]{0:T(1024)S(4)} %get-tuple-element.50.refs_0_, s32[8]{0:T(128)S(4)} %get-tuple-element.51.refs_4_.refs_1_, bf16[128,256,256]{2,1,0:T(8,128)(2,1)S(1)} %get-tuple-element.52.refs_2_, bf16[16,256,128]{2,1,0:T(8,128)(2,1)S(1)} %get-tuple-element.54.refs_3_, ...), custom_call_target="tpu_custom_call" | custom-call | flops 1073741824 | bytes 8388608 | tf_op jit(solution)/shard_map/forward_tiles/pallas_call | solution.py:64
  31.4 2.0 %collective-permute-start.11 = (bf16[1024,128]{1,0:T(8,128)(2,1)S(1)}, bf16[1024,128]{1,0:T(8,128)(2,1)S(1)}, u32[]{:S(2)}, u32[]{:S(2)}) collective-permute-start(bf16[1024,128]{1,0:T(8,128)(2,1)S(1)} %get-tuple-element.60), channel_id=1, source_target_pairs={{0,96},{16,112},{32,0},{48,16},{64,32},{80,48},{96,64},{112,80},{1... | collective-permute-start | bytes 786440 | tf_op jit(solution)/shard_map/sum_aggregates/ppermute | solution.py:38
  35.1 3.2 %collective-permute-start.13 = (bf16[1024,128]{1,0:T(8,128)(2,1)S(1)}, bf16[1024,128]{1,0:T(8,128)(2,1)S(1)}, u32[]{:S(2)}, u32[]{:S(2)}) collective-permute-start(bf16[1024,128]{1,0:T(8,128)(2,1)S(1)} %get-tuple-element.62), channel_id=1, source_target_pairs={{0,16},{16,0},{32,48},{48,32},{64,80},{80,64},{96,112},{112,96},{1... | collective-permute-start | bytes 786440 | tf_op jit(solution)/shard_map/sum_aggregates/ppermute | solution.py:38
  41.5 3.8 %collective-permute-done.13.refs_4_ = bf16[1024,128]{1,0:T(8,128)(2,1)S(1)} collective-permute-done((bf16[1024,128]{1,0:T(8,128)(2,1)S(1)}, bf16[1024,128]{1,0:T(8,128)(2,1)S(1)}, u32[]{:S(2)}, u32[]{:S(2)}) %collective-permute-start.13) | collective-permute-done | bytes 262176 | tf_op jit(solution)/shard_map/sum_aggregates/ppermute | solution.py:38
  45.5 2.5 %collective-permute-start.14 = (bf16[1024,128]{1,0:T(8,128)(2,1)S(1)}, bf16[1024,128]{1,0:T(8,128)(2,1)S(1)}, u32[]{:S(2)}, u32[]{:S(2)}) collective-permute-start(bf16[1024,128]{1,0:T(8,128)(2,1)S(1)} %get-tuple-element.63), channel_id=1, source_target_pairs={{0,64},{16,80},{32,96},{48,112},{64,0},{80,16},{96,32},{112,48},{1... | collective-permute-start | bytes 786440 | tf_op jit(solution)/shard_map/sum_aggregates/ppermute | solution.py:38
  48.9 6.7 %collective-permute-done.14.refs_8_ = bf16[1024,128]{1,0:T(8,128)(2,1)S(1)} collective-permute-done((bf16[1024,128]{1,0:T(8,128)(2,1)S(1)}, bf16[1024,128]{1,0:T(8,128)(2,1)S(1)}, u32[]{:S(2)}, u32[]{:S(2)}) %collective-permute-start.14) | collective-permute-done | bytes 262176 | tf_op jit(solution)/shard_map/sum_aggregates/ppermute | solution.py:38
  55.7 1.8 %collective-permute-done.15.refs_9_ = bf16[1024,128]{1,0:T(8,128)(2,1)S(1)} collective-permute-done((bf16[1024,128]{1,0:T(8,128)(2,1)S(1)}, bf16[1024,128]{1,0:T(8,128)(2,1)S(1)}, u32[]{:S(2)}, u32[]{:S(2)}) %collective-permute-start.15) | collective-permute-done | bytes 262176 | tf_op jit(solution)/shard_map/sum_aggregates/ppermute | solution.py:38
  57.5 2.1 %dense.1 = (bf16[1024,256]{1,0:T(8,128)(2,1)}, bf16[1024,256]{1,0:T(8,128)(2,1)S(1)}, bf16[1024,128]{1,0:T(8,128)(2,1)S(1)}, bf16[128,1024]{1,0:T(8,128)(2,1)S(1)}) custom-call(f32[1,256]{1,0:T(1,128)S(1)} %bitcast.6, bf16[1024,128]{1,0:T(8,128)(2,1)S(1)} %copy-done, bf16[1024,256]{1,0:T(8,128)(2,1)S(1)} %copy-done.1, bf16[128,256]{1,0:T(8,128)(2,1)S(1)} %copy-done.2, ...), custom_call_target="tpu_custom_call" | custom-call | flops 201326592 | bytes 6291456 | tf_op jit(solution)/shard_map/dense/pallas_call | solution.py:64
  61.3 3.2 %collective-permute-start.16 = (bf16[128,1024]{1,0:T(8,128)(2,1)S(1)}, bf16[128,1024]{1,0:T(8,128)(2,1)S(1)}, u32[]{:S(2)}, u32[]{:S(2)}) collective-permute-start(bf16[128,1024]{1,0:T(8,128)(2,1)S(1)} %get-tuple-element.69.refs_3_), channel_id=1, source_target_pairs={{0,64},{16,80},{32,96},{48,112},{64,0},{80,16},{96,32},{112,48},{1... | collective-permute-start | bytes 786440 | tf_op jit(solution)/shard_map/gather_dz/ppermute | solution.py:38
  66.8 2.0 %collective-permute-start.22 = (bf16[128,1024]{1,0:T(8,128)(2,1)S(1)}, bf16[128,1024]{1,0:T(8,128)(2,1)S(1)}, u32[]{:S(2)}, u32[]{:S(2)}) collective-permute-start(bf16[128,1024]{1,0:T(8,128)(2,1)S(1)} %get-tuple-element.69.refs_3_), channel_id=1, source_target_pairs={{0,96},{16,112},{32,0},{48,16},{64,32},{80,48},{96,64},{112,80},{1... | collective-permute-start | bytes 786440 | tf_op jit(solution)/shard_map/gather_dz/ppermute | solution.py:38
  68.9 3.1 %collective-permute-done.24.refs_1_ = f32[32,256]{1,0:T(8,128)S(1)} collective-permute-done((f32[32,256]{1,0:T(8,128)S(1)}, f32[32,256]{1,0:T(8,128)S(1)}, u32[]{:S(2)}, u32[]{:S(2)}) %collective-permute-start.24) | collective-permute-done | bytes 32800 | tf_op jit(solution)/shard_map/weights/ppermute | solution.py:30
  72.8 4.6 %collective-permute-done.25.refs_2_ = f32[32,256]{1,0:T(8,128)S(1)} collective-permute-done((f32[32,256]{1,0:T(8,128)S(1)}, f32[32,256]{1,0:T(8,128)S(1)}, u32[]{:S(2)}, u32[]{:S(2)}) %collective-permute-start.25) | collective-permute-done | bytes 32800 | tf_op jit(solution)/shard_map/weights/ppermute | solution.py:30
  78.7 2.6 %collective-permute-done.26.refs_3_ = f32[32,256]{1,0:T(8,128)S(1)} collective-permute-done((f32[32,256]{1,0:T(8,128)S(1)}, f32[32,256]{1,0:T(8,128)S(1)}, u32[]{:S(2)}, u32[]{:S(2)}) %collective-permute-start.26) | collective-permute-done | bytes 32800 | tf_op jit(solution)/shard_map/weights/ppermute | solution.py:30
  81.4 3.4 %collective-permute-start.28 = (f32[8,256]{1,0:T(8,128)S(1)}, f32[8,256]{1,0:T(8,128)S(1)}, u32[]{:S(2)}, u32[]{:S(2)}) collective-permute-start(f32[8,256]{1,0:T(8,128)S(1)} %get-tuple-element.80), channel_id=1, source_target_pairs={{0,64},{16,80},{32,96},{48,112},{64,0},{80,16},{96,32},{112,48},{1... | collective-permute-start | bytes 24584 | tf_op jit(solution)/shard_map/weights/ppermute | solution.py:38
  86.9 3.1 %collective-permute-start.19 = (bf16[128,1024]{1,0:T(8,128)(2,1)S(1)}, bf16[128,1024]{1,0:T(8,128)(2,1)S(1)}, u32[]{:S(2)}, u32[]{:S(2)}) collective-permute-start(bf16[128,1024]{1,0:T(8,128)(2,1)S(1)} %collective-permute-done.17.refs_4_.refs_6_), channel_id=1, source_target_pairs={{0,96},{16,112},{32,0},{48,16},{64,32},{80,48},{96,64},{112,80},{1... | collective-permute-start | bytes 786440 | tf_op jit(solution)/shard_map/gather_dz/ppermute | solution.py:38
  91.4 3.2 %collective-permute-start.31 = (f32[8,256]{1,0:T(8,128)S(1)}, f32[8,256]{1,0:T(8,128)S(1)}, u32[]{:S(2)}, u32[]{:S(2)}) collective-permute-start(f32[8,256]{1,0:T(8,128)S(1)} %weights.8.refs_0_), channel_id=1, source_target_pairs={{0,16},{16,0},{32,48},{48,32},{64,80},{80,64},{96,112},{112,96},{1... | collective-permute-start | bytes 24584 | tf_op jit(solution)/shard_map/weights/ppermute | solution.py:38
  95.7 2.7 %collective-permute-start.32 = (f32[8,256]{1,0:T(8,128)S(1)}, f32[8,256]{1,0:T(8,128)S(1)}, u32[]{:S(2)}, u32[]{:S(2)}) collective-permute-start(f32[8,256]{1,0:T(8,128)S(1)} %weights.8.refs_0_), channel_id=1, source_target_pairs={{0,24},{1,25},{2,26},{3,27},{4,28},{5,29},{6,30},{7,31},{8,16},{9,... | collective-permute-start | bytes 24584 | tf_op jit(solution)/shard_map/weights/ppermute | solution.py:46
  98.5 2.7 %backward_tiles.3 = (f32[33,128,256]{2,1,0:T(8,128)S(1)}, f32[33,128,256]{2,1,0:T(8,128)S(1)}) custom-call(s32[1152]{0:T(1024)S(4)} %get-tuple-element.50.refs_0_, s32[8]{0:T(128)S(4)} %get-tuple-element.51.refs_4_.refs_1_, bf16[128,256,256]{2,1,0:T(8,128)(2,1)S(1)} %get-tuple-element.52.refs_2_, bf16[128,1024]{1,0:T(8,128)(2,1)S(1)} %get-tuple-element.69.refs_3_, ...), custom_call_target="tpu_custom_call" | custom-call | flops 1073741824 | bytes 8388608 | tf_op jit(solution)/shard_map/backward_tiles/pallas_call | solution.py:64
  103.9 2.5 %collective-permute-done.39.refs_1_ = bf16[3,128,1024]{2,1,0:T(8,128)(2,1)S(1)} collective-permute-done((bf16[3,128,1024]{2,1,0:T(8,128)(2,1)S(1)}, bf16[3,128,1024]{2,1,0:T(8,128)(2,1)S(1)}, u32[]{:S(2)}, u32[]{:S(2)}) %collective-permute-start.39) | collective-permute-done | bytes 786464 | tf_op jit(solution)/shard_map/sum_grads/ppermute | solution.py:30
  106.6 2.1 %collective-permute-start.40 = (bf16[128,1024]{1,0:T(8,128)(2,1)S(1)}, bf16[128,1024]{1,0:T(8,128)(2,1)S(1)}, u32[]{:S(2)}, u32[]{:S(2)}) collective-permute-start(bf16[128,1024]{1,0:T(8,128)(2,1)S(1)} %get-tuple-element.89), channel_id=1, source_target_pairs={{0,6},{1,7},{2,0},{3,1},{4,2},{5,3},{6,4},{7,5},{8,14},{9,15},{10,... | collective-permute-start | bytes 786440 | tf_op jit(solution)/shard_map/sum_grads/ppermute | solution.py:30
  110.4 2.3 %collective-permute-done.34.refs_1_ = f32[8,256]{1,0:T(8,128)S(1)} collective-permute-done((f32[8,256]{1,0:T(8,128)S(1)}, f32[8,256]{1,0:T(8,128)S(1)}, u32[]{:S(2)}, u32[]{:S(2)}) %collective-permute-start.34) | collective-permute-done | bytes 8224 | tf_op jit(solution)/shard_map/gather_weights/ppermute | solution.py:38
  113.5 4.4 %collective-permute-done.35.refs_2_ = f32[8,256]{1,0:T(8,128)S(1)} collective-permute-done((f32[8,256]{1,0:T(8,128)S(1)}, f32[8,256]{1,0:T(8,128)S(1)}, u32[]{:S(2)}, u32[]{:S(2)}) %collective-permute-start.35) | collective-permute-done | bytes 8224 | tf_op jit(solution)/shard_map/gather_weights/ppermute | solution.py:38
  117.9 4.9 %collective-permute-done.36.refs_3_ = f32[8,256]{1,0:T(8,128)S(1)} collective-permute-done((f32[8,256]{1,0:T(8,128)S(1)}, f32[8,256]{1,0:T(8,128)S(1)}, u32[]{:S(2)}, u32[]{:S(2)}) %collective-permute-start.36) | collective-permute-done | bytes 8224 | tf_op jit(solution)/shard_map/gather_weights/ppermute | solution.py:38
  122.7 3.0 %collective-permute-start.43 = (f32[32,256]{1,0:T(8,128)S(1)}, f32[32,256]{1,0:T(8,128)S(1)}, u32[]{:S(2)}, u32[]{:S(2)}) collective-permute-start(f32[32,256]{1,0:T(8,128)S(1)} %gather_weights.3.refs_2_.refs_0_), channel_id=1, source_target_pairs={{0,6},{1,7},{2,0},{3,1},{4,2},{5,3},{6,4},{7,5},{8,14},{9,15},{10,... | collective-permute-start | bytes 98312 | tf_op jit(solution)/shard_map/gather_weights/ppermute | solution.py:30
  129.1 3.8 %collective-permute-done.44.refs_2_ = f32[32,256]{1,0:T(8,128)S(1)} collective-permute-done((f32[32,256]{1,0:T(8,128)S(1)}, f32[32,256]{1,0:T(8,128)S(1)}, u32[]{:S(2)}, u32[]{:S(2)}) %collective-permute-start.44) | collective-permute-done | bytes 32800 | tf_op jit(solution)/shard_map/gather_weights/ppermute | solution.py:30
  133.7 5.8 %collective-permute-done.45.refs_3_ = f32[32,256]{1,0:T(8,128)S(1)} collective-permute-done((f32[32,256]{1,0:T(8,128)S(1)}, f32[32,256]{1,0:T(8,128)S(1)}, u32[]{:S(2)}, u32[]{:S(2)}) %collective-permute-start.45) | collective-permute-done | bytes 32800 | tf_op jit(solution)/shard_map/gather_weights/ppermute | solution.py:30
  142.8 1.8 %collective-permute-start.47 = (bf16[128,1024]{1,0:T(8,128)(2,1)S(1)}, bf16[128,1024]{1,0:T(8,128)(2,1)S(1)}, u32[]{:S(2)}, u32[]{:S(2)}) collective-permute-start(bf16[128,1024]{1,0:T(8,128)(2,1)S(1)} %get-tuple-element.93), channel_id=1, source_target_pairs={{0,8},{1,9},{2,10},{3,11},{4,12},{5,13},{6,14},{7,15},{8,0},{9,1},... | collective-permute-start | bytes 786440 | tf_op jit(solution)/shard_map/sum_grads/ppermute | solution.py:30
  146.6 4.7 %collective-permute-done.38.refs_3_ = bf16[128,1024]{1,0:T(8,128)(2,1)S(1)} collective-permute-done((bf16[128,1024]{1,0:T(8,128)(2,1)S(1)}, bf16[128,1024]{1,0:T(8,128)(2,1)S(1)}, u32[]{:S(2)}, u32[]{:S(2)}) %collective-permute-start.38) | collective-permute-done | bytes 262176 | tf_op jit(solution)/shard_map/sum_grads/ppermute | solution.py:30
  (101 shorter events, 45.8 us)
Async XLA Ops:
  0.6 14.9 %collective-permute-start.1 = (bf16[1024,128]{1,0:T(8,128)(2,1)}, bf16[1024,128]{1,0:T(8,128)(2,1)S(1)}, u32[]{:S(2)}, u32[]{:S(2)}) collective-permute-start(bf16[1024,128]{1,0:T(8,128)(2,1)} %refs_0_.3), channel_id=1, source_target_pairs={{0,2},{1,3},{2,4},{3,5},{4,6},{5,7},{6,0},{7,1},{8,10},{9,11},{10,... | collective-permute-start | bytes 786440 | tf_op jit(solution)/shard_map/gather_features/ppermute | solution.py:30
  2.3 13.2 %collective-permute-start.2 = (bf16[1024,128]{1,0:T(8,128)(2,1)}, bf16[1024,128]{1,0:T(8,128)(2,1)S(1)}, u32[]{:S(2)}, u32[]{:S(2)}) collective-permute-start(bf16[1024,128]{1,0:T(8,128)(2,1)} %refs_0_.3), channel_id=1, source_target_pairs={{0,6},{1,7},{2,0},{3,1},{4,2},{5,3},{6,4},{7,5},{8,14},{9,15},{10,... | collective-permute-start | bytes 786440 | tf_op jit(solution)/shard_map/gather_features/ppermute | solution.py:30
  3.9 11.6 %collective-permute-start.3 = (bf16[1024,128]{1,0:T(8,128)(2,1)}, bf16[1024,128]{1,0:T(8,128)(2,1)S(1)}, u32[]{:S(2)}, u32[]{:S(2)}) collective-permute-start(bf16[1024,128]{1,0:T(8,128)(2,1)} %refs_0_.3), channel_id=1, source_target_pairs={{0,8},{1,9},{2,10},{3,11},{4,12},{5,13},{6,14},{7,15},{8,0},{9,1},... | collective-permute-start | bytes 786440 | tf_op jit(solution)/shard_map/gather_features/ppermute | solution.py:30
  5.6 13.4 %collective-permute-start = (bf16[1024,128]{1,0:T(8,128)(2,1)}, bf16[1024,128]{1,0:T(8,128)(2,1)S(1)}, u32[]{:S(2)}, u32[]{:S(2)}) collective-permute-start(bf16[1024,128]{1,0:T(8,128)(2,1)} %refs_0_.3), channel_id=1, source_target_pairs={{0,4},{1,5},{2,6},{3,7},{4,0},{5,1},{6,2},{7,3},{8,12},{9,13},{10,... | collective-permute-start | bytes 786440 | tf_op jit(solution)/shard_map/gather_features/ppermute | solution.py:30
  15.7 8.2 %collective-permute-start.4 = (bf16[1024,128]{1,0:T(8,128)(2,1)S(1)}, bf16[1024,128]{1,0:T(8,128)(2,1)S(1)}, u32[]{:S(2)}, u32[]{:S(2)}) collective-permute-start(bf16[1024,128]{1,0:T(8,128)(2,1)S(1)} %get-tuple-element.53), channel_id=1, source_target_pairs={{0,2},{1,3},{2,4},{3,5},{4,6},{5,7},{6,0},{7,1},{8,10},{9,11},{10,... | collective-permute-start | bytes 786440 | tf_op jit(solution)/shard_map/gather_features/ppermute | solution.py:30
  16.3 7.5 %collective-permute-start.5 = (bf16[1024,128]{1,0:T(8,128)(2,1)S(1)}, bf16[1024,128]{1,0:T(8,128)(2,1)S(1)}, u32[]{:S(2)}, u32[]{:S(2)}) collective-permute-start(bf16[1024,128]{1,0:T(8,128)(2,1)S(1)} %get-tuple-element.53), channel_id=1, source_target_pairs={{0,6},{1,7},{2,0},{3,1},{4,2},{5,3},{6,4},{7,5},{8,14},{9,15},{10,... | collective-permute-start | bytes 786440 | tf_op jit(solution)/shard_map/gather_features/ppermute | solution.py:30
  19.0 6.4 %collective-permute-start.6 = (bf16[1024,128]{1,0:T(8,128)(2,1)S(1)}, bf16[1024,128]{1,0:T(8,128)(2,1)S(1)}, u32[]{:S(2)}, u32[]{:S(2)}) collective-permute-start(bf16[1024,128]{1,0:T(8,128)(2,1)S(1)} %collective-permute-done.refs_0_), channel_id=1, source_target_pairs={{0,8},{1,9},{2,10},{3,11},{4,12},{5,13},{6,14},{7,15},{8,0},{9,1},... | collective-permute-start | bytes 786440 | tf_op jit(solution)/shard_map/gather_features/ppermute | solution.py:30
  31.4 9.8 %collective-permute-start.11 = (bf16[1024,128]{1,0:T(8,128)(2,1)S(1)}, bf16[1024,128]{1,0:T(8,128)(2,1)S(1)}, u32[]{:S(2)}, u32[]{:S(2)}) collective-permute-start(bf16[1024,128]{1,0:T(8,128)(2,1)S(1)} %get-tuple-element.60), channel_id=1, source_target_pairs={{0,96},{16,112},{32,0},{48,16},{64,32},{80,48},{96,64},{112,80},{1... | collective-permute-start | bytes 786440 | tf_op jit(solution)/shard_map/sum_aggregates/ppermute | solution.py:38
  33.4 8.1 %collective-permute-start.12 = (bf16[1024,128]{1,0:T(8,128)(2,1)S(1)}, bf16[1024,128]{1,0:T(8,128)(2,1)S(1)}, u32[]{:S(2)}, u32[]{:S(2)}) collective-permute-start(bf16[1024,128]{1,0:T(8,128)(2,1)S(1)} %get-tuple-element.61), channel_id=1, source_target_pairs={{0,32},{16,48},{32,64},{48,80},{64,96},{80,112},{96,0},{112,16},{1... | collective-permute-start | bytes 786440 | tf_op jit(solution)/shard_map/sum_aggregates/ppermute | solution.py:38
  35.1 10.2 %collective-permute-start.13 = (bf16[1024,128]{1,0:T(8,128)(2,1)S(1)}, bf16[1024,128]{1,0:T(8,128)(2,1)S(1)}, u32[]{:S(2)}, u32[]{:S(2)}) collective-permute-start(bf16[1024,128]{1,0:T(8,128)(2,1)S(1)} %get-tuple-element.62), channel_id=1, source_target_pairs={{0,16},{16,0},{32,48},{48,32},{64,80},{80,64},{96,112},{112,96},{1... | collective-permute-start | bytes 786440 | tf_op jit(solution)/shard_map/sum_aggregates/ppermute | solution.py:38
  38.3 10.6 %collective-permute-start.9 = (bf16[1024,128]{1,0:T(8,128)(2,1)S(1)}, bf16[1024,128]{1,0:T(8,128)(2,1)S(1)}, u32[]{:S(2)}, u32[]{:S(2)}) collective-permute-start(bf16[1024,128]{1,0:T(8,128)(2,1)S(1)} %get-tuple-element.56), channel_id=1, source_target_pairs={{0,96},{16,112},{32,0},{48,16},{64,32},{80,48},{96,64},{112,80},{1... | collective-permute-start | bytes 786440 | tf_op jit(solution)/shard_map/sum_aggregates/ppermute | solution.py:38
  39.8 9.1 %collective-permute-start.10 = (bf16[1024,128]{1,0:T(8,128)(2,1)S(1)}, bf16[1024,128]{1,0:T(8,128)(2,1)S(1)}, u32[]{:S(2)}, u32[]{:S(2)}) collective-permute-start(bf16[1024,128]{1,0:T(8,128)(2,1)S(1)} %get-tuple-element.57), channel_id=1, source_target_pairs={{0,32},{16,48},{32,64},{48,80},{64,96},{80,112},{96,0},{112,16},{1... | collective-permute-start | bytes 786440 | tf_op jit(solution)/shard_map/sum_aggregates/ppermute | solution.py:38
  45.5 10.2 %collective-permute-start.14 = (bf16[1024,128]{1,0:T(8,128)(2,1)S(1)}, bf16[1024,128]{1,0:T(8,128)(2,1)S(1)}, u32[]{:S(2)}, u32[]{:S(2)}) collective-permute-start(bf16[1024,128]{1,0:T(8,128)(2,1)S(1)} %get-tuple-element.63), channel_id=1, source_target_pairs={{0,64},{16,80},{32,96},{48,112},{64,0},{80,16},{96,32},{112,48},{1... | collective-permute-start | bytes 786440 | tf_op jit(solution)/shard_map/sum_aggregates/ppermute | solution.py:38
  47.9 9.6 %collective-permute-start.15 = (bf16[1024,128]{1,0:T(8,128)(2,1)S(1)}, bf16[1024,128]{1,0:T(8,128)(2,1)S(1)}, u32[]{:S(2)}, u32[]{:S(2)}) collective-permute-start(bf16[1024,128]{1,0:T(8,128)(2,1)S(1)} %get-tuple-element.64), channel_id=1, source_target_pairs={{0,16},{16,0},{32,48},{48,32},{64,80},{80,64},{96,112},{112,96},{1... | collective-permute-start | bytes 786440 | tf_op jit(solution)/shard_map/sum_aggregates/ppermute | solution.py:38
  59.6 21.7 %collective-permute-start.17 = (bf16[128,1024]{1,0:T(8,128)(2,1)S(1)}, bf16[128,1024]{1,0:T(8,128)(2,1)S(1)}, u32[]{:S(2)}, u32[]{:S(2)}) collective-permute-start(bf16[128,1024]{1,0:T(8,128)(2,1)S(1)} %get-tuple-element.69.refs_3_), channel_id=1, source_target_pairs={{0,16},{16,0},{32,48},{48,32},{64,80},{80,64},{96,112},{112,96},{1... | collective-permute-start | bytes 786440 | tf_op jit(solution)/shard_map/gather_dz/ppermute | solution.py:38
  61.3 23.5 %collective-permute-start.16 = (bf16[128,1024]{1,0:T(8,128)(2,1)S(1)}, bf16[128,1024]{1,0:T(8,128)(2,1)S(1)}, u32[]{:S(2)}, u32[]{:S(2)}) collective-permute-start(bf16[128,1024]{1,0:T(8,128)(2,1)S(1)} %get-tuple-element.69.refs_3_), channel_id=1, source_target_pairs={{0,64},{16,80},{32,96},{48,112},{64,0},{80,16},{96,32},{112,48},{1... | collective-permute-start | bytes 786440 | tf_op jit(solution)/shard_map/gather_dz/ppermute | solution.py:38
  65.2 25.0 %collective-permute-start.21 = (bf16[128,1024]{1,0:T(8,128)(2,1)S(1)}, bf16[128,1024]{1,0:T(8,128)(2,1)S(1)}, u32[]{:S(2)}, u32[]{:S(2)}) collective-permute-start(bf16[128,1024]{1,0:T(8,128)(2,1)S(1)} %get-tuple-element.69.refs_3_), channel_id=1, source_target_pairs={{0,32},{16,48},{32,64},{48,80},{64,96},{80,112},{96,0},{112,16},{1... | collective-permute-start | bytes 786440 | tf_op jit(solution)/shard_map/gather_dz/ppermute | solution.py:38
  66.8 24.5 %collective-permute-start.22 = (bf16[128,1024]{1,0:T(8,128)(2,1)S(1)}, bf16[128,1024]{1,0:T(8,128)(2,1)S(1)}, u32[]{:S(2)}, u32[]{:S(2)}) collective-permute-start(bf16[128,1024]{1,0:T(8,128)(2,1)S(1)} %get-tuple-element.69.refs_3_), channel_id=1, source_target_pairs={{0,96},{16,112},{32,0},{48,16},{64,32},{80,48},{96,64},{112,80},{1... | collective-permute-start | bytes 786440 | tf_op jit(solution)/shard_map/gather_dz/ppermute | solution.py:38
  86.3 14.9 %collective-permute-start.18 = (bf16[128,1024]{1,0:T(8,128)(2,1)S(1)}, bf16[128,1024]{1,0:T(8,128)(2,1)S(1)}, u32[]{:S(2)}, u32[]{:S(2)}) collective-permute-start(bf16[128,1024]{1,0:T(8,128)(2,1)S(1)} %collective-permute-done.17.refs_4_.refs_6_), channel_id=1, source_target_pairs={{0,32},{16,48},{32,64},{48,80},{64,96},{80,112},{96,0},{112,16},{1... | collective-permute-start | bytes 786440 | tf_op jit(solution)/shard_map/gather_dz/ppermute | solution.py:38
  86.9 14.4 %collective-permute-start.19 = (bf16[128,1024]{1,0:T(8,128)(2,1)S(1)}, bf16[128,1024]{1,0:T(8,128)(2,1)S(1)}, u32[]{:S(2)}, u32[]{:S(2)}) collective-permute-start(bf16[128,1024]{1,0:T(8,128)(2,1)S(1)} %collective-permute-done.17.refs_4_.refs_6_), channel_id=1, source_target_pairs={{0,96},{16,112},{32,0},{48,16},{64,32},{80,48},{96,64},{112,80},{1... | collective-permute-start | bytes 786440 | tf_op jit(solution)/shard_map/gather_dz/ppermute | solution.py:38
  89.9 11.3 %collective-permute-start.20 = (bf16[128,1024]{1,0:T(8,128)(2,1)S(1)}, bf16[128,1024]{1,0:T(8,128)(2,1)S(1)}, u32[]{:S(2)}, u32[]{:S(2)}) collective-permute-start(bf16[128,1024]{1,0:T(8,128)(2,1)S(1)} %collective-permute-done.16.refs_3_), channel_id=1, source_target_pairs={{0,16},{16,0},{32,48},{48,32},{64,80},{80,64},{96,112},{112,96},{1... | collective-permute-start | bytes 786440 | tf_op jit(solution)/shard_map/gather_dz/ppermute | solution.py:38
  91.4 9.9 %collective-permute-start.31 = (f32[8,256]{1,0:T(8,128)S(1)}, f32[8,256]{1,0:T(8,128)S(1)}, u32[]{:S(2)}, u32[]{:S(2)}) collective-permute-start(f32[8,256]{1,0:T(8,128)S(1)} %weights.8.refs_0_), channel_id=1, source_target_pairs={{0,16},{16,0},{32,48},{48,32},{64,80},{80,64},{96,112},{112,96},{1... | collective-permute-start | bytes 24584 | tf_op jit(solution)/shard_map/weights/ppermute | solution.py:38
  102.2 37.4 %collective-permute-start.33 = (bf16[5,128,1024]{2,1,0:T(8,128)(2,1)S(1)}, bf16[5,128,1024]{2,1,0:T(8,128)(2,1)S(1)}, u32[]{:S(2)}, u32[]{:S(2)}) collective-permute-start(bf16[5,128,1024]{2,1,0:T(8,128)(2,1)S(1)} %get-tuple-element.82), channel_id=1, source_target_pairs={{0,1},{1,0},{2,3},{3,2},{4,5},{5,4},{6,7},{7,6},{8,9},{9,8},{10,11... | collective-permute-start | bytes 3932168 | tf_op jit(solution)/shard_map/sum_grads/ppermute | solution.py:30
  106.6 35.3 %collective-permute-start.40 = (bf16[128,1024]{1,0:T(8,128)(2,1)S(1)}, bf16[128,1024]{1,0:T(8,128)(2,1)S(1)}, u32[]{:S(2)}, u32[]{:S(2)}) collective-permute-start(bf16[128,1024]{1,0:T(8,128)(2,1)S(1)} %get-tuple-element.89), channel_id=1, source_target_pairs={{0,6},{1,7},{2,0},{3,1},{4,2},{5,3},{6,4},{7,5},{8,14},{9,15},{10,... | collective-permute-start | bytes 786440 | tf_op jit(solution)/shard_map/sum_grads/ppermute | solution.py:30
  108.7 33.2 %collective-permute-start.41 = (bf16[128,1024]{1,0:T(8,128)(2,1)S(1)}, bf16[128,1024]{1,0:T(8,128)(2,1)S(1)}, u32[]{:S(2)}, u32[]{:S(2)}) collective-permute-start(bf16[128,1024]{1,0:T(8,128)(2,1)S(1)} %get-tuple-element.90), channel_id=1, source_target_pairs={{0,2},{1,3},{2,4},{3,5},{4,6},{5,7},{6,0},{7,1},{8,10},{9,11},{10,... | collective-permute-start | bytes 786440 | tf_op jit(solution)/shard_map/sum_grads/ppermute | solution.py:30
  108.7 33.2 %collective-permute-start.42 = (bf16[128,1024]{1,0:T(8,128)(2,1)S(1)}, bf16[128,1024]{1,0:T(8,128)(2,1)S(1)}, u32[]{:S(2)}, u32[]{:S(2)}) collective-permute-start(bf16[128,1024]{1,0:T(8,128)(2,1)S(1)} %get-tuple-element.91), channel_id=1, source_target_pairs={{0,8},{1,9},{2,10},{3,11},{4,12},{5,13},{6,14},{7,15},{8,0},{9,1},... | collective-permute-start | bytes 786440 | tf_op jit(solution)/shard_map/sum_grads/ppermute | solution.py:30
  127.4 5.6 %collective-permute-start.44 = (f32[32,256]{1,0:T(8,128)S(1)}, f32[32,256]{1,0:T(8,128)S(1)}, u32[]{:S(2)}, u32[]{:S(2)}) collective-permute-start(f32[32,256]{1,0:T(8,128)S(1)} %gather_weights.3.refs_2_.refs_0_), channel_id=1, source_target_pairs={{0,4},{1,5},{2,6},{3,7},{4,0},{5,1},{6,2},{7,3},{8,12},{9,13},{10,... | collective-permute-start | bytes 98312 | tf_op jit(solution)/shard_map/gather_weights/ppermute | solution.py:30
  133.0 6.5 %collective-permute-start.45 = (f32[32,256]{1,0:T(8,128)S(1)}, f32[32,256]{1,0:T(8,128)S(1)}, u32[]{:S(2)}, u32[]{:S(2)}) collective-permute-start(f32[32,256]{1,0:T(8,128)S(1)} %gather_weights.3.refs_2_.refs_0_), channel_id=1, source_target_pairs={{0,2},{1,3},{2,4},{3,5},{4,6},{5,7},{6,0},{7,1},{8,10},{9,11},{10,... | collective-permute-start | bytes 98312 | tf_op jit(solution)/shard_map/gather_weights/ppermute | solution.py:30
  139.8 6.9 %collective-permute-start.37 = (bf16[128,1024]{1,0:T(8,128)(2,1)S(1)}, bf16[128,1024]{1,0:T(8,128)(2,1)S(1)}, u32[]{:S(2)}, u32[]{:S(2)}) collective-permute-start(bf16[128,1024]{1,0:T(8,128)(2,1)S(1)} %get-tuple-element.84), channel_id=1, source_target_pairs={{0,6},{1,7},{2,0},{3,1},{4,2},{5,3},{6,4},{7,5},{8,14},{9,15},{10,... | collective-permute-start | bytes 786440 | tf_op jit(solution)/shard_map/sum_grads/ppermute | solution.py:30
  141.0 10.4 %collective-permute-start.38 = (bf16[128,1024]{1,0:T(8,128)(2,1)S(1)}, bf16[128,1024]{1,0:T(8,128)(2,1)S(1)}, u32[]{:S(2)}, u32[]{:S(2)}) collective-permute-start(bf16[128,1024]{1,0:T(8,128)(2,1)S(1)} %get-tuple-element.85), channel_id=1, source_target_pairs={{0,2},{1,3},{2,4},{3,5},{4,6},{5,7},{6,0},{7,1},{8,10},{9,11},{10,... | collective-permute-start | bytes 786440 | tf_op jit(solution)/shard_map/sum_grads/ppermute | solution.py:30
  142.0 9.4 %collective-permute-start.46 = (bf16[128,1024]{1,0:T(8,128)(2,1)S(1)}, bf16[128,1024]{1,0:T(8,128)(2,1)S(1)}, u32[]{:S(2)}, u32[]{:S(2)}) collective-permute-start(bf16[128,1024]{1,0:T(8,128)(2,1)S(1)} %get-tuple-element.92), channel_id=1, source_target_pairs={{0,4},{1,5},{2,6},{3,7},{4,0},{5,1},{6,2},{7,3},{8,12},{9,13},{10,... | collective-permute-start | bytes 786440 | tf_op jit(solution)/shard_map/sum_grads/ppermute | solution.py:30
  142.8 8.6 %collective-permute-start.47 = (bf16[128,1024]{1,0:T(8,128)(2,1)S(1)}, bf16[128,1024]{1,0:T(8,128)(2,1)S(1)}, u32[]{:S(2)}, u32[]{:S(2)}) collective-permute-start(bf16[128,1024]{1,0:T(8,128)(2,1)S(1)} %get-tuple-element.93), channel_id=1, source_target_pairs={{0,8},{1,9},{2,10},{3,11},{4,12},{5,13},{6,14},{7,15},{8,0},{9,1},... | collective-permute-start | bytes 786440 | tf_op jit(solution)/shard_map/sum_grads/ppermute | solution.py:30
  (22 other events, 193.5 us)

commit v3 on v2

v3 whole, which is shorter than its diff:
```python
import functools

import jax
import jax.numpy as jnp
from jax import lax
from jax.experimental import pallas as pl
from jax.experimental.pallas import tpu as pltpu
from jax.sharding import PartitionSpec as P

TILE = 256
VMEM = pltpu.VMEM
BF16 = jnp.bfloat16
F32 = jnp.float32
LIMIT = 12 * 1024 * 1024
GROUP = 16
ROOM = 144

NEAR = 5
ORDER = [(0, 0), (0, 3), (0, 1), (1, 0), (0, 2), (1, 3), (1, 1), (1, 2)]
OWN, LEFT, RIGHT, PAIR, OPPOSITE, PAIR_LEFT, PAIR_RIGHT, PAIR_OPPOSITE = range(8)
PLACE = sum(ORDER.index((k // 4, k % 4)) << (4 * k) for k in range(8))


def hop_col(value, dy, dx, dc=0):
    pairs = []
    for y in range(2):
        for x in range(4):
            for c in range(2):
                to = (((y + dy) % 2) * 4 + (x + dx) % 4) * 2 + (c + dc) % 2
                pairs.append(((y * 4 + x) * 2 + c, to))
    return lax.ppermute(value, "col", pairs)


def hop_row(value, dy, dz):
    pairs = []
    for z in range(4):
        for y in range(2):
            pairs.append((z * 2 + y, ((z + dz) % 4) * 2 + (y + dy) % 2))
    return lax.ppermute(value, "row", pairs)


def in_vmem(*values):
    return [pltpu.with_memory_space_constraint(v, VMEM) for v in values]


def vmem_specs(n):
    return [pl.BlockSpec(memory_space=VMEM)] * n


def call(
    body,
    outs,
    vmem_args,
    smem_args=(),
    after=(),
    scratch=(),
    alias=None,
    flops=0,
    nbytes=0,
):
    single = not isinstance(outs, (list, tuple))
    skip = len(smem_args) + len(vmem_args)

    def run(*refs):
        body(*refs[:skip], *refs[skip + len(after) :])

    return pl.pallas_call(
        run,
        out_shape=outs,
        in_specs=[pl.BlockSpec(memory_space=pltpu.SMEM)] * len(smem_args)
        + vmem_specs(len(vmem_args))
        + [pl.BlockSpec(memory_space=pl.ANY)] * len(after),
        out_specs=pl.BlockSpec(memory_space=VMEM) if single else vmem_specs(len(outs)),
        scratch_shapes=list(scratch),
        input_output_aliases=alias or {},
        compiler_params=pltpu.CompilerParams(vmem_limit_bytes=LIMIT),
        cost_estimate=pl.CostEstimate(flops=flops, bytes_accessed=nbytes, transcendentals=0),
    )(*smem_args, *in_vmem(*vmem_args), *after)


def write_extra(ref, row, value):
    for j in range(4):
        ref[row : row + 16, j * 256 : (j + 1) * 256] = value[16 * j : 16 * j + 16].astype(BF16)


def read_extra(ref, row):
    return jnp.concatenate(
        [ref[row : row + 16, j * 256 : (j + 1) * 256].astype(F32) for j in range(4)], axis=0
    )


def rounded(value):
    return value.astype(BF16).astype(F32)


def write_fine(ref, row, value):
    write_extra(ref, row, value)
    write_extra(ref, row + 16, value - rounded(value))


def read_fine(ref, row):
    return read_extra(ref, row) + read_extra(ref, row + 16)


def fine(value):
    high = rounded(value)
    return high + rounded(value - high)


def places():
    return lax.axis_index("col"), lax.axis_index("row")


def first_round(value, step, swap, to=None):
    to = to or [value] * 3
    return [value, step(to[0], 1), step(to[1], -1), swap(value), step(to[2], 2)]


def second_round(near, step, swap):
    return [step(near[PAIR], 1), step(near[PAIR], -1), swap(near[OPPOSITE])]


def place_of(index, me, other_bit, ring_shift):
    other = ((index ^ me) >> other_bit) & 1
    offset = ((index >> ring_shift) - (me >> ring_shift)) & 3
    return (PLACE >> ((other * 4 + offset) * 4)) & 15


def bring(first, last, stored, tiles, sems):
    copies = []
    for k, at in enumerate(range(first, last, 8)):
        part = pl.ds(at, 8)
        copies.append(pltpu.make_async_copy(stored.at[part], tiles.at[part], sems.at[k]))
        copies[-1].start()
    return copies


def plan_body(pairs, count, stored, tiles, lists, sizes, sems):
    copies = bring(0, 128, stored, tiles, sems)
    col, row = places()

    def put(base, which, entry, counts):
        at = (counts >> (which * 8)) & 255
        lists[(base + which) * ROOM + at] = entry
        return counts + (jnp.int32(1) << (which * 8))

    def sort(i, carry):
        d = pairs[0, i]
        s = pairs[1, i]
        c = s >> 2
        q = d >> 2
        sib = (c ^ col) & 1
        source = place_of(c, col, 3, 1) * 4 + (s & 3)
        target = place_of(q, row, 0, 1) * 4 + (d & 3)
        far = (source >= 4 * NEAR).astype(jnp.int32)
        entry = i | (target << 8) | ((source - far * 4 * NEAR) << 16)
        ahead = put(0, far * 2 + sib, entry, carry[0])
        far = (target >= 4 * NEAR).astype(jnp.int32)
        entry = i | ((target - far * 4 * NEAR) << 8) | (source << 16)
        back = put(4, far * 2 + sib, entry, carry[1])
        return ahead, back

    counts = lax.fori_loop(0, count[0], sort, (jnp.int32(0), jnp.int32(0)))
    for k in range(8):
        at = (counts[k // 4] >> (8 * (k % 4))) & 255
        sizes[k] = at
        for j in range(GROUP - 1):
            lists[k * ROOM + at + j] = 32 << 8 if k < 4 else 32 << 16
    for copy in copies:
        copy.wait()


def over_list(which, lists, sizes, product, total, to_target):
    def step(g, carry):
        news = []
        for j in range(GROUP):
            entry = lists[which * ROOM + g * GROUP + j]
            i = entry & 255
            d = (entry >> 8) & 255
            s = entry >> 16
            news.append((d if to_target else s, product(i, d, s)))
        for at, new in news:
            total[at] += new
        return carry

    lax.fori_loop(0, (sizes[which] + GROUP - 1) // GROUP, step, 0)


def pack_body(n, *rest):
    for k in range(n):
        rest[n][4 * k : 4 * k + 4] = rest[k][...].reshape(4, TILE, 128)
    for out in rest[n + 1 :]:
        out[...] = rest[PAIR][...]


def forward_step(lists, sizes, tiles, which, blocks, total):
    def product(i, d, s):
        return jnp.dot(tiles[i], blocks[s], preferred_element_type=F32)

    over_list(which, lists, sizes, product, total, True)


def forward_near_body(lists, sizes, tiles, mine, sib, total):
    total[...] = jnp.zeros_like(total)
    forward_step(lists, sizes, tiles, 0, mine, total)
    forward_step(lists, sizes, tiles, 1, sib, total)


def forward_far_body(lists, sizes, tiles, mine, before, total):
    forward_step(lists, sizes, tiles, 2, mine, total)


def forward_last_body(lists, sizes, tiles, sib, before, total, *outs):
    forward_step(lists, sizes, tiles, 3, sib, total)
    for k in range(8):
        outs[k][...] = total[4 * k : 4 * k + 4].reshape(1024, 128).astype(outs[k].dtype)


def hold_dz(parts, held):
    for k, ref in enumerate(parts):
        for b in range(4):
            held[4 * k + b] = ref[0:128, b * TILE : (b + 1) * TILE]


def backward_step(lists, sizes, tiles, which, held, total):
    def product(i, d, s):
        return jnp.dot(held[d], tiles[i], preferred_element_type=F32)

    over_list(which, lists, sizes, product, total, False)


def backward_near_body(lists, sizes, tiles, *rest):
    parts, (mine, sib, held) = rest[:NEAR], rest[NEAR:]
    hold_dz(parts, held)
    mine[...] = jnp.zeros_like(mine)
    sib[...] = jnp.zeros_like(sib)
    backward_step(lists, sizes, tiles, 5, held, sib)
    backward_step(lists, sizes, tiles, 4, held, mine)


def write_places(total, first, outs):
    for k, ref in enumerate(outs):
        for b in range(4):
            new = total[4 * (first + k) + b].astype(ref.dtype)
            ref[0:128, b * TILE : (b + 1) * TILE] = new


def backward_sib_body(lists, sizes, tiles, *rest):
    parts, (quarter, other, before, sib, far, near, quarter_out, held) = rest[:3], rest[3:]
    hold_dz(parts, held)
    backward_step(lists, sizes, tiles, 7, held, sib)
    write_places(sib, PAIR_LEFT, [far.at[pl.ds(128 * k, 128)] for k in range(3)])
    write_places(sib, OWN, [near.at[k] for k in range(5)])
    total = read_fine(quarter, 0) + read_fine(other, 0)
    quarter_out[...] = fine(total)
    write_fine(far, 384, total)


def backward_mine_body(lists, sizes, tiles, *rest):
    parts, (before, mine, held) = rest[:3], rest[3:]
    hold_dz(parts, held)
    backward_step(lists, sizes, tiles, 6, held, mine)


def add_sib_near_body(mine, got, *outs):
    for k, ref in enumerate(outs):
        for b in range(4):
            nodes = slice(b * TILE, (b + 1) * TILE)
            new = mine[4 * k + b] + got[k, :, nodes].astype(F32)
            ref[:, nodes] = new.astype(ref.dtype)


def add_sib_far_body(mine, got, quarter, *rest):
    outs, quarter_out = rest[:3], rest[3]
    total = quarter[...] + read_fine(got, 384)
    quarter_out[...] = rounded(total)
    for k, ref in enumerate(outs):
        for b in range(4):
            nodes = slice(b * TILE, (b + 1) * TILE)
            new = mine[4 * (PAIR_LEFT + k) + b] + got[128 * k : 128 * k + 128, nodes].astype(F32)
            ref[0:128, nodes] = new.astype(BF16)
        write_extra(ref, 128, total)


def add_round_body(n, own_extra, pair, opposite, a, b, c, *rest):
    pair_out, opposite_out = rest[-2:]
    new = pair[...] + (a[0:n].astype(F32) + b[0:n].astype(F32))
    pair_out[0:n] = new.astype(BF16)
    opposite_out[0:n] = (opposite[...] + c[0:n].astype(F32)).astype(BF16)
    if own_extra:
        own = rest[0]
        write_extra(opposite_out, n, own[...])
        opposite_out[n + 16 : n + 32] = c[n : n + 16]
        pair_out[n : n + 16] = b[n : n + 16]
        pair_out[n + 16 : n + 32] = a[n : n + 16]


def reduce_places(parts, step, swap, own_extra=()):
    n, lanes = parts[OWN].shape
    from_right = step(parts[PAIR_LEFT], -1)
    from_left = step(parts[PAIR_RIGHT], 1)
    from_pair = swap(parts[PAIR_OPPOSITE])
    sent = VMEM((n + 32 * len(own_extra), lanes), BF16)
    left = step(parts[LEFT], -1)
    right = step(parts[RIGHT], 1)
    pair, opposite = call(
        functools.partial(add_round_body, n, bool(own_extra)),
        [sent, sent],
        [parts[PAIR], parts[OPPOSITE], from_right, from_left, from_pair, *own_extra],
        nbytes=4 << 20,
    )
    opposite = step(opposite, 2)
    pair = swap(pair)
    return [parts[OWN], left, right, opposite, pair], [from_left, from_right, from_pair]


def dense_body(bias, feats, upstream, w_self, w_neigh, *rest):
    sums = rest[:5]
    hidden, dpre_out, dz_out, *dz_to, quarter, agg_out, grads = rest[5:]
    for b in range(4):
        rows = slice(b * TILE, (b + 1) * TILE)
        agg = sums[0][rows]
        for ref in sums[1:]:
            agg = agg + ref[rows].astype(F32)
        agg = agg.astype(BF16)
        agg_out[rows] = agg
        pre = jnp.dot(feats[rows], w_self[...], preferred_element_type=F32)
        pre = pre + jnp.dot(agg, w_neigh[...], preferred_element_type=F32) + bias[...]
        sig = jax.nn.sigmoid(pre)
        hidden[rows] = (pre * sig).astype(BF16)
        slope = sig * (1.0 + pre * (1.0 - sig))
        dpre = (upstream[rows].astype(F32) * slope).astype(BF16)
        dpre_out[rows] = dpre
        dz = lax.dot_general(
            w_neigh[...], dpre, (((1,), (1,)), ((), ())), preferred_element_type=F32
        ).astype(BF16)
        for ref in [dz_out, *dz_to]:
            ref[0:128, rows] = dz
    over_nodes = (((0,), (0,)), ((), ()))
    grads[0:128] = lax.dot_general(
        feats[...], dpre_out[...], over_nodes, preferred_element_type=F32
    )
    grads[128:256] = lax.dot_general(
        agg_out[...], dpre_out[...], over_nodes, preferred_element_type=F32
    )
    z = lax.axis_index("row") >> 1

    def piece(k):
        return grads[pl.ds(pl.multiple_of(((z + k) & 3) * 64, 64), 64), :]

    quarter[...] = piece(0)
    for ref, k in zip(dz_to, (1, 3, 2)):
        write_extra(ref, 128, piece(k))


def ring_sum_body(quarter, opposite, left, right, out):
    total = quarter[...] + read_extra(left, 128)
    write_fine(out, 0, total + (read_extra(right, 128) + read_extra(opposite, 128)))


def own_grad_body(dpre, w_self, own_grad):
    own_grad[...] = lax.dot_general(
        w_self[...], dpre[...], (((1,), (1,)), ((), ())), preferred_element_type=F32
    )


def finish_body(own_grad, *rest):
    out = rest[-1]
    for b in range(4):
        nodes = slice(b * TILE, (b + 1) * TILE)
        total = own_grad[:, nodes]
        for ref in rest[:-1]:
            total = total + ref[0:128, nodes].astype(F32)
        out[nodes] = total.T.astype(BF16)


def weight_sum_body(own, left, right, pair, from_opposite, from_pair, out, parts):
    col, _ = places()
    y, x = col >> 3, (col >> 1) & 3
    parts[y * 4 + x] = own[...]
    parts[y * 4 + ((x + 3) & 3)] = read_extra(left, 128)
    parts[y * 4 + ((x + 1) & 3)] = read_extra(right, 128)
    parts[(1 - y) * 4 + x] = read_extra(pair, 128)
    parts[y * 4 + ((x + 2) & 3)] = read_extra(from_opposite, 128)
    parts[(1 - y) * 4 + ((x + 2) & 3)] = read_extra(from_opposite, 144)
    parts[(1 - y) * 4 + ((x + 3) & 3)] = read_extra(from_pair, 128)
    parts[(1 - y) * 4 + ((x + 1) & 3)] = read_extra(from_pair, 144)
    total = parts[0]
    for k in range(1, 8):
        total = total + parts[k]
    out[...] = total


def weight_join_body(scale, own, *rest):
    others, (grad_self, grad_neigh, held) = rest[:3], rest[3:]
    z = lax.axis_index("row") >> 1
    for k, ref in enumerate([own, *others]):
        at = pl.multiple_of(((z + k) & 3) * 64, 64)
        held[pl.ds(at, 64), :] = ref[...] * scale
    grad_self[...] = held[0:128]
    grad_neigh[...] = held[128:256]


def shards(
    features, weight_self, weight_neigh, bias_term, upstream, tile_values, block_pairs, tile_counts
):
    nodes = 131072
    tile_bytes = 128 * TILE * TILE * 2
    share = 32 * 2 * TILE * TILE * 128
    in_hbm = pltpu.with_memory_space_constraint(tile_values.reshape(128, TILE, TILE), pltpu.HBM)
    with jax.named_scope("plan"):
        tiles, lists, sizes = pl.pallas_call(
            plan_body,
            out_shape=[
                VMEM((128, TILE, TILE), BF16),
                pltpu.SMEM((8 * ROOM,), jnp.int32),
                pltpu.SMEM((8,), jnp.int32),
            ],
            in_specs=[pl.BlockSpec(memory_space=pltpu.SMEM)] * 2
            + [pl.BlockSpec(memory_space=pl.ANY)],
            out_specs=[pl.BlockSpec(memory_space=VMEM)]
            + [pl.BlockSpec(memory_space=pltpu.SMEM)] * 2,
            scratch_shapes=[pltpu.SemaphoreType.DMA((16,))],
            compiler_params=pltpu.CompilerParams(vmem_limit_bytes=LIMIT),
            cost_estimate=pl.CostEstimate(flops=0, bytes_accessed=tile_bytes, transcendentals=0),
        )(block_pairs[0, 0].T, tile_counts.reshape(-1), in_hbm)
    by_list = [lists, sizes]

    with jax.named_scope("gather_features"):
        step, swap = (lambda v, d: hop_col(v, 0, d)), (lambda v: hop_col(v, 1, 0))
        near_blocks, far_blocks = VMEM((4 * NEAR, TILE, 128), BF16), VMEM((12, TILE, 128), BF16)
        near = first_round(features, step, swap)
        near_mine, near[PAIR] = call(
            functools.partial(pack_body, NEAR),
            [near_blocks, VMEM((1024, 128), BF16)],
            near,
            after=[sizes],
        )
        far = second_round(near, step, swap)
        near_sib = hop_col(near_mine, 0, 0, 1)
    with jax.named_scope("forward_tiles"):
        total = VMEM((33, TILE, 128), F32)
        sums = call(
            forward_near_body,
            total,
            [tiles, near_mine, near_sib],
            by_list,
        )
        far_mine = call(functools.partial(pack_body, 3), far_blocks, far, after=[sums])
        far_sib = hop_col(far_mine, 0, 0, 1)
        sums = call(
            forward_far_body,
            total,
            [tiles, far_mine, sums],
            by_list,
            alias={4: 0},
            flops=share,
            nbytes=tile_bytes // 4,
        )
        f32, bf16 = VMEM((1024, 128), F32), VMEM((1024, 128), BF16)
        _, *partial = call(
            forward_last_body,
            [total, f32, bf16, bf16, f32, f32, bf16, bf16, bf16],
            [tiles, far_sib, sums],
            by_list,
            alias={4: 0},
            flops=share,
            nbytes=tile_bytes // 4,
        )
    with jax.named_scope("sum_aggregates"):
        step, swap = (lambda v, d: hop_row(v, 0, d)), (lambda v: hop_row(v, 1, 0))
        sums, _ = reduce_places(partial, step, swap)
    with jax.named_scope("dense"):
        longer = VMEM((144, 1024), BF16)
        block = VMEM((64, 256), F32)
        hidden, dpre, dz, *dz_to, quarter = call(
            dense_body,
            [
                jax.ShapeDtypeStruct((1024, 256), BF16),
                VMEM((1024, 256), BF16),
                VMEM((128, 1024), BF16),
                longer,
                longer,
                longer,
                block,
            ],
            [bias_term.reshape(1, 256), features, upstream, weight_self, weight_neigh, *sums],
            scratch=[VMEM((1024, 128), BF16), VMEM((256, 256), F32)],
            flops=5 * 2 * 1024 * 128 * 256,
            nbytes=6 << 20,
        )
    with jax.named_scope("gather_dz"):
        near = first_round(dz, step, swap, dz_to)
        quarter = call(
            ring_sum_body,
            VMEM((32, 1024), BF16),
            [quarter, near[OPPOSITE], near[LEFT], near[RIGHT]],
        )
        quarter_pair = swap(quarter)
        far = second_round(near, step, swap)
    with jax.named_scope("own_grad"):
        own_grad = call(
            own_grad_body,
            VMEM((128, 1024), F32),
            [dpre, weight_self],
            flops=2 * 1024 * 128 * 256,
            nbytes=2 << 20,
        )
    with jax.named_scope("backward_tiles"):
        total = VMEM((33, 128, TILE), F32)
        held = [VMEM((4 * NEAR, 128, TILE), BF16)]
        mine, sib = call(
            backward_near_body,
            [total, total],
            [tiles, *near],
            by_list,
            after=[own_grad],
            scratch=held,
            flops=2 * share,
            nbytes=tile_bytes // 2,
        )
        _, sib_far, sib_near, quarter = call(
            backward_sib_body,
            [total, VMEM((416, 1024), BF16), VMEM((5, 128, 1024), BF16), block],
            [tiles, *far, quarter, quarter_pair, sib],
            by_list,
            alias={8: 0},
            scratch=held,
            flops=share,
            nbytes=tile_bytes // 4,
        )
        mine = call(
            backward_mine_body,
            total,
            [tiles, *far, mine],
            by_list,
            scratch=held,
            alias={6: 0},
            flops=share,
            nbytes=tile_bytes // 4,
        )
    with jax.named_scope("sum_grads"):
        step, swap = (lambda v, d: hop_col(v, 0, d)), (lambda v: hop_col(v, 1, 0))
        f32, bf16 = VMEM((128, 1024), F32), VMEM((128, 1024), BF16)
        *far, quarter = call(
            add_sib_far_body,
            [longer, longer, longer, block],
            [mine, hop_col(sib_far, 0, 0, 1), quarter],
            nbytes=3 << 20,
        )
        near = call(
            add_sib_near_body,
            [f32, bf16, bf16, f32, f32],
            [mine, hop_col(sib_near, 0, 0, 1)],
            nbytes=5 << 20,
        )
        sums, came = reduce_places([*near, *far], step, swap, [quarter])
    with jax.named_scope("sum_weights"):
        quarter = call(
            weight_sum_body,
            block,
            [quarter, *came, sums[3], sums[4]],
            scratch=[VMEM((8, 64, 256), F32)],
            nbytes=1 << 20,
        )
        shape = jax.ShapeDtypeStruct((128, 256), F32)
        grad_self, grad_neigh = call(
            functools.partial(weight_join_body, float(nodes) ** -0.5),
            [shape, shape],
            [quarter, *[hop_row(quarter, 0, -k) for k in (1, 2, 3)]],
            scratch=[VMEM((256, 256), F32)],
            nbytes=1 << 20,
        )
    with jax.named_scope("finish"):
        grad_features = call(
            finish_body,
            jax.ShapeDtypeStruct((1024, 128), BF16),
            [own_grad, *sums],
            nbytes=4 << 20,
        )
    return hidden, grad_features, grad_self, grad_neigh


def solution(mesh):
    placed = (
        P(("row", "col"), None),
        P(),
        P(),
        P(),
        P(("row", "col"), None),
        P("row", "col", None, None, None),
        P("row", "col", None, None),
        P("row", "col"),
    )
    return jax.shard_map(
        shards,
        mesh=mesh,
        in_specs=placed,
        out_specs=(P(("row", "col"), None), P(("row", "col"), None), P(), P()),
        check_vma=False,
    )
```

time: 154 us -> 121 us (0.79)
  waiting for transfers between devices: 64 us -> 43.9 us
  starting transfers between devices: 63.4 us -> 48.9 us
  Pallas kernels: 22.4 us -> 25.8 us
    ppermute x27 -> x18, starting transfers between devices: 28.7 us -> 17.5 us  [hop_col(): return lax.ppermute(value, 'col', pairs)]
    ppermute x27 -> x18, waiting for transfers between devices: 37.3 us -> 26.2 us  [hop_col(): return lax.ppermute(value, 'col', pairs)]
    ppermute x21 -> x18, waiting for transfers between devices: 26.7 us -> 17.7 us  [hop_row(): return lax.ppermute(value, 'row', pairs)]
    pallas_call x22 -> x18, Pallas kernels: 15.9 us -> 19.3 us  [call(): pl.pallas_call(run, out_shape=outs, in_specs=[pl.BlockSpec(memory_space=p...]
    ppermute x1 -> x0, starting transfers between devices: 2.73 us -> none  [hop_diag(): return lax.ppermute(value, ('row', 'col'), pairs)]
    ppermute x21 -> x18, starting transfers between devices: 31.9 us -> 31.4 us  [hop_row(): return lax.ppermute(value, 'row', pairs)]
  transfers between devices with their start and end apart: 49 -> 36, of which waited for: 22 -> 16; matrix products, arithmetic and copies ran while one was open for 1% -> 0% of each run, Pallas kernels for 11% -> 16%
where the time goes in v3:
time: 121 us
  starting transfers between devices  48.9 us (40%)
  waiting for transfers between devices  43.9 us (36%)
  Pallas kernels  25.8 us (21%)
  between operations  1.57 us (1%)
    ppermute x18, starting transfers between devices, hop_row(): return lax.ppermute(value, 'row', pairs)  31.4 us
    ppermute x18, waiting for transfers between devices, hop_col(): return lax.ppermute(value, 'col', pairs)  26.2 us
    pallas_call x18, Pallas kernels, call(): pl.pallas_call(run, out_shape=outs, in_specs=[pl.BlockSpec(memory_space=p...  19.3 us
    ppermute x18, waiting for transfers between devices, hop_row(): return lax.ppermute(value, 'row', pairs)  17.7 us
    ppermute x18, starting transfers between devices, hop_col(): return lax.ppermute(value, 'col', pairs)  17.5 us
    pallas_call x1, Pallas kernels, shards(): pl.pallas_call(plan_body, out_shape=[VMEM((128, TILE, TILE), BF16), pltpu...  6.48 us
  transfers between devices with their start and end apart: 36, of which 16 were waited for; matrix products, arithmetic and copies ran while one was open for 0% of the time, Pallas kernels for 16%

profile of v3, /device:TPU:0, one launch (start us, length us, event | category | flops | bytes accessed | tf_op | source)
XLA Modules:
  0.0 120.8 jit_solution(13843885398681355277)
XLA Ops:
  0.6 3.2 %collective-permute-start.3 = (bf16[1024,128]{1,0:T(8,128)(2,1)}, bf16[1024,128]{1,0:T(8,128)(2,1)S(1)}, u32[]{:S(2)}, u32[]{:S(2)}) collective-permute-start(bf16[1024,128]{1,0:T(8,128)(2,1)} %refs_1_.2), channel_id=1, source_target_pairs={{0,4},{1,5},{2,6},{3,7},{4,0},{5,1},{6,2},{7,3},{8,12},{9,13},{10,... | collective-permute-start | bytes 786440 | tf_op jit(solution)/shard_map/gather_features/ppermute | solution.py:31
  3.8 1.6 %collective-permute-start.2 = (bf16[1024,128]{1,0:T(8,128)(2,1)}, bf16[1024,128]{1,0:T(8,128)(2,1)S(1)}, u32[]{:S(2)}, u32[]{:S(2)}) collective-permute-start(bf16[1024,128]{1,0:T(8,128)(2,1)} %refs_1_.2), channel_id=1, source_target_pairs={{0,8},{1,9},{2,10},{3,11},{4,12},{5,13},{6,14},{7,15},{8,0},{9,1},... | collective-permute-start | bytes 786440 | tf_op jit(solution)/shard_map/gather_features/ppermute | solution.py:31
  8.8 6.5 %plan.1 = (bf16[128,256,256]{2,1,0:T(8,128)(2,1)S(1)}, s32[1152]{0:T(1024)S(4)}, s32[8]{0:T(128)S(4)}) custom-call(s32[2,128]{1,0:T(2,128)S(1)} %bitcast.7, s32[1]{0:T(128)} %bitcast.6.count, bf16[128,256,256]{2,1,0:T(8,128)(2,1)} %bitcast.9), custom_call_target="tpu_custom_call" | custom-call | bytes 16777216 | tf_op jit(solution)/shard_map/plan/pallas_call | solution.py:412
  16.5 1.7 %collective-permute-start.6 = (bf16[1024,128]{1,0:T(8,128)(2,1)S(1)}, bf16[1024,128]{1,0:T(8,128)(2,1)S(1)}, u32[]{:S(2)}, u32[]{:S(2)}) collective-permute-start(bf16[1024,128]{1,0:T(8,128)(2,1)S(1)} %collective-permute-done.3.refs_4_), channel_id=1, source_target_pairs={{0,8},{1,9},{2,10},{3,11},{4,12},{5,13},{6,14},{7,15},{8,0},{9,1},... | collective-permute-start | bytes 786440 | tf_op jit(solution)/shard_map/gather_features/ppermute | solution.py:31
  18.2 2.6 %collective-permute-start.5 = (bf16[1024,128]{1,0:T(8,128)(2,1)S(1)}, bf16[1024,128]{1,0:T(8,128)(2,1)S(1)}, u32[]{:S(2)}, u32[]{:S(2)}) collective-permute-start(bf16[1024,128]{1,0:T(8,128)(2,1)S(1)} %get-tuple-element.47), channel_id=1, source_target_pairs={{0,6},{1,7},{2,0},{3,1},{4,2},{5,3},{6,4},{7,5},{8,14},{9,15},{10,... | collective-permute-start | bytes 786440 | tf_op jit(solution)/shard_map/gather_features/ppermute | solution.py:31
  20.8 4.6 %forward_tiles.4.refs_3_.refs_4_ = f32[33,256,128]{2,1,0:T(8,128)S(1)} custom-call(s32[1152]{0:T(1024)S(4)} %get-tuple-element.44.refs_0_, s32[8]{0:T(128)S(4)} %get-tuple-element.45.refs_5_.refs_1_, bf16[128,256,256]{2,1,0:T(8,128)(2,1)S(1)} %get-tuple-element.46.refs_2_, bf16[20,256,128]{2,1,0:T(8,128)(2,1)S(1)} %get-tuple-element.48.refs_3_, ...), custom_call_target="tpu_custom_call" | custom-call | tf_op jit(solution)/shard_map/forward_tiles/pallas_call | solution.py:67
  26.7 3.4 %collective-permute-done.4.refs_0_ = bf16[1024,128]{1,0:T(8,128)(2,1)S(1)} collective-permute-done((bf16[1024,128]{1,0:T(8,128)(2,1)S(1)}, bf16[1024,128]{1,0:T(8,128)(2,1)S(1)}, u32[]{:S(2)}, u32[]{:S(2)}) %collective-permute-start.4) | collective-permute-done | bytes 262176 | tf_op jit(solution)/shard_map/gather_features/ppermute | solution.py:31
  30.2 1.4 %forward_tiles.6.refs_4_ = f32[33,256,128]{2,1,0:T(8,128)S(1)} custom-call(s32[1152]{0:T(1024)S(4)} %get-tuple-element.44.refs_0_, s32[8]{0:T(128)S(4)} %get-tuple-element.45.refs_5_.refs_1_, bf16[128,256,256]{2,1,0:T(8,128)(2,1)S(1)} %get-tuple-element.46.refs_2_, bf16[12,256,128]{2,1,0:T(8,128)(2,1)S(1)} %forward_tiles.5.refs_3_, ...), custom_call_target="tpu_custom_call", output_to_operand_aliasing={{}: (4, {})} | custom-call | flops 536870912 | bytes 4194304 | tf_op jit(solution)/shard_map/forward_tiles/pallas_call | solution.py:67
  32.5 1.6 %forward_tiles.7 = (f32[33,256,128]{2,1,0:T(8,128)S(1)}, f32[1024,128]{1,0:T(8,128)S(1)}, bf16[1024,128]{1,0:T(8,128)(2,1)S(1)}, bf16[1024,128]{1,0:T(8,128)(2,1...) custom-call(s32[1152]{0:T(1024)S(4)} %get-tuple-element.44.refs_0_, ...), custom_call_target="tpu_custom_call", output_to_operand_aliasing={{0}: (4, {})} | custom-call | flops 536870912 | bytes 4194304 | tf_op jit(solution)/shard_map/forward_tiles/pallas_call | solution.py:67
  34.2 4.1 %collective-permute-start.11 = (bf16[1024,128]{1,0:T(8,128)(2,1)S(1)}, bf16[1024,128]{1,0:T(8,128)(2,1)S(1)}, u32[]{:S(2)}, u32[]{:S(2)}) collective-permute-start(bf16[1024,128]{1,0:T(8,128)(2,1)S(1)} %get-tuple-element.54), channel_id=1, source_target_pairs={{0,96},{16,112},{32,0},{48,16},{64,32},{80,48},{96,64},{112,80},{1... | collective-permute-start | bytes 786440 | tf_op jit(solution)/shard_map/sum_aggregates/ppermute | solution.py:39
  38.3 2.2 %collective-permute-start.13 = (bf16[1024,128]{1,0:T(8,128)(2,1)S(1)}, bf16[1024,128]{1,0:T(8,128)(2,1)S(1)}, u32[]{:S(2)}, u32[]{:S(2)}) collective-permute-start(bf16[1024,128]{1,0:T(8,128)(2,1)S(1)} %get-tuple-element.56), channel_id=1, source_target_pairs={{0,16},{16,0},{32,48},{48,32},{64,80},{80,64},{96,112},{112,96},{1... | collective-permute-start | bytes 786440 | tf_op jit(solution)/shard_map/sum_aggregates/ppermute | solution.py:39
  40.5 3.2 %collective-permute-start.9 = (bf16[1024,128]{1,0:T(8,128)(2,1)S(1)}, bf16[1024,128]{1,0:T(8,128)(2,1)S(1)}, u32[]{:S(2)}, u32[]{:S(2)}) collective-permute-start(bf16[1024,128]{1,0:T(8,128)(2,1)S(1)} %get-tuple-element.50), channel_id=1, source_target_pairs={{0,96},{16,112},{32,0},{48,16},{64,32},{80,48},{96,64},{112,80},{1... | collective-permute-start | bytes 786440 | tf_op jit(solution)/shard_map/sum_aggregates/ppermute | solution.py:39
  44.9 3.6 %collective-permute-done.12.refs_3_ = bf16[1024,128]{1,0:T(8,128)(2,1)S(1)} collective-permute-done((bf16[1024,128]{1,0:T(8,128)(2,1)S(1)}, bf16[1024,128]{1,0:T(8,128)(2,1)S(1)}, u32[]{:S(2)}, u32[]{:S(2)}) %collective-permute-start.12) | collective-permute-done | bytes 262176 | tf_op jit(solution)/shard_map/sum_aggregates/ppermute | solution.py:39
  49.6 2.2 %collective-permute-start.15 = (bf16[1024,128]{1,0:T(8,128)(2,1)S(1)}, bf16[1024,128]{1,0:T(8,128)(2,1)S(1)}, u32[]{:S(2)}, u32[]{:S(2)}) collective-permute-start(bf16[1024,128]{1,0:T(8,128)(2,1)S(1)} %get-tuple-element.58), channel_id=1, source_target_pairs={{0,16},{16,0},{32,48},{48,32},{64,80},{80,64},{96,112},{112,96},{1... | collective-permute-start | bytes 786440 | tf_op jit(solution)/shard_map/sum_aggregates/ppermute | solution.py:39
  51.8 7.0 %collective-permute-done.10.refs_7_ = bf16[1024,128]{1,0:T(8,128)(2,1)S(1)} collective-permute-done((bf16[1024,128]{1,0:T(8,128)(2,1)S(1)}, bf16[1024,128]{1,0:T(8,128)(2,1)S(1)}, u32[]{:S(2)}, u32[]{:S(2)}) %collective-permute-start.10) | collective-permute-done | bytes 262176 | tf_op jit(solution)/shard_map/sum_aggregates/ppermute | solution.py:39
  58.8 2.3 %dense.1 = (bf16[1024,256]{1,0:T(8,128)(2,1)}, bf16[1024,256]{1,0:T(8,128)(2,1)S(1)}, bf16[128,1024]{1,0:T(8,128)(2,1)S(1)}, bf16[144,1024]{1,0:T(8,128)(2,1)S(1...) custom-call(f32[1,256]{1,0:T(1,128)S(1)} %bitcast.8, ...), custom_call_target="tpu_custom_call" | custom-call | flops 335544320 | bytes 6291456 | tf_op jit(solution)/shard_map/dense/pallas_call | solution.py:67
  61.1 1.3 %collective-permute-start.19 = (bf16[144,1024]{1,0:T(8,128)(2,1)S(1)}, bf16[144,1024]{1,0:T(8,128)(2,1)S(1)}, u32[]{:S(2)}, u32[]{:S(2)}) collective-permute-start(bf16[144,1024]{1,0:T(8,128)(2,1)S(1)} %get-tuple-element.62), channel_id=1, source_target_pairs={{0,64},{16,80},{32,96},{48,112},{64,0},{80,16},{96,32},{112,48},{1... | collective-permute-start | bytes 884744 | tf_op jit(solution)/shard_map/gather_dz/ppermute | solution.py:39
  62.4 2.3 %collective-permute-start.16 = (bf16[128,1024]{1,0:T(8,128)(2,1)S(1)}, bf16[128,1024]{1,0:T(8,128)(2,1)S(1)}, u32[]{:S(2)}, u32[]{:S(2)}) collective-permute-start(bf16[128,1024]{1,0:T(8,128)(2,1)S(1)} %get-tuple-element.61.refs_3_), channel_id=1, source_target_pairs={{0,16},{16,0},{32,48},{48,32},{64,80},{80,64},{96,112},{112,96},{1... | collective-permute-start | bytes 786440 | tf_op jit(solution)/shard_map/gather_dz/ppermute | solution.py:39
  64.8 3.2 %collective-permute-start.22 = (bf16[144,1024]{1,0:T(8,128)(2,1)S(1)}, bf16[144,1024]{1,0:T(8,128)(2,1)S(1)}, u32[]{:S(2)}, u32[]{:S(2)}) collective-permute-start(bf16[144,1024]{1,0:T(8,128)(2,1)S(1)} %get-tuple-element.64), channel_id=1, source_target_pairs={{0,96},{16,112},{32,0},{48,16},{64,32},{80,48},{96,64},{112,80},{1... | collective-permute-start | bytes 884744 | tf_op jit(solution)/shard_map/gather_dz/ppermute | solution.py:39
  68.0 4.6 %collective-permute-done.19.refs_7_.refs_1_ = bf16[144,1024]{1,0:T(8,128)(2,1)S(1)} collective-permute-done((bf16[144,1024]{1,0:T(8,128)(2,1)S(1)}, bf16[144,1024]{1,0:T(8,128)(2,1)S(1)}, u32[]{:S(2)}, u32[]{:S(2)}) %collective-permute-start.19) | collective-permute-done | bytes 294944 | tf_op jit(solution)/shard_map/gather_dz/ppermute | solution.py:39
  72.6 2.2 %collective-permute-start.20 = (bf16[144,1024]{1,0:T(8,128)(2,1)S(1)}, bf16[144,1024]{1,0:T(8,128)(2,1)S(1)}, u32[]{:S(2)}, u32[]{:S(2)}) collective-permute-start(bf16[144,1024]{1,0:T(8,128)(2,1)S(1)} %collective-permute-done.19.refs_7_.refs_1_), channel_id=1, source_target_pairs={{0,16},{16,0},{32,48},{48,32},{64,80},{80,64},{96,112},{112,96},{1... | collective-permute-start | bytes 884744 | tf_op jit(solution)/shard_map/gather_dz/ppermute | solution.py:39
  75.0 1.8 %collective-permute-start.17 = (bf16[128,1024]{1,0:T(8,128)(2,1)S(1)}, bf16[128,1024]{1,0:T(8,128)(2,1)S(1)}, u32[]{:S(2)}, u32[]{:S(2)}) collective-permute-start(bf16[128,1024]{1,0:T(8,128)(2,1)S(1)} %collective-permute-done.16.refs_6_), channel_id=1, source_target_pairs={{0,32},{16,48},{32,64},{48,80},{64,96},{80,112},{96,0},{112,16},{1... | collective-permute-start | bytes 786440 | tf_op jit(solution)/shard_map/gather_dz/ppermute | solution.py:39
  77.5 1.7 %collective-permute-start.23 = (bf16[32,1024]{1,0:T(8,128)(2,1)S(1)}, bf16[32,1024]{1,0:T(8,128)(2,1)S(1)}, u32[]{:S(2)}, u32[]{:S(2)}) collective-permute-start(bf16[32,1024]{1,0:T(8,128)(2,1)S(1)} %gather_dz.1.refs_6_), channel_id=1, source_target_pairs={{0,16},{16,0},{32,48},{48,32},{64,80},{80,64},{96,112},{112,96},{1... | collective-permute-start | bytes 196616 | tf_op jit(solution)/shard_map/gather_dz/ppermute | solution.py:39
  79.2 4.1 %backward_tiles.3 = (f32[33,128,256]{2,1,0:T(8,128)S(1)}, f32[33,128,256]{2,1,0:T(8,128)S(1)}) custom-call(s32[1152]{0:T(1024)S(4)} %get-tuple-element.44.refs_0_, s32[8]{0:T(128)S(4)} %get-tuple-element.45.refs_5_.refs_1_, bf16[128,256,256]{2,1,0:T(8,128)(2,1)S(1)} %get-tuple-element.46.refs_2_, bf16[128,1024]{1,0:T(8,128)(2,1)S(1)} %get-tuple-element.61.refs_3_, ...), custom_call_target="tpu_custom_call" | custom-call | flops 1073741824 | bytes 8388608 | tf_op jit(solution)/shard_map/backward_tiles/pallas_call | solution.py:67
  83.4 1.4 %backward_tiles.5 = (f32[33,128,256]{2,1,0:T(8,128)S(1)}, bf16[416,1024]{1,0:T(8,128)(2,1)S(1)}, bf16[5,128,1024]{2,1,0:T(8,128)(2,1)S(1)}, f32[64,256]{1,0:T(8,128)S(1)}) custom-call(s32[1152]{0:T(1024)S(4)} %get-tuple-element.44.refs_0_, s32[8]{0:T(128)S(4)} %get-tuple-element.45.refs_5_.refs_1_, ...), custom_call_target="tpu_custom_call", output_to_operand_aliasing={{0}: (8, {})} | custom-call | flops 536870912 | bytes 4194304 | tf_op jit(solution)/shard_map/backward_tiles/pallas_call | solution.py:67
  86.4 2.7 %collective-permute-done.27.refs_1_ = bf16[416,1024]{1,0:T(8,128)(2,1)S(1)} collective-permute-done((bf16[416,1024]{1,0:T(8,128)(2,1)S(1)}, bf16[416,1024]{1,0:T(8,128)(2,1)S(1)}, u32[]{:S(2)}, u32[]{:S(2)}) %collective-permute-start.27) | collective-permute-done | bytes 852000 | tf_op jit(solution)/shard_map/sum_grads/ppermute | solution.py:31
  89.3 2.0 %collective-permute-start.29 = (bf16[144,1024]{1,0:T(8,128)(2,1)S(1)}, bf16[144,1024]{1,0:T(8,128)(2,1)S(1)}, u32[]{:S(2)}, u32[]{:S(2)}) collective-permute-start(bf16[144,1024]{1,0:T(8,128)(2,1)S(1)} %get-tuple-element.77), channel_id=1, source_target_pairs={{0,2},{1,3},{2,4},{3,5},{4,6},{5,7},{6,0},{7,1},{8,10},{9,11},{10,... | collective-permute-start | bytes 884744 | tf_op jit(solution)/shard_map/sum_grads/ppermute | solution.py:31
  91.9 6.5 %collective-permute-done.28.refs_2_ = bf16[144,1024]{1,0:T(8,128)(2,1)S(1)} collective-permute-done((bf16[144,1024]{1,0:T(8,128)(2,1)S(1)}, bf16[144,1024]{1,0:T(8,128)(2,1)S(1)}, u32[]{:S(2)}, u32[]{:S(2)}) %collective-permute-start.28) | collective-permute-done | bytes 294944 | tf_op jit(solution)/shard_map/sum_grads/ppermute | solution.py:31
  100.9 2.3 %collective-permute-start.25 = (bf16[128,1024]{1,0:T(8,128)(2,1)S(1)}, bf16[128,1024]{1,0:T(8,128)(2,1)S(1)}, u32[]{:S(2)}, u32[]{:S(2)}) collective-permute-start(bf16[128,1024]{1,0:T(8,128)(2,1)S(1)} %get-tuple-element.70), channel_id=1, source_target_pairs={{0,6},{1,7},{2,0},{3,1},{4,2},{5,3},{6,4},{7,5},{8,14},{9,15},{10,... | collective-permute-start | bytes 786440 | tf_op jit(solution)/shard_map/sum_grads/ppermute | solution.py:31
  103.3 8.9 %collective-permute-done.31.refs_4_ = bf16[160,1024]{1,0:T(8,128)(2,1)S(1)} collective-permute-done((bf16[160,1024]{1,0:T(8,128)(2,1)S(1)}, bf16[160,1024]{1,0:T(8,128)(2,1)S(1)}, u32[]{:S(2)}, u32[]{:S(2)}) %collective-permute-start.31) | collective-permute-done | bytes 327712 | tf_op jit(solution)/shard_map/sum_grads/ppermute | solution.py:31
  113.4 2.4 %collective-permute-start.34 = (f32[64,256]{1,0:T(8,128)S(1)}, f32[64,256]{1,0:T(8,128)S(1)}, u32[]{:S(2)}, u32[]{:S(2)}) collective-permute-start(f32[64,256]{1,0:T(8,128)S(1)} %sum_weights.2.refs_0_), channel_id=1, source_target_pairs={{0,64},{16,80},{32,96},{48,112},{64,0},{80,16},{96,32},{112,48},{1... | collective-permute-start | bytes 196616 | tf_op jit(solution)/shard_map/sum_weights/ppermute | solution.py:39
  115.8 2.3 %collective-permute-start.33 = (f32[64,256]{1,0:T(8,128)S(1)}, f32[64,256]{1,0:T(8,128)S(1)}, u32[]{:S(2)}, u32[]{:S(2)}) collective-permute-start(f32[64,256]{1,0:T(8,128)S(1)} %sum_weights.2.refs_0_), channel_id=1, source_target_pairs={{0,96},{16,112},{32,0},{48,16},{64,32},{80,48},{96,64},{112,80},{1... | collective-permute-start | bytes 196616 | tf_op jit(solution)/shard_map/sum_weights/ppermute | solution.py:39
  (71 shorter events, 18.2 us)
Async XLA Ops:
  0.6 14.6 %collective-permute-start.3 = (bf16[1024,128]{1,0:T(8,128)(2,1)}, bf16[1024,128]{1,0:T(8,128)(2,1)S(1)}, u32[]{:S(2)}, u32[]{:S(2)}) collective-permute-start(bf16[1024,128]{1,0:T(8,128)(2,1)} %refs_1_.2), channel_id=1, source_target_pairs={{0,4},{1,5},{2,6},{3,7},{4,0},{5,1},{6,2},{7,3},{8,12},{9,13},{10,... | collective-permute-start | bytes 786440 | tf_op jit(solution)/shard_map/gather_features/ppermute | solution.py:31
  3.8 11.4 %collective-permute-start.2 = (bf16[1024,128]{1,0:T(8,128)(2,1)}, bf16[1024,128]{1,0:T(8,128)(2,1)S(1)}, u32[]{:S(2)}, u32[]{:S(2)}) collective-permute-start(bf16[1024,128]{1,0:T(8,128)(2,1)} %refs_1_.2), channel_id=1, source_target_pairs={{0,8},{1,9},{2,10},{3,11},{4,12},{5,13},{6,14},{7,15},{8,0},{9,1},... | collective-permute-start | bytes 786440 | tf_op jit(solution)/shard_map/gather_features/ppermute | solution.py:31
  5.4 10.9 %collective-permute-start.1 = (bf16[1024,128]{1,0:T(8,128)(2,1)}, bf16[1024,128]{1,0:T(8,128)(2,1)S(1)}, u32[]{:S(2)}, u32[]{:S(2)}) collective-permute-start(bf16[1024,128]{1,0:T(8,128)(2,1)} %refs_1_.2), channel_id=1, source_target_pairs={{0,6},{1,7},{2,0},{3,1},{4,2},{5,3},{6,4},{7,5},{8,14},{9,15},{10,... | collective-permute-start | bytes 786440 | tf_op jit(solution)/shard_map/gather_features/ppermute | solution.py:31
  6.5 9.8 %collective-permute-start = (bf16[1024,128]{1,0:T(8,128)(2,1)}, bf16[1024,128]{1,0:T(8,128)(2,1)S(1)}, u32[]{:S(2)}, u32[]{:S(2)}) collective-permute-start(bf16[1024,128]{1,0:T(8,128)(2,1)} %refs_1_.2), channel_id=1, source_target_pairs={{0,2},{1,3},{2,4},{3,5},{4,6},{5,7},{6,0},{7,1},{8,10},{9,11},{10,... | collective-permute-start | bytes 786440 | tf_op jit(solution)/shard_map/gather_features/ppermute | solution.py:31
  16.5 8.9 %collective-permute-start.6 = (bf16[1024,128]{1,0:T(8,128)(2,1)S(1)}, bf16[1024,128]{1,0:T(8,128)(2,1)S(1)}, u32[]{:S(2)}, u32[]{:S(2)}) collective-permute-start(bf16[1024,128]{1,0:T(8,128)(2,1)S(1)} %collective-permute-done.3.refs_4_), channel_id=1, source_target_pairs={{0,8},{1,9},{2,10},{3,11},{4,12},{5,13},{6,14},{7,15},{8,0},{9,1},... | collective-permute-start | bytes 786440 | tf_op jit(solution)/shard_map/gather_features/ppermute | solution.py:31
  18.2 8.5 %collective-permute-start.5 = (bf16[1024,128]{1,0:T(8,128)(2,1)S(1)}, bf16[1024,128]{1,0:T(8,128)(2,1)S(1)}, u32[]{:S(2)}, u32[]{:S(2)}) collective-permute-start(bf16[1024,128]{1,0:T(8,128)(2,1)S(1)} %get-tuple-element.47), channel_id=1, source_target_pairs={{0,6},{1,7},{2,0},{3,1},{4,2},{5,3},{6,4},{7,5},{8,14},{9,15},{10,... | collective-permute-start | bytes 786440 | tf_op jit(solution)/shard_map/gather_features/ppermute | solution.py:31
  20.8 9.3 %collective-permute-start.4 = (bf16[1024,128]{1,0:T(8,128)(2,1)S(1)}, bf16[1024,128]{1,0:T(8,128)(2,1)S(1)}, u32[]{:S(2)}, u32[]{:S(2)}) collective-permute-start(bf16[1024,128]{1,0:T(8,128)(2,1)S(1)} %get-tuple-element.47), channel_id=1, source_target_pairs={{0,2},{1,3},{2,4},{3,5},{4,6},{5,7},{6,0},{7,1},{8,10},{9,11},{10,... | collective-permute-start | bytes 786440 | tf_op jit(solution)/shard_map/gather_features/ppermute | solution.py:31
  34.2 10.8 %collective-permute-start.11 = (bf16[1024,128]{1,0:T(8,128)(2,1)S(1)}, bf16[1024,128]{1,0:T(8,128)(2,1)S(1)}, u32[]{:S(2)}, u32[]{:S(2)}) collective-permute-start(bf16[1024,128]{1,0:T(8,128)(2,1)S(1)} %get-tuple-element.54), channel_id=1, source_target_pairs={{0,96},{16,112},{32,0},{48,16},{64,32},{80,48},{96,64},{112,80},{1... | collective-permute-start | bytes 786440 | tf_op jit(solution)/shard_map/sum_aggregates/ppermute | solution.py:39
  38.3 10.2 %collective-permute-start.12 = (bf16[1024,128]{1,0:T(8,128)(2,1)S(1)}, bf16[1024,128]{1,0:T(8,128)(2,1)S(1)}, u32[]{:S(2)}, u32[]{:S(2)}) collective-permute-start(bf16[1024,128]{1,0:T(8,128)(2,1)S(1)} %get-tuple-element.55), channel_id=1, source_target_pairs={{0,32},{16,48},{32,64},{48,80},{64,96},{80,112},{96,0},{112,16},{1... | collective-permute-start | bytes 786440 | tf_op jit(solution)/shard_map/sum_aggregates/ppermute | solution.py:39
  38.3 10.2 %collective-permute-start.13 = (bf16[1024,128]{1,0:T(8,128)(2,1)S(1)}, bf16[1024,128]{1,0:T(8,128)(2,1)S(1)}, u32[]{:S(2)}, u32[]{:S(2)}) collective-permute-start(bf16[1024,128]{1,0:T(8,128)(2,1)S(1)} %get-tuple-element.56), channel_id=1, source_target_pairs={{0,16},{16,0},{32,48},{48,32},{64,80},{80,64},{96,112},{112,96},{1... | collective-permute-start | bytes 786440 | tf_op jit(solution)/shard_map/sum_aggregates/ppermute | solution.py:39
  40.5 11.4 %collective-permute-start.9 = (bf16[1024,128]{1,0:T(8,128)(2,1)S(1)}, bf16[1024,128]{1,0:T(8,128)(2,1)S(1)}, u32[]{:S(2)}, u32[]{:S(2)}) collective-permute-start(bf16[1024,128]{1,0:T(8,128)(2,1)S(1)} %get-tuple-element.50), channel_id=1, source_target_pairs={{0,96},{16,112},{32,0},{48,16},{64,32},{80,48},{96,64},{112,80},{1... | collective-permute-start | bytes 786440 | tf_op jit(solution)/shard_map/sum_aggregates/ppermute | solution.py:39
  43.7 15.1 %collective-permute-start.10 = (bf16[1024,128]{1,0:T(8,128)(2,1)S(1)}, bf16[1024,128]{1,0:T(8,128)(2,1)S(1)}, u32[]{:S(2)}, u32[]{:S(2)}) collective-permute-start(bf16[1024,128]{1,0:T(8,128)(2,1)S(1)} %get-tuple-element.51), channel_id=1, source_target_pairs={{0,32},{16,48},{32,64},{48,80},{64,96},{80,112},{96,0},{112,16},{1... | collective-permute-start | bytes 786440 | tf_op jit(solution)/shard_map/sum_aggregates/ppermute | solution.py:39
  48.6 10.1 %collective-permute-start.14 = (bf16[1024,128]{1,0:T(8,128)(2,1)S(1)}, bf16[1024,128]{1,0:T(8,128)(2,1)S(1)}, u32[]{:S(2)}, u32[]{:S(2)}) collective-permute-start(bf16[1024,128]{1,0:T(8,128)(2,1)S(1)} %get-tuple-element.57), channel_id=1, source_target_pairs={{0,64},{16,80},{32,96},{48,112},{64,0},{80,16},{96,32},{112,48},{1... | collective-permute-start | bytes 786440 | tf_op jit(solution)/shard_map/sum_aggregates/ppermute | solution.py:39
  49.6 9.2 %collective-permute-start.15 = (bf16[1024,128]{1,0:T(8,128)(2,1)S(1)}, bf16[1024,128]{1,0:T(8,128)(2,1)S(1)}, u32[]{:S(2)}, u32[]{:S(2)}) collective-permute-start(bf16[1024,128]{1,0:T(8,128)(2,1)S(1)} %get-tuple-element.58), channel_id=1, source_target_pairs={{0,16},{16,0},{32,48},{48,32},{64,80},{80,64},{96,112},{112,96},{1... | collective-permute-start | bytes 786440 | tf_op jit(solution)/shard_map/sum_aggregates/ppermute | solution.py:39
  61.1 11.5 %collective-permute-start.19 = (bf16[144,1024]{1,0:T(8,128)(2,1)S(1)}, bf16[144,1024]{1,0:T(8,128)(2,1)S(1)}, u32[]{:S(2)}, u32[]{:S(2)}) collective-permute-start(bf16[144,1024]{1,0:T(8,128)(2,1)S(1)} %get-tuple-element.62), channel_id=1, source_target_pairs={{0,64},{16,80},{32,96},{48,112},{64,0},{80,16},{96,32},{112,48},{1... | collective-permute-start | bytes 884744 | tf_op jit(solution)/shard_map/gather_dz/ppermute | solution.py:39
  62.4 12.4 %collective-permute-start.16 = (bf16[128,1024]{1,0:T(8,128)(2,1)S(1)}, bf16[128,1024]{1,0:T(8,128)(2,1)S(1)}, u32[]{:S(2)}, u32[]{:S(2)}) collective-permute-start(bf16[128,1024]{1,0:T(8,128)(2,1)S(1)} %get-tuple-element.61.refs_3_), channel_id=1, source_target_pairs={{0,16},{16,0},{32,48},{48,32},{64,80},{80,64},{96,112},{112,96},{1... | collective-permute-start | bytes 786440 | tf_op jit(solution)/shard_map/gather_dz/ppermute | solution.py:39
  64.8 12.7 %collective-permute-start.21 = (bf16[144,1024]{1,0:T(8,128)(2,1)S(1)}, bf16[144,1024]{1,0:T(8,128)(2,1)S(1)}, u32[]{:S(2)}, u32[]{:S(2)}) collective-permute-start(bf16[144,1024]{1,0:T(8,128)(2,1)S(1)} %get-tuple-element.63), channel_id=1, source_target_pairs={{0,32},{16,48},{32,64},{48,80},{64,96},{80,112},{96,0},{112,16},{1... | collective-permute-start | bytes 884744 | tf_op jit(solution)/shard_map/gather_dz/ppermute | solution.py:39
  64.8 12.6 %collective-permute-start.22 = (bf16[144,1024]{1,0:T(8,128)(2,1)S(1)}, bf16[144,1024]{1,0:T(8,128)(2,1)S(1)}, u32[]{:S(2)}, u32[]{:S(2)}) collective-permute-start(bf16[144,1024]{1,0:T(8,128)(2,1)S(1)} %get-tuple-element.64), channel_id=1, source_target_pairs={{0,96},{16,112},{32,0},{48,16},{64,32},{80,48},{96,64},{112,80},{1... | collective-permute-start | bytes 884744 | tf_op jit(solution)/shard_map/gather_dz/ppermute | solution.py:39
  72.6 10.8 %collective-permute-start.20 = (bf16[144,1024]{1,0:T(8,128)(2,1)S(1)}, bf16[144,1024]{1,0:T(8,128)(2,1)S(1)}, u32[]{:S(2)}, u32[]{:S(2)}) collective-permute-start(bf16[144,1024]{1,0:T(8,128)(2,1)S(1)} %collective-permute-done.19.refs_7_.refs_1_), channel_id=1, source_target_pairs={{0,16},{16,0},{32,48},{48,32},{64,80},{80,64},{96,112},{112,96},{1... | collective-permute-start | bytes 884744 | tf_op jit(solution)/shard_map/gather_dz/ppermute | solution.py:39
  74.8 8.6 %collective-permute-start.18 = (bf16[128,1024]{1,0:T(8,128)(2,1)S(1)}, bf16[128,1024]{1,0:T(8,128)(2,1)S(1)}, u32[]{:S(2)}, u32[]{:S(2)}) collective-permute-start(bf16[128,1024]{1,0:T(8,128)(2,1)S(1)} %collective-permute-done.16.refs_6_), channel_id=1, source_target_pairs={{0,96},{16,112},{32,0},{48,16},{64,32},{80,48},{96,64},{112,80},{1... | collective-permute-start | bytes 786440 | tf_op jit(solution)/shard_map/gather_dz/ppermute | solution.py:39
  75.0 8.4 %collective-permute-start.17 = (bf16[128,1024]{1,0:T(8,128)(2,1)S(1)}, bf16[128,1024]{1,0:T(8,128)(2,1)S(1)}, u32[]{:S(2)}, u32[]{:S(2)}) collective-permute-start(bf16[128,1024]{1,0:T(8,128)(2,1)S(1)} %collective-permute-done.16.refs_6_), channel_id=1, source_target_pairs={{0,32},{16,48},{32,64},{48,80},{64,96},{80,112},{96,0},{112,16},{1... | collective-permute-start | bytes 786440 | tf_op jit(solution)/shard_map/gather_dz/ppermute | solution.py:39
  77.5 5.9 %collective-permute-start.23 = (bf16[32,1024]{1,0:T(8,128)(2,1)S(1)}, bf16[32,1024]{1,0:T(8,128)(2,1)S(1)}, u32[]{:S(2)}, u32[]{:S(2)}) collective-permute-start(bf16[32,1024]{1,0:T(8,128)(2,1)S(1)} %gather_dz.1.refs_6_), channel_id=1, source_target_pairs={{0,16},{16,0},{32,48},{48,32},{64,80},{80,64},{96,112},{112,96},{1... | collective-permute-start | bytes 196616 | tf_op jit(solution)/shard_map/gather_dz/ppermute | solution.py:39
  84.8 6.9 %collective-permute-start.24 = (bf16[5,128,1024]{2,1,0:T(8,128)(2,1)S(1)}, bf16[5,128,1024]{2,1,0:T(8,128)(2,1)S(1)}, u32[]{:S(2)}, u32[]{:S(2)}) collective-permute-start(bf16[5,128,1024]{2,1,0:T(8,128)(2,1)S(1)} %get-tuple-element.68), channel_id=1, source_target_pairs={{0,1},{1,0},{2,3},{3,2},{4,5},{5,4},{6,7},{7,6},{8,9},{9,8},{10,11... | collective-permute-start | bytes 3932168 | tf_op jit(solution)/shard_map/sum_grads/ppermute | solution.py:31
  89.2 9.1 %collective-permute-start.28 = (bf16[144,1024]{1,0:T(8,128)(2,1)S(1)}, bf16[144,1024]{1,0:T(8,128)(2,1)S(1)}, u32[]{:S(2)}, u32[]{:S(2)}) collective-permute-start(bf16[144,1024]{1,0:T(8,128)(2,1)S(1)} %get-tuple-element.76), channel_id=1, source_target_pairs={{0,6},{1,7},{2,0},{3,1},{4,2},{5,3},{6,4},{7,5},{8,14},{9,15},{10,... | collective-permute-start | bytes 884744 | tf_op jit(solution)/shard_map/sum_grads/ppermute | solution.py:31
  89.3 10.3 %collective-permute-start.29 = (bf16[144,1024]{1,0:T(8,128)(2,1)S(1)}, bf16[144,1024]{1,0:T(8,128)(2,1)S(1)}, u32[]{:S(2)}, u32[]{:S(2)}) collective-permute-start(bf16[144,1024]{1,0:T(8,128)(2,1)S(1)} %get-tuple-element.77), channel_id=1, source_target_pairs={{0,2},{1,3},{2,4},{3,5},{4,6},{5,7},{6,0},{7,1},{8,10},{9,11},{10,... | collective-permute-start | bytes 884744 | tf_op jit(solution)/shard_map/sum_grads/ppermute | solution.py:31
  91.3 8.5 %collective-permute-start.30 = (bf16[144,1024]{1,0:T(8,128)(2,1)S(1)}, bf16[144,1024]{1,0:T(8,128)(2,1)S(1)}, u32[]{:S(2)}, u32[]{:S(2)}) collective-permute-start(bf16[144,1024]{1,0:T(8,128)(2,1)S(1)} %get-tuple-element.78), channel_id=1, source_target_pairs={{0,8},{1,9},{2,10},{3,11},{4,12},{5,13},{6,14},{7,15},{8,0},{9,1},... | collective-permute-start | bytes 884744 | tf_op jit(solution)/shard_map/sum_grads/ppermute | solution.py:31
  100.0 12.3 %collective-permute-start.31 = (bf16[160,1024]{1,0:T(8,128)(2,1)S(1)}, bf16[160,1024]{1,0:T(8,128)(2,1)S(1)}, u32[]{:S(2)}, u32[]{:S(2)}) collective-permute-start(bf16[160,1024]{1,0:T(8,128)(2,1)S(1)} %get-tuple-element.80), channel_id=1, source_target_pairs={{0,4},{1,5},{2,6},{3,7},{4,0},{5,1},{6,2},{7,3},{8,12},{9,13},{10,... | collective-permute-start | bytes 983048 | tf_op jit(solution)/shard_map/sum_grads/ppermute | solution.py:31
  100.6 11.6 %collective-permute-start.32 = (bf16[160,1024]{1,0:T(8,128)(2,1)S(1)}, bf16[160,1024]{1,0:T(8,128)(2,1)S(1)}, u32[]{:S(2)}, u32[]{:S(2)}) collective-permute-start(bf16[160,1024]{1,0:T(8,128)(2,1)S(1)} %get-tuple-element.81), channel_id=1, source_target_pairs={{0,8},{1,9},{2,10},{3,11},{4,12},{5,13},{6,14},{7,15},{8,0},{9,1},... | collective-permute-start | bytes 983048 | tf_op jit(solution)/shard_map/sum_grads/ppermute | solution.py:31
  100.9 17.2 %collective-permute-start.25 = (bf16[128,1024]{1,0:T(8,128)(2,1)S(1)}, bf16[128,1024]{1,0:T(8,128)(2,1)S(1)}, u32[]{:S(2)}, u32[]{:S(2)}) collective-permute-start(bf16[128,1024]{1,0:T(8,128)(2,1)S(1)} %get-tuple-element.70), channel_id=1, source_target_pairs={{0,6},{1,7},{2,0},{3,1},{4,2},{5,3},{6,4},{7,5},{8,14},{9,15},{10,... | collective-permute-start | bytes 786440 | tf_op jit(solution)/shard_map/sum_grads/ppermute | solution.py:31
  103.3 14.8 %collective-permute-start.26 = (bf16[128,1024]{1,0:T(8,128)(2,1)S(1)}, bf16[128,1024]{1,0:T(8,128)(2,1)S(1)}, u32[]{:S(2)}, u32[]{:S(2)}) collective-permute-start(bf16[128,1024]{1,0:T(8,128)(2,1)S(1)} %get-tuple-element.71), channel_id=1, source_target_pairs={{0,2},{1,3},{2,4},{3,5},{4,6},{5,7},{6,0},{7,1},{8,10},{9,11},{10,... | collective-permute-start | bytes 786440 | tf_op jit(solution)/shard_map/sum_grads/ppermute | solution.py:31
  112.3 6.7 %collective-permute-start.35 = (f32[64,256]{1,0:T(8,128)S(1)}, f32[64,256]{1,0:T(8,128)S(1)}, u32[]{:S(2)}, u32[]{:S(2)}) collective-permute-start(f32[64,256]{1,0:T(8,128)S(1)} %sum_weights.2.refs_0_), channel_id=1, source_target_pairs={{0,32},{16,48},{32,64},{48,80},{64,96},{80,112},{96,0},{112,16},{1... | collective-permute-start | bytes 196616 | tf_op jit(solution)/shard_map/sum_weights/ppermute | solution.py:39
  113.4 5.8 %collective-permute-start.34 = (f32[64,256]{1,0:T(8,128)S(1)}, f32[64,256]{1,0:T(8,128)S(1)}, u32[]{:S(2)}, u32[]{:S(2)}) collective-permute-start(f32[64,256]{1,0:T(8,128)S(1)} %sum_weights.2.refs_0_), channel_id=1, source_target_pairs={{0,64},{16,80},{32,96},{48,112},{64,0},{80,16},{96,32},{112,48},{1... | collective-permute-start | bytes 196616 | tf_op jit(solution)/shard_map/sum_weights/ppermute | solution.py:39
  (10 other events, 131.9 us)

commit v4 on v3

--- a/solution.py
+++ b/solution.py
@@ -246,11 +246,10 @@
 
 
 def backward_sib_body(lists, sizes, tiles, *rest):
-    parts, (quarter, other, before, sib, far, near, quarter_out, held) = rest[:3], rest[3:]
+    parts, (quarter, other, before, sib, far, quarter_out, held) = rest[:3], rest[3:]
     hold_dz(parts, held)
     backward_step(lists, sizes, tiles, 7, held, sib)
     write_places(sib, PAIR_LEFT, [far.at[pl.ds(128 * k, 128)] for k in range(3)])
-    write_places(sib, OWN, [near.at[k] for k in range(5)])
     total = read_fine(quarter, 0) + read_fine(other, 0)
     quarter_out[...] = fine(total)
     write_fine(far, 384, total)
@@ -262,16 +261,8 @@
     backward_step(lists, sizes, tiles, 6, held, mine)
 
 
-def add_sib_near_body(mine, got, *outs):
-    for k, ref in enumerate(outs):
-        for b in range(4):
-            nodes = slice(b * TILE, (b + 1) * TILE)
-            new = mine[4 * k + b] + got[k, :, nodes].astype(F32)
-            ref[:, nodes] = new.astype(ref.dtype)
-
-
-def add_sib_far_body(mine, got, quarter, *rest):
-    outs, quarter_out = rest[:3], rest[3]
+def add_sib_far_body(mine, sib, got, quarter, *rest):
+    outs, quarter_out, near = rest[:3], rest[3], rest[4]
     total = quarter[...] + read_fine(got, 384)
     quarter_out[...] = rounded(total)
     for k, ref in enumerate(outs):
@@ -280,38 +271,37 @@
             new = mine[4 * (PAIR_LEFT + k) + b] + got[128 * k : 128 * k + 128, nodes].astype(F32)
             ref[0:128, nodes] = new.astype(BF16)
         write_extra(ref, 128, total)
-
-
-def add_round_body(n, own_extra, pair, opposite, a, b, c, *rest):
-    pair_out, opposite_out = rest[-2:]
-    new = pair[...] + (a[0:n].astype(F32) + b[0:n].astype(F32))
-    pair_out[0:n] = new.astype(BF16)
-    opposite_out[0:n] = (opposite[...] + c[0:n].astype(F32)).astype(BF16)
-    if own_extra:
-        own = rest[0]
-        write_extra(opposite_out, n, own[...])
-        opposite_out[n + 16 : n + 32] = c[n : n + 16]
-        pair_out[n : n + 16] = b[n : n + 16]
-        pair_out[n + 16 : n + 32] = a[n : n + 16]
-
-
-def reduce_places(parts, step, swap, own_extra=()):
-    n, lanes = parts[OWN].shape
-    from_right = step(parts[PAIR_LEFT], -1)
-    from_left = step(parts[PAIR_RIGHT], 1)
-    from_pair = swap(parts[PAIR_OPPOSITE])
-    sent = VMEM((n + 32 * len(own_extra), lanes), BF16)
-    left = step(parts[LEFT], -1)
-    right = step(parts[RIGHT], 1)
-    pair, opposite = call(
-        functools.partial(add_round_body, n, bool(own_extra)),
-        [sent, sent],
-        [parts[PAIR], parts[OPPOSITE], from_right, from_left, from_pair, *own_extra],
-        nbytes=4 << 20,
-    )
-    opposite = step(opposite, 2)
-    pair = swap(pair)
-    return [parts[OWN], left, right, opposite, pair], [from_left, from_right, from_pair]
+    write_places(sib, OWN, [near.at[k] for k in range(5)])
+
+
+def add_round_body(pair, opposite, from_right, from_left, from_pair, pair_out, opposite_out):
+    new = pair[...] + (from_right[...].astype(F32) + from_left[...].astype(F32))
+    pair_out[...] = new.astype(BF16)
+    opposite_out[...] = (opposite[...] + from_pair[...].astype(F32)).astype(BF16)
+
+
+def add_near_body(mine, got, from_right, from_left, from_pair, quarter, *outs):
+    more = {PAIR: [from_right, from_left], OPPOSITE: [from_pair]}
+    for place, ref in enumerate(outs):
+        for b in range(4):
+            nodes = slice(b * TILE, (b + 1) * TILE)
+            new = mine[4 * place + b] + got[place, :, nodes].astype(F32)
+            for came in more.get(place, []):
+                new = new + came[0:128, nodes].astype(F32)
+            ref[0:128, nodes] = new.astype(ref.dtype)
+    pair, opposite = outs[PAIR], outs[OPPOSITE]
+    write_extra(opposite, 128, quarter[...])
+    opposite[144:160] = from_pair[128:144]
+    pair[128:144] = from_left[128:144]
+    pair[144:160] = from_right[128:144]
+
+
+def first_sums(parts, step, swap):
+    return step(parts[0], -1), step(parts[1], 1), swap(parts[2])
+
+
+def second_sums(own, left, right, pair, opposite, step, swap):
+    return [own, step(left, -1), step(right, 1), step(opposite, 2), swap(pair)]
 
 
 def dense_body(bias, feats, upstream, w_self, w_neigh, *rest):
@@ -469,7 +459,14 @@
         )
     with jax.named_scope("sum_aggregates"):
         step, swap = (lambda v, d: hop_row(v, 0, d)), (lambda v: hop_row(v, 1, 0))
-        sums, _ = reduce_places(partial, step, swap)
+        own, left, right, pair, opposite, *far = partial
+        pair, opposite = call(
+            add_round_body,
+            [bf16, bf16],
+            [pair, opposite, *first_sums(far, step, swap)],
+            nbytes=4 << 20,
+        )
+        sums = second_sums(own, left, right, pair, opposite, step, swap)
     with jax.named_scope("dense"):
         longer = VMEM((144, 1024), BF16)
         block = VMEM((64, 256), F32)
@@ -519,9 +516,9 @@
             flops=2 * share,
             nbytes=tile_bytes // 2,
         )
-        _, sib_far, sib_near, quarter = call(
+        sib, sib_far, quarter = call(
             backward_sib_body,
-            [total, VMEM((416, 1024), BF16), VMEM((5, 128, 1024), BF16), block],
+            [total, VMEM((416, 1024), BF16), block],
             [tiles, *far, quarter, quarter_pair, sib],
             by_list,
             alias={8: 0},
@@ -542,19 +539,22 @@
     with jax.named_scope("sum_grads"):
         step, swap = (lambda v, d: hop_col(v, 0, d)), (lambda v: hop_col(v, 1, 0))
         f32, bf16 = VMEM((128, 1024), F32), VMEM((128, 1024), BF16)
-        *far, quarter = call(
+        *far, quarter, sib_near = call(
             add_sib_far_body,
-            [longer, longer, longer, block],
-            [mine, hop_col(sib_far, 0, 0, 1), quarter],
+            [longer, longer, longer, block, VMEM((5, 128, 1024), BF16)],
+            [mine, sib, hop_col(sib_far, 0, 0, 1), quarter],
             nbytes=3 << 20,
         )
+        from_right, from_left, from_pair = first_sums(far, step, swap)
+        longest = VMEM((160, 1024), BF16)
         near = call(
-            add_sib_near_body,
-            [f32, bf16, bf16, f32, f32],
-            [mine, hop_col(sib_near, 0, 0, 1)],
+            add_near_body,
+            [f32, bf16, bf16, longest, longest],
+            [mine, hop_col(sib_near, 0, 0, 1), from_right, from_left, from_pair, quarter],
             nbytes=5 << 20,
         )
-        sums, came = reduce_places([*near, *far], step, swap, [quarter])
+        sums = second_sums(*near, step, swap)
+        came = [from_left, from_right, from_pair]
     with jax.named_scope("sum_weights"):
         quarter = call(
             weight_sum_body,

time: 121 us -> 119 us (0.983)
  Pallas kernels: 25.8 us -> 18 us
  waiting for transfers between devices: 43.9 us -> 48 us
  starting transfers between devices: 48.9 us -> 51.6 us
    pallas_call x18 -> x17, Pallas kernels: 19.3 us -> 11.5 us  [call(): pl.pallas_call(run, out_shape=outs, in_specs=[pl.BlockSpec(memory_space=p...]
    ppermute x18, waiting for transfers between devices: 26.2 us -> 29.6 us  [hop_col(): return lax.ppermute(value, 'col', pairs)]
    ppermute x18, starting transfers between devices: 31.4 us -> 34.4 us  [hop_row(): return lax.ppermute(value, 'row', pairs)]
  transfers between devices with their start and end apart: 36 -> 36, of which waited for: 16 -> 16; matrix products, arithmetic and copies ran while one was open for 0% -> 0% of each run, Pallas kernels for 16% -> 10%
where the time goes in v4:
time: 119 us; the launch traced here: 120 us
  starting transfers between devices  51.6 us (43%)
  waiting for transfers between devices  48 us (40%)
  Pallas kernels  18 us (15%)
  between operations  1.53 us (1%)
    ppermute x18, starting transfers between devices, hop_row(): return lax.ppermute(value, 'row', pairs)  34.4 us
    ppermute x18, waiting for transfers between devices, hop_col(): return lax.ppermute(value, 'col', pairs)  29.6 us
    ppermute x18, waiting for transfers between devices, hop_row(): return lax.ppermute(value, 'row', pairs)  18.4 us
    ppermute x18, starting transfers between devices, hop_col(): return lax.ppermute(value, 'col', pairs)  17.2 us
    pallas_call x17, Pallas kernels, call(): pl.pallas_call(run, out_shape=outs, in_specs=[pl.BlockSpec(memory_space=p...  11.5 us
    pallas_call x1, Pallas kernels, shards(): pl.pallas_call(plan_body, out_shape=[VMEM((128, TILE, TILE), BF16), pltpu...  6.48 us
  transfers between devices with their start and end apart: 36, of which 16 were waited for; matrix products, arithmetic and copies ran while one was open for 0% of the time, Pallas kernels for 10%

profile of v4, /device:TPU:0, one launch (start us, length us, event | category | flops | bytes accessed | tf_op | source)
XLA Modules:
  0.0 119.9 jit_solution(2128899309127048570)
XLA Ops:
  0.6 3.2 %collective-permute-start.3 = (bf16[1024,128]{1,0:T(8,128)(2,1)}, bf16[1024,128]{1,0:T(8,128)(2,1)S(1)}, u32[]{:S(2)}, u32[]{:S(2)}) collective-permute-start(bf16[1024,128]{1,0:T(8,128)(2,1)} %refs_1_.2), channel_id=1, source_target_pairs={{0,4},{1,5},{2,6},{3,7},{4,0},{5,1},{6,2},{7,3},{8,12},{9,13},{10,... | collective-permute-start | bytes 786440 | tf_op jit(solution)/shard_map/gather_features/ppermute | solution.py:31
  3.8 1.6 %collective-permute-start.2 = (bf16[1024,128]{1,0:T(8,128)(2,1)}, bf16[1024,128]{1,0:T(8,128)(2,1)S(1)}, u32[]{:S(2)}, u32[]{:S(2)}) collective-permute-start(bf16[1024,128]{1,0:T(8,128)(2,1)} %refs_1_.2), channel_id=1, source_target_pairs={{0,8},{1,9},{2,10},{3,11},{4,12},{5,13},{6,14},{7,15},{8,0},{9,1},... | collective-permute-start | bytes 786440 | tf_op jit(solution)/shard_map/gather_features/ppermute | solution.py:31
  8.8 6.5 %plan.1 = (bf16[128,256,256]{2,1,0:T(8,128)(2,1)S(1)}, s32[1152]{0:T(1024)S(4)}, s32[8]{0:T(128)S(4)}) custom-call(s32[2,128]{1,0:T(2,128)S(1)} %bitcast.7, s32[1]{0:T(128)} %bitcast.6.count, bf16[128,256,256]{2,1,0:T(8,128)(2,1)} %bitcast.9), custom_call_target="tpu_custom_call" | custom-call | bytes 16777216 | tf_op jit(solution)/shard_map/plan/pallas_call | solution.py:402
  16.5 1.7 %collective-permute-start.6 = (bf16[1024,128]{1,0:T(8,128)(2,1)S(1)}, bf16[1024,128]{1,0:T(8,128)(2,1)S(1)}, u32[]{:S(2)}, u32[]{:S(2)}) collective-permute-start(bf16[1024,128]{1,0:T(8,128)(2,1)S(1)} %collective-permute-done.3.refs_4_), channel_id=1, source_target_pairs={{0,8},{1,9},{2,10},{3,11},{4,12},{5,13},{6,14},{7,15},{8,0},{9,1},... | collective-permute-start | bytes 786440 | tf_op jit(solution)/shard_map/gather_features/ppermute | solution.py:31
  18.2 2.6 %collective-permute-start.5 = (bf16[1024,128]{1,0:T(8,128)(2,1)S(1)}, bf16[1024,128]{1,0:T(8,128)(2,1)S(1)}, u32[]{:S(2)}, u32[]{:S(2)}) collective-permute-start(bf16[1024,128]{1,0:T(8,128)(2,1)S(1)} %get-tuple-element.46), channel_id=1, source_target_pairs={{0,6},{1,7},{2,0},{3,1},{4,2},{5,3},{6,4},{7,5},{8,14},{9,15},{10,... | collective-permute-start | bytes 786440 | tf_op jit(solution)/shard_map/gather_features/ppermute | solution.py:31
  20.8 1.7 %forward_tiles.4.refs_3_.refs_4_ = f32[33,256,128]{2,1,0:T(8,128)S(1)} custom-call(s32[1152]{0:T(1024)S(4)} %get-tuple-element.43.refs_0_, s32[8]{0:T(128)S(4)} %get-tuple-element.44.refs_5_.refs_1_, bf16[128,256,256]{2,1,0:T(8,128)(2,1)S(1)} %get-tuple-element.45.refs_2_, bf16[20,256,128]{2,1,0:T(8,128)(2,1)S(1)} %get-tuple-element.47.refs_3_, ...), custom_call_target="tpu_custom_call" | custom-call | tf_op jit(solution)/shard_map/forward_tiles/pallas_call | solution.py:67
  22.5 2.7 %collective-permute-done.6.refs_2_ = bf16[1024,128]{1,0:T(8,128)(2,1)S(1)} collective-permute-done((bf16[1024,128]{1,0:T(8,128)(2,1)S(1)}, bf16[1024,128]{1,0:T(8,128)(2,1)S(1)}, u32[]{:S(2)}, u32[]{:S(2)}) %collective-permute-start.6) | collective-permute-done | bytes 262176 | tf_op jit(solution)/shard_map/gather_features/ppermute | solution.py:31
  25.2 1.4 %collective-permute-done.5.refs_1_ = bf16[1024,128]{1,0:T(8,128)(2,1)S(1)} collective-permute-done((bf16[1024,128]{1,0:T(8,128)(2,1)S(1)}, bf16[1024,128]{1,0:T(8,128)(2,1)S(1)}, u32[]{:S(2)}, u32[]{:S(2)}) %collective-permute-start.5) | collective-permute-done | bytes 262176 | tf_op jit(solution)/shard_map/gather_features/ppermute | solution.py:31
  26.7 3.4 %collective-permute-done.4.refs_0_ = bf16[1024,128]{1,0:T(8,128)(2,1)S(1)} collective-permute-done((bf16[1024,128]{1,0:T(8,128)(2,1)S(1)}, bf16[1024,128]{1,0:T(8,128)(2,1)S(1)}, u32[]{:S(2)}, u32[]{:S(2)}) %collective-permute-start.4) | collective-permute-done | bytes 262176 | tf_op jit(solution)/shard_map/gather_features/ppermute | solution.py:31
  31.0 1.5 %collective-permute-done.8.refs_3_ = bf16[12,256,128]{2,1,0:T(8,128)(2,1)S(1)} collective-permute-done((bf16[12,256,128]{2,1,0:T(8,128)(2,1)S(1)}, bf16[12,256,128]{2,1,0:T(8,128)(2,1)S(1)}, u32[]{:S(2)}, u32[]{:S(2)}) %collective-permute-start.8) | collective-permute-done | bytes 786464 | tf_op jit(solution)/shard_map/forward_tiles/ppermute | solution.py:31
  33.5 4.1 %collective-permute-start.11 = (bf16[1024,128]{1,0:T(8,128)(2,1)S(1)}, bf16[1024,128]{1,0:T(8,128)(2,1)S(1)}, u32[]{:S(2)}, u32[]{:S(2)}) collective-permute-start(bf16[1024,128]{1,0:T(8,128)(2,1)S(1)} %get-tuple-element.53), channel_id=1, source_target_pairs={{0,96},{16,112},{32,0},{48,16},{64,32},{80,48},{96,64},{112,80},{1... | collective-permute-start | bytes 786440 | tf_op jit(solution)/shard_map/sum_aggregates/ppermute | solution.py:39
  37.6 2.9 %collective-permute-start.13 = (bf16[1024,128]{1,0:T(8,128)(2,1)S(1)}, bf16[1024,128]{1,0:T(8,128)(2,1)S(1)}, u32[]{:S(2)}, u32[]{:S(2)}) collective-permute-start(bf16[1024,128]{1,0:T(8,128)(2,1)S(1)} %get-tuple-element.55), channel_id=1, source_target_pairs={{0,16},{16,0},{32,48},{48,32},{64,80},{80,64},{96,112},{112,96},{1... | collective-permute-start | bytes 786440 | tf_op jit(solution)/shard_map/sum_aggregates/ppermute | solution.py:39
  40.5 3.2 %collective-permute-start.9 = (bf16[1024,128]{1,0:T(8,128)(2,1)S(1)}, bf16[1024,128]{1,0:T(8,128)(2,1)S(1)}, u32[]{:S(2)}, u32[]{:S(2)}) collective-permute-start(bf16[1024,128]{1,0:T(8,128)(2,1)S(1)} %get-tuple-element.49), channel_id=1, source_target_pairs={{0,96},{16,112},{32,0},{48,16},{64,32},{80,48},{96,64},{112,80},{1... | collective-permute-start | bytes 786440 | tf_op jit(solution)/shard_map/sum_aggregates/ppermute | solution.py:39
  43.7 3.4 %collective-permute-done.12.refs_3_ = bf16[1024,128]{1,0:T(8,128)(2,1)S(1)} collective-permute-done((bf16[1024,128]{1,0:T(8,128)(2,1)S(1)}, bf16[1024,128]{1,0:T(8,128)(2,1)S(1)}, u32[]{:S(2)}, u32[]{:S(2)}) %collective-permute-start.12) | collective-permute-done | bytes 262176 | tf_op jit(solution)/shard_map/sum_aggregates/ppermute | solution.py:39
  47.3 2.0 %collective-permute-start.14 = (bf16[1024,128]{1,0:T(8,128)(2,1)S(1)}, bf16[1024,128]{1,0:T(8,128)(2,1)S(1)}, u32[]{:S(2)}, u32[]{:S(2)}) collective-permute-start(bf16[1024,128]{1,0:T(8,128)(2,1)S(1)} %get-tuple-element.56), channel_id=1, source_target_pairs={{0,64},{16,80},{32,96},{48,112},{64,0},{80,16},{96,32},{112,48},{1... | collective-permute-start | bytes 786440 | tf_op jit(solution)/shard_map/sum_aggregates/ppermute | solution.py:39
  49.3 3.2 %collective-permute-start.15 = (bf16[1024,128]{1,0:T(8,128)(2,1)S(1)}, bf16[1024,128]{1,0:T(8,128)(2,1)S(1)}, u32[]{:S(2)}, u32[]{:S(2)}) collective-permute-start(bf16[1024,128]{1,0:T(8,128)(2,1)S(1)} %get-tuple-element.57), channel_id=1, source_target_pairs={{0,16},{16,0},{32,48},{48,32},{64,80},{80,64},{96,112},{112,96},{1... | collective-permute-start | bytes 786440 | tf_op jit(solution)/shard_map/sum_aggregates/ppermute | solution.py:39
  52.5 5.5 %collective-permute-done.10.refs_7_ = bf16[1024,128]{1,0:T(8,128)(2,1)S(1)} collective-permute-done((bf16[1024,128]{1,0:T(8,128)(2,1)S(1)}, bf16[1024,128]{1,0:T(8,128)(2,1)S(1)}, u32[]{:S(2)}, u32[]{:S(2)}) %collective-permute-start.10) | collective-permute-done | bytes 262176 | tf_op jit(solution)/shard_map/sum_aggregates/ppermute | solution.py:39
  58.2 2.3 %dense.1 = (bf16[1024,256]{1,0:T(8,128)(2,1)}, bf16[1024,256]{1,0:T(8,128)(2,1)S(1)}, bf16[128,1024]{1,0:T(8,128)(2,1)S(1)}, bf16[144,1024]{1,0:T(8,128)(2,1)S(1...) custom-call(f32[1,256]{1,0:T(1,128)S(1)} %bitcast.8, ...), custom_call_target="tpu_custom_call" | custom-call | flops 335544320 | bytes 6291456 | tf_op jit(solution)/shard_map/dense/pallas_call | solution.py:67
  61.6 3.2 %collective-permute-start.16 = (bf16[128,1024]{1,0:T(8,128)(2,1)S(1)}, bf16[128,1024]{1,0:T(8,128)(2,1)S(1)}, u32[]{:S(2)}, u32[]{:S(2)}) collective-permute-start(bf16[128,1024]{1,0:T(8,128)(2,1)S(1)} %get-tuple-element.60.refs_3_), channel_id=1, source_target_pairs={{0,16},{16,0},{32,48},{48,32},{64,80},{80,64},{96,112},{112,96},{1... | collective-permute-start | bytes 786440 | tf_op jit(solution)/shard_map/gather_dz/ppermute | solution.py:39
  65.0 3.0 %collective-permute-start.22 = (bf16[144,1024]{1,0:T(8,128)(2,1)S(1)}, bf16[144,1024]{1,0:T(8,128)(2,1)S(1)}, u32[]{:S(2)}, u32[]{:S(2)}) collective-permute-start(bf16[144,1024]{1,0:T(8,128)(2,1)S(1)} %get-tuple-element.63), channel_id=1, source_target_pairs={{0,96},{16,112},{32,0},{48,16},{64,32},{80,48},{96,64},{112,80},{1... | collective-permute-start | bytes 884744 | tf_op jit(solution)/shard_map/gather_dz/ppermute | solution.py:39
  68.0 3.9 %collective-permute-done.19.refs_7_.refs_1_ = bf16[144,1024]{1,0:T(8,128)(2,1)S(1)} collective-permute-done((bf16[144,1024]{1,0:T(8,128)(2,1)S(1)}, bf16[144,1024]{1,0:T(8,128)(2,1)S(1)}, u32[]{:S(2)}, u32[]{:S(2)}) %collective-permute-start.19) | collective-permute-done | bytes 294944 | tf_op jit(solution)/shard_map/gather_dz/ppermute | solution.py:39
  71.9 3.2 %collective-permute-start.20 = (bf16[144,1024]{1,0:T(8,128)(2,1)S(1)}, bf16[144,1024]{1,0:T(8,128)(2,1)S(1)}, u32[]{:S(2)}, u32[]{:S(2)}) collective-permute-start(bf16[144,1024]{1,0:T(8,128)(2,1)S(1)} %collective-permute-done.19.refs_7_.refs_1_), channel_id=1, source_target_pairs={{0,16},{16,0},{32,48},{48,32},{64,80},{80,64},{96,112},{112,96},{1... | collective-permute-start | bytes 884744 | tf_op jit(solution)/shard_map/gather_dz/ppermute | solution.py:39
  75.6 1.6 %collective-permute-start.17 = (bf16[128,1024]{1,0:T(8,128)(2,1)S(1)}, bf16[128,1024]{1,0:T(8,128)(2,1)S(1)}, u32[]{:S(2)}, u32[]{:S(2)}) collective-permute-start(bf16[128,1024]{1,0:T(8,128)(2,1)S(1)} %collective-permute-done.16.refs_6_), channel_id=1, source_target_pairs={{0,32},{16,48},{32,64},{48,80},{64,96},{80,112},{96,0},{112,16},{1... | collective-permute-start | bytes 786440 | tf_op jit(solution)/shard_map/gather_dz/ppermute | solution.py:39
  77.6 1.4 %collective-permute-start.23 = (bf16[32,1024]{1,0:T(8,128)(2,1)S(1)}, bf16[32,1024]{1,0:T(8,128)(2,1)S(1)}, u32[]{:S(2)}, u32[]{:S(2)}) collective-permute-start(bf16[32,1024]{1,0:T(8,128)(2,1)S(1)} %gather_dz.1.refs_6_), channel_id=1, source_target_pairs={{0,16},{16,0},{32,48},{48,32},{64,80},{80,64},{96,112},{112,96},{1... | collective-permute-start | bytes 196616 | tf_op jit(solution)/shard_map/gather_dz/ppermute | solution.py:39
  79.0 1.6 %backward_tiles.3 = (f32[33,128,256]{2,1,0:T(8,128)S(1)}, f32[33,128,256]{2,1,0:T(8,128)S(1)}) custom-call(s32[1152]{0:T(1024)S(4)} %get-tuple-element.43.refs_0_, s32[8]{0:T(128)S(4)} %get-tuple-element.44.refs_5_.refs_1_, bf16[128,256,256]{2,1,0:T(8,128)(2,1)S(1)} %get-tuple-element.45.refs_2_, bf16[128,1024]{1,0:T(8,128)(2,1)S(1)} %get-tuple-element.60.refs_3_, ...), custom_call_target="tpu_custom_call" | custom-call | flops 1073741824 | bytes 8388608 | tf_op jit(solution)/shard_map/backward_tiles/pallas_call | solution.py:67
  80.6 2.8 %collective-permute-done.23.refs_7_ = bf16[32,1024]{1,0:T(8,128)(2,1)S(1)} collective-permute-done((bf16[32,1024]{1,0:T(8,128)(2,1)S(1)}, bf16[32,1024]{1,0:T(8,128)(2,1)S(1)}, u32[]{:S(2)}, u32[]{:S(2)}) %collective-permute-start.23) | collective-permute-done | bytes 65568 | tf_op jit(solution)/shard_map/gather_dz/ppermute | solution.py:39
  84.8 1.8 %collective-permute-done.24.refs_2_ = bf16[416,1024]{1,0:T(8,128)(2,1)S(1)} collective-permute-done((bf16[416,1024]{1,0:T(8,128)(2,1)S(1)}, bf16[416,1024]{1,0:T(8,128)(2,1)S(1)}, u32[]{:S(2)}, u32[]{:S(2)}) %collective-permute-start.24) | collective-permute-done | bytes 852000 | tf_op jit(solution)/shard_map/sum_grads/ppermute | solution.py:31
  89.4 7.0 %collective-permute-done.26.refs_2_ = bf16[144,1024]{1,0:T(8,128)(2,1)S(1)} collective-permute-done((bf16[144,1024]{1,0:T(8,128)(2,1)S(1)}, bf16[144,1024]{1,0:T(8,128)(2,1)S(1)}, u32[]{:S(2)}, u32[]{:S(2)}) %collective-permute-start.26) | collective-permute-done | bytes 294944 | tf_op jit(solution)/shard_map/sum_grads/ppermute | solution.py:31
  96.4 1.8 %collective-permute-done.27.refs_3_.refs_1_ = bf16[144,1024]{1,0:T(8,128)(2,1)S(1)} collective-permute-done((bf16[144,1024]{1,0:T(8,128)(2,1)S(1)}, bf16[144,1024]{1,0:T(8,128)(2,1)S(1)}, u32[]{:S(2)}, u32[]{:S(2)}) %collective-permute-start.27) | collective-permute-done | bytes 294944 | tf_op jit(solution)/shard_map/sum_grads/ppermute | solution.py:31
  99.5 2.3 %collective-permute-start.29 = (bf16[128,1024]{1,0:T(8,128)(2,1)S(1)}, bf16[128,1024]{1,0:T(8,128)(2,1)S(1)}, u32[]{:S(2)}, u32[]{:S(2)}) collective-permute-start(bf16[128,1024]{1,0:T(8,128)(2,1)S(1)} %get-tuple-element.76), channel_id=1, source_target_pairs={{0,6},{1,7},{2,0},{3,1},{4,2},{5,3},{6,4},{7,5},{8,14},{9,15},{10,... | collective-permute-start | bytes 786440 | tf_op jit(solution)/shard_map/sum_grads/ppermute | solution.py:31
  101.9 8.9 %collective-permute-done.31.refs_4_ = bf16[160,1024]{1,0:T(8,128)(2,1)S(1)} collective-permute-done((bf16[160,1024]{1,0:T(8,128)(2,1)S(1)}, bf16[160,1024]{1,0:T(8,128)(2,1)S(1)}, u32[]{:S(2)}, u32[]{:S(2)}) %collective-permute-start.31) | collective-permute-done | bytes 327712 | tf_op jit(solution)/shard_map/sum_grads/ppermute | solution.py:31
  111.3 3.5 %collective-permute-start.34 = (f32[64,256]{1,0:T(8,128)S(1)}, f32[64,256]{1,0:T(8,128)S(1)}, u32[]{:S(2)}, u32[]{:S(2)}) collective-permute-start(f32[64,256]{1,0:T(8,128)S(1)} %sum_weights.2.refs_0_), channel_id=1, source_target_pairs={{0,64},{16,80},{32,96},{48,112},{64,0},{80,16},{96,32},{112,48},{1... | collective-permute-start | bytes 196616 | tf_op jit(solution)/shard_map/sum_weights/ppermute | solution.py:39
  (70 shorter events, 19.3 us)
Async XLA Ops:
  0.6 14.6 %collective-permute-start.3 = (bf16[1024,128]{1,0:T(8,128)(2,1)}, bf16[1024,128]{1,0:T(8,128)(2,1)S(1)}, u32[]{:S(2)}, u32[]{:S(2)}) collective-permute-start(bf16[1024,128]{1,0:T(8,128)(2,1)} %refs_1_.2), channel_id=1, source_target_pairs={{0,4},{1,5},{2,6},{3,7},{4,0},{5,1},{6,2},{7,3},{8,12},{9,13},{10,... | collective-permute-start | bytes 786440 | tf_op jit(solution)/shard_map/gather_features/ppermute | solution.py:31
  3.8 11.4 %collective-permute-start.2 = (bf16[1024,128]{1,0:T(8,128)(2,1)}, bf16[1024,128]{1,0:T(8,128)(2,1)S(1)}, u32[]{:S(2)}, u32[]{:S(2)}) collective-permute-start(bf16[1024,128]{1,0:T(8,128)(2,1)} %refs_1_.2), channel_id=1, source_target_pairs={{0,8},{1,9},{2,10},{3,11},{4,12},{5,13},{6,14},{7,15},{8,0},{9,1},... | collective-permute-start | bytes 786440 | tf_op jit(solution)/shard_map/gather_features/ppermute | solution.py:31
  5.4 10.9 %collective-permute-start.1 = (bf16[1024,128]{1,0:T(8,128)(2,1)}, bf16[1024,128]{1,0:T(8,128)(2,1)S(1)}, u32[]{:S(2)}, u32[]{:S(2)}) collective-permute-start(bf16[1024,128]{1,0:T(8,128)(2,1)} %refs_1_.2), channel_id=1, source_target_pairs={{0,6},{1,7},{2,0},{3,1},{4,2},{5,3},{6,4},{7,5},{8,14},{9,15},{10,... | collective-permute-start | bytes 786440 | tf_op jit(solution)/shard_map/gather_features/ppermute | solution.py:31
  6.5 9.8 %collective-permute-start = (bf16[1024,128]{1,0:T(8,128)(2,1)}, bf16[1024,128]{1,0:T(8,128)(2,1)S(1)}, u32[]{:S(2)}, u32[]{:S(2)}) collective-permute-start(bf16[1024,128]{1,0:T(8,128)(2,1)} %refs_1_.2), channel_id=1, source_target_pairs={{0,2},{1,3},{2,4},{3,5},{4,6},{5,7},{6,0},{7,1},{8,10},{9,11},{10,... | collective-permute-start | bytes 786440 | tf_op jit(solution)/shard_map/gather_features/ppermute | solution.py:31
  16.5 8.7 %collective-permute-start.6 = (bf16[1024,128]{1,0:T(8,128)(2,1)S(1)}, bf16[1024,128]{1,0:T(8,128)(2,1)S(1)}, u32[]{:S(2)}, u32[]{:S(2)}) collective-permute-start(bf16[1024,128]{1,0:T(8,128)(2,1)S(1)} %collective-permute-done.3.refs_4_), channel_id=1, source_target_pairs={{0,8},{1,9},{2,10},{3,11},{4,12},{5,13},{6,14},{7,15},{8,0},{9,1},... | collective-permute-start | bytes 786440 | tf_op jit(solution)/shard_map/gather_features/ppermute | solution.py:31
  18.2 8.5 %collective-permute-start.5 = (bf16[1024,128]{1,0:T(8,128)(2,1)S(1)}, bf16[1024,128]{1,0:T(8,128)(2,1)S(1)}, u32[]{:S(2)}, u32[]{:S(2)}) collective-permute-start(bf16[1024,128]{1,0:T(8,128)(2,1)S(1)} %get-tuple-element.46), channel_id=1, source_target_pairs={{0,6},{1,7},{2,0},{3,1},{4,2},{5,3},{6,4},{7,5},{8,14},{9,15},{10,... | collective-permute-start | bytes 786440 | tf_op jit(solution)/shard_map/gather_features/ppermute | solution.py:31
  20.8 9.3 %collective-permute-start.4 = (bf16[1024,128]{1,0:T(8,128)(2,1)S(1)}, bf16[1024,128]{1,0:T(8,128)(2,1)S(1)}, u32[]{:S(2)}, u32[]{:S(2)}) collective-permute-start(bf16[1024,128]{1,0:T(8,128)(2,1)S(1)} %get-tuple-element.46), channel_id=1, source_target_pairs={{0,2},{1,3},{2,4},{3,5},{4,6},{5,7},{6,0},{7,1},{8,10},{9,11},{10,... | collective-permute-start | bytes 786440 | tf_op jit(solution)/shard_map/gather_features/ppermute | solution.py:31
  33.5 10.2 %collective-permute-start.11 = (bf16[1024,128]{1,0:T(8,128)(2,1)S(1)}, bf16[1024,128]{1,0:T(8,128)(2,1)S(1)}, u32[]{:S(2)}, u32[]{:S(2)}) collective-permute-start(bf16[1024,128]{1,0:T(8,128)(2,1)S(1)} %get-tuple-element.53), channel_id=1, source_target_pairs={{0,96},{16,112},{32,0},{48,16},{64,32},{80,48},{96,64},{112,80},{1... | collective-permute-start | bytes 786440 | tf_op jit(solution)/shard_map/sum_aggregates/ppermute | solution.py:39
  37.6 9.5 %collective-permute-start.12 = (bf16[1024,128]{1,0:T(8,128)(2,1)S(1)}, bf16[1024,128]{1,0:T(8,128)(2,1)S(1)}, u32[]{:S(2)}, u32[]{:S(2)}) collective-permute-start(bf16[1024,128]{1,0:T(8,128)(2,1)S(1)} %get-tuple-element.54), channel_id=1, source_target_pairs={{0,32},{16,48},{32,64},{48,80},{64,96},{80,112},{96,0},{112,16},{1... | collective-permute-start | bytes 786440 | tf_op jit(solution)/shard_map/sum_aggregates/ppermute | solution.py:39
  37.6 9.6 %collective-permute-start.13 = (bf16[1024,128]{1,0:T(8,128)(2,1)S(1)}, bf16[1024,128]{1,0:T(8,128)(2,1)S(1)}, u32[]{:S(2)}, u32[]{:S(2)}) collective-permute-start(bf16[1024,128]{1,0:T(8,128)(2,1)S(1)} %get-tuple-element.55), channel_id=1, source_target_pairs={{0,16},{16,0},{32,48},{48,32},{64,80},{80,64},{96,112},{112,96},{1... | collective-permute-start | bytes 786440 | tf_op jit(solution)/shard_map/sum_aggregates/ppermute | solution.py:39
  40.5 12.1 %collective-permute-start.9 = (bf16[1024,128]{1,0:T(8,128)(2,1)S(1)}, bf16[1024,128]{1,0:T(8,128)(2,1)S(1)}, u32[]{:S(2)}, u32[]{:S(2)}) collective-permute-start(bf16[1024,128]{1,0:T(8,128)(2,1)S(1)} %get-tuple-element.49), channel_id=1, source_target_pairs={{0,96},{16,112},{32,0},{48,16},{64,32},{80,48},{96,64},{112,80},{1... | collective-permute-start | bytes 786440 | tf_op jit(solution)/shard_map/sum_aggregates/ppermute | solution.py:39
  43.7 14.4 %collective-permute-start.10 = (bf16[1024,128]{1,0:T(8,128)(2,1)S(1)}, bf16[1024,128]{1,0:T(8,128)(2,1)S(1)}, u32[]{:S(2)}, u32[]{:S(2)}) collective-permute-start(bf16[1024,128]{1,0:T(8,128)(2,1)S(1)} %get-tuple-element.50), channel_id=1, source_target_pairs={{0,32},{16,48},{32,64},{48,80},{64,96},{80,112},{96,0},{112,16},{1... | collective-permute-start | bytes 786440 | tf_op jit(solution)/shard_map/sum_aggregates/ppermute | solution.py:39
  47.3 10.8 %collective-permute-start.14 = (bf16[1024,128]{1,0:T(8,128)(2,1)S(1)}, bf16[1024,128]{1,0:T(8,128)(2,1)S(1)}, u32[]{:S(2)}, u32[]{:S(2)}) collective-permute-start(bf16[1024,128]{1,0:T(8,128)(2,1)S(1)} %get-tuple-element.56), channel_id=1, source_target_pairs={{0,64},{16,80},{32,96},{48,112},{64,0},{80,16},{96,32},{112,48},{1... | collective-permute-start | bytes 786440 | tf_op jit(solution)/shard_map/sum_aggregates/ppermute | solution.py:39
  49.3 8.9 %collective-permute-start.15 = (bf16[1024,128]{1,0:T(8,128)(2,1)S(1)}, bf16[1024,128]{1,0:T(8,128)(2,1)S(1)}, u32[]{:S(2)}, u32[]{:S(2)}) collective-permute-start(bf16[1024,128]{1,0:T(8,128)(2,1)S(1)} %get-tuple-element.57), channel_id=1, source_target_pairs={{0,16},{16,0},{32,48},{48,32},{64,80},{80,64},{96,112},{112,96},{1... | collective-permute-start | bytes 786440 | tf_op jit(solution)/shard_map/sum_aggregates/ppermute | solution.py:39
  60.5 11.4 %collective-permute-start.19 = (bf16[144,1024]{1,0:T(8,128)(2,1)S(1)}, bf16[144,1024]{1,0:T(8,128)(2,1)S(1)}, u32[]{:S(2)}, u32[]{:S(2)}) collective-permute-start(bf16[144,1024]{1,0:T(8,128)(2,1)S(1)} %get-tuple-element.61), channel_id=1, source_target_pairs={{0,64},{16,80},{32,96},{48,112},{64,0},{80,16},{96,32},{112,48},{1... | collective-permute-start | bytes 884744 | tf_op jit(solution)/shard_map/gather_dz/ppermute | solution.py:39
  61.6 13.6 %collective-permute-start.16 = (bf16[128,1024]{1,0:T(8,128)(2,1)S(1)}, bf16[128,1024]{1,0:T(8,128)(2,1)S(1)}, u32[]{:S(2)}, u32[]{:S(2)}) collective-permute-start(bf16[128,1024]{1,0:T(8,128)(2,1)S(1)} %get-tuple-element.60.refs_3_), channel_id=1, source_target_pairs={{0,16},{16,0},{32,48},{48,32},{64,80},{80,64},{96,112},{112,96},{1... | collective-permute-start | bytes 786440 | tf_op jit(solution)/shard_map/gather_dz/ppermute | solution.py:39
  64.8 12.8 %collective-permute-start.21 = (bf16[144,1024]{1,0:T(8,128)(2,1)S(1)}, bf16[144,1024]{1,0:T(8,128)(2,1)S(1)}, u32[]{:S(2)}, u32[]{:S(2)}) collective-permute-start(bf16[144,1024]{1,0:T(8,128)(2,1)S(1)} %get-tuple-element.62), channel_id=1, source_target_pairs={{0,32},{16,48},{32,64},{48,80},{64,96},{80,112},{96,0},{112,16},{1... | collective-permute-start | bytes 884744 | tf_op jit(solution)/shard_map/gather_dz/ppermute | solution.py:39
  65.0 12.5 %collective-permute-start.22 = (bf16[144,1024]{1,0:T(8,128)(2,1)S(1)}, bf16[144,1024]{1,0:T(8,128)(2,1)S(1)}, u32[]{:S(2)}, u32[]{:S(2)}) collective-permute-start(bf16[144,1024]{1,0:T(8,128)(2,1)S(1)} %get-tuple-element.63), channel_id=1, source_target_pairs={{0,96},{16,112},{32,0},{48,16},{64,32},{80,48},{96,64},{112,80},{1... | collective-permute-start | bytes 884744 | tf_op jit(solution)/shard_map/gather_dz/ppermute | solution.py:39
  71.9 11.5 %collective-permute-start.20 = (bf16[144,1024]{1,0:T(8,128)(2,1)S(1)}, bf16[144,1024]{1,0:T(8,128)(2,1)S(1)}, u32[]{:S(2)}, u32[]{:S(2)}) collective-permute-start(bf16[144,1024]{1,0:T(8,128)(2,1)S(1)} %collective-permute-done.19.refs_7_.refs_1_), channel_id=1, source_target_pairs={{0,16},{16,0},{32,48},{48,32},{64,80},{80,64},{96,112},{112,96},{1... | collective-permute-start | bytes 884744 | tf_op jit(solution)/shard_map/gather_dz/ppermute | solution.py:39
  75.2 8.2 %collective-permute-start.18 = (bf16[128,1024]{1,0:T(8,128)(2,1)S(1)}, bf16[128,1024]{1,0:T(8,128)(2,1)S(1)}, u32[]{:S(2)}, u32[]{:S(2)}) collective-permute-start(bf16[128,1024]{1,0:T(8,128)(2,1)S(1)} %collective-permute-done.16.refs_6_), channel_id=1, source_target_pairs={{0,96},{16,112},{32,0},{48,16},{64,32},{80,48},{96,64},{112,80},{1... | collective-permute-start | bytes 786440 | tf_op jit(solution)/shard_map/gather_dz/ppermute | solution.py:39
  75.6 7.8 %collective-permute-start.17 = (bf16[128,1024]{1,0:T(8,128)(2,1)S(1)}, bf16[128,1024]{1,0:T(8,128)(2,1)S(1)}, u32[]{:S(2)}, u32[]{:S(2)}) collective-permute-start(bf16[128,1024]{1,0:T(8,128)(2,1)S(1)} %collective-permute-done.16.refs_6_), channel_id=1, source_target_pairs={{0,32},{16,48},{32,64},{48,80},{64,96},{80,112},{96,0},{112,16},{1... | collective-permute-start | bytes 786440 | tf_op jit(solution)/shard_map/gather_dz/ppermute | solution.py:39
  77.6 5.8 %collective-permute-start.23 = (bf16[32,1024]{1,0:T(8,128)(2,1)S(1)}, bf16[32,1024]{1,0:T(8,128)(2,1)S(1)}, u32[]{:S(2)}, u32[]{:S(2)}) collective-permute-start(bf16[32,1024]{1,0:T(8,128)(2,1)S(1)} %gather_dz.1.refs_6_), channel_id=1, source_target_pairs={{0,16},{16,0},{32,48},{48,32},{64,80},{80,64},{96,112},{112,96},{1... | collective-permute-start | bytes 196616 | tf_op jit(solution)/shard_map/gather_dz/ppermute | solution.py:39
  86.9 11.3 %collective-permute-start.25 = (bf16[5,128,1024]{2,1,0:T(8,128)(2,1)S(1)}, bf16[5,128,1024]{2,1,0:T(8,128)(2,1)S(1)}, u32[]{:S(2)}, u32[]{:S(2)}) collective-permute-start(bf16[5,128,1024]{2,1,0:T(8,128)(2,1)S(1)} %get-tuple-element.70), channel_id=1, source_target_pairs={{0,1},{1,0},{2,3},{3,2},{4,5},{5,4},{6,7},{7,6},{8,9},{9,8},{10,11... | collective-permute-start | bytes 3932168 | tf_op jit(solution)/shard_map/sum_grads/ppermute | solution.py:31
  87.1 9.3 %collective-permute-start.26 = (bf16[144,1024]{1,0:T(8,128)(2,1)S(1)}, bf16[144,1024]{1,0:T(8,128)(2,1)S(1)}, u32[]{:S(2)}, u32[]{:S(2)}) collective-permute-start(bf16[144,1024]{1,0:T(8,128)(2,1)S(1)} %get-tuple-element.71), channel_id=1, source_target_pairs={{0,6},{1,7},{2,0},{3,1},{4,2},{5,3},{6,4},{7,5},{8,14},{9,15},{10,... | collective-permute-start | bytes 884744 | tf_op jit(solution)/shard_map/sum_grads/ppermute | solution.py:31
  88.0 10.2 %collective-permute-start.27 = (bf16[144,1024]{1,0:T(8,128)(2,1)S(1)}, bf16[144,1024]{1,0:T(8,128)(2,1)S(1)}, u32[]{:S(2)}, u32[]{:S(2)}) collective-permute-start(bf16[144,1024]{1,0:T(8,128)(2,1)S(1)} %get-tuple-element.72), channel_id=1, source_target_pairs={{0,2},{1,3},{2,4},{3,5},{4,6},{5,7},{6,0},{7,1},{8,10},{9,11},{10,... | collective-permute-start | bytes 884744 | tf_op jit(solution)/shard_map/sum_grads/ppermute | solution.py:31
  89.2 9.0 %collective-permute-start.28 = (bf16[144,1024]{1,0:T(8,128)(2,1)S(1)}, bf16[144,1024]{1,0:T(8,128)(2,1)S(1)}, u32[]{:S(2)}, u32[]{:S(2)}) collective-permute-start(bf16[144,1024]{1,0:T(8,128)(2,1)S(1)} %get-tuple-element.73), channel_id=1, source_target_pairs={{0,8},{1,9},{2,10},{3,11},{4,12},{5,13},{6,14},{7,15},{8,0},{9,1},... | collective-permute-start | bytes 884744 | tf_op jit(solution)/shard_map/sum_grads/ppermute | solution.py:31
  98.5 12.3 %collective-permute-start.31 = (bf16[160,1024]{1,0:T(8,128)(2,1)S(1)}, bf16[160,1024]{1,0:T(8,128)(2,1)S(1)}, u32[]{:S(2)}, u32[]{:S(2)}) collective-permute-start(bf16[160,1024]{1,0:T(8,128)(2,1)S(1)} %get-tuple-element.78), channel_id=1, source_target_pairs={{0,4},{1,5},{2,6},{3,7},{4,0},{5,1},{6,2},{7,3},{8,12},{9,13},{10,... | collective-permute-start | bytes 983048 | tf_op jit(solution)/shard_map/sum_grads/ppermute | solution.py:31
  99.2 11.5 %collective-permute-start.32 = (bf16[160,1024]{1,0:T(8,128)(2,1)S(1)}, bf16[160,1024]{1,0:T(8,128)(2,1)S(1)}, u32[]{:S(2)}, u32[]{:S(2)}) collective-permute-start(bf16[160,1024]{1,0:T(8,128)(2,1)S(1)} %get-tuple-element.79), channel_id=1, source_target_pairs={{0,8},{1,9},{2,10},{3,11},{4,12},{5,13},{6,14},{7,15},{8,0},{9,1},... | collective-permute-start | bytes 983048 | tf_op jit(solution)/shard_map/sum_grads/ppermute | solution.py:31
  99.5 16.1 %collective-permute-start.29 = (bf16[128,1024]{1,0:T(8,128)(2,1)S(1)}, bf16[128,1024]{1,0:T(8,128)(2,1)S(1)}, u32[]{:S(2)}, u32[]{:S(2)}) collective-permute-start(bf16[128,1024]{1,0:T(8,128)(2,1)S(1)} %get-tuple-element.76), channel_id=1, source_target_pairs={{0,6},{1,7},{2,0},{3,1},{4,2},{5,3},{6,4},{7,5},{8,14},{9,15},{10,... | collective-permute-start | bytes 786440 | tf_op jit(solution)/shard_map/sum_grads/ppermute | solution.py:31
  101.9 13.7 %collective-permute-start.30 = (bf16[128,1024]{1,0:T(8,128)(2,1)S(1)}, bf16[128,1024]{1,0:T(8,128)(2,1)S(1)}, u32[]{:S(2)}, u32[]{:S(2)}) collective-permute-start(bf16[128,1024]{1,0:T(8,128)(2,1)S(1)} %get-tuple-element.77), channel_id=1, source_target_pairs={{0,2},{1,3},{2,4},{3,5},{4,6},{5,7},{6,0},{7,1},{8,10},{9,11},{10,... | collective-permute-start | bytes 786440 | tf_op jit(solution)/shard_map/sum_grads/ppermute | solution.py:31
  110.9 5.7 %collective-permute-start.35 = (f32[64,256]{1,0:T(8,128)S(1)}, f32[64,256]{1,0:T(8,128)S(1)}, u32[]{:S(2)}, u32[]{:S(2)}) collective-permute-start(f32[64,256]{1,0:T(8,128)S(1)} %sum_weights.2.refs_0_), channel_id=1, source_target_pairs={{0,32},{16,48},{32,64},{48,80},{64,96},{80,112},{96,0},{112,16},{1... | collective-permute-start | bytes 196616 | tf_op jit(solution)/shard_map/sum_weights/ppermute | solution.py:39
  111.3 6.5 %collective-permute-start.34 = (f32[64,256]{1,0:T(8,128)S(1)}, f32[64,256]{1,0:T(8,128)S(1)}, u32[]{:S(2)}, u32[]{:S(2)}) collective-permute-start(f32[64,256]{1,0:T(8,128)S(1)} %sum_weights.2.refs_0_), channel_id=1, source_target_pairs={{0,64},{16,80},{32,96},{48,112},{64,0},{80,16},{96,32},{112,48},{1... | collective-permute-start | bytes 196616 | tf_op jit(solution)/shard_map/sum_weights/ppermute | solution.py:39
  (10 other events, 130.6 us)

commit v5 on v4

--- a/solution.py
+++ b/solution.py
@@ -262,7 +262,7 @@
 
 
 def add_sib_far_body(mine, sib, got, quarter, *rest):
-    outs, quarter_out, near = rest[:3], rest[3], rest[4]
+    outs, (quarter_out, near, extra) = rest[:3], rest[3:]
     total = quarter[...] + read_fine(got, 384)
     quarter_out[...] = rounded(total)
     for k, ref in enumerate(outs):
@@ -271,6 +271,7 @@
             new = mine[4 * (PAIR_LEFT + k) + b] + got[128 * k : 128 * k + 128, nodes].astype(F32)
             ref[0:128, nodes] = new.astype(BF16)
         write_extra(ref, 128, total)
+    write_extra(extra, 0, total)
     write_places(sib, OWN, [near.at[k] for k in range(5)])
 
 
@@ -280,20 +281,29 @@
     opposite_out[...] = (opposite[...] + from_pair[...].astype(F32)).astype(BF16)
 
 
-def add_near_body(mine, got, from_right, from_left, from_pair, quarter, *outs):
+def add_sides_body(mine, got, left, right):
+    for place, ref in ((LEFT, left), (RIGHT, right)):
+        for b in range(4):
+            nodes = slice(b * TILE, (b + 1) * TILE)
+            new = mine[4 * place + b] + got[place, :, nodes].astype(F32)
+            ref[:, nodes] = new.astype(BF16)
+
+
+def add_near_body(mine, got, from_right, from_left, from_pair, *outs):
     more = {PAIR: [from_right, from_left], OPPOSITE: [from_pair]}
-    for place, ref in enumerate(outs):
+    for place, ref in zip((OWN, PAIR, OPPOSITE), outs):
         for b in range(4):
             nodes = slice(b * TILE, (b + 1) * TILE)
             new = mine[4 * place + b] + got[place, :, nodes].astype(F32)
             for came in more.get(place, []):
                 new = new + came[0:128, nodes].astype(F32)
-            ref[0:128, nodes] = new.astype(ref.dtype)
-    pair, opposite = outs[PAIR], outs[OPPOSITE]
-    write_extra(opposite, 128, quarter[...])
-    opposite[144:160] = from_pair[128:144]
-    pair[128:144] = from_left[128:144]
-    pair[144:160] = from_right[128:144]
+            ref[:, nodes] = new.astype(ref.dtype)
+
+
+def extras_body(from_right, from_left, from_opposite, pair):
+    pair[0:16] = from_left[128:144]
+    pair[16:32] = from_right[128:144]
+    pair[32:48] = from_opposite[...]
 
 
 def first_sums(parts, step, swap):
@@ -364,17 +374,18 @@
         out[nodes] = total.T.astype(BF16)
 
 
-def weight_sum_body(own, left, right, pair, from_opposite, from_pair, out, parts):
+def weight_sum_body(own, left, right, pair, opposite, pair_ring, out, parts):
     col, _ = places()
     y, x = col >> 3, (col >> 1) & 3
-    parts[y * 4 + x] = own[...]
-    parts[y * 4 + ((x + 3) & 3)] = read_extra(left, 128)
-    parts[y * 4 + ((x + 1) & 3)] = read_extra(right, 128)
-    parts[(1 - y) * 4 + x] = read_extra(pair, 128)
-    parts[y * 4 + ((x + 2) & 3)] = read_extra(from_opposite, 128)
-    parts[(1 - y) * 4 + ((x + 2) & 3)] = read_extra(from_opposite, 144)
-    parts[(1 - y) * 4 + ((x + 3) & 3)] = read_extra(from_pair, 128)
-    parts[(1 - y) * 4 + ((x + 1) & 3)] = read_extra(from_pair, 144)
+    ring, other = y * 4, (1 - y) * 4
+    parts[ring + x] = own[...]
+    parts[ring + ((x + 3) & 3)] = read_extra(left, 128)
+    parts[ring + ((x + 1) & 3)] = read_extra(right, 128)
+    parts[ring + ((x + 2) & 3)] = read_extra(opposite, 0)
+    parts[other + x] = read_extra(pair, 128)
+    parts[other + ((x + 3) & 3)] = read_extra(pair_ring, 0)
+    parts[other + ((x + 1) & 3)] = read_extra(pair_ring, 16)
+    parts[other + ((x + 2) & 3)] = read_extra(pair_ring, 32)
     total = parts[0]
     for k in range(1, 8):
         total = total + parts[k]
@@ -539,27 +550,32 @@
     with jax.named_scope("sum_grads"):
         step, swap = (lambda v, d: hop_col(v, 0, d)), (lambda v: hop_col(v, 1, 0))
         f32, bf16 = VMEM((128, 1024), F32), VMEM((128, 1024), BF16)
-        *far, quarter, sib_near = call(
+        *far, quarter, sib_near, extra = call(
             add_sib_far_body,
-            [longer, longer, longer, block, VMEM((5, 128, 1024), BF16)],
+            [longer, longer, longer, block, VMEM((5, 128, 1024), BF16), VMEM((16, 1024), BF16)],
             [mine, sib, hop_col(sib_far, 0, 0, 1), quarter],
             nbytes=3 << 20,
         )
         from_right, from_left, from_pair = first_sums(far, step, swap)
-        longest = VMEM((160, 1024), BF16)
-        near = call(
+        sib_near = hop_col(sib_near, 0, 0, 1)
+        left, right = call(add_sides_body, [bf16, bf16], [mine, sib_near], nbytes=2 << 20)
+        left, right = step(left, -1), step(right, 1)
+        from_opposite = step(extra, 2)
+        extras = call(extras_body, VMEM((48, 1024), BF16), [from_right, from_left, from_opposite])
+        came = [from_left, from_right, from_pair, from_opposite, swap(extras)]
+        own, pair, opposite = call(
             add_near_body,
-            [f32, bf16, bf16, longest, longest],
-            [mine, hop_col(sib_near, 0, 0, 1), from_right, from_left, from_pair, quarter],
+            [f32, bf16, bf16],
+            [mine, sib_near, from_right, from_left, from_pair],
+            after=[came[4], left, right],
             nbytes=5 << 20,
         )
-        sums = second_sums(*near, step, swap)
-        came = [from_left, from_right, from_pair]
+        sums = [own, left, right, step(opposite, 2), swap(pair)]
     with jax.named_scope("sum_weights"):
         quarter = call(
             weight_sum_body,
             block,
-            [quarter, *came, sums[3], sums[4]],
+            [quarter, *came],
             scratch=[VMEM((8, 64, 256), F32)],
             nbytes=1 << 20,
         )

time: 119 us -> 119 us (level)
  waiting for transfers between devices: 48 us -> 34.7 us
  Pallas kernels: 18 us -> 25.2 us
  starting transfers between devices: 51.6 us -> 57.4 us
    ppermute x18 -> x20, waiting for transfers between devices: 29.6 us -> 18.6 us  [hop_col(): return lax.ppermute(value, 'col', pairs)]
    pallas_call x17 -> x19, Pallas kernels: 11.5 us -> 18.8 us  [call(): pl.pallas_call(run, out_shape=outs, in_specs=[pl.BlockSpec(memory_space=p...]
    ppermute x18 -> x20, starting transfers between devices: 17.2 us -> 22.5 us  [hop_col(): return lax.ppermute(value, 'col', pairs)]
    ppermute x18, waiting for transfers between devices: 18.4 us -> 16 us  [hop_row(): return lax.ppermute(value, 'row', pairs)]
  transfers between devices with their start and end apart: 36 -> 38, of which waited for: 16 -> 16; matrix products, arithmetic and copies ran while one was open for 0% -> 0% of each run, Pallas kernels for 10% -> 15%
where the time goes in v5:
time: 119 us; the launch traced here: 120 us
  starting transfers between devices  57.4 us (48%)
  waiting for transfers between devices  34.7 us (29%)
  Pallas kernels  25.2 us (21%)
  between operations  1.54 us (1%)
    ppermute x18, starting transfers between devices, hop_row(): return lax.ppermute(value, 'row', pairs)  34.9 us
    ppermute x20, starting transfers between devices, hop_col(): return lax.ppermute(value, 'col', pairs)  22.5 us
    pallas_call x19, Pallas kernels, call(): pl.pallas_call(run, out_shape=outs, in_specs=[pl.BlockSpec(memory_space=p...  18.8 us
    ppermute x20, waiting for transfers between devices, hop_col(): return lax.ppermute(value, 'col', pairs)  18.6 us
    ppermute x18, waiting for transfers between devices, hop_row(): return lax.ppermute(value, 'row', pairs)  16 us
    pallas_call x1, Pallas kernels, shards(): pl.pallas_call(plan_body, out_shape=[VMEM((128, TILE, TILE), BF16), pltpu...  6.48 us
  transfers between devices with their start and end apart: 38, of which 16 were waited for; matrix products, arithmetic and copies ran while one was open for 0% of the time, Pallas kernels for 15%

profile of v5, /device:TPU:0, one launch (start us, length us, event | category | flops | bytes accessed | tf_op | source)
XLA Modules:
  0.0 119.6 jit_solution(7276812131697371526)
XLA Ops:
  0.6 3.2 %collective-permute-start.3 = (bf16[1024,128]{1,0:T(8,128)(2,1)}, bf16[1024,128]{1,0:T(8,128)(2,1)S(1)}, u32[]{:S(2)}, u32[]{:S(2)}) collective-permute-start(bf16[1024,128]{1,0:T(8,128)(2,1)} %refs_1_.2), channel_id=1, source_target_pairs={{0,4},{1,5},{2,6},{3,7},{4,0},{5,1},{6,2},{7,3},{8,12},{9,13},{10,... | collective-permute-start | bytes 786440 | tf_op jit(solution)/shard_map/gather_features/ppermute | solution.py:31
  3.8 1.6 %collective-permute-start.2 = (bf16[1024,128]{1,0:T(8,128)(2,1)}, bf16[1024,128]{1,0:T(8,128)(2,1)S(1)}, u32[]{:S(2)}, u32[]{:S(2)}) collective-permute-start(bf16[1024,128]{1,0:T(8,128)(2,1)} %refs_1_.2), channel_id=1, source_target_pairs={{0,8},{1,9},{2,10},{3,11},{4,12},{5,13},{6,14},{7,15},{8,0},{9,1},... | collective-permute-start | bytes 786440 | tf_op jit(solution)/shard_map/gather_features/ppermute | solution.py:31
  8.8 6.5 %plan.1 = (bf16[128,256,256]{2,1,0:T(8,128)(2,1)S(1)}, s32[1152]{0:T(1024)S(4)}, s32[8]{0:T(128)S(4)}) custom-call(s32[2,128]{1,0:T(2,128)S(1)} %bitcast.7, s32[1]{0:T(128)} %bitcast.6.count, bf16[128,256,256]{2,1,0:T(8,128)(2,1)} %bitcast.9), custom_call_target="tpu_custom_call" | custom-call | bytes 16777216 | tf_op jit(solution)/shard_map/plan/pallas_call | solution.py:413
  16.5 1.7 %collective-permute-start.6 = (bf16[1024,128]{1,0:T(8,128)(2,1)S(1)}, bf16[1024,128]{1,0:T(8,128)(2,1)S(1)}, u32[]{:S(2)}, u32[]{:S(2)}) collective-permute-start(bf16[1024,128]{1,0:T(8,128)(2,1)S(1)} %collective-permute-done.3.refs_4_), channel_id=1, source_target_pairs={{0,8},{1,9},{2,10},{3,11},{4,12},{5,13},{6,14},{7,15},{8,0},{9,1},... | collective-permute-start | bytes 786440 | tf_op jit(solution)/shard_map/gather_features/ppermute | solution.py:31
  18.2 2.6 %collective-permute-start.5 = (bf16[1024,128]{1,0:T(8,128)(2,1)S(1)}, bf16[1024,128]{1,0:T(8,128)(2,1)S(1)}, u32[]{:S(2)}, u32[]{:S(2)}) collective-permute-start(bf16[1024,128]{1,0:T(8,128)(2,1)S(1)} %get-tuple-element.47), channel_id=1, source_target_pairs={{0,6},{1,7},{2,0},{3,1},{4,2},{5,3},{6,4},{7,5},{8,14},{9,15},{10,... | collective-permute-start | bytes 786440 | tf_op jit(solution)/shard_map/gather_features/ppermute | solution.py:31
  20.8 4.6 %forward_tiles.4.refs_3_.refs_4_ = f32[33,256,128]{2,1,0:T(8,128)S(1)} custom-call(s32[1152]{0:T(1024)S(4)} %get-tuple-element.44.refs_0_, s32[8]{0:T(128)S(4)} %get-tuple-element.45.refs_5_.refs_1_, bf16[128,256,256]{2,1,0:T(8,128)(2,1)S(1)} %get-tuple-element.46.refs_2_, bf16[20,256,128]{2,1,0:T(8,128)(2,1)S(1)} %get-tuple-element.48.refs_3_, ...), custom_call_target="tpu_custom_call" | custom-call | tf_op jit(solution)/shard_map/forward_tiles/pallas_call | solution.py:67
  26.7 3.4 %collective-permute-done.4.refs_0_ = bf16[1024,128]{1,0:T(8,128)(2,1)S(1)} collective-permute-done((bf16[1024,128]{1,0:T(8,128)(2,1)S(1)}, bf16[1024,128]{1,0:T(8,128)(2,1)S(1)}, u32[]{:S(2)}, u32[]{:S(2)}) %collective-permute-start.4) | collective-permute-done | bytes 262176 | tf_op jit(solution)/shard_map/gather_features/ppermute | solution.py:31
  30.2 1.4 %forward_tiles.6.refs_4_ = f32[33,256,128]{2,1,0:T(8,128)S(1)} custom-call(s32[1152]{0:T(1024)S(4)} %get-tuple-element.44.refs_0_, s32[8]{0:T(128)S(4)} %get-tuple-element.45.refs_5_.refs_1_, bf16[128,256,256]{2,1,0:T(8,128)(2,1)S(1)} %get-tuple-element.46.refs_2_, bf16[12,256,128]{2,1,0:T(8,128)(2,1)S(1)} %forward_tiles.5.refs_3_, ...), custom_call_target="tpu_custom_call", output_to_operand_aliasing={{}: (4, {})} | custom-call | flops 536870912 | bytes 4194304 | tf_op jit(solution)/shard_map/forward_tiles/pallas_call | solution.py:67
  32.5 1.6 %forward_tiles.7 = (f32[33,256,128]{2,1,0:T(8,128)S(1)}, f32[1024,128]{1,0:T(8,128)S(1)}, bf16[1024,128]{1,0:T(8,128)(2,1)S(1)}, bf16[1024,128]{1,0:T(8,128)(2,1...) custom-call(s32[1152]{0:T(1024)S(4)} %get-tuple-element.44.refs_0_, ...), custom_call_target="tpu_custom_call", output_to_operand_aliasing={{0}: (4, {})} | custom-call | flops 536870912 | bytes 4194304 | tf_op jit(solution)/shard_map/forward_tiles/pallas_call | solution.py:67
  34.2 3.4 %collective-permute-start.11 = (bf16[1024,128]{1,0:T(8,128)(2,1)S(1)}, bf16[1024,128]{1,0:T(8,128)(2,1)S(1)}, u32[]{:S(2)}, u32[]{:S(2)}) collective-permute-start(bf16[1024,128]{1,0:T(8,128)(2,1)S(1)} %get-tuple-element.54), channel_id=1, source_target_pairs={{0,96},{16,112},{32,0},{48,16},{64,32},{80,48},{96,64},{112,80},{1... | collective-permute-start | bytes 786440 | tf_op jit(solution)/shard_map/sum_aggregates/ppermute | solution.py:39
  37.6 3.6 %collective-permute-start.13 = (bf16[1024,128]{1,0:T(8,128)(2,1)S(1)}, bf16[1024,128]{1,0:T(8,128)(2,1)S(1)}, u32[]{:S(2)}, u32[]{:S(2)}) collective-permute-start(bf16[1024,128]{1,0:T(8,128)(2,1)S(1)} %get-tuple-element.56), channel_id=1, source_target_pairs={{0,16},{16,0},{32,48},{48,32},{64,80},{80,64},{96,112},{112,96},{1... | collective-permute-start | bytes 786440 | tf_op jit(solution)/shard_map/sum_aggregates/ppermute | solution.py:39
  41.2 3.2 %collective-permute-start.9 = (bf16[1024,128]{1,0:T(8,128)(2,1)S(1)}, bf16[1024,128]{1,0:T(8,128)(2,1)S(1)}, u32[]{:S(2)}, u32[]{:S(2)}) collective-permute-start(bf16[1024,128]{1,0:T(8,128)(2,1)S(1)} %get-tuple-element.50), channel_id=1, source_target_pairs={{0,96},{16,112},{32,0},{48,16},{64,32},{80,48},{96,64},{112,80},{1... | collective-permute-start | bytes 786440 | tf_op jit(solution)/shard_map/sum_aggregates/ppermute | solution.py:39
  44.4 2.7 %collective-permute-done.12.refs_3_ = bf16[1024,128]{1,0:T(8,128)(2,1)S(1)} collective-permute-done((bf16[1024,128]{1,0:T(8,128)(2,1)S(1)}, bf16[1024,128]{1,0:T(8,128)(2,1)S(1)}, u32[]{:S(2)}, u32[]{:S(2)}) %collective-permute-start.12) | collective-permute-done | bytes 262176 | tf_op jit(solution)/shard_map/sum_aggregates/ppermute | solution.py:39
  47.3 1.7 %collective-permute-start.14 = (bf16[1024,128]{1,0:T(8,128)(2,1)S(1)}, bf16[1024,128]{1,0:T(8,128)(2,1)S(1)}, u32[]{:S(2)}, u32[]{:S(2)}) collective-permute-start(bf16[1024,128]{1,0:T(8,128)(2,1)S(1)} %get-tuple-element.57), channel_id=1, source_target_pairs={{0,64},{16,80},{32,96},{48,112},{64,0},{80,16},{96,32},{112,48},{1... | collective-permute-start | bytes 786440 | tf_op jit(solution)/shard_map/sum_aggregates/ppermute | solution.py:39
  48.9 3.0 %collective-permute-start.15 = (bf16[1024,128]{1,0:T(8,128)(2,1)S(1)}, bf16[1024,128]{1,0:T(8,128)(2,1)S(1)}, u32[]{:S(2)}, u32[]{:S(2)}) collective-permute-start(bf16[1024,128]{1,0:T(8,128)(2,1)S(1)} %get-tuple-element.58), channel_id=1, source_target_pairs={{0,16},{16,0},{32,48},{48,32},{64,80},{80,64},{96,112},{112,96},{1... | collective-permute-start | bytes 786440 | tf_op jit(solution)/shard_map/sum_aggregates/ppermute | solution.py:39
  51.9 6.1 %collective-permute-done.10.refs_7_ = bf16[1024,128]{1,0:T(8,128)(2,1)S(1)} collective-permute-done((bf16[1024,128]{1,0:T(8,128)(2,1)S(1)}, bf16[1024,128]{1,0:T(8,128)(2,1)S(1)}, u32[]{:S(2)}, u32[]{:S(2)}) %collective-permute-start.10) | collective-permute-done | bytes 262176 | tf_op jit(solution)/shard_map/sum_aggregates/ppermute | solution.py:39
  58.1 2.3 %dense.1 = (bf16[1024,256]{1,0:T(8,128)(2,1)}, bf16[1024,256]{1,0:T(8,128)(2,1)S(1)}, bf16[128,1024]{1,0:T(8,128)(2,1)S(1)}, bf16[144,1024]{1,0:T(8,128)(2,1)S(1...) custom-call(f32[1,256]{1,0:T(1,128)S(1)} %bitcast.8, ...), custom_call_target="tpu_custom_call" | custom-call | flops 335544320 | bytes 6291456 | tf_op jit(solution)/shard_map/dense/pallas_call | solution.py:67
  60.4 1.6 %collective-permute-start.19 = (bf16[144,1024]{1,0:T(8,128)(2,1)S(1)}, bf16[144,1024]{1,0:T(8,128)(2,1)S(1)}, u32[]{:S(2)}, u32[]{:S(2)}) collective-permute-start(bf16[144,1024]{1,0:T(8,128)(2,1)S(1)} %get-tuple-element.62), channel_id=1, source_target_pairs={{0,64},{16,80},{32,96},{48,112},{64,0},{80,16},{96,32},{112,48},{1... | collective-permute-start | bytes 884744 | tf_op jit(solution)/shard_map/gather_dz/ppermute | solution.py:39
  62.0 3.5 %collective-permute-start.16 = (bf16[128,1024]{1,0:T(8,128)(2,1)S(1)}, bf16[128,1024]{1,0:T(8,128)(2,1)S(1)}, u32[]{:S(2)}, u32[]{:S(2)}) collective-permute-start(bf16[128,1024]{1,0:T(8,128)(2,1)S(1)} %get-tuple-element.61.refs_3_), channel_id=1, source_target_pairs={{0,16},{16,0},{32,48},{48,32},{64,80},{80,64},{96,112},{112,96},{1... | collective-permute-start | bytes 786440 | tf_op jit(solution)/shard_map/gather_dz/ppermute | solution.py:39
  65.5 3.2 %collective-permute-start.22 = (bf16[144,1024]{1,0:T(8,128)(2,1)S(1)}, bf16[144,1024]{1,0:T(8,128)(2,1)S(1)}, u32[]{:S(2)}, u32[]{:S(2)}) collective-permute-start(bf16[144,1024]{1,0:T(8,128)(2,1)S(1)} %get-tuple-element.64), channel_id=1, source_target_pairs={{0,96},{16,112},{32,0},{48,16},{64,32},{80,48},{96,64},{112,80},{1... | collective-permute-start | bytes 884744 | tf_op jit(solution)/shard_map/gather_dz/ppermute | solution.py:39
  68.8 2.8 %collective-permute-done.19.refs_7_.refs_1_ = bf16[144,1024]{1,0:T(8,128)(2,1)S(1)} collective-permute-done((bf16[144,1024]{1,0:T(8,128)(2,1)S(1)}, bf16[144,1024]{1,0:T(8,128)(2,1)S(1)}, u32[]{:S(2)}, u32[]{:S(2)}) %collective-permute-start.19) | collective-permute-done | bytes 294944 | tf_op jit(solution)/shard_map/gather_dz/ppermute | solution.py:39
  71.6 1.6 %collective-permute-start.20 = (bf16[144,1024]{1,0:T(8,128)(2,1)S(1)}, bf16[144,1024]{1,0:T(8,128)(2,1)S(1)}, u32[]{:S(2)}, u32[]{:S(2)}) collective-permute-start(bf16[144,1024]{1,0:T(8,128)(2,1)S(1)} %collective-permute-done.19.refs_7_.refs_1_), channel_id=1, source_target_pairs={{0,16},{16,0},{32,48},{48,32},{64,80},{80,64},{96,112},{112,96},{1... | collective-permute-start | bytes 884744 | tf_op jit(solution)/shard_map/gather_dz/ppermute | solution.py:39
  76.0 1.4 %collective-permute-done.21.refs_4_.refs_2_ = bf16[144,1024]{1,0:T(8,128)(2,1)S(1)} collective-permute-done((bf16[144,1024]{1,0:T(8,128)(2,1)S(1)}, bf16[144,1024]{1,0:T(8,128)(2,1)S(1)}, u32[]{:S(2)}, u32[]{:S(2)}) %collective-permute-start.21) | collective-permute-done | bytes 294944 | tf_op jit(solution)/shard_map/gather_dz/ppermute | solution.py:39
  78.7 3.6 %backward_tiles.3 = (f32[33,128,256]{2,1,0:T(8,128)S(1)}, f32[33,128,256]{2,1,0:T(8,128)S(1)}) custom-call(s32[1152]{0:T(1024)S(4)} %get-tuple-element.44.refs_0_, s32[8]{0:T(128)S(4)} %get-tuple-element.45.refs_5_.refs_1_, bf16[128,256,256]{2,1,0:T(8,128)(2,1)S(1)} %get-tuple-element.46.refs_2_, bf16[128,1024]{1,0:T(8,128)(2,1)S(1)} %get-tuple-element.61.refs_3_, ...), custom_call_target="tpu_custom_call" | custom-call | flops 1073741824 | bytes 8388608 | tf_op jit(solution)/shard_map/backward_tiles/pallas_call | solution.py:67
  87.9 1.6 %collective-permute-start.27 = (bf16[144,1024]{1,0:T(8,128)(2,1)S(1)}, bf16[144,1024]{1,0:T(8,128)(2,1)S(1)}, u32[]{:S(2)}, u32[]{:S(2)}) collective-permute-start(bf16[144,1024]{1,0:T(8,128)(2,1)S(1)} %get-tuple-element.73), channel_id=1, source_target_pairs={{0,2},{1,3},{2,4},{3,5},{4,6},{5,7},{6,0},{7,1},{8,10},{9,11},{10,... | collective-permute-start | bytes 884744 | tf_op jit(solution)/shard_map/sum_grads/ppermute | solution.py:31
  91.0 2.7 %collective-permute-start.31 = (bf16[128,1024]{1,0:T(8,128)(2,1)S(1)}, bf16[128,1024]{1,0:T(8,128)(2,1)S(1)}, u32[]{:S(2)}, u32[]{:S(2)}) collective-permute-start(bf16[128,1024]{1,0:T(8,128)(2,1)S(1)} %get-tuple-element.76), channel_id=1, source_target_pairs={{0,6},{1,7},{2,0},{3,1},{4,2},{5,3},{6,4},{7,5},{8,14},{9,15},{10,... | collective-permute-start | bytes 786440 | tf_op jit(solution)/shard_map/sum_grads/ppermute | solution.py:31
  93.7 4.0 %collective-permute-done.29.refs_2_.refs_4_ = bf16[16,1024]{1,0:T(8,128)(2,1)S(1)} collective-permute-done((bf16[16,1024]{1,0:T(8,128)(2,1)S(1)}, bf16[16,1024]{1,0:T(8,128)(2,1)S(1)}, u32[]{:S(2)}, u32[]{:S(2)}) %collective-permute-start.29) | collective-permute-done | bytes 32800 | tf_op jit(solution)/shard_map/sum_grads/ppermute | solution.py:31
  100.1 3.4 %collective-permute-done.30.refs_5_ = bf16[48,1024]{1,0:T(8,128)(2,1)S(1)} collective-permute-done((bf16[48,1024]{1,0:T(8,128)(2,1)S(1)}, bf16[48,1024]{1,0:T(8,128)(2,1)S(1)}, u32[]{:S(2)}, u32[]{:S(2)}) %collective-permute-start.30) | collective-permute-done | bytes 98336 | tf_op jit(solution)/shard_map/sum_grads/ppermute | solution.py:31
  103.5 2.4 %collective-permute-done.32.refs_7_.refs_3_ = bf16[128,1024]{1,0:T(8,128)(2,1)S(1)} collective-permute-done((bf16[128,1024]{1,0:T(8,128)(2,1)S(1)}, bf16[128,1024]{1,0:T(8,128)(2,1)S(1)}, u32[]{:S(2)}, u32[]{:S(2)}) %collective-permute-start.32) | collective-permute-done | bytes 262176 | tf_op jit(solution)/shard_map/sum_grads/ppermute | solution.py:31
  106.2 2.0 %collective-permute-start.33 = (bf16[128,1024]{1,0:T(8,128)(2,1)S(1)}, bf16[128,1024]{1,0:T(8,128)(2,1)S(1)}, u32[]{:S(2)}, u32[]{:S(2)}) collective-permute-start(bf16[128,1024]{1,0:T(8,128)(2,1)S(1)} %get-tuple-element.79), channel_id=1, source_target_pairs={{0,4},{1,5},{2,6},{3,7},{4,0},{5,1},{6,2},{7,3},{8,12},{9,13},{10,... | collective-permute-start | bytes 786440 | tf_op jit(solution)/shard_map/sum_grads/ppermute | solution.py:31
  110.9 2.5 %collective-permute-start.36 = (f32[64,256]{1,0:T(8,128)S(1)}, f32[64,256]{1,0:T(8,128)S(1)}, u32[]{:S(2)}, u32[]{:S(2)}) collective-permute-start(f32[64,256]{1,0:T(8,128)S(1)} %sum_weights.2.refs_0_), channel_id=1, source_target_pairs={{0,64},{16,80},{32,96},{48,112},{64,0},{80,16},{96,32},{112,48},{1... | collective-permute-start | bytes 196616 | tf_op jit(solution)/shard_map/sum_weights/ppermute | solution.py:39
  113.4 2.5 %collective-permute-start.35 = (f32[64,256]{1,0:T(8,128)S(1)}, f32[64,256]{1,0:T(8,128)S(1)}, u32[]{:S(2)}, u32[]{:S(2)}) collective-permute-start(f32[64,256]{1,0:T(8,128)S(1)} %sum_weights.2.refs_0_), channel_id=1, source_target_pairs={{0,96},{16,112},{32,0},{48,16},{64,32},{80,48},{96,64},{112,80},{1... | collective-permute-start | bytes 196616 | tf_op jit(solution)/shard_map/sum_weights/ppermute | solution.py:39
  (76 shorter events, 26.4 us)
Async XLA Ops:
  0.6 14.6 %collective-permute-start.3 = (bf16[1024,128]{1,0:T(8,128)(2,1)}, bf16[1024,128]{1,0:T(8,128)(2,1)S(1)}, u32[]{:S(2)}, u32[]{:S(2)}) collective-permute-start(bf16[1024,128]{1,0:T(8,128)(2,1)} %refs_1_.2), channel_id=1, source_target_pairs={{0,4},{1,5},{2,6},{3,7},{4,0},{5,1},{6,2},{7,3},{8,12},{9,13},{10,... | collective-permute-start | bytes 786440 | tf_op jit(solution)/shard_map/gather_features/ppermute | solution.py:31
  3.8 11.4 %collective-permute-start.2 = (bf16[1024,128]{1,0:T(8,128)(2,1)}, bf16[1024,128]{1,0:T(8,128)(2,1)S(1)}, u32[]{:S(2)}, u32[]{:S(2)}) collective-permute-start(bf16[1024,128]{1,0:T(8,128)(2,1)} %refs_1_.2), channel_id=1, source_target_pairs={{0,8},{1,9},{2,10},{3,11},{4,12},{5,13},{6,14},{7,15},{8,0},{9,1},... | collective-permute-start | bytes 786440 | tf_op jit(solution)/shard_map/gather_features/ppermute | solution.py:31
  5.4 10.9 %collective-permute-start.1 = (bf16[1024,128]{1,0:T(8,128)(2,1)}, bf16[1024,128]{1,0:T(8,128)(2,1)S(1)}, u32[]{:S(2)}, u32[]{:S(2)}) collective-permute-start(bf16[1024,128]{1,0:T(8,128)(2,1)} %refs_1_.2), channel_id=1, source_target_pairs={{0,6},{1,7},{2,0},{3,1},{4,2},{5,3},{6,4},{7,5},{8,14},{9,15},{10,... | collective-permute-start | bytes 786440 | tf_op jit(solution)/shard_map/gather_features/ppermute | solution.py:31
  6.5 9.8 %collective-permute-start = (bf16[1024,128]{1,0:T(8,128)(2,1)}, bf16[1024,128]{1,0:T(8,128)(2,1)S(1)}, u32[]{:S(2)}, u32[]{:S(2)}) collective-permute-start(bf16[1024,128]{1,0:T(8,128)(2,1)} %refs_1_.2), channel_id=1, source_target_pairs={{0,2},{1,3},{2,4},{3,5},{4,6},{5,7},{6,0},{7,1},{8,10},{9,11},{10,... | collective-permute-start | bytes 786440 | tf_op jit(solution)/shard_map/gather_features/ppermute | solution.py:31
  16.5 8.9 %collective-permute-start.6 = (bf16[1024,128]{1,0:T(8,128)(2,1)S(1)}, bf16[1024,128]{1,0:T(8,128)(2,1)S(1)}, u32[]{:S(2)}, u32[]{:S(2)}) collective-permute-start(bf16[1024,128]{1,0:T(8,128)(2,1)S(1)} %collective-permute-done.3.refs_4_), channel_id=1, source_target_pairs={{0,8},{1,9},{2,10},{3,11},{4,12},{5,13},{6,14},{7,15},{8,0},{9,1},... | collective-permute-start | bytes 786440 | tf_op jit(solution)/shard_map/gather_features/ppermute | solution.py:31
  18.2 8.5 %collective-permute-start.5 = (bf16[1024,128]{1,0:T(8,128)(2,1)S(1)}, bf16[1024,128]{1,0:T(8,128)(2,1)S(1)}, u32[]{:S(2)}, u32[]{:S(2)}) collective-permute-start(bf16[1024,128]{1,0:T(8,128)(2,1)S(1)} %get-tuple-element.47), channel_id=1, source_target_pairs={{0,6},{1,7},{2,0},{3,1},{4,2},{5,3},{6,4},{7,5},{8,14},{9,15},{10,... | collective-permute-start | bytes 786440 | tf_op jit(solution)/shard_map/gather_features/ppermute | solution.py:31
  20.8 9.3 %collective-permute-start.4 = (bf16[1024,128]{1,0:T(8,128)(2,1)S(1)}, bf16[1024,128]{1,0:T(8,128)(2,1)S(1)}, u32[]{:S(2)}, u32[]{:S(2)}) collective-permute-start(bf16[1024,128]{1,0:T(8,128)(2,1)S(1)} %get-tuple-element.47), channel_id=1, source_target_pairs={{0,2},{1,3},{2,4},{3,5},{4,6},{5,7},{6,0},{7,1},{8,10},{9,11},{10,... | collective-permute-start | bytes 786440 | tf_op jit(solution)/shard_map/gather_features/ppermute | solution.py:31
  34.2 10.2 %collective-permute-start.11 = (bf16[1024,128]{1,0:T(8,128)(2,1)S(1)}, bf16[1024,128]{1,0:T(8,128)(2,1)S(1)}, u32[]{:S(2)}, u32[]{:S(2)}) collective-permute-start(bf16[1024,128]{1,0:T(8,128)(2,1)S(1)} %get-tuple-element.54), channel_id=1, source_target_pairs={{0,96},{16,112},{32,0},{48,16},{64,32},{80,48},{96,64},{112,80},{1... | collective-permute-start | bytes 786440 | tf_op jit(solution)/shard_map/sum_aggregates/ppermute | solution.py:39
  37.6 9.5 %collective-permute-start.12 = (bf16[1024,128]{1,0:T(8,128)(2,1)S(1)}, bf16[1024,128]{1,0:T(8,128)(2,1)S(1)}, u32[]{:S(2)}, u32[]{:S(2)}) collective-permute-start(bf16[1024,128]{1,0:T(8,128)(2,1)S(1)} %get-tuple-element.55), channel_id=1, source_target_pairs={{0,32},{16,48},{32,64},{48,80},{64,96},{80,112},{96,0},{112,16},{1... | collective-permute-start | bytes 786440 | tf_op jit(solution)/shard_map/sum_aggregates/ppermute | solution.py:39
  37.6 9.6 %collective-permute-start.13 = (bf16[1024,128]{1,0:T(8,128)(2,1)S(1)}, bf16[1024,128]{1,0:T(8,128)(2,1)S(1)}, u32[]{:S(2)}, u32[]{:S(2)}) collective-permute-start(bf16[1024,128]{1,0:T(8,128)(2,1)S(1)} %get-tuple-element.56), channel_id=1, source_target_pairs={{0,16},{16,0},{32,48},{48,32},{64,80},{80,64},{96,112},{112,96},{1... | collective-permute-start | bytes 786440 | tf_op jit(solution)/shard_map/sum_aggregates/ppermute | solution.py:39
  41.2 10.8 %collective-permute-start.9 = (bf16[1024,128]{1,0:T(8,128)(2,1)S(1)}, bf16[1024,128]{1,0:T(8,128)(2,1)S(1)}, u32[]{:S(2)}, u32[]{:S(2)}) collective-permute-start(bf16[1024,128]{1,0:T(8,128)(2,1)S(1)} %get-tuple-element.50), channel_id=1, source_target_pairs={{0,96},{16,112},{32,0},{48,16},{64,32},{80,48},{96,64},{112,80},{1... | collective-permute-start | bytes 786440 | tf_op jit(solution)/shard_map/sum_aggregates/ppermute | solution.py:39
  44.4 13.7 %collective-permute-start.10 = (bf16[1024,128]{1,0:T(8,128)(2,1)S(1)}, bf16[1024,128]{1,0:T(8,128)(2,1)S(1)}, u32[]{:S(2)}, u32[]{:S(2)}) collective-permute-start(bf16[1024,128]{1,0:T(8,128)(2,1)S(1)} %get-tuple-element.51), channel_id=1, source_target_pairs={{0,32},{16,48},{32,64},{48,80},{64,96},{80,112},{96,0},{112,16},{1... | collective-permute-start | bytes 786440 | tf_op jit(solution)/shard_map/sum_aggregates/ppermute | solution.py:39
  47.3 10.8 %collective-permute-start.14 = (bf16[1024,128]{1,0:T(8,128)(2,1)S(1)}, bf16[1024,128]{1,0:T(8,128)(2,1)S(1)}, u32[]{:S(2)}, u32[]{:S(2)}) collective-permute-start(bf16[1024,128]{1,0:T(8,128)(2,1)S(1)} %get-tuple-element.57), channel_id=1, source_target_pairs={{0,64},{16,80},{32,96},{48,112},{64,0},{80,16},{96,32},{112,48},{1... | collective-permute-start | bytes 786440 | tf_op jit(solution)/shard_map/sum_aggregates/ppermute | solution.py:39
  48.9 9.2 %collective-permute-start.15 = (bf16[1024,128]{1,0:T(8,128)(2,1)S(1)}, bf16[1024,128]{1,0:T(8,128)(2,1)S(1)}, u32[]{:S(2)}, u32[]{:S(2)}) collective-permute-start(bf16[1024,128]{1,0:T(8,128)(2,1)S(1)} %get-tuple-element.58), channel_id=1, source_target_pairs={{0,16},{16,0},{32,48},{48,32},{64,80},{80,64},{96,112},{112,96},{1... | collective-permute-start | bytes 786440 | tf_op jit(solution)/shard_map/sum_aggregates/ppermute | solution.py:39
  60.4 11.2 %collective-permute-start.19 = (bf16[144,1024]{1,0:T(8,128)(2,1)S(1)}, bf16[144,1024]{1,0:T(8,128)(2,1)S(1)}, u32[]{:S(2)}, u32[]{:S(2)}) collective-permute-start(bf16[144,1024]{1,0:T(8,128)(2,1)S(1)} %get-tuple-element.62), channel_id=1, source_target_pairs={{0,64},{16,80},{32,96},{48,112},{64,0},{80,16},{96,32},{112,48},{1... | collective-permute-start | bytes 884744 | tf_op jit(solution)/shard_map/gather_dz/ppermute | solution.py:39
  62.0 11.1 %collective-permute-start.16 = (bf16[128,1024]{1,0:T(8,128)(2,1)S(1)}, bf16[128,1024]{1,0:T(8,128)(2,1)S(1)}, u32[]{:S(2)}, u32[]{:S(2)}) collective-permute-start(bf16[128,1024]{1,0:T(8,128)(2,1)S(1)} %get-tuple-element.61.refs_3_), channel_id=1, source_target_pairs={{0,16},{16,0},{32,48},{48,32},{64,80},{80,64},{96,112},{112,96},{1... | collective-permute-start | bytes 786440 | tf_op jit(solution)/shard_map/gather_dz/ppermute | solution.py:39
  65.5 11.9 %collective-permute-start.21 = (bf16[144,1024]{1,0:T(8,128)(2,1)S(1)}, bf16[144,1024]{1,0:T(8,128)(2,1)S(1)}, u32[]{:S(2)}, u32[]{:S(2)}) collective-permute-start(bf16[144,1024]{1,0:T(8,128)(2,1)S(1)} %get-tuple-element.63), channel_id=1, source_target_pairs={{0,32},{16,48},{32,64},{48,80},{64,96},{80,112},{96,0},{112,16},{1... | collective-permute-start | bytes 884744 | tf_op jit(solution)/shard_map/gather_dz/ppermute | solution.py:39
  65.5 11.9 %collective-permute-start.22 = (bf16[144,1024]{1,0:T(8,128)(2,1)S(1)}, bf16[144,1024]{1,0:T(8,128)(2,1)S(1)}, u32[]{:S(2)}, u32[]{:S(2)}) collective-permute-start(bf16[144,1024]{1,0:T(8,128)(2,1)S(1)} %get-tuple-element.64), channel_id=1, source_target_pairs={{0,96},{16,112},{32,0},{48,16},{64,32},{80,48},{96,64},{112,80},{1... | collective-permute-start | bytes 884744 | tf_op jit(solution)/shard_map/gather_dz/ppermute | solution.py:39
  71.6 11.7 %collective-permute-start.20 = (bf16[144,1024]{1,0:T(8,128)(2,1)S(1)}, bf16[144,1024]{1,0:T(8,128)(2,1)S(1)}, u32[]{:S(2)}, u32[]{:S(2)}) collective-permute-start(bf16[144,1024]{1,0:T(8,128)(2,1)S(1)} %collective-permute-done.19.refs_7_.refs_1_), channel_id=1, source_target_pairs={{0,16},{16,0},{32,48},{48,32},{64,80},{80,64},{96,112},{112,96},{1... | collective-permute-start | bytes 884744 | tf_op jit(solution)/shard_map/gather_dz/ppermute | solution.py:39
  73.2 10.2 %collective-permute-start.18 = (bf16[128,1024]{1,0:T(8,128)(2,1)S(1)}, bf16[128,1024]{1,0:T(8,128)(2,1)S(1)}, u32[]{:S(2)}, u32[]{:S(2)}) collective-permute-start(bf16[128,1024]{1,0:T(8,128)(2,1)S(1)} %collective-permute-done.16.refs_6_), channel_id=1, source_target_pairs={{0,96},{16,112},{32,0},{48,16},{64,32},{80,48},{96,64},{112,80},{1... | collective-permute-start | bytes 786440 | tf_op jit(solution)/shard_map/gather_dz/ppermute | solution.py:39
  74.5 8.8 %collective-permute-start.17 = (bf16[128,1024]{1,0:T(8,128)(2,1)S(1)}, bf16[128,1024]{1,0:T(8,128)(2,1)S(1)}, u32[]{:S(2)}, u32[]{:S(2)}) collective-permute-start(bf16[128,1024]{1,0:T(8,128)(2,1)S(1)} %collective-permute-done.16.refs_6_), channel_id=1, source_target_pairs={{0,32},{16,48},{32,64},{48,80},{64,96},{80,112},{96,0},{112,16},{1... | collective-permute-start | bytes 786440 | tf_op jit(solution)/shard_map/gather_dz/ppermute | solution.py:39
  77.5 5.8 %collective-permute-start.23 = (bf16[32,1024]{1,0:T(8,128)(2,1)S(1)}, bf16[32,1024]{1,0:T(8,128)(2,1)S(1)}, u32[]{:S(2)}, u32[]{:S(2)}) collective-permute-start(bf16[32,1024]{1,0:T(8,128)(2,1)S(1)} %gather_dz.1.refs_6_), channel_id=1, source_target_pairs={{0,16},{16,0},{32,48},{48,32},{64,80},{80,64},{96,112},{112,96},{1... | collective-permute-start | bytes 196616 | tf_op jit(solution)/shard_map/gather_dz/ppermute | solution.py:39
  87.5 10.3 %collective-permute-start.26 = (bf16[144,1024]{1,0:T(8,128)(2,1)S(1)}, bf16[144,1024]{1,0:T(8,128)(2,1)S(1)}, u32[]{:S(2)}, u32[]{:S(2)}) collective-permute-start(bf16[144,1024]{1,0:T(8,128)(2,1)S(1)} %get-tuple-element.72), channel_id=1, source_target_pairs={{0,6},{1,7},{2,0},{3,1},{4,2},{5,3},{6,4},{7,5},{8,14},{9,15},{10,... | collective-permute-start | bytes 884744 | tf_op jit(solution)/shard_map/sum_grads/ppermute | solution.py:31
  87.9 10.9 %collective-permute-start.27 = (bf16[144,1024]{1,0:T(8,128)(2,1)S(1)}, bf16[144,1024]{1,0:T(8,128)(2,1)S(1)}, u32[]{:S(2)}, u32[]{:S(2)}) collective-permute-start(bf16[144,1024]{1,0:T(8,128)(2,1)S(1)} %get-tuple-element.73), channel_id=1, source_target_pairs={{0,2},{1,3},{2,4},{3,5},{4,6},{5,7},{6,0},{7,1},{8,10},{9,11},{10,... | collective-permute-start | bytes 884744 | tf_op jit(solution)/shard_map/sum_grads/ppermute | solution.py:31
  89.5 10.6 %collective-permute-start.28 = (bf16[144,1024]{1,0:T(8,128)(2,1)S(1)}, bf16[144,1024]{1,0:T(8,128)(2,1)S(1)}, u32[]{:S(2)}, u32[]{:S(2)}) collective-permute-start(bf16[144,1024]{1,0:T(8,128)(2,1)S(1)} %get-tuple-element.74), channel_id=1, source_target_pairs={{0,8},{1,9},{2,10},{3,11},{4,12},{5,13},{6,14},{7,15},{8,0},{9,1},... | collective-permute-start | bytes 884744 | tf_op jit(solution)/shard_map/sum_grads/ppermute | solution.py:31
  90.9 6.8 %collective-permute-start.29 = (bf16[16,1024]{1,0:T(8,128)(2,1)S(1)}, bf16[16,1024]{1,0:T(8,128)(2,1)S(1)}, u32[]{:S(2)}, u32[]{:S(2)}) collective-permute-start(bf16[16,1024]{1,0:T(8,128)(2,1)S(1)} %get-tuple-element.75), channel_id=1, source_target_pairs={{0,4},{1,5},{2,6},{3,7},{4,0},{5,1},{6,2},{7,3},{8,12},{9,13},{10,... | collective-permute-start | bytes 98312 | tf_op jit(solution)/shard_map/sum_grads/ppermute | solution.py:31
  91.0 12.6 %collective-permute-start.31 = (bf16[128,1024]{1,0:T(8,128)(2,1)S(1)}, bf16[128,1024]{1,0:T(8,128)(2,1)S(1)}, u32[]{:S(2)}, u32[]{:S(2)}) collective-permute-start(bf16[128,1024]{1,0:T(8,128)(2,1)S(1)} %get-tuple-element.76), channel_id=1, source_target_pairs={{0,6},{1,7},{2,0},{3,1},{4,2},{5,3},{6,4},{7,5},{8,14},{9,15},{10,... | collective-permute-start | bytes 786440 | tf_op jit(solution)/shard_map/sum_grads/ppermute | solution.py:31
  97.7 8.3 %collective-permute-start.32 = (bf16[128,1024]{1,0:T(8,128)(2,1)S(1)}, bf16[128,1024]{1,0:T(8,128)(2,1)S(1)}, u32[]{:S(2)}, u32[]{:S(2)}) collective-permute-start(bf16[128,1024]{1,0:T(8,128)(2,1)S(1)} %get-tuple-element.77), channel_id=1, source_target_pairs={{0,2},{1,3},{2,4},{3,5},{4,6},{5,7},{6,0},{7,1},{8,10},{9,11},{10,... | collective-permute-start | bytes 786440 | tf_op jit(solution)/shard_map/sum_grads/ppermute | solution.py:31
  106.2 12.4 %collective-permute-start.33 = (bf16[128,1024]{1,0:T(8,128)(2,1)S(1)}, bf16[128,1024]{1,0:T(8,128)(2,1)S(1)}, u32[]{:S(2)}, u32[]{:S(2)}) collective-permute-start(bf16[128,1024]{1,0:T(8,128)(2,1)S(1)} %get-tuple-element.79), channel_id=1, source_target_pairs={{0,4},{1,5},{2,6},{3,7},{4,0},{5,1},{6,2},{7,3},{8,12},{9,13},{10,... | collective-permute-start | bytes 786440 | tf_op jit(solution)/shard_map/sum_grads/ppermute | solution.py:31
  108.2 10.4 %collective-permute-start.34 = (bf16[128,1024]{1,0:T(8,128)(2,1)S(1)}, bf16[128,1024]{1,0:T(8,128)(2,1)S(1)}, u32[]{:S(2)}, u32[]{:S(2)}) collective-permute-start(bf16[128,1024]{1,0:T(8,128)(2,1)S(1)} %get-tuple-element.80), channel_id=1, source_target_pairs={{0,8},{1,9},{2,10},{3,11},{4,12},{5,13},{6,14},{7,15},{8,0},{9,1},... | collective-permute-start | bytes 786440 | tf_op jit(solution)/shard_map/sum_grads/ppermute | solution.py:31
  109.6 6.3 %collective-permute-start.37 = (f32[64,256]{1,0:T(8,128)S(1)}, f32[64,256]{1,0:T(8,128)S(1)}, u32[]{:S(2)}, u32[]{:S(2)}) collective-permute-start(f32[64,256]{1,0:T(8,128)S(1)} %sum_weights.2.refs_0_), channel_id=1, source_target_pairs={{0,32},{16,48},{32,64},{48,80},{64,96},{80,112},{96,0},{112,16},{1... | collective-permute-start | bytes 196616 | tf_op jit(solution)/shard_map/sum_weights/ppermute | solution.py:39
  110.9 5.8 %collective-permute-start.36 = (f32[64,256]{1,0:T(8,128)S(1)}, f32[64,256]{1,0:T(8,128)S(1)}, u32[]{:S(2)}, u32[]{:S(2)}) collective-permute-start(f32[64,256]{1,0:T(8,128)S(1)} %sum_weights.2.refs_0_), channel_id=1, source_target_pairs={{0,64},{16,80},{32,96},{48,112},{64,0},{80,16},{96,32},{112,48},{1... | collective-permute-start | bytes 196616 | tf_op jit(solution)/shard_map/sum_weights/ppermute | solution.py:39
  (12 other events, 135.8 us)

commit v6 on v4

--- a/solution.py
+++ b/solution.py
@@ -261,47 +261,47 @@
     backward_step(lists, sizes, tiles, 6, held, mine)
 
 
-def add_sib_far_body(mine, sib, got, quarter, *rest):
-    outs, quarter_out, near = rest[:3], rest[3], rest[4]
-    total = quarter[...] + read_fine(got, 384)
-    quarter_out[...] = rounded(total)
-    for k, ref in enumerate(outs):
+def add_sib_far_body(mine, sib, got, quarter, to_left, to_right, to_pair, quarter_out, near):
+    for k, ref in enumerate((to_left, to_right, to_pair)):
         for b in range(4):
             nodes = slice(b * TILE, (b + 1) * TILE)
             new = mine[4 * (PAIR_LEFT + k) + b] + got[128 * k : 128 * k + 128, nodes].astype(F32)
             ref[0:128, nodes] = new.astype(BF16)
-        write_extra(ref, 128, total)
+    total = quarter[...] + read_fine(got, 384)
+    quarter_out[...] = fine(total)
+    write_fine(to_pair, 128, total)
     write_places(sib, OWN, [near.at[k] for k in range(5)])
 
 
-def add_round_body(pair, opposite, from_right, from_left, from_pair, pair_out, opposite_out):
-    new = pair[...] + (from_right[...].astype(F32) + from_left[...].astype(F32))
-    pair_out[...] = new.astype(BF16)
-    opposite_out[...] = (opposite[...] + from_pair[...].astype(F32)).astype(BF16)
-
-
-def add_near_body(mine, got, from_right, from_left, from_pair, quarter, *outs):
-    more = {PAIR: [from_right, from_left], OPPOSITE: [from_pair]}
-    for place, ref in enumerate(outs):
+def add_body(own, *rest):
+    new = own[...]
+    for ref in rest[:-1]:
+        new = new + ref[...].astype(F32)
+    rest[-1][...] = new.astype(rest[-1].dtype)
+
+
+def add_cores(mine, place, got, b):
+    return mine[4 * place + b] + got[place, :, b * TILE : (b + 1) * TILE].astype(F32)
+
+
+def add_ring_body(mine, got, from_pair, quarter, left, right, opposite, quarter_out):
+    total = quarter[...] + read_fine(from_pair, 128)
+    quarter_out[...] = rounded(total)
+    for place, ref in ((LEFT, left), (RIGHT, right), (OPPOSITE, opposite)):
         for b in range(4):
             nodes = slice(b * TILE, (b + 1) * TILE)
-            new = mine[4 * place + b] + got[place, :, nodes].astype(F32)
-            for came in more.get(place, []):
-                new = new + came[0:128, nodes].astype(F32)
-            ref[0:128, nodes] = new.astype(ref.dtype)
-    pair, opposite = outs[PAIR], outs[OPPOSITE]
-    write_extra(opposite, 128, quarter[...])
-    opposite[144:160] = from_pair[128:144]
-    pair[128:144] = from_left[128:144]
-    pair[144:160] = from_right[128:144]
-
-
-def first_sums(parts, step, swap):
-    return step(parts[0], -1), step(parts[1], 1), swap(parts[2])
-
-
-def second_sums(own, left, right, pair, opposite, step, swap):
-    return [own, step(left, -1), step(right, 1), step(opposite, 2), swap(pair)]
+            new = add_cores(mine, place, got, b)
+            if place == OPPOSITE:
+                new = new + from_pair[0:128, nodes].astype(F32)
+            ref[0:128, nodes] = new.astype(BF16)
+        write_extra(ref, 128, total)
+
+
+def add_pair_body(mine, got, from_right, from_left, out):
+    for b in range(4):
+        nodes = slice(b * TILE, (b + 1) * TILE)
+        came = from_right[:, nodes].astype(F32) + from_left[:, nodes].astype(F32)
+        out[:, nodes] = (add_cores(mine, PAIR, got, b) + came).astype(BF16)
 
 
 def dense_body(bias, feats, upstream, w_self, w_neigh, *rest):
@@ -354,31 +354,22 @@
     )
 
 
-def finish_body(own_grad, *rest):
+def finish_body(own_grad, mine, got, *rest):
     out = rest[-1]
     for b in range(4):
         nodes = slice(b * TILE, (b + 1) * TILE)
-        total = own_grad[:, nodes]
+        total = own_grad[:, nodes] + add_cores(mine, OWN, got, b)
         for ref in rest[:-1]:
             total = total + ref[0:128, nodes].astype(F32)
         out[nodes] = total.T.astype(BF16)
 
 
-def weight_sum_body(own, left, right, pair, from_opposite, from_pair, out, parts):
-    col, _ = places()
-    y, x = col >> 3, (col >> 1) & 3
-    parts[y * 4 + x] = own[...]
-    parts[y * 4 + ((x + 3) & 3)] = read_extra(left, 128)
-    parts[y * 4 + ((x + 1) & 3)] = read_extra(right, 128)
-    parts[(1 - y) * 4 + x] = read_extra(pair, 128)
-    parts[y * 4 + ((x + 2) & 3)] = read_extra(from_opposite, 128)
-    parts[(1 - y) * 4 + ((x + 2) & 3)] = read_extra(from_opposite, 144)
-    parts[(1 - y) * 4 + ((x + 3) & 3)] = read_extra(from_pair, 128)
-    parts[(1 - y) * 4 + ((x + 1) & 3)] = read_extra(from_pair, 144)
-    total = parts[0]
-    for k in range(1, 8):
-        total = total + parts[k]
-    out[...] = total
+def weight_sum_body(own, left, right, opposite, out, parts):
+    x = (lax.axis_index("col") >> 1) & 3
+    parts[x] = own[...]
+    for k, ref in ((3, left), (1, right), (2, opposite)):
+        parts[(x + k) & 3] = read_extra(ref, 128)
+    out[...] = ((parts[0] + parts[1]) + parts[2]) + parts[3]
 
 
 def weight_join_body(scale, own, *rest):
@@ -460,13 +451,10 @@
     with jax.named_scope("sum_aggregates"):
         step, swap = (lambda v, d: hop_row(v, 0, d)), (lambda v: hop_row(v, 1, 0))
         own, left, right, pair, opposite, *far = partial
-        pair, opposite = call(
-            add_round_body,
-            [bf16, bf16],
-            [pair, opposite, *first_sums(far, step, swap)],
-            nbytes=4 << 20,
-        )
-        sums = second_sums(own, left, right, pair, opposite, step, swap)
+        from_right, from_left, from_pair = step(far[0], -1), step(far[1], 1), swap(far[2])
+        opposite = call(add_body, bf16, [opposite, from_pair], nbytes=1 << 20)
+        pair = call(add_body, bf16, [pair, from_right, from_left], nbytes=1 << 20)
+        sums = [own, step(left, -1), step(right, 1), step(opposite, 2), swap(pair)]
     with jax.named_scope("dense"):
         longer = VMEM((144, 1024), BF16)
         block = VMEM((64, 256), F32)
@@ -541,27 +529,24 @@
         f32, bf16 = VMEM((128, 1024), F32), VMEM((128, 1024), BF16)
         *far, quarter, sib_near = call(
             add_sib_far_body,
-            [longer, longer, longer, block, VMEM((5, 128, 1024), BF16)],
+            [bf16, bf16, VMEM((160, 1024), BF16), block, VMEM((5, 128, 1024), BF16)],
             [mine, sib, hop_col(sib_far, 0, 0, 1), quarter],
             nbytes=3 << 20,
         )
-        from_right, from_left, from_pair = first_sums(far, step, swap)
-        longest = VMEM((160, 1024), BF16)
-        near = call(
-            add_near_body,
-            [f32, bf16, bf16, longest, longest],
-            [mine, hop_col(sib_near, 0, 0, 1), from_right, from_left, from_pair, quarter],
-            nbytes=5 << 20,
-        )
-        sums = second_sums(*near, step, swap)
-        came = [from_left, from_right, from_pair]
+        from_right, from_left, from_pair = step(far[0], -1), step(far[1], 1), swap(far[2])
+        sib_near = hop_col(sib_near, 0, 0, 1)
+        left, right, opposite, quarter = call(
+            add_ring_body,
+            [longer, longer, longer, block],
+            [mine, sib_near, from_pair, quarter],
+            nbytes=2 << 20,
+        )
+        pair = call(add_pair_body, bf16, [mine, sib_near, from_right, from_left], nbytes=1 << 20)
+        ring = [step(right, 1), step(left, -1), step(opposite, 2)]
+        sums = [*ring, swap(pair)]
     with jax.named_scope("sum_weights"):
         quarter = call(
-            weight_sum_body,
-            block,
-            [quarter, *came, sums[3], sums[4]],
-            scratch=[VMEM((8, 64, 256), F32)],
-            nbytes=1 << 20,
+            weight_sum_body, block, [quarter, *ring], scratch=[VMEM((4, 64, 256), F32)]
         )
         shape = jax.ShapeDtypeStruct((128, 256), F32)
         grad_self, grad_neigh = call(
@@ -575,7 +560,7 @@
         grad_features = call(
             finish_body,
             jax.ShapeDtypeStruct((1024, 128), BF16),
-            [own_grad, *sums],
+            [own_grad, mine, sib_near, *sums],
             nbytes=4 << 20,
         )
     return hidden, grad_features, grad_self, grad_neigh

time: 119 us -> 125 us (1.050)
  waiting for transfers between devices: 48 us -> 57.9 us
  starting transfers between devices: 51.6 us -> 44 us
  Pallas kernels: 18 us -> 20.9 us
    ppermute x18, waiting for transfers between devices: 18.4 us -> 27.7 us  [hop_row(): return lax.ppermute(value, 'row', pairs)]
    ppermute x18, starting transfers between devices: 34.4 us -> 26.7 us  [hop_row(): return lax.ppermute(value, 'row', pairs)]
    pallas_call x17 -> x19, Pallas kernels: 11.5 us -> 14.4 us  [call(): pl.pallas_call(run, out_shape=outs, in_specs=[pl.BlockSpec(memory_space=p...]
  transfers between devices with their start and end apart: 36 -> 36, of which waited for: 16 -> 18; matrix products, arithmetic and copies ran while one was open for 0% -> 0% of each run, Pallas kernels for 10% -> 13%
where the time goes in v6:
time: 125 us
  waiting for transfers between devices  57.9 us (46%)
  starting transfers between devices  44 us (35%)
  Pallas kernels  20.9 us (17%)
  between operations  1.55 us (1%)
    ppermute x18, waiting for transfers between devices, hop_col(): return lax.ppermute(value, 'col', pairs)  30.2 us
    ppermute x18, waiting for transfers between devices, hop_row(): return lax.ppermute(value, 'row', pairs)  27.7 us
    ppermute x18, starting transfers between devices, hop_row(): return lax.ppermute(value, 'row', pairs)  26.7 us
    ppermute x18, starting transfers between devices, hop_col(): return lax.ppermute(value, 'col', pairs)  17.3 us
    pallas_call x19, Pallas kernels, call(): pl.pallas_call(run, out_shape=outs, in_specs=[pl.BlockSpec(memory_space=p...  14.4 us
    pallas_call x1, Pallas kernels, shards(): pl.pallas_call(plan_body, out_shape=[VMEM((128, TILE, TILE), BF16), pltpu...  6.48 us
  transfers between devices with their start and end apart: 36, of which 18 were waited for; matrix products, arithmetic and copies ran while one was open for 0% of the time, Pallas kernels for 13%

profile of v6, /device:TPU:0, one launch (start us, length us, event | category | flops | bytes accessed | tf_op | source)
XLA Modules:
  0.0 125.0 jit_solution(16643761214710231930)
XLA Ops:
  0.6 3.2 %collective-permute-start.3 = (bf16[1024,128]{1,0:T(8,128)(2,1)}, bf16[1024,128]{1,0:T(8,128)(2,1)S(1)}, u32[]{:S(2)}, u32[]{:S(2)}) collective-permute-start(bf16[1024,128]{1,0:T(8,128)(2,1)} %refs_1_.2), channel_id=1, source_target_pairs={{0,4},{1,5},{2,6},{3,7},{4,0},{5,1},{6,2},{7,3},{8,12},{9,13},{10,... | collective-permute-start | bytes 786440 | tf_op jit(solution)/shard_map/gather_features/ppermute | solution.py:31
  3.8 1.6 %collective-permute-start.2 = (bf16[1024,128]{1,0:T(8,128)(2,1)}, bf16[1024,128]{1,0:T(8,128)(2,1)S(1)}, u32[]{:S(2)}, u32[]{:S(2)}) collective-permute-start(bf16[1024,128]{1,0:T(8,128)(2,1)} %refs_1_.2), channel_id=1, source_target_pairs={{0,8},{1,9},{2,10},{3,11},{4,12},{5,13},{6,14},{7,15},{8,0},{9,1},... | collective-permute-start | bytes 786440 | tf_op jit(solution)/shard_map/gather_features/ppermute | solution.py:31
  8.8 6.5 %plan.1 = (bf16[128,256,256]{2,1,0:T(8,128)(2,1)S(1)}, s32[1152]{0:T(1024)S(4)}, s32[8]{0:T(128)S(4)}) custom-call(s32[2,128]{1,0:T(2,128)S(1)} %bitcast.7, s32[1]{0:T(128)} %bitcast.6.count, bf16[128,256,256]{2,1,0:T(8,128)(2,1)} %bitcast.9), custom_call_target="tpu_custom_call" | custom-call | bytes 16777216 | tf_op jit(solution)/shard_map/plan/pallas_call | solution.py:393
  16.5 1.7 %collective-permute-start.6 = (bf16[1024,128]{1,0:T(8,128)(2,1)S(1)}, bf16[1024,128]{1,0:T(8,128)(2,1)S(1)}, u32[]{:S(2)}, u32[]{:S(2)}) collective-permute-start(bf16[1024,128]{1,0:T(8,128)(2,1)S(1)} %collective-permute-done.3.refs_4_), channel_id=1, source_target_pairs={{0,8},{1,9},{2,10},{3,11},{4,12},{5,13},{6,14},{7,15},{8,0},{9,1},... | collective-permute-start | bytes 786440 | tf_op jit(solution)/shard_map/gather_features/ppermute | solution.py:31
  18.2 2.6 %collective-permute-start.5 = (bf16[1024,128]{1,0:T(8,128)(2,1)S(1)}, bf16[1024,128]{1,0:T(8,128)(2,1)S(1)}, u32[]{:S(2)}, u32[]{:S(2)}) collective-permute-start(bf16[1024,128]{1,0:T(8,128)(2,1)S(1)} %get-tuple-element.43), channel_id=1, source_target_pairs={{0,6},{1,7},{2,0},{3,1},{4,2},{5,3},{6,4},{7,5},{8,14},{9,15},{10,... | collective-permute-start | bytes 786440 | tf_op jit(solution)/shard_map/gather_features/ppermute | solution.py:31
  20.8 3.1 %forward_tiles.4.refs_3_.refs_4_ = f32[33,256,128]{2,1,0:T(8,128)S(1)} custom-call(s32[1152]{0:T(1024)S(4)} %get-tuple-element.40.refs_0_, s32[8]{0:T(128)S(4)} %get-tuple-element.41.refs_5_.refs_1_, bf16[128,256,256]{2,1,0:T(8,128)(2,1)S(1)} %get-tuple-element.42.refs_2_, bf16[20,256,128]{2,1,0:T(8,128)(2,1)S(1)} %get-tuple-element.44.refs_3_, ...), custom_call_target="tpu_custom_call" | custom-call | tf_op jit(solution)/shard_map/forward_tiles/pallas_call | solution.py:67
  25.2 1.4 %collective-permute-done.5.refs_1_ = bf16[1024,128]{1,0:T(8,128)(2,1)S(1)} collective-permute-done((bf16[1024,128]{1,0:T(8,128)(2,1)S(1)}, bf16[1024,128]{1,0:T(8,128)(2,1)S(1)}, u32[]{:S(2)}, u32[]{:S(2)}) %collective-permute-start.5) | collective-permute-done | bytes 262176 | tf_op jit(solution)/shard_map/gather_features/ppermute | solution.py:31
  26.7 3.4 %collective-permute-done.4.refs_0_ = bf16[1024,128]{1,0:T(8,128)(2,1)S(1)} collective-permute-done((bf16[1024,128]{1,0:T(8,128)(2,1)S(1)}, bf16[1024,128]{1,0:T(8,128)(2,1)S(1)}, u32[]{:S(2)}, u32[]{:S(2)}) %collective-permute-start.4) | collective-permute-done | bytes 262176 | tf_op jit(solution)/shard_map/gather_features/ppermute | solution.py:31
  31.0 1.5 %collective-permute-done.8.refs_3_ = bf16[12,256,128]{2,1,0:T(8,128)(2,1)S(1)} collective-permute-done((bf16[12,256,128]{2,1,0:T(8,128)(2,1)S(1)}, bf16[12,256,128]{2,1,0:T(8,128)(2,1)S(1)}, u32[]{:S(2)}, u32[]{:S(2)}) %collective-permute-start.8) | collective-permute-done | bytes 786464 | tf_op jit(solution)/shard_map/forward_tiles/ppermute | solution.py:31
  33.5 3.0 %collective-permute-start.11 = (bf16[1024,128]{1,0:T(8,128)(2,1)S(1)}, bf16[1024,128]{1,0:T(8,128)(2,1)S(1)}, u32[]{:S(2)}, u32[]{:S(2)}) collective-permute-start(bf16[1024,128]{1,0:T(8,128)(2,1)S(1)} %get-tuple-element.49), channel_id=1, source_target_pairs={{0,16},{16,0},{32,48},{48,32},{64,80},{80,64},{96,112},{112,96},{1... | collective-permute-start | bytes 786440 | tf_op jit(solution)/shard_map/sum_aggregates/ppermute | solution.py:39
  36.4 4.0 %collective-permute-start.13 = (bf16[1024,128]{1,0:T(8,128)(2,1)S(1)}, bf16[1024,128]{1,0:T(8,128)(2,1)S(1)}, u32[]{:S(2)}, u32[]{:S(2)}) collective-permute-start(bf16[1024,128]{1,0:T(8,128)(2,1)S(1)} %get-tuple-element.51), channel_id=1, source_target_pairs={{0,96},{16,112},{32,0},{48,16},{64,32},{80,48},{96,64},{112,80},{1... | collective-permute-start | bytes 786440 | tf_op jit(solution)/shard_map/sum_aggregates/ppermute | solution.py:39
  40.5 3.2 %collective-permute-start.9 = (bf16[1024,128]{1,0:T(8,128)(2,1)S(1)}, bf16[1024,128]{1,0:T(8,128)(2,1)S(1)}, u32[]{:S(2)}, u32[]{:S(2)}) collective-permute-start(bf16[1024,128]{1,0:T(8,128)(2,1)S(1)} %get-tuple-element.46), channel_id=1, source_target_pairs={{0,96},{16,112},{32,0},{48,16},{64,32},{80,48},{96,64},{112,80},{1... | collective-permute-start | bytes 786440 | tf_op jit(solution)/shard_map/sum_aggregates/ppermute | solution.py:39
  44.1 3.2 %collective-permute-start.12 = (bf16[1024,128]{1,0:T(8,128)(2,1)S(1)}, bf16[1024,128]{1,0:T(8,128)(2,1)S(1)}, u32[]{:S(2)}, u32[]{:S(2)}) collective-permute-start(bf16[1024,128]{1,0:T(8,128)(2,1)S(1)} %sum_aggregates.2), channel_id=1, source_target_pairs={{0,64},{16,80},{32,96},{48,112},{64,0},{80,16},{96,32},{112,48},{1... | collective-permute-start | bytes 786440 | tf_op jit(solution)/shard_map/sum_aggregates/ppermute | solution.py:39
  47.4 3.4 %collective-permute-done.14.refs_2_ = bf16[1024,128]{1,0:T(8,128)(2,1)S(1)} collective-permute-done((bf16[1024,128]{1,0:T(8,128)(2,1)S(1)}, bf16[1024,128]{1,0:T(8,128)(2,1)S(1)}, u32[]{:S(2)}, u32[]{:S(2)}) %collective-permute-start.14) | collective-permute-done | bytes 262176 | tf_op jit(solution)/shard_map/sum_aggregates/ppermute | solution.py:39
  50.9 1.5 %collective-permute-start.15 = (bf16[1024,128]{1,0:T(8,128)(2,1)S(1)}, bf16[1024,128]{1,0:T(8,128)(2,1)S(1)}, u32[]{:S(2)}, u32[]{:S(2)}) collective-permute-start(bf16[1024,128]{1,0:T(8,128)(2,1)S(1)} %sum_aggregates.3), channel_id=1, source_target_pairs={{0,16},{16,0},{32,48},{48,32},{64,80},{80,64},{96,112},{112,96},{1... | collective-permute-start | bytes 786440 | tf_op jit(solution)/shard_map/sum_aggregates/ppermute | solution.py:39
  52.4 5.6 %collective-permute-done.9.refs_6_ = bf16[1024,128]{1,0:T(8,128)(2,1)S(1)} collective-permute-done((bf16[1024,128]{1,0:T(8,128)(2,1)S(1)}, bf16[1024,128]{1,0:T(8,128)(2,1)S(1)}, u32[]{:S(2)}, u32[]{:S(2)}) %collective-permute-start.9) | collective-permute-done | bytes 262176 | tf_op jit(solution)/shard_map/sum_aggregates/ppermute | solution.py:39
  58.0 3.4 %collective-permute-done.10.refs_7_ = bf16[1024,128]{1,0:T(8,128)(2,1)S(1)} collective-permute-done((bf16[1024,128]{1,0:T(8,128)(2,1)S(1)}, bf16[1024,128]{1,0:T(8,128)(2,1)S(1)}, u32[]{:S(2)}, u32[]{:S(2)}) %collective-permute-start.10) | collective-permute-done | bytes 262176 | tf_op jit(solution)/shard_map/sum_aggregates/ppermute | solution.py:39
  61.5 2.3 %dense.1 = (bf16[1024,256]{1,0:T(8,128)(2,1)}, bf16[1024,256]{1,0:T(8,128)(2,1)S(1)}, bf16[128,1024]{1,0:T(8,128)(2,1)S(1)}, bf16[144,1024]{1,0:T(8,128)(2,1)S(1...) custom-call(f32[1,256]{1,0:T(1,128)S(1)} %bitcast.8, ...), custom_call_target="tpu_custom_call" | custom-call | flops 335544320 | bytes 6291456 | tf_op jit(solution)/shard_map/dense/pallas_call | solution.py:67
  65.5 2.7 %collective-permute-start.22 = (bf16[144,1024]{1,0:T(8,128)(2,1)S(1)}, bf16[144,1024]{1,0:T(8,128)(2,1)S(1)}, u32[]{:S(2)}, u32[]{:S(2)}) collective-permute-start(bf16[144,1024]{1,0:T(8,128)(2,1)S(1)} %get-tuple-element.58), channel_id=1, source_target_pairs={{0,96},{16,112},{32,0},{48,16},{64,32},{80,48},{96,64},{112,80},{1... | collective-permute-start | bytes 884744 | tf_op jit(solution)/shard_map/gather_dz/ppermute | solution.py:39
  68.2 7.1 %collective-permute-done.19.refs_7_.refs_1_ = bf16[144,1024]{1,0:T(8,128)(2,1)S(1)} collective-permute-done((bf16[144,1024]{1,0:T(8,128)(2,1)S(1)}, bf16[144,1024]{1,0:T(8,128)(2,1)S(1)}, u32[]{:S(2)}, u32[]{:S(2)}) %collective-permute-start.19) | collective-permute-done | bytes 294944 | tf_op jit(solution)/shard_map/gather_dz/ppermute | solution.py:39
  75.5 1.8 %collective-permute-start.17 = (bf16[128,1024]{1,0:T(8,128)(2,1)S(1)}, bf16[128,1024]{1,0:T(8,128)(2,1)S(1)}, u32[]{:S(2)}, u32[]{:S(2)}) collective-permute-start(bf16[128,1024]{1,0:T(8,128)(2,1)S(1)} %collective-permute-done.16.refs_6_), channel_id=1, source_target_pairs={{0,32},{16,48},{32,64},{48,80},{64,96},{80,112},{96,0},{112,16},{1... | collective-permute-start | bytes 786440 | tf_op jit(solution)/shard_map/gather_dz/ppermute | solution.py:39
  77.6 2.5 %collective-permute-done.21.refs_4_.refs_2_ = bf16[144,1024]{1,0:T(8,128)(2,1)S(1)} collective-permute-done((bf16[144,1024]{1,0:T(8,128)(2,1)S(1)}, bf16[144,1024]{1,0:T(8,128)(2,1)S(1)}, u32[]{:S(2)}, u32[]{:S(2)}) %collective-permute-start.21) | collective-permute-done | bytes 294944 | tf_op jit(solution)/shard_map/gather_dz/ppermute | solution.py:39
  81.2 2.6 %backward_tiles.3 = (f32[33,128,256]{2,1,0:T(8,128)S(1)}, f32[33,128,256]{2,1,0:T(8,128)S(1)}) custom-call(s32[1152]{0:T(1024)S(4)} %get-tuple-element.40.refs_0_, s32[8]{0:T(128)S(4)} %get-tuple-element.41.refs_5_.refs_1_, bf16[128,256,256]{2,1,0:T(8,128)(2,1)S(1)} %get-tuple-element.42.refs_2_, bf16[128,1024]{1,0:T(8,128)(2,1)S(1)} %get-tuple-element.55.refs_3_, ...), custom_call_target="tpu_custom_call" | custom-call | flops 1073741824 | bytes 8388608 | tf_op jit(solution)/shard_map/backward_tiles/pallas_call | solution.py:67
  83.9 2.0 %collective-permute-done.23.refs_7_ = bf16[32,1024]{1,0:T(8,128)(2,1)S(1)} collective-permute-done((bf16[32,1024]{1,0:T(8,128)(2,1)S(1)}, bf16[32,1024]{1,0:T(8,128)(2,1)S(1)}, u32[]{:S(2)}, u32[]{:S(2)}) %collective-permute-start.23) | collective-permute-done | bytes 65568 | tf_op jit(solution)/shard_map/gather_dz/ppermute | solution.py:39
  87.8 1.3 %collective-permute-done.24.refs_2_ = bf16[416,1024]{1,0:T(8,128)(2,1)S(1)} collective-permute-done((bf16[416,1024]{1,0:T(8,128)(2,1)S(1)}, bf16[416,1024]{1,0:T(8,128)(2,1)S(1)}, u32[]{:S(2)}, u32[]{:S(2)}) %collective-permute-start.24) | collective-permute-done | bytes 852000 | tf_op jit(solution)/shard_map/sum_grads/ppermute | solution.py:31
  89.7 2.0 %collective-permute-start.31 = (bf16[128,1024]{1,0:T(8,128)(2,1)S(1)}, bf16[128,1024]{1,0:T(8,128)(2,1)S(1)}, u32[]{:S(2)}, u32[]{:S(2)}) collective-permute-start(bf16[128,1024]{1,0:T(8,128)(2,1)S(1)} %get-tuple-element.72), channel_id=1, source_target_pairs={{0,2},{1,3},{2,4},{3,5},{4,6},{5,7},{6,0},{7,1},{8,10},{9,11},{10,... | collective-permute-start | bytes 786440 | tf_op jit(solution)/shard_map/sum_grads/ppermute | solution.py:31
  91.7 7.9 %collective-permute-done.26.refs_2_ = bf16[160,1024]{1,0:T(8,128)(2,1)S(1)} collective-permute-done((bf16[160,1024]{1,0:T(8,128)(2,1)S(1)}, bf16[160,1024]{1,0:T(8,128)(2,1)S(1)}, u32[]{:S(2)}, u32[]{:S(2)}) %collective-permute-start.26) | collective-permute-done | bytes 327712 | tf_op jit(solution)/shard_map/sum_grads/ppermute | solution.py:31
  99.9 3.2 %collective-permute-start.28 = (bf16[144,1024]{1,0:T(8,128)(2,1)S(1)}, bf16[144,1024]{1,0:T(8,128)(2,1)S(1)}, u32[]{:S(2)}, u32[]{:S(2)}) collective-permute-start(bf16[144,1024]{1,0:T(8,128)(2,1)S(1)} %get-tuple-element.69), channel_id=1, source_target_pairs={{0,6},{1,7},{2,0},{3,1},{4,2},{5,3},{6,4},{7,5},{8,14},{9,15},{10,... | collective-permute-start | bytes 884744 | tf_op jit(solution)/shard_map/sum_grads/ppermute | solution.py:31
  103.6 12.3 %collective-permute-done.27.refs_3_.refs_1_ = bf16[144,1024]{1,0:T(8,128)(2,1)S(1)} collective-permute-done((bf16[144,1024]{1,0:T(8,128)(2,1)S(1)}, bf16[144,1024]{1,0:T(8,128)(2,1)S(1)}, u32[]{:S(2)}, u32[]{:S(2)}) %collective-permute-start.27) | collective-permute-done | bytes 294944 | tf_op jit(solution)/shard_map/sum_grads/ppermute | solution.py:31
  116.5 3.5 %collective-permute-start.34 = (f32[64,256]{1,0:T(8,128)S(1)}, f32[64,256]{1,0:T(8,128)S(1)}, u32[]{:S(2)}, u32[]{:S(2)}) collective-permute-start(f32[64,256]{1,0:T(8,128)S(1)} %sum_weights.2.refs_0_), channel_id=1, source_target_pairs={{0,64},{16,80},{32,96},{48,112},{64,0},{80,16},{96,32},{112,48},{1... | collective-permute-start | bytes 196616 | tf_op jit(solution)/shard_map/sum_weights/ppermute | solution.py:39
  121.5 1.5 %collective-permute-done.34.refs_2_ = f32[64,256]{1,0:T(8,128)S(1)} collective-permute-done((f32[64,256]{1,0:T(8,128)S(1)}, f32[64,256]{1,0:T(8,128)S(1)}, u32[]{:S(2)}, u32[]{:S(2)}) %collective-permute-start.34) | collective-permute-done | bytes 65568 | tf_op jit(solution)/shard_map/sum_weights/ppermute | solution.py:39
  123.0 1.3 %collective-permute-done.33.refs_1_ = f32[64,256]{1,0:T(8,128)S(1)} collective-permute-done((f32[64,256]{1,0:T(8,128)S(1)}, f32[64,256]{1,0:T(8,128)S(1)}, u32[]{:S(2)}, u32[]{:S(2)}) %collective-permute-start.33) | collective-permute-done | bytes 65568 | tf_op jit(solution)/shard_map/sum_weights/ppermute | solution.py:39
  (72 shorter events, 17.1 us)
Async XLA Ops:
  0.6 14.6 %collective-permute-start.3 = (bf16[1024,128]{1,0:T(8,128)(2,1)}, bf16[1024,128]{1,0:T(8,128)(2,1)S(1)}, u32[]{:S(2)}, u32[]{:S(2)}) collective-permute-start(bf16[1024,128]{1,0:T(8,128)(2,1)} %refs_1_.2), channel_id=1, source_target_pairs={{0,4},{1,5},{2,6},{3,7},{4,0},{5,1},{6,2},{7,3},{8,12},{9,13},{10,... | collective-permute-start | bytes 786440 | tf_op jit(solution)/shard_map/gather_features/ppermute | solution.py:31
  3.8 11.4 %collective-permute-start.2 = (bf16[1024,128]{1,0:T(8,128)(2,1)}, bf16[1024,128]{1,0:T(8,128)(2,1)S(1)}, u32[]{:S(2)}, u32[]{:S(2)}) collective-permute-start(bf16[1024,128]{1,0:T(8,128)(2,1)} %refs_1_.2), channel_id=1, source_target_pairs={{0,8},{1,9},{2,10},{3,11},{4,12},{5,13},{6,14},{7,15},{8,0},{9,1},... | collective-permute-start | bytes 786440 | tf_op jit(solution)/shard_map/gather_features/ppermute | solution.py:31
  5.4 10.9 %collective-permute-start.1 = (bf16[1024,128]{1,0:T(8,128)(2,1)}, bf16[1024,128]{1,0:T(8,128)(2,1)S(1)}, u32[]{:S(2)}, u32[]{:S(2)}) collective-permute-start(bf16[1024,128]{1,0:T(8,128)(2,1)} %refs_1_.2), channel_id=1, source_target_pairs={{0,6},{1,7},{2,0},{3,1},{4,2},{5,3},{6,4},{7,5},{8,14},{9,15},{10,... | collective-permute-start | bytes 786440 | tf_op jit(solution)/shard_map/gather_features/ppermute | solution.py:31
  6.5 9.8 %collective-permute-start = (bf16[1024,128]{1,0:T(8,128)(2,1)}, bf16[1024,128]{1,0:T(8,128)(2,1)S(1)}, u32[]{:S(2)}, u32[]{:S(2)}) collective-permute-start(bf16[1024,128]{1,0:T(8,128)(2,1)} %refs_1_.2), channel_id=1, source_target_pairs={{0,2},{1,3},{2,4},{3,5},{4,6},{5,7},{6,0},{7,1},{8,10},{9,11},{10,... | collective-permute-start | bytes 786440 | tf_op jit(solution)/shard_map/gather_features/ppermute | solution.py:31
  16.5 8.7 %collective-permute-start.6 = (bf16[1024,128]{1,0:T(8,128)(2,1)S(1)}, bf16[1024,128]{1,0:T(8,128)(2,1)S(1)}, u32[]{:S(2)}, u32[]{:S(2)}) collective-permute-start(bf16[1024,128]{1,0:T(8,128)(2,1)S(1)} %collective-permute-done.3.refs_4_), channel_id=1, source_target_pairs={{0,8},{1,9},{2,10},{3,11},{4,12},{5,13},{6,14},{7,15},{8,0},{9,1},... | collective-permute-start | bytes 786440 | tf_op jit(solution)/shard_map/gather_features/ppermute | solution.py:31
  18.2 8.5 %collective-permute-start.5 = (bf16[1024,128]{1,0:T(8,128)(2,1)S(1)}, bf16[1024,128]{1,0:T(8,128)(2,1)S(1)}, u32[]{:S(2)}, u32[]{:S(2)}) collective-permute-start(bf16[1024,128]{1,0:T(8,128)(2,1)S(1)} %get-tuple-element.43), channel_id=1, source_target_pairs={{0,6},{1,7},{2,0},{3,1},{4,2},{5,3},{6,4},{7,5},{8,14},{9,15},{10,... | collective-permute-start | bytes 786440 | tf_op jit(solution)/shard_map/gather_features/ppermute | solution.py:31
  20.8 9.3 %collective-permute-start.4 = (bf16[1024,128]{1,0:T(8,128)(2,1)S(1)}, bf16[1024,128]{1,0:T(8,128)(2,1)S(1)}, u32[]{:S(2)}, u32[]{:S(2)}) collective-permute-start(bf16[1024,128]{1,0:T(8,128)(2,1)S(1)} %get-tuple-element.43), channel_id=1, source_target_pairs={{0,2},{1,3},{2,4},{3,5},{4,6},{5,7},{6,0},{7,1},{8,10},{9,11},{10,... | collective-permute-start | bytes 786440 | tf_op jit(solution)/shard_map/gather_features/ppermute | solution.py:31
  33.5 10.6 %collective-permute-start.11 = (bf16[1024,128]{1,0:T(8,128)(2,1)S(1)}, bf16[1024,128]{1,0:T(8,128)(2,1)S(1)}, u32[]{:S(2)}, u32[]{:S(2)}) collective-permute-start(bf16[1024,128]{1,0:T(8,128)(2,1)S(1)} %get-tuple-element.49), channel_id=1, source_target_pairs={{0,16},{16,0},{32,48},{48,32},{64,80},{80,64},{96,112},{112,96},{1... | collective-permute-start | bytes 786440 | tf_op jit(solution)/shard_map/sum_aggregates/ppermute | solution.py:39
  36.4 11.0 %collective-permute-start.13 = (bf16[1024,128]{1,0:T(8,128)(2,1)S(1)}, bf16[1024,128]{1,0:T(8,128)(2,1)S(1)}, u32[]{:S(2)}, u32[]{:S(2)}) collective-permute-start(bf16[1024,128]{1,0:T(8,128)(2,1)S(1)} %get-tuple-element.51), channel_id=1, source_target_pairs={{0,96},{16,112},{32,0},{48,16},{64,32},{80,48},{96,64},{112,80},{1... | collective-permute-start | bytes 786440 | tf_op jit(solution)/shard_map/sum_aggregates/ppermute | solution.py:39
  40.5 10.3 %collective-permute-start.14 = (bf16[1024,128]{1,0:T(8,128)(2,1)S(1)}, bf16[1024,128]{1,0:T(8,128)(2,1)S(1)}, u32[]{:S(2)}, u32[]{:S(2)}) collective-permute-start(bf16[1024,128]{1,0:T(8,128)(2,1)S(1)} %get-tuple-element.52), channel_id=1, source_target_pairs={{0,32},{16,48},{32,64},{48,80},{64,96},{80,112},{96,0},{112,16},{1... | collective-permute-start | bytes 786440 | tf_op jit(solution)/shard_map/sum_aggregates/ppermute | solution.py:39
  40.5 17.5 %collective-permute-start.9 = (bf16[1024,128]{1,0:T(8,128)(2,1)S(1)}, bf16[1024,128]{1,0:T(8,128)(2,1)S(1)}, u32[]{:S(2)}, u32[]{:S(2)}) collective-permute-start(bf16[1024,128]{1,0:T(8,128)(2,1)S(1)} %get-tuple-element.46), channel_id=1, source_target_pairs={{0,96},{16,112},{32,0},{48,16},{64,32},{80,48},{96,64},{112,80},{1... | collective-permute-start | bytes 786440 | tf_op jit(solution)/shard_map/sum_aggregates/ppermute | solution.py:39
  43.7 17.7 %collective-permute-start.10 = (bf16[1024,128]{1,0:T(8,128)(2,1)S(1)}, bf16[1024,128]{1,0:T(8,128)(2,1)S(1)}, u32[]{:S(2)}, u32[]{:S(2)}) collective-permute-start(bf16[1024,128]{1,0:T(8,128)(2,1)S(1)} %get-tuple-element.47), channel_id=1, source_target_pairs={{0,32},{16,48},{32,64},{48,80},{64,96},{80,112},{96,0},{112,16},{1... | collective-permute-start | bytes 786440 | tf_op jit(solution)/shard_map/sum_aggregates/ppermute | solution.py:39
  44.1 17.3 %collective-permute-start.12 = (bf16[1024,128]{1,0:T(8,128)(2,1)S(1)}, bf16[1024,128]{1,0:T(8,128)(2,1)S(1)}, u32[]{:S(2)}, u32[]{:S(2)}) collective-permute-start(bf16[1024,128]{1,0:T(8,128)(2,1)S(1)} %sum_aggregates.2), channel_id=1, source_target_pairs={{0,64},{16,80},{32,96},{48,112},{64,0},{80,16},{96,32},{112,48},{1... | collective-permute-start | bytes 786440 | tf_op jit(solution)/shard_map/sum_aggregates/ppermute | solution.py:39
  50.9 10.5 %collective-permute-start.15 = (bf16[1024,128]{1,0:T(8,128)(2,1)S(1)}, bf16[1024,128]{1,0:T(8,128)(2,1)S(1)}, u32[]{:S(2)}, u32[]{:S(2)}) collective-permute-start(bf16[1024,128]{1,0:T(8,128)(2,1)S(1)} %sum_aggregates.3), channel_id=1, source_target_pairs={{0,16},{16,0},{32,48},{48,32},{64,80},{80,64},{96,112},{112,96},{1... | collective-permute-start | bytes 786440 | tf_op jit(solution)/shard_map/sum_aggregates/ppermute | solution.py:39
  63.7 11.5 %collective-permute-start.19 = (bf16[144,1024]{1,0:T(8,128)(2,1)S(1)}, bf16[144,1024]{1,0:T(8,128)(2,1)S(1)}, u32[]{:S(2)}, u32[]{:S(2)}) collective-permute-start(bf16[144,1024]{1,0:T(8,128)(2,1)S(1)} %get-tuple-element.56), channel_id=1, source_target_pairs={{0,64},{16,80},{32,96},{48,112},{64,0},{80,16},{96,32},{112,48},{1... | collective-permute-start | bytes 884744 | tf_op jit(solution)/shard_map/gather_dz/ppermute | solution.py:39
  64.3 10.9 %collective-permute-start.16 = (bf16[128,1024]{1,0:T(8,128)(2,1)S(1)}, bf16[128,1024]{1,0:T(8,128)(2,1)S(1)}, u32[]{:S(2)}, u32[]{:S(2)}) collective-permute-start(bf16[128,1024]{1,0:T(8,128)(2,1)S(1)} %get-tuple-element.55.refs_3_), channel_id=1, source_target_pairs={{0,16},{16,0},{32,48},{48,32},{64,80},{80,64},{96,112},{112,96},{1... | collective-permute-start | bytes 786440 | tf_op jit(solution)/shard_map/gather_dz/ppermute | solution.py:39
  64.9 15.1 %collective-permute-start.21 = (bf16[144,1024]{1,0:T(8,128)(2,1)S(1)}, bf16[144,1024]{1,0:T(8,128)(2,1)S(1)}, u32[]{:S(2)}, u32[]{:S(2)}) collective-permute-start(bf16[144,1024]{1,0:T(8,128)(2,1)S(1)} %get-tuple-element.57), channel_id=1, source_target_pairs={{0,32},{16,48},{32,64},{48,80},{64,96},{80,112},{96,0},{112,16},{1... | collective-permute-start | bytes 884744 | tf_op jit(solution)/shard_map/gather_dz/ppermute | solution.py:39
  65.5 14.5 %collective-permute-start.22 = (bf16[144,1024]{1,0:T(8,128)(2,1)S(1)}, bf16[144,1024]{1,0:T(8,128)(2,1)S(1)}, u32[]{:S(2)}, u32[]{:S(2)}) collective-permute-start(bf16[144,1024]{1,0:T(8,128)(2,1)S(1)} %get-tuple-element.58), channel_id=1, source_target_pairs={{0,96},{16,112},{32,0},{48,16},{64,32},{80,48},{96,64},{112,80},{1... | collective-permute-start | bytes 884744 | tf_op jit(solution)/shard_map/gather_dz/ppermute | solution.py:39
  75.2 10.7 %collective-permute-start.20 = (bf16[144,1024]{1,0:T(8,128)(2,1)S(1)}, bf16[144,1024]{1,0:T(8,128)(2,1)S(1)}, u32[]{:S(2)}, u32[]{:S(2)}) collective-permute-start(bf16[144,1024]{1,0:T(8,128)(2,1)S(1)} %collective-permute-done.19.refs_7_.refs_1_), channel_id=1, source_target_pairs={{0,16},{16,0},{32,48},{48,32},{64,80},{80,64},{96,112},{112,96},{1... | collective-permute-start | bytes 884744 | tf_op jit(solution)/shard_map/gather_dz/ppermute | solution.py:39
  75.2 10.7 %collective-permute-start.18 = (bf16[128,1024]{1,0:T(8,128)(2,1)S(1)}, bf16[128,1024]{1,0:T(8,128)(2,1)S(1)}, u32[]{:S(2)}, u32[]{:S(2)}) collective-permute-start(bf16[128,1024]{1,0:T(8,128)(2,1)S(1)} %collective-permute-done.16.refs_6_), channel_id=1, source_target_pairs={{0,96},{16,112},{32,0},{48,16},{64,32},{80,48},{96,64},{112,80},{1... | collective-permute-start | bytes 786440 | tf_op jit(solution)/shard_map/gather_dz/ppermute | solution.py:39
  75.5 10.4 %collective-permute-start.17 = (bf16[128,1024]{1,0:T(8,128)(2,1)S(1)}, bf16[128,1024]{1,0:T(8,128)(2,1)S(1)}, u32[]{:S(2)}, u32[]{:S(2)}) collective-permute-start(bf16[128,1024]{1,0:T(8,128)(2,1)S(1)} %collective-permute-done.16.refs_6_), channel_id=1, source_target_pairs={{0,32},{16,48},{32,64},{48,80},{64,96},{80,112},{96,0},{112,16},{1... | collective-permute-start | bytes 786440 | tf_op jit(solution)/shard_map/gather_dz/ppermute | solution.py:39
  80.1 5.8 %collective-permute-start.23 = (bf16[32,1024]{1,0:T(8,128)(2,1)S(1)}, bf16[32,1024]{1,0:T(8,128)(2,1)S(1)}, u32[]{:S(2)}, u32[]{:S(2)}) collective-permute-start(bf16[32,1024]{1,0:T(8,128)(2,1)S(1)} %gather_dz.1.refs_6_), channel_id=1, source_target_pairs={{0,16},{16,0},{32,48},{48,32},{64,80},{80,64},{96,112},{112,96},{1... | collective-permute-start | bytes 196616 | tf_op jit(solution)/shard_map/gather_dz/ppermute | solution.py:39
  89.4 10.2 %collective-permute-start.25 = (bf16[5,128,1024]{2,1,0:T(8,128)(2,1)S(1)}, bf16[5,128,1024]{2,1,0:T(8,128)(2,1)S(1)}, u32[]{:S(2)}, u32[]{:S(2)}) collective-permute-start(bf16[5,128,1024]{2,1,0:T(8,128)(2,1)S(1)} %get-tuple-element.65), channel_id=1, source_target_pairs={{0,1},{1,0},{2,3},{3,2},{4,5},{5,4},{6,7},{7,6},{8,9},{9,8},{10,11... | collective-permute-start | bytes 3932168 | tf_op jit(solution)/shard_map/sum_grads/ppermute | solution.py:31
  89.6 10.0 %collective-permute-start.26 = (bf16[160,1024]{1,0:T(8,128)(2,1)S(1)}, bf16[160,1024]{1,0:T(8,128)(2,1)S(1)}, u32[]{:S(2)}, u32[]{:S(2)}) collective-permute-start(bf16[160,1024]{1,0:T(8,128)(2,1)S(1)} %get-tuple-element.66), channel_id=1, source_target_pairs={{0,8},{1,9},{2,10},{3,11},{4,12},{5,13},{6,14},{7,15},{8,0},{9,1},... | collective-permute-start | bytes 983048 | tf_op jit(solution)/shard_map/sum_grads/ppermute | solution.py:31
  89.6 13.5 %collective-permute-start.30 = (bf16[128,1024]{1,0:T(8,128)(2,1)S(1)}, bf16[128,1024]{1,0:T(8,128)(2,1)S(1)}, u32[]{:S(2)}, u32[]{:S(2)}) collective-permute-start(bf16[128,1024]{1,0:T(8,128)(2,1)S(1)} %get-tuple-element.71), channel_id=1, source_target_pairs={{0,6},{1,7},{2,0},{3,1},{4,2},{5,3},{6,4},{7,5},{8,14},{9,15},{10,... | collective-permute-start | bytes 786440 | tf_op jit(solution)/shard_map/sum_grads/ppermute | solution.py:31
  89.7 13.4 %collective-permute-start.31 = (bf16[128,1024]{1,0:T(8,128)(2,1)S(1)}, bf16[128,1024]{1,0:T(8,128)(2,1)S(1)}, u32[]{:S(2)}, u32[]{:S(2)}) collective-permute-start(bf16[128,1024]{1,0:T(8,128)(2,1)S(1)} %get-tuple-element.72), channel_id=1, source_target_pairs={{0,2},{1,3},{2,4},{3,5},{4,6},{5,7},{6,0},{7,1},{8,10},{9,11},{10,... | collective-permute-start | bytes 786440 | tf_op jit(solution)/shard_map/sum_grads/ppermute | solution.py:31
  99.8 16.1 %collective-permute-start.27 = (bf16[144,1024]{1,0:T(8,128)(2,1)S(1)}, bf16[144,1024]{1,0:T(8,128)(2,1)S(1)}, u32[]{:S(2)}, u32[]{:S(2)}) collective-permute-start(bf16[144,1024]{1,0:T(8,128)(2,1)S(1)} %get-tuple-element.68), channel_id=1, source_target_pairs={{0,2},{1,3},{2,4},{3,5},{4,6},{5,7},{6,0},{7,1},{8,10},{9,11},{10,... | collective-permute-start | bytes 884744 | tf_op jit(solution)/shard_map/sum_grads/ppermute | solution.py:31
  99.9 16.0 %collective-permute-start.28 = (bf16[144,1024]{1,0:T(8,128)(2,1)S(1)}, bf16[144,1024]{1,0:T(8,128)(2,1)S(1)}, u32[]{:S(2)}, u32[]{:S(2)}) collective-permute-start(bf16[144,1024]{1,0:T(8,128)(2,1)S(1)} %get-tuple-element.69), channel_id=1, source_target_pairs={{0,6},{1,7},{2,0},{3,1},{4,2},{5,3},{6,4},{7,5},{8,14},{9,15},{10,... | collective-permute-start | bytes 884744 | tf_op jit(solution)/shard_map/sum_grads/ppermute | solution.py:31
  103.1 12.8 %collective-permute-start.29 = (bf16[144,1024]{1,0:T(8,128)(2,1)S(1)}, bf16[144,1024]{1,0:T(8,128)(2,1)S(1)}, u32[]{:S(2)}, u32[]{:S(2)}) collective-permute-start(bf16[144,1024]{1,0:T(8,128)(2,1)S(1)} %get-tuple-element.70), channel_id=1, source_target_pairs={{0,4},{1,5},{2,6},{3,7},{4,0},{5,1},{6,2},{7,3},{8,12},{9,13},{10,... | collective-permute-start | bytes 884744 | tf_op jit(solution)/shard_map/sum_grads/ppermute | solution.py:31
  103.3 16.8 %collective-permute-start.32 = (bf16[128,1024]{1,0:T(8,128)(2,1)S(1)}, bf16[128,1024]{1,0:T(8,128)(2,1)S(1)}, u32[]{:S(2)}, u32[]{:S(2)}) collective-permute-start(bf16[128,1024]{1,0:T(8,128)(2,1)S(1)} %sum_grads.5), channel_id=1, source_target_pairs={{0,8},{1,9},{2,10},{3,11},{4,12},{5,13},{6,14},{7,15},{8,0},{9,1},... | collective-permute-start | bytes 786440 | tf_op jit(solution)/shard_map/sum_grads/ppermute | solution.py:31
  115.9 5.5 %collective-permute-start.35 = (f32[64,256]{1,0:T(8,128)S(1)}, f32[64,256]{1,0:T(8,128)S(1)}, u32[]{:S(2)}, u32[]{:S(2)}) collective-permute-start(f32[64,256]{1,0:T(8,128)S(1)} %sum_weights.2.refs_0_), channel_id=1, source_target_pairs={{0,32},{16,48},{32,64},{48,80},{64,96},{80,112},{96,0},{112,16},{1... | collective-permute-start | bytes 196616 | tf_op jit(solution)/shard_map/sum_weights/ppermute | solution.py:39
  116.5 6.4 %collective-permute-start.34 = (f32[64,256]{1,0:T(8,128)S(1)}, f32[64,256]{1,0:T(8,128)S(1)}, u32[]{:S(2)}, u32[]{:S(2)}) collective-permute-start(f32[64,256]{1,0:T(8,128)S(1)} %sum_weights.2.refs_0_), channel_id=1, source_target_pairs={{0,64},{16,80},{32,96},{48,112},{64,0},{80,16},{96,32},{112,48},{1... | collective-permute-start | bytes 196616 | tf_op jit(solution)/shard_map/sum_weights/ppermute | solution.py:39
  (10 other events, 143.5 us)

commit v7 on v5

--- a/solution.py
+++ b/solution.py
@@ -270,8 +270,8 @@
             nodes = slice(b * TILE, (b + 1) * TILE)
             new = mine[4 * (PAIR_LEFT + k) + b] + got[128 * k : 128 * k + 128, nodes].astype(F32)
             ref[0:128, nodes] = new.astype(BF16)
-        write_extra(ref, 128, total)
-    write_extra(extra, 0, total)
+    for ref, row in ((outs[0], 128), (outs[1], 128), (extra, 0)):
+        write_extra(ref, row, total)
     write_places(sib, OWN, [near.at[k] for k in range(5)])
 
 
@@ -300,10 +300,13 @@
             ref[:, nodes] = new.astype(ref.dtype)
 
 
-def extras_body(from_right, from_left, from_opposite, pair):
-    pair[0:16] = from_left[128:144]
-    pair[16:32] = from_right[128:144]
-    pair[32:48] = from_opposite[...]
+def ring_x_body(quarter, from_right, from_left, from_opposite, out, parts):
+    x = (lax.axis_index("col") >> 1) & 3
+    parts[x] = quarter[...]
+    parts[(x + 3) & 3] = read_extra(from_left, 128)
+    parts[(x + 1) & 3] = read_extra(from_right, 128)
+    parts[(x + 2) & 3] = read_extra(from_opposite, 0)
+    write_fine(out, 0, ((parts[0] + parts[1]) + parts[2]) + parts[3])
 
 
 def first_sums(parts, step, swap):
@@ -374,22 +377,8 @@
         out[nodes] = total.T.astype(BF16)
 
 
-def weight_sum_body(own, left, right, pair, opposite, pair_ring, out, parts):
-    col, _ = places()
-    y, x = col >> 3, (col >> 1) & 3
-    ring, other = y * 4, (1 - y) * 4
-    parts[ring + x] = own[...]
-    parts[ring + ((x + 3) & 3)] = read_extra(left, 128)
-    parts[ring + ((x + 1) & 3)] = read_extra(right, 128)
-    parts[ring + ((x + 2) & 3)] = read_extra(opposite, 0)
-    parts[other + x] = read_extra(pair, 128)
-    parts[other + ((x + 3) & 3)] = read_extra(pair_ring, 0)
-    parts[other + ((x + 1) & 3)] = read_extra(pair_ring, 16)
-    parts[other + ((x + 2) & 3)] = read_extra(pair_ring, 32)
-    total = parts[0]
-    for k in range(1, 8):
-        total = total + parts[k]
-    out[...] = total
+def weight_sum_body(ring, pair, out):
+    out[...] = read_fine(ring, 0) + read_fine(pair, 0)
 
 
 def weight_join_body(scale, own, *rest):
@@ -552,7 +541,7 @@
         f32, bf16 = VMEM((128, 1024), F32), VMEM((128, 1024), BF16)
         *far, quarter, sib_near, extra = call(
             add_sib_far_body,
-            [longer, longer, longer, block, VMEM((5, 128, 1024), BF16), VMEM((16, 1024), BF16)],
+            [longer, longer, bf16, block, VMEM((5, 128, 1024), BF16), VMEM((16, 1024), BF16)],
             [mine, sib, hop_col(sib_far, 0, 0, 1), quarter],
             nbytes=3 << 20,
         )
@@ -560,25 +549,23 @@
         sib_near = hop_col(sib_near, 0, 0, 1)
         left, right = call(add_sides_body, [bf16, bf16], [mine, sib_near], nbytes=2 << 20)
         left, right = step(left, -1), step(right, 1)
-        from_opposite = step(extra, 2)
-        extras = call(extras_body, VMEM((48, 1024), BF16), [from_right, from_left, from_opposite])
-        came = [from_left, from_right, from_pair, from_opposite, swap(extras)]
+        ring = call(
+            ring_x_body,
+            VMEM((32, 1024), BF16),
+            [quarter, from_right, from_left, step(extra, 2)],
+            scratch=[VMEM((4, 64, 256), F32)],
+        )
+        pair_ring = swap(ring)
         own, pair, opposite = call(
             add_near_body,
             [f32, bf16, bf16],
             [mine, sib_near, from_right, from_left, from_pair],
-            after=[came[4], left, right],
+            after=[pair_ring],
             nbytes=5 << 20,
         )
         sums = [own, left, right, step(opposite, 2), swap(pair)]
     with jax.named_scope("sum_weights"):
-        quarter = call(
-            weight_sum_body,
-            block,
-            [quarter, *came],
-            scratch=[VMEM((8, 64, 256), F32)],
-            nbytes=1 << 20,
-        )
+        quarter = call(weight_sum_body, block, [ring, pair_ring], after=[left, right])
         shape = jax.ShapeDtypeStruct((128, 256), F32)
         grad_self, grad_neigh = call(
             functools.partial(weight_join_body, float(nodes) ** -0.5),

time: 119 us -> 124 us (1.042)
  waiting for transfers between devices: 34.7 us -> 46.4 us
  starting transfers between devices: 57.4 us -> 51.2 us
    ppermute x20, waiting for transfers between devices: 18.6 us -> 28.8 us  [hop_col(): return lax.ppermute(value, 'col', pairs)]
    ppermute x20, starting transfers between devices: 22.5 us -> 17.9 us  [hop_col(): return lax.ppermute(value, 'col', pairs)]
    ppermute x18, starting transfers between devices: 34.9 us -> 33.3 us  [hop_row(): return lax.ppermute(value, 'row', pairs)]
    ppermute x18, waiting for transfers between devices: 16 us -> 17.6 us  [hop_row(): return lax.ppermute(value, 'row', pairs)]
  transfers between devices with their start and end apart: 38 -> 38, of which waited for: 16 -> 18; matrix products, arithmetic and copies ran while one was open for 0% -> 0% of each run, Pallas kernels for 15% -> 14%
where the time goes in v7:
time: 124 us
  starting transfers between devices  51.2 us (41%)
  waiting for transfers between devices  46.4 us (37%)
  Pallas kernels  24 us (19%)
  between operations  1.55 us (1%)
    ppermute x18, starting transfers between devices, hop_row(): return lax.ppermute(value, 'row', pairs)  33.3 us
    ppermute x20, waiting for transfers between devices, hop_col(): return lax.ppermute(value, 'col', pairs)  28.8 us
    ppermute x20, starting transfers between devices, hop_col(): return lax.ppermute(value, 'col', pairs)  17.9 us
    ppermute x18, waiting for transfers between devices, hop_row(): return lax.ppermute(value, 'row', pairs)  17.6 us
    pallas_call x19, Pallas kernels, call(): pl.pallas_call(run, out_shape=outs, in_specs=[pl.BlockSpec(memory_space=p...  17.5 us
    pallas_call x1, Pallas kernels, shards(): pl.pallas_call(plan_body, out_shape=[VMEM((128, TILE, TILE), BF16), pltpu...  6.48 us
  transfers between devices with their start and end apart: 38, of which 18 were waited for; matrix products, arithmetic and copies ran while one was open for 0% of the time, Pallas kernels for 14%

profile of v7, /device:TPU:0, one launch (start us, length us, event | category | flops | bytes accessed | tf_op | source)
XLA Modules:
  0.0 123.9 jit_solution(2062199661795628694)
XLA Ops:
  0.6 3.2 %collective-permute-start.3 = (bf16[1024,128]{1,0:T(8,128)(2,1)}, bf16[1024,128]{1,0:T(8,128)(2,1)S(1)}, u32[]{:S(2)}, u32[]{:S(2)}) collective-permute-start(bf16[1024,128]{1,0:T(8,128)(2,1)} %refs_1_.2), channel_id=1, source_target_pairs={{0,4},{1,5},{2,6},{3,7},{4,0},{5,1},{6,2},{7,3},{8,12},{9,13},{10,... | collective-permute-start | bytes 786440 | tf_op jit(solution)/shard_map/gather_features/ppermute | solution.py:31
  3.8 1.6 %collective-permute-start.2 = (bf16[1024,128]{1,0:T(8,128)(2,1)}, bf16[1024,128]{1,0:T(8,128)(2,1)S(1)}, u32[]{:S(2)}, u32[]{:S(2)}) collective-permute-start(bf16[1024,128]{1,0:T(8,128)(2,1)} %refs_1_.2), channel_id=1, source_target_pairs={{0,8},{1,9},{2,10},{3,11},{4,12},{5,13},{6,14},{7,15},{8,0},{9,1},... | collective-permute-start | bytes 786440 | tf_op jit(solution)/shard_map/gather_features/ppermute | solution.py:31
  8.8 6.5 %plan.1 = (bf16[128,256,256]{2,1,0:T(8,128)(2,1)S(1)}, s32[1152]{0:T(1024)S(4)}, s32[8]{0:T(128)S(4)}) custom-call(s32[2,128]{1,0:T(2,128)S(1)} %bitcast.7, s32[1]{0:T(128)} %bitcast.6.count, bf16[128,256,256]{2,1,0:T(8,128)(2,1)} %bitcast.9), custom_call_target="tpu_custom_call" | custom-call | bytes 16777216 | tf_op jit(solution)/shard_map/plan/pallas_call | solution.py:402
  16.5 1.7 %collective-permute-start.6 = (bf16[1024,128]{1,0:T(8,128)(2,1)S(1)}, bf16[1024,128]{1,0:T(8,128)(2,1)S(1)}, u32[]{:S(2)}, u32[]{:S(2)}) collective-permute-start(bf16[1024,128]{1,0:T(8,128)(2,1)S(1)} %collective-permute-done.3.refs_4_), channel_id=1, source_target_pairs={{0,8},{1,9},{2,10},{3,11},{4,12},{5,13},{6,14},{7,15},{8,0},{9,1},... | collective-permute-start | bytes 786440 | tf_op jit(solution)/shard_map/gather_features/ppermute | solution.py:31
  18.2 2.6 %collective-permute-start.5 = (bf16[1024,128]{1,0:T(8,128)(2,1)S(1)}, bf16[1024,128]{1,0:T(8,128)(2,1)S(1)}, u32[]{:S(2)}, u32[]{:S(2)}) collective-permute-start(bf16[1024,128]{1,0:T(8,128)(2,1)S(1)} %get-tuple-element.47), channel_id=1, source_target_pairs={{0,6},{1,7},{2,0},{3,1},{4,2},{5,3},{6,4},{7,5},{8,14},{9,15},{10,... | collective-permute-start | bytes 786440 | tf_op jit(solution)/shard_map/gather_features/ppermute | solution.py:31
  20.8 3.9 %forward_tiles.4.refs_3_.refs_4_ = f32[33,256,128]{2,1,0:T(8,128)S(1)} custom-call(s32[1152]{0:T(1024)S(4)} %get-tuple-element.44.refs_0_, s32[8]{0:T(128)S(4)} %get-tuple-element.45.refs_5_.refs_1_, bf16[128,256,256]{2,1,0:T(8,128)(2,1)S(1)} %get-tuple-element.46.refs_2_, bf16[20,256,128]{2,1,0:T(8,128)(2,1)S(1)} %get-tuple-element.48.refs_3_, ...), custom_call_target="tpu_custom_call" | custom-call | tf_op jit(solution)/shard_map/forward_tiles/pallas_call | solution.py:67
  26.7 3.4 %collective-permute-done.4.refs_0_ = bf16[1024,128]{1,0:T(8,128)(2,1)S(1)} collective-permute-done((bf16[1024,128]{1,0:T(8,128)(2,1)S(1)}, bf16[1024,128]{1,0:T(8,128)(2,1)S(1)}, u32[]{:S(2)}, u32[]{:S(2)}) %collective-permute-start.4) | collective-permute-done | bytes 262176 | tf_op jit(solution)/shard_map/gather_features/ppermute | solution.py:31
  32.5 1.6 %forward_tiles.7 = (f32[33,256,128]{2,1,0:T(8,128)S(1)}, f32[1024,128]{1,0:T(8,128)S(1)}, bf16[1024,128]{1,0:T(8,128)(2,1)S(1)}, bf16[1024,128]{1,0:T(8,128)(2,1...) custom-call(s32[1152]{0:T(1024)S(4)} %get-tuple-element.44.refs_0_, ...), custom_call_target="tpu_custom_call", output_to_operand_aliasing={{0}: (4, {})} | custom-call | flops 536870912 | bytes 4194304 | tf_op jit(solution)/shard_map/forward_tiles/pallas_call | solution.py:67
  34.2 3.4 %collective-permute-start.11 = (bf16[1024,128]{1,0:T(8,128)(2,1)S(1)}, bf16[1024,128]{1,0:T(8,128)(2,1)S(1)}, u32[]{:S(2)}, u32[]{:S(2)}) collective-permute-start(bf16[1024,128]{1,0:T(8,128)(2,1)S(1)} %get-tuple-element.54), channel_id=1, source_target_pairs={{0,96},{16,112},{32,0},{48,16},{64,32},{80,48},{96,64},{112,80},{1... | collective-permute-start | bytes 786440 | tf_op jit(solution)/shard_map/sum_aggregates/ppermute | solution.py:39
  37.6 2.9 %collective-permute-start.13 = (bf16[1024,128]{1,0:T(8,128)(2,1)S(1)}, bf16[1024,128]{1,0:T(8,128)(2,1)S(1)}, u32[]{:S(2)}, u32[]{:S(2)}) collective-permute-start(bf16[1024,128]{1,0:T(8,128)(2,1)S(1)} %get-tuple-element.56), channel_id=1, source_target_pairs={{0,16},{16,0},{32,48},{48,32},{64,80},{80,64},{96,112},{112,96},{1... | collective-permute-start | bytes 786440 | tf_op jit(solution)/shard_map/sum_aggregates/ppermute | solution.py:39
  40.5 3.2 %collective-permute-start.9 = (bf16[1024,128]{1,0:T(8,128)(2,1)S(1)}, bf16[1024,128]{1,0:T(8,128)(2,1)S(1)}, u32[]{:S(2)}, u32[]{:S(2)}) collective-permute-start(bf16[1024,128]{1,0:T(8,128)(2,1)S(1)} %get-tuple-element.50), channel_id=1, source_target_pairs={{0,96},{16,112},{32,0},{48,16},{64,32},{80,48},{96,64},{112,80},{1... | collective-permute-start | bytes 786440 | tf_op jit(solution)/shard_map/sum_aggregates/ppermute | solution.py:39
  44.3 3.6 %collective-permute-done.12.refs_3_ = bf16[1024,128]{1,0:T(8,128)(2,1)S(1)} collective-permute-done((bf16[1024,128]{1,0:T(8,128)(2,1)S(1)}, bf16[1024,128]{1,0:T(8,128)(2,1)S(1)}, u32[]{:S(2)}, u32[]{:S(2)}) %collective-permute-start.12) | collective-permute-done | bytes 262176 | tf_op jit(solution)/shard_map/sum_aggregates/ppermute | solution.py:39
  48.0 1.6 %collective-permute-start.14 = (bf16[1024,128]{1,0:T(8,128)(2,1)S(1)}, bf16[1024,128]{1,0:T(8,128)(2,1)S(1)}, u32[]{:S(2)}, u32[]{:S(2)}) collective-permute-start(bf16[1024,128]{1,0:T(8,128)(2,1)S(1)} %get-tuple-element.57), channel_id=1, source_target_pairs={{0,64},{16,80},{32,96},{48,112},{64,0},{80,16},{96,32},{112,48},{1... | collective-permute-start | bytes 786440 | tf_op jit(solution)/shard_map/sum_aggregates/ppermute | solution.py:39
  49.6 2.2 %collective-permute-start.15 = (bf16[1024,128]{1,0:T(8,128)(2,1)S(1)}, bf16[1024,128]{1,0:T(8,128)(2,1)S(1)}, u32[]{:S(2)}, u32[]{:S(2)}) collective-permute-start(bf16[1024,128]{1,0:T(8,128)(2,1)S(1)} %get-tuple-element.58), channel_id=1, source_target_pairs={{0,16},{16,0},{32,48},{48,32},{64,80},{80,64},{96,112},{112,96},{1... | collective-permute-start | bytes 786440 | tf_op jit(solution)/shard_map/sum_aggregates/ppermute | solution.py:39
  51.8 7.0 %collective-permute-done.10.refs_7_ = bf16[1024,128]{1,0:T(8,128)(2,1)S(1)} collective-permute-done((bf16[1024,128]{1,0:T(8,128)(2,1)S(1)}, bf16[1024,128]{1,0:T(8,128)(2,1)S(1)}, u32[]{:S(2)}, u32[]{:S(2)}) %collective-permute-start.10) | collective-permute-done | bytes 262176 | tf_op jit(solution)/shard_map/sum_aggregates/ppermute | solution.py:39
  58.8 2.3 %dense.1 = (bf16[1024,256]{1,0:T(8,128)(2,1)}, bf16[1024,256]{1,0:T(8,128)(2,1)S(1)}, bf16[128,1024]{1,0:T(8,128)(2,1)S(1)}, bf16[144,1024]{1,0:T(8,128)(2,1)S(1...) custom-call(f32[1,256]{1,0:T(1,128)S(1)} %bitcast.8, ...), custom_call_target="tpu_custom_call" | custom-call | flops 335544320 | bytes 6291456 | tf_op jit(solution)/shard_map/dense/pallas_call | solution.py:67
  61.1 2.0 %collective-permute-start.19 = (bf16[144,1024]{1,0:T(8,128)(2,1)S(1)}, bf16[144,1024]{1,0:T(8,128)(2,1)S(1)}, u32[]{:S(2)}, u32[]{:S(2)}) collective-permute-start(bf16[144,1024]{1,0:T(8,128)(2,1)S(1)} %get-tuple-element.62), channel_id=1, source_target_pairs={{0,64},{16,80},{32,96},{48,112},{64,0},{80,16},{96,32},{112,48},{1... | collective-permute-start | bytes 884744 | tf_op jit(solution)/shard_map/gather_dz/ppermute | solution.py:39
  63.1 1.7 %collective-permute-start.16 = (bf16[128,1024]{1,0:T(8,128)(2,1)S(1)}, bf16[128,1024]{1,0:T(8,128)(2,1)S(1)}, u32[]{:S(2)}, u32[]{:S(2)}) collective-permute-start(bf16[128,1024]{1,0:T(8,128)(2,1)S(1)} %get-tuple-element.61.refs_3_), channel_id=1, source_target_pairs={{0,16},{16,0},{32,48},{48,32},{64,80},{80,64},{96,112},{112,96},{1... | collective-permute-start | bytes 786440 | tf_op jit(solution)/shard_map/gather_dz/ppermute | solution.py:39
  64.8 3.2 %collective-permute-start.22 = (bf16[144,1024]{1,0:T(8,128)(2,1)S(1)}, bf16[144,1024]{1,0:T(8,128)(2,1)S(1)}, u32[]{:S(2)}, u32[]{:S(2)}) collective-permute-start(bf16[144,1024]{1,0:T(8,128)(2,1)S(1)} %get-tuple-element.64), channel_id=1, source_target_pairs={{0,96},{16,112},{32,0},{48,16},{64,32},{80,48},{96,64},{112,80},{1... | collective-permute-start | bytes 884744 | tf_op jit(solution)/shard_map/gather_dz/ppermute | solution.py:39
  68.0 4.6 %collective-permute-done.19.refs_7_.refs_1_ = bf16[144,1024]{1,0:T(8,128)(2,1)S(1)} collective-permute-done((bf16[144,1024]{1,0:T(8,128)(2,1)S(1)}, bf16[144,1024]{1,0:T(8,128)(2,1)S(1)}, u32[]{:S(2)}, u32[]{:S(2)}) %collective-permute-start.19) | collective-permute-done | bytes 294944 | tf_op jit(solution)/shard_map/gather_dz/ppermute | solution.py:39
  72.6 2.2 %collective-permute-start.20 = (bf16[144,1024]{1,0:T(8,128)(2,1)S(1)}, bf16[144,1024]{1,0:T(8,128)(2,1)S(1)}, u32[]{:S(2)}, u32[]{:S(2)}) collective-permute-start(bf16[144,1024]{1,0:T(8,128)(2,1)S(1)} %collective-permute-done.19.refs_7_.refs_1_), channel_id=1, source_target_pairs={{0,16},{16,0},{32,48},{48,32},{64,80},{80,64},{96,112},{112,96},{1... | collective-permute-start | bytes 884744 | tf_op jit(solution)/shard_map/gather_dz/ppermute | solution.py:39
  74.8 2.0 %collective-permute-start.17 = (bf16[128,1024]{1,0:T(8,128)(2,1)S(1)}, bf16[128,1024]{1,0:T(8,128)(2,1)S(1)}, u32[]{:S(2)}, u32[]{:S(2)}) collective-permute-start(bf16[128,1024]{1,0:T(8,128)(2,1)S(1)} %collective-permute-done.16.refs_6_), channel_id=1, source_target_pairs={{0,32},{16,48},{32,64},{48,80},{64,96},{80,112},{96,0},{112,16},{1... | collective-permute-start | bytes 786440 | tf_op jit(solution)/shard_map/gather_dz/ppermute | solution.py:39
  77.5 2.1 %collective-permute-start.23 = (bf16[32,1024]{1,0:T(8,128)(2,1)S(1)}, bf16[32,1024]{1,0:T(8,128)(2,1)S(1)}, u32[]{:S(2)}, u32[]{:S(2)}) collective-permute-start(bf16[32,1024]{1,0:T(8,128)(2,1)S(1)} %gather_dz.1.refs_6_), channel_id=1, source_target_pairs={{0,16},{16,0},{32,48},{48,32},{64,80},{80,64},{96,112},{112,96},{1... | collective-permute-start | bytes 196616 | tf_op jit(solution)/shard_map/gather_dz/ppermute | solution.py:39
  79.6 3.1 %backward_tiles.3 = (f32[33,128,256]{2,1,0:T(8,128)S(1)}, f32[33,128,256]{2,1,0:T(8,128)S(1)}) custom-call(s32[1152]{0:T(1024)S(4)} %get-tuple-element.44.refs_0_, s32[8]{0:T(128)S(4)} %get-tuple-element.45.refs_5_.refs_1_, bf16[128,256,256]{2,1,0:T(8,128)(2,1)S(1)} %get-tuple-element.46.refs_2_, bf16[128,1024]{1,0:T(8,128)(2,1)S(1)} %get-tuple-element.61.refs_3_, ...), custom_call_target="tpu_custom_call" | custom-call | flops 1073741824 | bytes 8388608 | tf_op jit(solution)/shard_map/backward_tiles/pallas_call | solution.py:67
  87.7 1.8 %collective-permute-start.27 = (bf16[144,1024]{1,0:T(8,128)(2,1)S(1)}, bf16[144,1024]{1,0:T(8,128)(2,1)S(1)}, u32[]{:S(2)}, u32[]{:S(2)}) collective-permute-start(bf16[144,1024]{1,0:T(8,128)(2,1)S(1)} %get-tuple-element.73), channel_id=1, source_target_pairs={{0,2},{1,3},{2,4},{3,5},{4,6},{5,7},{6,0},{7,1},{8,10},{9,11},{10,... | collective-permute-start | bytes 884744 | tf_op jit(solution)/shard_map/sum_grads/ppermute | solution.py:31
  89.6 7.9 %collective-permute-done.29.refs_3_ = bf16[16,1024]{1,0:T(8,128)(2,1)S(1)} collective-permute-done((bf16[16,1024]{1,0:T(8,128)(2,1)S(1)}, bf16[16,1024]{1,0:T(8,128)(2,1)S(1)}, u32[]{:S(2)}, u32[]{:S(2)}) %collective-permute-start.29) | collective-permute-done | bytes 32800 | tf_op jit(solution)/shard_map/sum_grads/ppermute | solution.py:31
  101.1 2.0 %collective-permute-done.30.refs_5_.refs_1_ = bf16[32,1024]{1,0:T(8,128)(2,1)S(1)} collective-permute-done((bf16[32,1024]{1,0:T(8,128)(2,1)S(1)}, bf16[32,1024]{1,0:T(8,128)(2,1)S(1)}, u32[]{:S(2)}, u32[]{:S(2)}) %collective-permute-start.30) | collective-permute-done | bytes 65568 | tf_op jit(solution)/shard_map/sum_grads/ppermute | solution.py:31
  103.4 2.1 %collective-permute-start.33 = (bf16[128,1024]{1,0:T(8,128)(2,1)S(1)}, bf16[128,1024]{1,0:T(8,128)(2,1)S(1)}, u32[]{:S(2)}, u32[]{:S(2)}) collective-permute-start(bf16[128,1024]{1,0:T(8,128)(2,1)S(1)} %get-tuple-element.80), channel_id=1, source_target_pairs={{0,4},{1,5},{2,6},{3,7},{4,0},{5,1},{6,2},{7,3},{8,12},{9,13},{10,... | collective-permute-start | bytes 786440 | tf_op jit(solution)/shard_map/sum_grads/ppermute | solution.py:31
  105.5 2.8 %collective-permute-done.31.refs_2_ = bf16[128,1024]{1,0:T(8,128)(2,1)S(1)} collective-permute-done((bf16[128,1024]{1,0:T(8,128)(2,1)S(1)}, bf16[128,1024]{1,0:T(8,128)(2,1)S(1)}, u32[]{:S(2)}, u32[]{:S(2)}) %collective-permute-start.31) | collective-permute-done | bytes 262176 | tf_op jit(solution)/shard_map/sum_grads/ppermute | solution.py:31
  108.3 6.2 %collective-permute-done.32.refs_3_ = bf16[128,1024]{1,0:T(8,128)(2,1)S(1)} collective-permute-done((bf16[128,1024]{1,0:T(8,128)(2,1)S(1)}, bf16[128,1024]{1,0:T(8,128)(2,1)S(1)}, u32[]{:S(2)}, u32[]{:S(2)}) %collective-permute-start.32) | collective-permute-done | bytes 262176 | tf_op jit(solution)/shard_map/sum_grads/ppermute | solution.py:31
  116.1 2.6 %collective-permute-start.36 = (f32[64,256]{1,0:T(8,128)S(1)}, f32[64,256]{1,0:T(8,128)S(1)}, u32[]{:S(2)}, u32[]{:S(2)}) collective-permute-start(f32[64,256]{1,0:T(8,128)S(1)} %sum_weights.2.refs_0_), channel_id=1, source_target_pairs={{0,64},{16,80},{32,96},{48,112},{64,0},{80,16},{96,32},{112,48},{1... | collective-permute-start | bytes 196616 | tf_op jit(solution)/shard_map/sum_weights/ppermute | solution.py:39
  118.7 2.5 %collective-permute-start.35 = (f32[64,256]{1,0:T(8,128)S(1)}, f32[64,256]{1,0:T(8,128)S(1)}, u32[]{:S(2)}, u32[]{:S(2)}) collective-permute-start(f32[64,256]{1,0:T(8,128)S(1)} %sum_weights.2.refs_0_), channel_id=1, source_target_pairs={{0,96},{16,112},{32,0},{48,16},{64,32},{80,48},{96,64},{112,80},{1... | collective-permute-start | bytes 196616 | tf_op jit(solution)/shard_map/sum_weights/ppermute | solution.py:39
  (76 shorter events, 22.8 us)
Async XLA Ops:
  0.6 14.6 %collective-permute-start.3 = (bf16[1024,128]{1,0:T(8,128)(2,1)}, bf16[1024,128]{1,0:T(8,128)(2,1)S(1)}, u32[]{:S(2)}, u32[]{:S(2)}) collective-permute-start(bf16[1024,128]{1,0:T(8,128)(2,1)} %refs_1_.2), channel_id=1, source_target_pairs={{0,4},{1,5},{2,6},{3,7},{4,0},{5,1},{6,2},{7,3},{8,12},{9,13},{10,... | collective-permute-start | bytes 786440 | tf_op jit(solution)/shard_map/gather_features/ppermute | solution.py:31
  3.8 11.4 %collective-permute-start.2 = (bf16[1024,128]{1,0:T(8,128)(2,1)}, bf16[1024,128]{1,0:T(8,128)(2,1)S(1)}, u32[]{:S(2)}, u32[]{:S(2)}) collective-permute-start(bf16[1024,128]{1,0:T(8,128)(2,1)} %refs_1_.2), channel_id=1, source_target_pairs={{0,8},{1,9},{2,10},{3,11},{4,12},{5,13},{6,14},{7,15},{8,0},{9,1},... | collective-permute-start | bytes 786440 | tf_op jit(solution)/shard_map/gather_features/ppermute | solution.py:31
  5.4 10.9 %collective-permute-start.1 = (bf16[1024,128]{1,0:T(8,128)(2,1)}, bf16[1024,128]{1,0:T(8,128)(2,1)S(1)}, u32[]{:S(2)}, u32[]{:S(2)}) collective-permute-start(bf16[1024,128]{1,0:T(8,128)(2,1)} %refs_1_.2), channel_id=1, source_target_pairs={{0,6},{1,7},{2,0},{3,1},{4,2},{5,3},{6,4},{7,5},{8,14},{9,15},{10,... | collective-permute-start | bytes 786440 | tf_op jit(solution)/shard_map/gather_features/ppermute | solution.py:31
  6.5 9.8 %collective-permute-start = (bf16[1024,128]{1,0:T(8,128)(2,1)}, bf16[1024,128]{1,0:T(8,128)(2,1)S(1)}, u32[]{:S(2)}, u32[]{:S(2)}) collective-permute-start(bf16[1024,128]{1,0:T(8,128)(2,1)} %refs_1_.2), channel_id=1, source_target_pairs={{0,2},{1,3},{2,4},{3,5},{4,6},{5,7},{6,0},{7,1},{8,10},{9,11},{10,... | collective-permute-start | bytes 786440 | tf_op jit(solution)/shard_map/gather_features/ppermute | solution.py:31
  16.5 8.7 %collective-permute-start.6 = (bf16[1024,128]{1,0:T(8,128)(2,1)S(1)}, bf16[1024,128]{1,0:T(8,128)(2,1)S(1)}, u32[]{:S(2)}, u32[]{:S(2)}) collective-permute-start(bf16[1024,128]{1,0:T(8,128)(2,1)S(1)} %collective-permute-done.3.refs_4_), channel_id=1, source_target_pairs={{0,8},{1,9},{2,10},{3,11},{4,12},{5,13},{6,14},{7,15},{8,0},{9,1},... | collective-permute-start | bytes 786440 | tf_op jit(solution)/shard_map/gather_features/ppermute | solution.py:31
  18.2 8.5 %collective-permute-start.5 = (bf16[1024,128]{1,0:T(8,128)(2,1)S(1)}, bf16[1024,128]{1,0:T(8,128)(2,1)S(1)}, u32[]{:S(2)}, u32[]{:S(2)}) collective-permute-start(bf16[1024,128]{1,0:T(8,128)(2,1)S(1)} %get-tuple-element.47), channel_id=1, source_target_pairs={{0,6},{1,7},{2,0},{3,1},{4,2},{5,3},{6,4},{7,5},{8,14},{9,15},{10,... | collective-permute-start | bytes 786440 | tf_op jit(solution)/shard_map/gather_features/ppermute | solution.py:31
  20.8 9.3 %collective-permute-start.4 = (bf16[1024,128]{1,0:T(8,128)(2,1)S(1)}, bf16[1024,128]{1,0:T(8,128)(2,1)S(1)}, u32[]{:S(2)}, u32[]{:S(2)}) collective-permute-start(bf16[1024,128]{1,0:T(8,128)(2,1)S(1)} %get-tuple-element.47), channel_id=1, source_target_pairs={{0,2},{1,3},{2,4},{3,5},{4,6},{5,7},{6,0},{7,1},{8,10},{9,11},{10,... | collective-permute-start | bytes 786440 | tf_op jit(solution)/shard_map/gather_features/ppermute | solution.py:31
  34.2 10.1 %collective-permute-start.11 = (bf16[1024,128]{1,0:T(8,128)(2,1)S(1)}, bf16[1024,128]{1,0:T(8,128)(2,1)S(1)}, u32[]{:S(2)}, u32[]{:S(2)}) collective-permute-start(bf16[1024,128]{1,0:T(8,128)(2,1)S(1)} %get-tuple-element.54), channel_id=1, source_target_pairs={{0,96},{16,112},{32,0},{48,16},{64,32},{80,48},{96,64},{112,80},{1... | collective-permute-start | bytes 786440 | tf_op jit(solution)/shard_map/sum_aggregates/ppermute | solution.py:39
  37.6 10.3 %collective-permute-start.12 = (bf16[1024,128]{1,0:T(8,128)(2,1)S(1)}, bf16[1024,128]{1,0:T(8,128)(2,1)S(1)}, u32[]{:S(2)}, u32[]{:S(2)}) collective-permute-start(bf16[1024,128]{1,0:T(8,128)(2,1)S(1)} %get-tuple-element.55), channel_id=1, source_target_pairs={{0,32},{16,48},{32,64},{48,80},{64,96},{80,112},{96,0},{112,16},{1... | collective-permute-start | bytes 786440 | tf_op jit(solution)/shard_map/sum_aggregates/ppermute | solution.py:39
  37.6 10.3 %collective-permute-start.13 = (bf16[1024,128]{1,0:T(8,128)(2,1)S(1)}, bf16[1024,128]{1,0:T(8,128)(2,1)S(1)}, u32[]{:S(2)}, u32[]{:S(2)}) collective-permute-start(bf16[1024,128]{1,0:T(8,128)(2,1)S(1)} %get-tuple-element.56), channel_id=1, source_target_pairs={{0,16},{16,0},{32,48},{48,32},{64,80},{80,64},{96,112},{112,96},{1... | collective-permute-start | bytes 786440 | tf_op jit(solution)/shard_map/sum_aggregates/ppermute | solution.py:39
  40.5 11.4 %collective-permute-start.9 = (bf16[1024,128]{1,0:T(8,128)(2,1)S(1)}, bf16[1024,128]{1,0:T(8,128)(2,1)S(1)}, u32[]{:S(2)}, u32[]{:S(2)}) collective-permute-start(bf16[1024,128]{1,0:T(8,128)(2,1)S(1)} %get-tuple-element.50), channel_id=1, source_target_pairs={{0,96},{16,112},{32,0},{48,16},{64,32},{80,48},{96,64},{112,80},{1... | collective-permute-start | bytes 786440 | tf_op jit(solution)/shard_map/sum_aggregates/ppermute | solution.py:39
  43.7 15.1 %collective-permute-start.10 = (bf16[1024,128]{1,0:T(8,128)(2,1)S(1)}, bf16[1024,128]{1,0:T(8,128)(2,1)S(1)}, u32[]{:S(2)}, u32[]{:S(2)}) collective-permute-start(bf16[1024,128]{1,0:T(8,128)(2,1)S(1)} %get-tuple-element.51), channel_id=1, source_target_pairs={{0,32},{16,48},{32,64},{48,80},{64,96},{80,112},{96,0},{112,16},{1... | collective-permute-start | bytes 786440 | tf_op jit(solution)/shard_map/sum_aggregates/ppermute | solution.py:39
  48.0 10.8 %collective-permute-start.14 = (bf16[1024,128]{1,0:T(8,128)(2,1)S(1)}, bf16[1024,128]{1,0:T(8,128)(2,1)S(1)}, u32[]{:S(2)}, u32[]{:S(2)}) collective-permute-start(bf16[1024,128]{1,0:T(8,128)(2,1)S(1)} %get-tuple-element.57), channel_id=1, source_target_pairs={{0,64},{16,80},{32,96},{48,112},{64,0},{80,16},{96,32},{112,48},{1... | collective-permute-start | bytes 786440 | tf_op jit(solution)/shard_map/sum_aggregates/ppermute | solution.py:39
  49.6 9.2 %collective-permute-start.15 = (bf16[1024,128]{1,0:T(8,128)(2,1)S(1)}, bf16[1024,128]{1,0:T(8,128)(2,1)S(1)}, u32[]{:S(2)}, u32[]{:S(2)}) collective-permute-start(bf16[1024,128]{1,0:T(8,128)(2,1)S(1)} %get-tuple-element.58), channel_id=1, source_target_pairs={{0,16},{16,0},{32,48},{48,32},{64,80},{80,64},{96,112},{112,96},{1... | collective-permute-start | bytes 786440 | tf_op jit(solution)/shard_map/sum_aggregates/ppermute | solution.py:39
  61.1 11.5 %collective-permute-start.19 = (bf16[144,1024]{1,0:T(8,128)(2,1)S(1)}, bf16[144,1024]{1,0:T(8,128)(2,1)S(1)}, u32[]{:S(2)}, u32[]{:S(2)}) collective-permute-start(bf16[144,1024]{1,0:T(8,128)(2,1)S(1)} %get-tuple-element.62), channel_id=1, source_target_pairs={{0,64},{16,80},{32,96},{48,112},{64,0},{80,16},{96,32},{112,48},{1... | collective-permute-start | bytes 884744 | tf_op jit(solution)/shard_map/gather_dz/ppermute | solution.py:39
  63.1 11.7 %collective-permute-start.16 = (bf16[128,1024]{1,0:T(8,128)(2,1)S(1)}, bf16[128,1024]{1,0:T(8,128)(2,1)S(1)}, u32[]{:S(2)}, u32[]{:S(2)}) collective-permute-start(bf16[128,1024]{1,0:T(8,128)(2,1)S(1)} %get-tuple-element.61.refs_3_), channel_id=1, source_target_pairs={{0,16},{16,0},{32,48},{48,32},{64,80},{80,64},{96,112},{112,96},{1... | collective-permute-start | bytes 786440 | tf_op jit(solution)/shard_map/gather_dz/ppermute | solution.py:39
  64.8 12.7 %collective-permute-start.21 = (bf16[144,1024]{1,0:T(8,128)(2,1)S(1)}, bf16[144,1024]{1,0:T(8,128)(2,1)S(1)}, u32[]{:S(2)}, u32[]{:S(2)}) collective-permute-start(bf16[144,1024]{1,0:T(8,128)(2,1)S(1)} %get-tuple-element.63), channel_id=1, source_target_pairs={{0,32},{16,48},{32,64},{48,80},{64,96},{80,112},{96,0},{112,16},{1... | collective-permute-start | bytes 884744 | tf_op jit(solution)/shard_map/gather_dz/ppermute | solution.py:39
  64.8 12.6 %collective-permute-start.22 = (bf16[144,1024]{1,0:T(8,128)(2,1)S(1)}, bf16[144,1024]{1,0:T(8,128)(2,1)S(1)}, u32[]{:S(2)}, u32[]{:S(2)}) collective-permute-start(bf16[144,1024]{1,0:T(8,128)(2,1)S(1)} %get-tuple-element.64), channel_id=1, source_target_pairs={{0,96},{16,112},{32,0},{48,16},{64,32},{80,48},{96,64},{112,80},{1... | collective-permute-start | bytes 884744 | tf_op jit(solution)/shard_map/gather_dz/ppermute | solution.py:39
  72.6 10.7 %collective-permute-start.20 = (bf16[144,1024]{1,0:T(8,128)(2,1)S(1)}, bf16[144,1024]{1,0:T(8,128)(2,1)S(1)}, u32[]{:S(2)}, u32[]{:S(2)}) collective-permute-start(bf16[144,1024]{1,0:T(8,128)(2,1)S(1)} %collective-permute-done.19.refs_7_.refs_1_), channel_id=1, source_target_pairs={{0,16},{16,0},{32,48},{48,32},{64,80},{80,64},{96,112},{112,96},{1... | collective-permute-start | bytes 884744 | tf_op jit(solution)/shard_map/gather_dz/ppermute | solution.py:39
  74.8 8.5 %collective-permute-start.18 = (bf16[128,1024]{1,0:T(8,128)(2,1)S(1)}, bf16[128,1024]{1,0:T(8,128)(2,1)S(1)}, u32[]{:S(2)}, u32[]{:S(2)}) collective-permute-start(bf16[128,1024]{1,0:T(8,128)(2,1)S(1)} %collective-permute-done.16.refs_6_), channel_id=1, source_target_pairs={{0,96},{16,112},{32,0},{48,16},{64,32},{80,48},{96,64},{112,80},{1... | collective-permute-start | bytes 786440 | tf_op jit(solution)/shard_map/gather_dz/ppermute | solution.py:39
  74.8 8.5 %collective-permute-start.17 = (bf16[128,1024]{1,0:T(8,128)(2,1)S(1)}, bf16[128,1024]{1,0:T(8,128)(2,1)S(1)}, u32[]{:S(2)}, u32[]{:S(2)}) collective-permute-start(bf16[128,1024]{1,0:T(8,128)(2,1)S(1)} %collective-permute-done.16.refs_6_), channel_id=1, source_target_pairs={{0,32},{16,48},{32,64},{48,80},{64,96},{80,112},{96,0},{112,16},{1... | collective-permute-start | bytes 786440 | tf_op jit(solution)/shard_map/gather_dz/ppermute | solution.py:39
  87.3 11.6 %collective-permute-start.25 = (bf16[5,128,1024]{2,1,0:T(8,128)(2,1)S(1)}, bf16[5,128,1024]{2,1,0:T(8,128)(2,1)S(1)}, u32[]{:S(2)}, u32[]{:S(2)}) collective-permute-start(bf16[5,128,1024]{2,1,0:T(8,128)(2,1)S(1)} %get-tuple-element.71), channel_id=1, source_target_pairs={{0,1},{1,0},{2,3},{3,2},{4,5},{5,4},{6,7},{7,6},{8,9},{9,8},{10,11... | collective-permute-start | bytes 3932168 | tf_op jit(solution)/shard_map/sum_grads/ppermute | solution.py:31
  87.5 10.0 %collective-permute-start.26 = (bf16[144,1024]{1,0:T(8,128)(2,1)S(1)}, bf16[144,1024]{1,0:T(8,128)(2,1)S(1)}, u32[]{:S(2)}, u32[]{:S(2)}) collective-permute-start(bf16[144,1024]{1,0:T(8,128)(2,1)S(1)} %get-tuple-element.72), channel_id=1, source_target_pairs={{0,6},{1,7},{2,0},{3,1},{4,2},{5,3},{6,4},{7,5},{8,14},{9,15},{10,... | collective-permute-start | bytes 884744 | tf_op jit(solution)/shard_map/sum_grads/ppermute | solution.py:31
  87.7 11.0 %collective-permute-start.27 = (bf16[144,1024]{1,0:T(8,128)(2,1)S(1)}, bf16[144,1024]{1,0:T(8,128)(2,1)S(1)}, u32[]{:S(2)}, u32[]{:S(2)}) collective-permute-start(bf16[144,1024]{1,0:T(8,128)(2,1)S(1)} %get-tuple-element.73), channel_id=1, source_target_pairs={{0,2},{1,3},{2,4},{3,5},{4,6},{5,7},{6,0},{7,1},{8,10},{9,11},{10,... | collective-permute-start | bytes 884744 | tf_op jit(solution)/shard_map/sum_grads/ppermute | solution.py:31
  89.6 11.5 %collective-permute-start.28 = (bf16[128,1024]{1,0:T(8,128)(2,1)S(1)}, bf16[128,1024]{1,0:T(8,128)(2,1)S(1)}, u32[]{:S(2)}, u32[]{:S(2)}) collective-permute-start(bf16[128,1024]{1,0:T(8,128)(2,1)S(1)} %get-tuple-element.74), channel_id=1, source_target_pairs={{0,8},{1,9},{2,10},{3,11},{4,12},{5,13},{6,14},{7,15},{8,0},{9,1},... | collective-permute-start | bytes 786440 | tf_op jit(solution)/shard_map/sum_grads/ppermute | solution.py:31
  89.6 7.9 %collective-permute-start.29 = (bf16[16,1024]{1,0:T(8,128)(2,1)S(1)}, bf16[16,1024]{1,0:T(8,128)(2,1)S(1)}, u32[]{:S(2)}, u32[]{:S(2)}) collective-permute-start(bf16[16,1024]{1,0:T(8,128)(2,1)S(1)} %get-tuple-element.76), channel_id=1, source_target_pairs={{0,4},{1,5},{2,6},{3,7},{4,0},{5,1},{6,2},{7,3},{8,12},{9,13},{10,... | collective-permute-start | bytes 98312 | tf_op jit(solution)/shard_map/sum_grads/ppermute | solution.py:31
  99.0 9.3 %collective-permute-start.31 = (bf16[128,1024]{1,0:T(8,128)(2,1)S(1)}, bf16[128,1024]{1,0:T(8,128)(2,1)S(1)}, u32[]{:S(2)}, u32[]{:S(2)}) collective-permute-start(bf16[128,1024]{1,0:T(8,128)(2,1)S(1)} %get-tuple-element.78), channel_id=1, source_target_pairs={{0,6},{1,7},{2,0},{3,1},{4,2},{5,3},{6,4},{7,5},{8,14},{9,15},{10,... | collective-permute-start | bytes 786440 | tf_op jit(solution)/shard_map/sum_grads/ppermute | solution.py:31
  100.5 14.0 %collective-permute-start.32 = (bf16[128,1024]{1,0:T(8,128)(2,1)S(1)}, bf16[128,1024]{1,0:T(8,128)(2,1)S(1)}, u32[]{:S(2)}, u32[]{:S(2)}) collective-permute-start(bf16[128,1024]{1,0:T(8,128)(2,1)S(1)} %get-tuple-element.79), channel_id=1, source_target_pairs={{0,2},{1,3},{2,4},{3,5},{4,6},{5,7},{6,0},{7,1},{8,10},{9,11},{10,... | collective-permute-start | bytes 786440 | tf_op jit(solution)/shard_map/sum_grads/ppermute | solution.py:31
  103.4 17.9 %collective-permute-start.33 = (bf16[128,1024]{1,0:T(8,128)(2,1)S(1)}, bf16[128,1024]{1,0:T(8,128)(2,1)S(1)}, u32[]{:S(2)}, u32[]{:S(2)}) collective-permute-start(bf16[128,1024]{1,0:T(8,128)(2,1)S(1)} %get-tuple-element.80), channel_id=1, source_target_pairs={{0,4},{1,5},{2,6},{3,7},{4,0},{5,1},{6,2},{7,3},{8,12},{9,13},{10,... | collective-permute-start | bytes 786440 | tf_op jit(solution)/shard_map/sum_grads/ppermute | solution.py:31
  105.5 15.8 %collective-permute-start.34 = (bf16[128,1024]{1,0:T(8,128)(2,1)S(1)}, bf16[128,1024]{1,0:T(8,128)(2,1)S(1)}, u32[]{:S(2)}, u32[]{:S(2)}) collective-permute-start(bf16[128,1024]{1,0:T(8,128)(2,1)S(1)} %get-tuple-element.81), channel_id=1, source_target_pairs={{0,8},{1,9},{2,10},{3,11},{4,12},{5,13},{6,14},{7,15},{8,0},{9,1},... | collective-permute-start | bytes 786440 | tf_op jit(solution)/shard_map/sum_grads/ppermute | solution.py:31
  114.6 7.6 %collective-permute-start.37 = (f32[64,256]{1,0:T(8,128)S(1)}, f32[64,256]{1,0:T(8,128)S(1)}, u32[]{:S(2)}, u32[]{:S(2)}) collective-permute-start(f32[64,256]{1,0:T(8,128)S(1)} %sum_weights.2.refs_0_), channel_id=1, source_target_pairs={{0,32},{16,48},{32,64},{48,80},{64,96},{80,112},{96,0},{112,16},{1... | collective-permute-start | bytes 196616 | tf_op jit(solution)/shard_map/sum_weights/ppermute | solution.py:39
  116.1 6.1 %collective-permute-start.36 = (f32[64,256]{1,0:T(8,128)S(1)}, f32[64,256]{1,0:T(8,128)S(1)}, u32[]{:S(2)}, u32[]{:S(2)}) collective-permute-start(f32[64,256]{1,0:T(8,128)S(1)} %sum_weights.2.refs_0_), channel_id=1, source_target_pairs={{0,64},{16,80},{32,96},{48,112},{64,0},{80,16},{96,32},{112,48},{1... | collective-permute-start | bytes 196616 | tf_op jit(solution)/shard_map/sum_weights/ppermute | solution.py:39
  (12 other events, 140.5 us)

commit v8 on v5

--- a/solution.py
+++ b/solution.py
@@ -262,7 +262,7 @@
 
 
 def add_sib_far_body(mine, sib, got, quarter, *rest):
-    outs, (quarter_out, near, extra) = rest[:3], rest[3:]
+    outs, quarter_out, near = rest[:3], rest[3], rest[4]
     total = quarter[...] + read_fine(got, 384)
     quarter_out[...] = rounded(total)
     for k, ref in enumerate(outs):
@@ -271,7 +271,6 @@
             new = mine[4 * (PAIR_LEFT + k) + b] + got[128 * k : 128 * k + 128, nodes].astype(F32)
             ref[0:128, nodes] = new.astype(BF16)
         write_extra(ref, 128, total)
-    write_extra(extra, 0, total)
     write_places(sib, OWN, [near.at[k] for k in range(5)])
 
 
@@ -300,10 +299,11 @@
             ref[:, nodes] = new.astype(ref.dtype)
 
 
-def extras_body(from_right, from_left, from_opposite, pair):
+def extras_body(quarter, from_right, from_left, from_pair, pair, opposite):
+    write_extra(opposite, 0, quarter[...])
+    opposite[16:32] = from_pair[128:144]
     pair[0:16] = from_left[128:144]
     pair[16:32] = from_right[128:144]
-    pair[32:48] = from_opposite[...]
 
 
 def first_sums(parts, step, swap):
@@ -374,18 +374,17 @@
         out[nodes] = total.T.astype(BF16)
 
 
-def weight_sum_body(own, left, right, pair, opposite, pair_ring, out, parts):
+def weight_sum_body(own, left, right, pair, from_opposite, from_pair, out, parts):
     col, _ = places()
     y, x = col >> 3, (col >> 1) & 3
-    ring, other = y * 4, (1 - y) * 4
-    parts[ring + x] = own[...]
-    parts[ring + ((x + 3) & 3)] = read_extra(left, 128)
-    parts[ring + ((x + 1) & 3)] = read_extra(right, 128)
-    parts[ring + ((x + 2) & 3)] = read_extra(opposite, 0)
-    parts[other + x] = read_extra(pair, 128)
-    parts[other + ((x + 3) & 3)] = read_extra(pair_ring, 0)
-    parts[other + ((x + 1) & 3)] = read_extra(pair_ring, 16)
-    parts[other + ((x + 2) & 3)] = read_extra(pair_ring, 32)
+    parts[y * 4 + x] = own[...]
+    parts[y * 4 + ((x + 3) & 3)] = read_extra(left, 128)
+    parts[y * 4 + ((x + 1) & 3)] = read_extra(right, 128)
+    parts[(1 - y) * 4 + x] = read_extra(pair, 128)
+    parts[y * 4 + ((x + 2) & 3)] = read_extra(from_opposite, 0)
+    parts[(1 - y) * 4 + ((x + 2) & 3)] = read_extra(from_opposite, 16)
+    parts[(1 - y) * 4 + ((x + 3) & 3)] = read_extra(from_pair, 0)
+    parts[(1 - y) * 4 + ((x + 1) & 3)] = read_extra(from_pair, 16)
     total = parts[0]
     for k in range(1, 8):
         total = total + parts[k]
@@ -550,9 +549,9 @@
     with jax.named_scope("sum_grads"):
         step, swap = (lambda v, d: hop_col(v, 0, d)), (lambda v: hop_col(v, 1, 0))
         f32, bf16 = VMEM((128, 1024), F32), VMEM((128, 1024), BF16)
-        *far, quarter, sib_near, extra = call(
+        *far, quarter, sib_near = call(
             add_sib_far_body,
-            [longer, longer, longer, block, VMEM((5, 128, 1024), BF16), VMEM((16, 1024), BF16)],
+            [longer, longer, longer, block, VMEM((5, 128, 1024), BF16)],
             [mine, sib, hop_col(sib_far, 0, 0, 1), quarter],
             nbytes=3 << 20,
         )
@@ -560,14 +559,16 @@
         sib_near = hop_col(sib_near, 0, 0, 1)
         left, right = call(add_sides_body, [bf16, bf16], [mine, sib_near], nbytes=2 << 20)
         left, right = step(left, -1), step(right, 1)
-        from_opposite = step(extra, 2)
-        extras = call(extras_body, VMEM((48, 1024), BF16), [from_right, from_left, from_opposite])
-        came = [from_left, from_right, from_pair, from_opposite, swap(extras)]
+        extra = VMEM((32, 1024), BF16)
+        pair_extra, opposite_extra = call(
+            extras_body, [extra, extra], [quarter, from_right, from_left, from_pair]
+        )
+        came = [from_left, from_right, from_pair, step(opposite_extra, 2), swap(pair_extra)]
         own, pair, opposite = call(
             add_near_body,
             [f32, bf16, bf16],
             [mine, sib_near, from_right, from_left, from_pair],
-            after=[came[4], left, right],
+            after=[*came[3:], left, right],
             nbytes=5 << 20,
         )
         sums = [own, left, right, step(opposite, 2), swap(pair)]

time: 119 us -> 118 us (level); the launches traced: 120 us -> 117 us
  starting transfers between devices: 57.4 us -> 54.1 us
  waiting for transfers between devices: 34.7 us -> 37.6 us
  Pallas kernels: 25.2 us -> 22.8 us
    ppermute x20, waiting for transfers between devices: 18.6 us -> 21.9 us  [hop_col(): return lax.ppermute(value, 'col', pairs)]
    ppermute x20, starting transfers between devices: 22.5 us -> 19.3 us  [hop_col(): return lax.ppermute(value, 'col', pairs)]
    pallas_call x19, Pallas kernels: 18.8 us -> 16.4 us  [call(): pl.pallas_call(run, out_shape=outs, in_specs=[pl.BlockSpec(memory_space=p...]
  transfers between devices with their start and end apart: 38 -> 38, of which waited for: 16 -> 18; matrix products, arithmetic and copies ran while one was open for 0% -> 0% of each run, Pallas kernels for 15% -> 14%
where the time goes in v8:
time: 118 us; the launch traced here: 117 us
  starting transfers between devices  54.1 us (46%)
  waiting for transfers between devices  37.6 us (32%)
  Pallas kernels  22.8 us (19%)
  between operations  1.53 us (1%)
    ppermute x18, starting transfers between devices, hop_row(): return lax.ppermute(value, 'row', pairs)  34.8 us
    ppermute x20, waiting for transfers between devices, hop_col(): return lax.ppermute(value, 'col', pairs)  21.9 us
    ppermute x20, starting transfers between devices, hop_col(): return lax.ppermute(value, 'col', pairs)  19.3 us
    pallas_call x19, Pallas kernels, call(): pl.pallas_call(run, out_shape=outs, in_specs=[pl.BlockSpec(memory_space=p...  16.4 us
    ppermute x18, waiting for transfers between devices, hop_row(): return lax.ppermute(value, 'row', pairs)  15.7 us
    pallas_call x1, Pallas kernels, shards(): pl.pallas_call(plan_body, out_shape=[VMEM((128, TILE, TILE), BF16), pltpu...  6.48 us
  transfers between devices with their start and end apart: 38, of which 18 were waited for; matrix products, arithmetic and copies ran while one was open for 0% of the time, Pallas kernels for 14%

profile of v8, /device:TPU:0, one launch (start us, length us, event | category | flops | bytes accessed | tf_op | source)
XLA Modules:
  0.0 116.7 jit_solution(14549033071206788735)
XLA Ops:
  0.6 3.2 %collective-permute-start.3 = (bf16[1024,128]{1,0:T(8,128)(2,1)}, bf16[1024,128]{1,0:T(8,128)(2,1)S(1)}, u32[]{:S(2)}, u32[]{:S(2)}) collective-permute-start(bf16[1024,128]{1,0:T(8,128)(2,1)} %refs_1_.2), channel_id=1, source_target_pairs={{0,4},{1,5},{2,6},{3,7},{4,0},{5,1},{6,2},{7,3},{8,12},{9,13},{10,... | collective-permute-start | bytes 786440 | tf_op jit(solution)/shard_map/gather_features/ppermute | solution.py:31
  3.8 1.6 %collective-permute-start.2 = (bf16[1024,128]{1,0:T(8,128)(2,1)}, bf16[1024,128]{1,0:T(8,128)(2,1)S(1)}, u32[]{:S(2)}, u32[]{:S(2)}) collective-permute-start(bf16[1024,128]{1,0:T(8,128)(2,1)} %refs_1_.2), channel_id=1, source_target_pairs={{0,8},{1,9},{2,10},{3,11},{4,12},{5,13},{6,14},{7,15},{8,0},{9,1},... | collective-permute-start | bytes 786440 | tf_op jit(solution)/shard_map/gather_features/ppermute | solution.py:31
  8.8 6.5 %plan.1 = (bf16[128,256,256]{2,1,0:T(8,128)(2,1)S(1)}, s32[1152]{0:T(1024)S(4)}, s32[8]{0:T(128)S(4)}) custom-call(s32[2,128]{1,0:T(2,128)S(1)} %bitcast.7, s32[1]{0:T(128)} %bitcast.6.count, bf16[128,256,256]{2,1,0:T(8,128)(2,1)} %bitcast.9), custom_call_target="tpu_custom_call" | custom-call | bytes 16777216 | tf_op jit(solution)/shard_map/plan/pallas_call | solution.py:412
  16.5 1.7 %collective-permute-start.6 = (bf16[1024,128]{1,0:T(8,128)(2,1)S(1)}, bf16[1024,128]{1,0:T(8,128)(2,1)S(1)}, u32[]{:S(2)}, u32[]{:S(2)}) collective-permute-start(bf16[1024,128]{1,0:T(8,128)(2,1)S(1)} %collective-permute-done.3.refs_4_), channel_id=1, source_target_pairs={{0,8},{1,9},{2,10},{3,11},{4,12},{5,13},{6,14},{7,15},{8,0},{9,1},... | collective-permute-start | bytes 786440 | tf_op jit(solution)/shard_map/gather_features/ppermute | solution.py:31
  18.2 2.6 %collective-permute-start.5 = (bf16[1024,128]{1,0:T(8,128)(2,1)S(1)}, bf16[1024,128]{1,0:T(8,128)(2,1)S(1)}, u32[]{:S(2)}, u32[]{:S(2)}) collective-permute-start(bf16[1024,128]{1,0:T(8,128)(2,1)S(1)} %get-tuple-element.48), channel_id=1, source_target_pairs={{0,6},{1,7},{2,0},{3,1},{4,2},{5,3},{6,4},{7,5},{8,14},{9,15},{10,... | collective-permute-start | bytes 786440 | tf_op jit(solution)/shard_map/gather_features/ppermute | solution.py:31
  20.8 3.1 %forward_tiles.4.refs_3_.refs_4_ = f32[33,256,128]{2,1,0:T(8,128)S(1)} custom-call(s32[1152]{0:T(1024)S(4)} %get-tuple-element.45.refs_0_, s32[8]{0:T(128)S(4)} %get-tuple-element.46.refs_5_.refs_1_, bf16[128,256,256]{2,1,0:T(8,128)(2,1)S(1)} %get-tuple-element.47.refs_2_, bf16[20,256,128]{2,1,0:T(8,128)(2,1)S(1)} %get-tuple-element.49.refs_3_, ...), custom_call_target="tpu_custom_call" | custom-call | tf_op jit(solution)/shard_map/forward_tiles/pallas_call | solution.py:67
  25.2 1.4 %collective-permute-done.5.refs_1_ = bf16[1024,128]{1,0:T(8,128)(2,1)S(1)} collective-permute-done((bf16[1024,128]{1,0:T(8,128)(2,1)S(1)}, bf16[1024,128]{1,0:T(8,128)(2,1)S(1)}, u32[]{:S(2)}, u32[]{:S(2)}) %collective-permute-start.5) | collective-permute-done | bytes 262176 | tf_op jit(solution)/shard_map/gather_features/ppermute | solution.py:31
  26.7 3.4 %collective-permute-done.4.refs_0_ = bf16[1024,128]{1,0:T(8,128)(2,1)S(1)} collective-permute-done((bf16[1024,128]{1,0:T(8,128)(2,1)S(1)}, bf16[1024,128]{1,0:T(8,128)(2,1)S(1)}, u32[]{:S(2)}, u32[]{:S(2)}) %collective-permute-start.4) | collective-permute-done | bytes 262176 | tf_op jit(solution)/shard_map/gather_features/ppermute | solution.py:31
  30.2 1.4 %forward_tiles.6.refs_4_ = f32[33,256,128]{2,1,0:T(8,128)S(1)} custom-call(s32[1152]{0:T(1024)S(4)} %get-tuple-element.45.refs_0_, s32[8]{0:T(128)S(4)} %get-tuple-element.46.refs_5_.refs_1_, bf16[128,256,256]{2,1,0:T(8,128)(2,1)S(1)} %get-tuple-element.47.refs_2_, bf16[12,256,128]{2,1,0:T(8,128)(2,1)S(1)} %forward_tiles.5.refs_3_, ...), custom_call_target="tpu_custom_call", output_to_operand_aliasing={{}: (4, {})} | custom-call | flops 536870912 | bytes 4194304 | tf_op jit(solution)/shard_map/forward_tiles/pallas_call | solution.py:67
  32.5 1.6 %forward_tiles.7 = (f32[33,256,128]{2,1,0:T(8,128)S(1)}, f32[1024,128]{1,0:T(8,128)S(1)}, bf16[1024,128]{1,0:T(8,128)(2,1)S(1)}, bf16[1024,128]{1,0:T(8,128)(2,1...) custom-call(s32[1152]{0:T(1024)S(4)} %get-tuple-element.45.refs_0_, ...), custom_call_target="tpu_custom_call", output_to_operand_aliasing={{0}: (4, {})} | custom-call | flops 536870912 | bytes 4194304 | tf_op jit(solution)/shard_map/forward_tiles/pallas_call | solution.py:67
  34.2 4.1 %collective-permute-start.11 = (bf16[1024,128]{1,0:T(8,128)(2,1)S(1)}, bf16[1024,128]{1,0:T(8,128)(2,1)S(1)}, u32[]{:S(2)}, u32[]{:S(2)}) collective-permute-start(bf16[1024,128]{1,0:T(8,128)(2,1)S(1)} %get-tuple-element.55), channel_id=1, source_target_pairs={{0,96},{16,112},{32,0},{48,16},{64,32},{80,48},{96,64},{112,80},{1... | collective-permute-start | bytes 786440 | tf_op jit(solution)/shard_map/sum_aggregates/ppermute | solution.py:39
  38.3 2.9 %collective-permute-start.13 = (bf16[1024,128]{1,0:T(8,128)(2,1)S(1)}, bf16[1024,128]{1,0:T(8,128)(2,1)S(1)}, u32[]{:S(2)}, u32[]{:S(2)}) collective-permute-start(bf16[1024,128]{1,0:T(8,128)(2,1)S(1)} %get-tuple-element.57), channel_id=1, source_target_pairs={{0,16},{16,0},{32,48},{48,32},{64,80},{80,64},{96,112},{112,96},{1... | collective-permute-start | bytes 786440 | tf_op jit(solution)/shard_map/sum_aggregates/ppermute | solution.py:39
  41.2 3.2 %collective-permute-start.9 = (bf16[1024,128]{1,0:T(8,128)(2,1)S(1)}, bf16[1024,128]{1,0:T(8,128)(2,1)S(1)}, u32[]{:S(2)}, u32[]{:S(2)}) collective-permute-start(bf16[1024,128]{1,0:T(8,128)(2,1)S(1)} %get-tuple-element.51), channel_id=1, source_target_pairs={{0,96},{16,112},{32,0},{48,16},{64,32},{80,48},{96,64},{112,80},{1... | collective-permute-start | bytes 786440 | tf_op jit(solution)/shard_map/sum_aggregates/ppermute | solution.py:39
  44.4 2.7 %collective-permute-done.12.refs_3_ = bf16[1024,128]{1,0:T(8,128)(2,1)S(1)} collective-permute-done((bf16[1024,128]{1,0:T(8,128)(2,1)S(1)}, bf16[1024,128]{1,0:T(8,128)(2,1)S(1)}, u32[]{:S(2)}, u32[]{:S(2)}) %collective-permute-start.12) | collective-permute-done | bytes 262176 | tf_op jit(solution)/shard_map/sum_aggregates/ppermute | solution.py:39
  47.3 2.0 %collective-permute-start.14 = (bf16[1024,128]{1,0:T(8,128)(2,1)S(1)}, bf16[1024,128]{1,0:T(8,128)(2,1)S(1)}, u32[]{:S(2)}, u32[]{:S(2)}) collective-permute-start(bf16[1024,128]{1,0:T(8,128)(2,1)S(1)} %get-tuple-element.58), channel_id=1, source_target_pairs={{0,64},{16,80},{32,96},{48,112},{64,0},{80,16},{96,32},{112,48},{1... | collective-permute-start | bytes 786440 | tf_op jit(solution)/shard_map/sum_aggregates/ppermute | solution.py:39
  49.3 3.2 %collective-permute-start.15 = (bf16[1024,128]{1,0:T(8,128)(2,1)S(1)}, bf16[1024,128]{1,0:T(8,128)(2,1)S(1)}, u32[]{:S(2)}, u32[]{:S(2)}) collective-permute-start(bf16[1024,128]{1,0:T(8,128)(2,1)S(1)} %get-tuple-element.59), channel_id=1, source_target_pairs={{0,16},{16,0},{32,48},{48,32},{64,80},{80,64},{96,112},{112,96},{1... | collective-permute-start | bytes 786440 | tf_op jit(solution)/shard_map/sum_aggregates/ppermute | solution.py:39
  52.5 5.5 %collective-permute-done.10.refs_7_ = bf16[1024,128]{1,0:T(8,128)(2,1)S(1)} collective-permute-done((bf16[1024,128]{1,0:T(8,128)(2,1)S(1)}, bf16[1024,128]{1,0:T(8,128)(2,1)S(1)}, u32[]{:S(2)}, u32[]{:S(2)}) %collective-permute-start.10) | collective-permute-done | bytes 262176 | tf_op jit(solution)/shard_map/sum_aggregates/ppermute | solution.py:39
  58.1 2.3 %dense.1 = (bf16[1024,256]{1,0:T(8,128)(2,1)}, bf16[1024,256]{1,0:T(8,128)(2,1)S(1)}, bf16[128,1024]{1,0:T(8,128)(2,1)S(1)}, bf16[144,1024]{1,0:T(8,128)(2,1)S(1...) custom-call(f32[1,256]{1,0:T(1,128)S(1)} %bitcast.8, ...), custom_call_target="tpu_custom_call" | custom-call | flops 335544320 | bytes 6291456 | tf_op jit(solution)/shard_map/dense/pallas_call | solution.py:67
  60.4 1.6 %collective-permute-start.19 = (bf16[144,1024]{1,0:T(8,128)(2,1)S(1)}, bf16[144,1024]{1,0:T(8,128)(2,1)S(1)}, u32[]{:S(2)}, u32[]{:S(2)}) collective-permute-start(bf16[144,1024]{1,0:T(8,128)(2,1)S(1)} %get-tuple-element.63), channel_id=1, source_target_pairs={{0,64},{16,80},{32,96},{48,112},{64,0},{80,16},{96,32},{112,48},{1... | collective-permute-start | bytes 884744 | tf_op jit(solution)/shard_map/gather_dz/ppermute | solution.py:39
  62.0 3.5 %collective-permute-start.16 = (bf16[128,1024]{1,0:T(8,128)(2,1)S(1)}, bf16[128,1024]{1,0:T(8,128)(2,1)S(1)}, u32[]{:S(2)}, u32[]{:S(2)}) collective-permute-start(bf16[128,1024]{1,0:T(8,128)(2,1)S(1)} %get-tuple-element.62.refs_3_), channel_id=1, source_target_pairs={{0,16},{16,0},{32,48},{48,32},{64,80},{80,64},{96,112},{112,96},{1... | collective-permute-start | bytes 786440 | tf_op jit(solution)/shard_map/gather_dz/ppermute | solution.py:39
  65.5 3.2 %collective-permute-start.22 = (bf16[144,1024]{1,0:T(8,128)(2,1)S(1)}, bf16[144,1024]{1,0:T(8,128)(2,1)S(1)}, u32[]{:S(2)}, u32[]{:S(2)}) collective-permute-start(bf16[144,1024]{1,0:T(8,128)(2,1)S(1)} %get-tuple-element.65), channel_id=1, source_target_pairs={{0,96},{16,112},{32,0},{48,16},{64,32},{80,48},{96,64},{112,80},{1... | collective-permute-start | bytes 884744 | tf_op jit(solution)/shard_map/gather_dz/ppermute | solution.py:39
  68.8 2.8 %collective-permute-done.19.refs_7_.refs_1_ = bf16[144,1024]{1,0:T(8,128)(2,1)S(1)} collective-permute-done((bf16[144,1024]{1,0:T(8,128)(2,1)S(1)}, bf16[144,1024]{1,0:T(8,128)(2,1)S(1)}, u32[]{:S(2)}, u32[]{:S(2)}) %collective-permute-start.19) | collective-permute-done | bytes 294944 | tf_op jit(solution)/shard_map/gather_dz/ppermute | solution.py:39
  71.6 3.1 %collective-permute-start.20 = (bf16[144,1024]{1,0:T(8,128)(2,1)S(1)}, bf16[144,1024]{1,0:T(8,128)(2,1)S(1)}, u32[]{:S(2)}, u32[]{:S(2)}) collective-permute-start(bf16[144,1024]{1,0:T(8,128)(2,1)S(1)} %collective-permute-done.19.refs_7_.refs_1_), channel_id=1, source_target_pairs={{0,16},{16,0},{32,48},{48,32},{64,80},{80,64},{96,112},{112,96},{1... | collective-permute-start | bytes 884744 | tf_op jit(solution)/shard_map/gather_dz/ppermute | solution.py:39
  77.5 1.6 %collective-permute-start.23 = (bf16[32,1024]{1,0:T(8,128)(2,1)S(1)}, bf16[32,1024]{1,0:T(8,128)(2,1)S(1)}, u32[]{:S(2)}, u32[]{:S(2)}) collective-permute-start(bf16[32,1024]{1,0:T(8,128)(2,1)S(1)} %gather_dz.1.refs_6_), channel_id=1, source_target_pairs={{0,16},{16,0},{32,48},{48,32},{64,80},{80,64},{96,112},{112,96},{1... | collective-permute-start | bytes 196616 | tf_op jit(solution)/shard_map/gather_dz/ppermute | solution.py:39
  79.0 3.1 %backward_tiles.3 = (f32[33,128,256]{2,1,0:T(8,128)S(1)}, f32[33,128,256]{2,1,0:T(8,128)S(1)}) custom-call(s32[1152]{0:T(1024)S(4)} %get-tuple-element.45.refs_0_, s32[8]{0:T(128)S(4)} %get-tuple-element.46.refs_5_.refs_1_, bf16[128,256,256]{2,1,0:T(8,128)(2,1)S(1)} %get-tuple-element.47.refs_2_, bf16[128,1024]{1,0:T(8,128)(2,1)S(1)} %get-tuple-element.62.refs_3_, ...), custom_call_target="tpu_custom_call" | custom-call | flops 1073741824 | bytes 8388608 | tf_op jit(solution)/shard_map/backward_tiles/pallas_call | solution.py:67
  90.0 1.5 %collective-permute-start.31 = (bf16[128,1024]{1,0:T(8,128)(2,1)S(1)}, bf16[128,1024]{1,0:T(8,128)(2,1)S(1)}, u32[]{:S(2)}, u32[]{:S(2)}) collective-permute-start(bf16[128,1024]{1,0:T(8,128)(2,1)S(1)} %get-tuple-element.79), channel_id=1, source_target_pairs={{0,6},{1,7},{2,0},{3,1},{4,2},{5,3},{6,4},{7,5},{8,14},{9,15},{10,... | collective-permute-start | bytes 786440 | tf_op jit(solution)/shard_map/sum_grads/ppermute | solution.py:31
  92.1 4.8 %collective-permute-done.26.refs_1_.refs_2_ = bf16[144,1024]{1,0:T(8,128)(2,1)S(1)} collective-permute-done((bf16[144,1024]{1,0:T(8,128)(2,1)S(1)}, bf16[144,1024]{1,0:T(8,128)(2,1)S(1)}, u32[]{:S(2)}, u32[]{:S(2)}) %collective-permute-start.26) | collective-permute-done | bytes 294944 | tf_op jit(solution)/shard_map/sum_grads/ppermute | solution.py:31
  96.8 2.3 %collective-permute-done.27.refs_2_.refs_3_.refs_1_ = bf16[144,1024]{1,0:T(8,128)(2,1)S(1)} collective-permute-done((bf16[144,1024]{1,0:T(8,128)(2,1)S(1)}, bf16[144,1024]{1,0:T(8,128)(2,1)S(1)}, u32[]{:S(2)}, u32[]{:S(2)}) %collective-permute-start.27) | collective-permute-done | bytes 294944 | tf_op jit(solution)/shard_map/sum_grads/ppermute | solution.py:31
  99.8 5.3 %collective-permute-done.29.refs_5_.refs_4_ = bf16[32,1024]{1,0:T(8,128)(2,1)S(1)} collective-permute-done((bf16[32,1024]{1,0:T(8,128)(2,1)S(1)}, bf16[32,1024]{1,0:T(8,128)(2,1)S(1)}, u32[]{:S(2)}, u32[]{:S(2)}) %collective-permute-start.29) | collective-permute-done | bytes 65568 | tf_op jit(solution)/shard_map/sum_grads/ppermute | solution.py:31
  105.5 1.8 %collective-permute-start.33 = (bf16[128,1024]{1,0:T(8,128)(2,1)S(1)}, bf16[128,1024]{1,0:T(8,128)(2,1)S(1)}, u32[]{:S(2)}, u32[]{:S(2)}) collective-permute-start(bf16[128,1024]{1,0:T(8,128)(2,1)S(1)} %get-tuple-element.82), channel_id=1, source_target_pairs={{0,4},{1,5},{2,6},{3,7},{4,0},{5,1},{6,2},{7,3},{8,12},{9,13},{10,... | collective-permute-start | bytes 786440 | tf_op jit(solution)/shard_map/sum_grads/ppermute | solution.py:31
  108.0 2.8 %collective-permute-start.36 = (f32[64,256]{1,0:T(8,128)S(1)}, f32[64,256]{1,0:T(8,128)S(1)}, u32[]{:S(2)}, u32[]{:S(2)}) collective-permute-start(f32[64,256]{1,0:T(8,128)S(1)} %sum_weights.2.refs_0_), channel_id=1, source_target_pairs={{0,64},{16,80},{32,96},{48,112},{64,0},{80,16},{96,32},{112,48},{1... | collective-permute-start | bytes 196616 | tf_op jit(solution)/shard_map/sum_weights/ppermute | solution.py:39
  111.9 2.1 %collective-permute-done.37.refs_3_ = f32[64,256]{1,0:T(8,128)S(1)} collective-permute-done((f32[64,256]{1,0:T(8,128)S(1)}, f32[64,256]{1,0:T(8,128)S(1)}, u32[]{:S(2)}, u32[]{:S(2)}) %collective-permute-start.37) | collective-permute-done | bytes 65568 | tf_op jit(solution)/shard_map/sum_weights/ppermute | solution.py:39
  (76 shorter events, 23.0 us)
Async XLA Ops:
  0.6 14.6 %collective-permute-start.3 = (bf16[1024,128]{1,0:T(8,128)(2,1)}, bf16[1024,128]{1,0:T(8,128)(2,1)S(1)}, u32[]{:S(2)}, u32[]{:S(2)}) collective-permute-start(bf16[1024,128]{1,0:T(8,128)(2,1)} %refs_1_.2), channel_id=1, source_target_pairs={{0,4},{1,5},{2,6},{3,7},{4,0},{5,1},{6,2},{7,3},{8,12},{9,13},{10,... | collective-permute-start | bytes 786440 | tf_op jit(solution)/shard_map/gather_features/ppermute | solution.py:31
  3.8 11.4 %collective-permute-start.2 = (bf16[1024,128]{1,0:T(8,128)(2,1)}, bf16[1024,128]{1,0:T(8,128)(2,1)S(1)}, u32[]{:S(2)}, u32[]{:S(2)}) collective-permute-start(bf16[1024,128]{1,0:T(8,128)(2,1)} %refs_1_.2), channel_id=1, source_target_pairs={{0,8},{1,9},{2,10},{3,11},{4,12},{5,13},{6,14},{7,15},{8,0},{9,1},... | collective-permute-start | bytes 786440 | tf_op jit(solution)/shard_map/gather_features/ppermute | solution.py:31
  5.4 10.9 %collective-permute-start.1 = (bf16[1024,128]{1,0:T(8,128)(2,1)}, bf16[1024,128]{1,0:T(8,128)(2,1)S(1)}, u32[]{:S(2)}, u32[]{:S(2)}) collective-permute-start(bf16[1024,128]{1,0:T(8,128)(2,1)} %refs_1_.2), channel_id=1, source_target_pairs={{0,6},{1,7},{2,0},{3,1},{4,2},{5,3},{6,4},{7,5},{8,14},{9,15},{10,... | collective-permute-start | bytes 786440 | tf_op jit(solution)/shard_map/gather_features/ppermute | solution.py:31
  6.5 9.8 %collective-permute-start = (bf16[1024,128]{1,0:T(8,128)(2,1)}, bf16[1024,128]{1,0:T(8,128)(2,1)S(1)}, u32[]{:S(2)}, u32[]{:S(2)}) collective-permute-start(bf16[1024,128]{1,0:T(8,128)(2,1)} %refs_1_.2), channel_id=1, source_target_pairs={{0,2},{1,3},{2,4},{3,5},{4,6},{5,7},{6,0},{7,1},{8,10},{9,11},{10,... | collective-permute-start | bytes 786440 | tf_op jit(solution)/shard_map/gather_features/ppermute | solution.py:31
  16.5 8.7 %collective-permute-start.6 = (bf16[1024,128]{1,0:T(8,128)(2,1)S(1)}, bf16[1024,128]{1,0:T(8,128)(2,1)S(1)}, u32[]{:S(2)}, u32[]{:S(2)}) collective-permute-start(bf16[1024,128]{1,0:T(8,128)(2,1)S(1)} %collective-permute-done.3.refs_4_), channel_id=1, source_target_pairs={{0,8},{1,9},{2,10},{3,11},{4,12},{5,13},{6,14},{7,15},{8,0},{9,1},... | collective-permute-start | bytes 786440 | tf_op jit(solution)/shard_map/gather_features/ppermute | solution.py:31
  18.2 8.5 %collective-permute-start.5 = (bf16[1024,128]{1,0:T(8,128)(2,1)S(1)}, bf16[1024,128]{1,0:T(8,128)(2,1)S(1)}, u32[]{:S(2)}, u32[]{:S(2)}) collective-permute-start(bf16[1024,128]{1,0:T(8,128)(2,1)S(1)} %get-tuple-element.48), channel_id=1, source_target_pairs={{0,6},{1,7},{2,0},{3,1},{4,2},{5,3},{6,4},{7,5},{8,14},{9,15},{10,... | collective-permute-start | bytes 786440 | tf_op jit(solution)/shard_map/gather_features/ppermute | solution.py:31
  20.8 9.3 %collective-permute-start.4 = (bf16[1024,128]{1,0:T(8,128)(2,1)S(1)}, bf16[1024,128]{1,0:T(8,128)(2,1)S(1)}, u32[]{:S(2)}, u32[]{:S(2)}) collective-permute-start(bf16[1024,128]{1,0:T(8,128)(2,1)S(1)} %get-tuple-element.48), channel_id=1, source_target_pairs={{0,2},{1,3},{2,4},{3,5},{4,6},{5,7},{6,0},{7,1},{8,10},{9,11},{10,... | collective-permute-start | bytes 786440 | tf_op jit(solution)/shard_map/gather_features/ppermute | solution.py:31
  34.2 10.2 %collective-permute-start.11 = (bf16[1024,128]{1,0:T(8,128)(2,1)S(1)}, bf16[1024,128]{1,0:T(8,128)(2,1)S(1)}, u32[]{:S(2)}, u32[]{:S(2)}) collective-permute-start(bf16[1024,128]{1,0:T(8,128)(2,1)S(1)} %get-tuple-element.55), channel_id=1, source_target_pairs={{0,96},{16,112},{32,0},{48,16},{64,32},{80,48},{96,64},{112,80},{1... | collective-permute-start | bytes 786440 | tf_op jit(solution)/shard_map/sum_aggregates/ppermute | solution.py:39
  38.3 8.8 %collective-permute-start.12 = (bf16[1024,128]{1,0:T(8,128)(2,1)S(1)}, bf16[1024,128]{1,0:T(8,128)(2,1)S(1)}, u32[]{:S(2)}, u32[]{:S(2)}) collective-permute-start(bf16[1024,128]{1,0:T(8,128)(2,1)S(1)} %get-tuple-element.56), channel_id=1, source_target_pairs={{0,32},{16,48},{32,64},{48,80},{64,96},{80,112},{96,0},{112,16},{1... | collective-permute-start | bytes 786440 | tf_op jit(solution)/shard_map/sum_aggregates/ppermute | solution.py:39
  38.3 8.9 %collective-permute-start.13 = (bf16[1024,128]{1,0:T(8,128)(2,1)S(1)}, bf16[1024,128]{1,0:T(8,128)(2,1)S(1)}, u32[]{:S(2)}, u32[]{:S(2)}) collective-permute-start(bf16[1024,128]{1,0:T(8,128)(2,1)S(1)} %get-tuple-element.57), channel_id=1, source_target_pairs={{0,16},{16,0},{32,48},{48,32},{64,80},{80,64},{96,112},{112,96},{1... | collective-permute-start | bytes 786440 | tf_op jit(solution)/shard_map/sum_aggregates/ppermute | solution.py:39
  41.2 11.4 %collective-permute-start.9 = (bf16[1024,128]{1,0:T(8,128)(2,1)S(1)}, bf16[1024,128]{1,0:T(8,128)(2,1)S(1)}, u32[]{:S(2)}, u32[]{:S(2)}) collective-permute-start(bf16[1024,128]{1,0:T(8,128)(2,1)S(1)} %get-tuple-element.51), channel_id=1, source_target_pairs={{0,96},{16,112},{32,0},{48,16},{64,32},{80,48},{96,64},{112,80},{1... | collective-permute-start | bytes 786440 | tf_op jit(solution)/shard_map/sum_aggregates/ppermute | solution.py:39
  44.4 13.7 %collective-permute-start.10 = (bf16[1024,128]{1,0:T(8,128)(2,1)S(1)}, bf16[1024,128]{1,0:T(8,128)(2,1)S(1)}, u32[]{:S(2)}, u32[]{:S(2)}) collective-permute-start(bf16[1024,128]{1,0:T(8,128)(2,1)S(1)} %get-tuple-element.52), channel_id=1, source_target_pairs={{0,32},{16,48},{32,64},{48,80},{64,96},{80,112},{96,0},{112,16},{1... | collective-permute-start | bytes 786440 | tf_op jit(solution)/shard_map/sum_aggregates/ppermute | solution.py:39
  47.3 10.8 %collective-permute-start.14 = (bf16[1024,128]{1,0:T(8,128)(2,1)S(1)}, bf16[1024,128]{1,0:T(8,128)(2,1)S(1)}, u32[]{:S(2)}, u32[]{:S(2)}) collective-permute-start(bf16[1024,128]{1,0:T(8,128)(2,1)S(1)} %get-tuple-element.58), channel_id=1, source_target_pairs={{0,64},{16,80},{32,96},{48,112},{64,0},{80,16},{96,32},{112,48},{1... | collective-permute-start | bytes 786440 | tf_op jit(solution)/shard_map/sum_aggregates/ppermute | solution.py:39
  49.3 8.8 %collective-permute-start.15 = (bf16[1024,128]{1,0:T(8,128)(2,1)S(1)}, bf16[1024,128]{1,0:T(8,128)(2,1)S(1)}, u32[]{:S(2)}, u32[]{:S(2)}) collective-permute-start(bf16[1024,128]{1,0:T(8,128)(2,1)S(1)} %get-tuple-element.59), channel_id=1, source_target_pairs={{0,16},{16,0},{32,48},{48,32},{64,80},{80,64},{96,112},{112,96},{1... | collective-permute-start | bytes 786440 | tf_op jit(solution)/shard_map/sum_aggregates/ppermute | solution.py:39
  60.4 11.2 %collective-permute-start.19 = (bf16[144,1024]{1,0:T(8,128)(2,1)S(1)}, bf16[144,1024]{1,0:T(8,128)(2,1)S(1)}, u32[]{:S(2)}, u32[]{:S(2)}) collective-permute-start(bf16[144,1024]{1,0:T(8,128)(2,1)S(1)} %get-tuple-element.63), channel_id=1, source_target_pairs={{0,64},{16,80},{32,96},{48,112},{64,0},{80,16},{96,32},{112,48},{1... | collective-permute-start | bytes 884744 | tf_op jit(solution)/shard_map/gather_dz/ppermute | solution.py:39
  62.0 12.7 %collective-permute-start.16 = (bf16[128,1024]{1,0:T(8,128)(2,1)S(1)}, bf16[128,1024]{1,0:T(8,128)(2,1)S(1)}, u32[]{:S(2)}, u32[]{:S(2)}) collective-permute-start(bf16[128,1024]{1,0:T(8,128)(2,1)S(1)} %get-tuple-element.62.refs_3_), channel_id=1, source_target_pairs={{0,16},{16,0},{32,48},{48,32},{64,80},{80,64},{96,112},{112,96},{1... | collective-permute-start | bytes 786440 | tf_op jit(solution)/shard_map/gather_dz/ppermute | solution.py:39
  65.5 11.9 %collective-permute-start.21 = (bf16[144,1024]{1,0:T(8,128)(2,1)S(1)}, bf16[144,1024]{1,0:T(8,128)(2,1)S(1)}, u32[]{:S(2)}, u32[]{:S(2)}) collective-permute-start(bf16[144,1024]{1,0:T(8,128)(2,1)S(1)} %get-tuple-element.64), channel_id=1, source_target_pairs={{0,32},{16,48},{32,64},{48,80},{64,96},{80,112},{96,0},{112,16},{1... | collective-permute-start | bytes 884744 | tf_op jit(solution)/shard_map/gather_dz/ppermute | solution.py:39
  65.5 11.9 %collective-permute-start.22 = (bf16[144,1024]{1,0:T(8,128)(2,1)S(1)}, bf16[144,1024]{1,0:T(8,128)(2,1)S(1)}, u32[]{:S(2)}, u32[]{:S(2)}) collective-permute-start(bf16[144,1024]{1,0:T(8,128)(2,1)S(1)} %get-tuple-element.65), channel_id=1, source_target_pairs={{0,96},{16,112},{32,0},{48,16},{64,32},{80,48},{96,64},{112,80},{1... | collective-permute-start | bytes 884744 | tf_op jit(solution)/shard_map/gather_dz/ppermute | solution.py:39
  71.6 11.7 %collective-permute-start.20 = (bf16[144,1024]{1,0:T(8,128)(2,1)S(1)}, bf16[144,1024]{1,0:T(8,128)(2,1)S(1)}, u32[]{:S(2)}, u32[]{:S(2)}) collective-permute-start(bf16[144,1024]{1,0:T(8,128)(2,1)S(1)} %collective-permute-done.19.refs_7_.refs_1_), channel_id=1, source_target_pairs={{0,16},{16,0},{32,48},{48,32},{64,80},{80,64},{96,112},{112,96},{1... | collective-permute-start | bytes 884744 | tf_op jit(solution)/shard_map/gather_dz/ppermute | solution.py:39
  74.7 8.6 %collective-permute-start.18 = (bf16[128,1024]{1,0:T(8,128)(2,1)S(1)}, bf16[128,1024]{1,0:T(8,128)(2,1)S(1)}, u32[]{:S(2)}, u32[]{:S(2)}) collective-permute-start(bf16[128,1024]{1,0:T(8,128)(2,1)S(1)} %collective-permute-done.16.refs_6_), channel_id=1, source_target_pairs={{0,96},{16,112},{32,0},{48,16},{64,32},{80,48},{96,64},{112,80},{1... | collective-permute-start | bytes 786440 | tf_op jit(solution)/shard_map/gather_dz/ppermute | solution.py:39
  75.6 7.7 %collective-permute-start.17 = (bf16[128,1024]{1,0:T(8,128)(2,1)S(1)}, bf16[128,1024]{1,0:T(8,128)(2,1)S(1)}, u32[]{:S(2)}, u32[]{:S(2)}) collective-permute-start(bf16[128,1024]{1,0:T(8,128)(2,1)S(1)} %collective-permute-done.16.refs_6_), channel_id=1, source_target_pairs={{0,32},{16,48},{32,64},{48,80},{64,96},{80,112},{96,0},{112,16},{1... | collective-permute-start | bytes 786440 | tf_op jit(solution)/shard_map/gather_dz/ppermute | solution.py:39
  77.5 5.8 %collective-permute-start.23 = (bf16[32,1024]{1,0:T(8,128)(2,1)S(1)}, bf16[32,1024]{1,0:T(8,128)(2,1)S(1)}, u32[]{:S(2)}, u32[]{:S(2)}) collective-permute-start(bf16[32,1024]{1,0:T(8,128)(2,1)S(1)} %gather_dz.1.refs_6_), channel_id=1, source_target_pairs={{0,16},{16,0},{32,48},{48,32},{64,80},{80,64},{96,112},{112,96},{1... | collective-permute-start | bytes 196616 | tf_op jit(solution)/shard_map/gather_dz/ppermute | solution.py:39
  87.0 9.8 %collective-permute-start.26 = (bf16[144,1024]{1,0:T(8,128)(2,1)S(1)}, bf16[144,1024]{1,0:T(8,128)(2,1)S(1)}, u32[]{:S(2)}, u32[]{:S(2)}) collective-permute-start(bf16[144,1024]{1,0:T(8,128)(2,1)S(1)} %get-tuple-element.73), channel_id=1, source_target_pairs={{0,6},{1,7},{2,0},{3,1},{4,2},{5,3},{6,4},{7,5},{8,14},{9,15},{10,... | collective-permute-start | bytes 884744 | tf_op jit(solution)/shard_map/sum_grads/ppermute | solution.py:31
  88.1 11.1 %collective-permute-start.27 = (bf16[144,1024]{1,0:T(8,128)(2,1)S(1)}, bf16[144,1024]{1,0:T(8,128)(2,1)S(1)}, u32[]{:S(2)}, u32[]{:S(2)}) collective-permute-start(bf16[144,1024]{1,0:T(8,128)(2,1)S(1)} %get-tuple-element.74), channel_id=1, source_target_pairs={{0,2},{1,3},{2,4},{3,5},{4,6},{5,7},{6,0},{7,1},{8,10},{9,11},{10,... | collective-permute-start | bytes 884744 | tf_op jit(solution)/shard_map/sum_grads/ppermute | solution.py:31
  89.0 10.1 %collective-permute-start.28 = (bf16[144,1024]{1,0:T(8,128)(2,1)S(1)}, bf16[144,1024]{1,0:T(8,128)(2,1)S(1)}, u32[]{:S(2)}, u32[]{:S(2)}) collective-permute-start(bf16[144,1024]{1,0:T(8,128)(2,1)S(1)} %get-tuple-element.75), channel_id=1, source_target_pairs={{0,8},{1,9},{2,10},{3,11},{4,12},{5,13},{6,14},{7,15},{8,0},{9,1},... | collective-permute-start | bytes 884744 | tf_op jit(solution)/shard_map/sum_grads/ppermute | solution.py:31
  90.0 15.1 %collective-permute-start.31 = (bf16[128,1024]{1,0:T(8,128)(2,1)S(1)}, bf16[128,1024]{1,0:T(8,128)(2,1)S(1)}, u32[]{:S(2)}, u32[]{:S(2)}) collective-permute-start(bf16[128,1024]{1,0:T(8,128)(2,1)S(1)} %get-tuple-element.79), channel_id=1, source_target_pairs={{0,6},{1,7},{2,0},{3,1},{4,2},{5,3},{6,4},{7,5},{8,14},{9,15},{10,... | collective-permute-start | bytes 786440 | tf_op jit(solution)/shard_map/sum_grads/ppermute | solution.py:31
  91.5 13.8 %collective-permute-start.32 = (bf16[128,1024]{1,0:T(8,128)(2,1)S(1)}, bf16[128,1024]{1,0:T(8,128)(2,1)S(1)}, u32[]{:S(2)}, u32[]{:S(2)}) collective-permute-start(bf16[128,1024]{1,0:T(8,128)(2,1)S(1)} %get-tuple-element.80), channel_id=1, source_target_pairs={{0,2},{1,3},{2,4},{3,5},{4,6},{5,7},{6,0},{7,1},{8,10},{9,11},{10,... | collective-permute-start | bytes 786440 | tf_op jit(solution)/shard_map/sum_grads/ppermute | solution.py:31
  99.1 6.0 %collective-permute-start.29 = (bf16[32,1024]{1,0:T(8,128)(2,1)S(1)}, bf16[32,1024]{1,0:T(8,128)(2,1)S(1)}, u32[]{:S(2)}, u32[]{:S(2)}) collective-permute-start(bf16[32,1024]{1,0:T(8,128)(2,1)S(1)} %get-tuple-element.77), channel_id=1, source_target_pairs={{0,4},{1,5},{2,6},{3,7},{4,0},{5,1},{6,2},{7,3},{8,12},{9,13},{10,... | collective-permute-start | bytes 196616 | tf_op jit(solution)/shard_map/sum_grads/ppermute | solution.py:31
  105.5 10.3 %collective-permute-start.33 = (bf16[128,1024]{1,0:T(8,128)(2,1)S(1)}, bf16[128,1024]{1,0:T(8,128)(2,1)S(1)}, u32[]{:S(2)}, u32[]{:S(2)}) collective-permute-start(bf16[128,1024]{1,0:T(8,128)(2,1)S(1)} %get-tuple-element.82), channel_id=1, source_target_pairs={{0,4},{1,5},{2,6},{3,7},{4,0},{5,1},{6,2},{7,3},{8,12},{9,13},{10,... | collective-permute-start | bytes 786440 | tf_op jit(solution)/shard_map/sum_grads/ppermute | solution.py:31
  107.4 8.4 %collective-permute-start.34 = (bf16[128,1024]{1,0:T(8,128)(2,1)S(1)}, bf16[128,1024]{1,0:T(8,128)(2,1)S(1)}, u32[]{:S(2)}, u32[]{:S(2)}) collective-permute-start(bf16[128,1024]{1,0:T(8,128)(2,1)S(1)} %get-tuple-element.83), channel_id=1, source_target_pairs={{0,8},{1,9},{2,10},{3,11},{4,12},{5,13},{6,14},{7,15},{8,0},{9,1},... | collective-permute-start | bytes 786440 | tf_op jit(solution)/shard_map/sum_grads/ppermute | solution.py:31
  107.8 6.2 %collective-permute-start.37 = (f32[64,256]{1,0:T(8,128)S(1)}, f32[64,256]{1,0:T(8,128)S(1)}, u32[]{:S(2)}, u32[]{:S(2)}) collective-permute-start(f32[64,256]{1,0:T(8,128)S(1)} %sum_weights.2.refs_0_), channel_id=1, source_target_pairs={{0,32},{16,48},{32,64},{48,80},{64,96},{80,112},{96,0},{112,16},{1... | collective-permute-start | bytes 196616 | tf_op jit(solution)/shard_map/sum_weights/ppermute | solution.py:39
  108.0 6.0 %collective-permute-start.36 = (f32[64,256]{1,0:T(8,128)S(1)}, f32[64,256]{1,0:T(8,128)S(1)}, u32[]{:S(2)}, u32[]{:S(2)}) collective-permute-start(f32[64,256]{1,0:T(8,128)S(1)} %sum_weights.2.refs_0_), channel_id=1, source_target_pairs={{0,64},{16,80},{32,96},{48,112},{64,0},{80,16},{96,32},{112,48},{1... | collective-permute-start | bytes 196616 | tf_op jit(solution)/shard_map/sum_weights/ppermute | solution.py:39
  (12 other events, 136.2 us)

commit v9 on v7

--- a/solution.py
+++ b/solution.py
@@ -560,12 +560,12 @@
             add_near_body,
             [f32, bf16, bf16],
             [mine, sib_near, from_right, from_left, from_pair],
-            after=[pair_ring],
+            after=[pair_ring, left, right],
             nbytes=5 << 20,
         )
         sums = [own, left, right, step(opposite, 2), swap(pair)]
     with jax.named_scope("sum_weights"):
-        quarter = call(weight_sum_body, block, [ring, pair_ring], after=[left, right])
+        quarter = call(weight_sum_body, block, [ring, pair_ring])
         shape = jax.ShapeDtypeStruct((128, 256), F32)
         grad_self, grad_neigh = call(
             functools.partial(weight_join_body, float(nodes) ** -0.5),

time: 124 us -> 118 us (0.952)
  Pallas kernels: 24 us -> 18 us
  starting transfers between devices: 51.2 us -> 57.2 us
  waiting for transfers between devices: 46.4 us -> 40.6 us
    pallas_call x19, Pallas kernels: 17.5 us -> 11.5 us  [call(): pl.pallas_call(run, out_shape=outs, in_specs=[pl.BlockSpec(memory_space=p...]
    ppermute x20, waiting for transfers between devices: 28.8 us -> 23.5 us  [hop_col(): return lax.ppermute(value, 'col', pairs)]
    ppermute x20, starting transfers between devices: 17.9 us -> 21.6 us  [hop_col(): return lax.ppermute(value, 'col', pairs)]
    ppermute x18, starting transfers between devices: 33.3 us -> 35.7 us  [hop_row(): return lax.ppermute(value, 'row', pairs)]
  transfers between devices with their start and end apart: 38 -> 38, of which waited for: 18 -> 16; matrix products, arithmetic and copies ran while one was open for 0% -> 0% of each run, Pallas kernels for 14% -> 11%
where the time goes in v9:
time: 118 us
  starting transfers between devices  57.2 us (48%)
  waiting for transfers between devices  40.6 us (34%)
  Pallas kernels  18 us (15%)
  between operations  1.55 us (1%)
    ppermute x18, starting transfers between devices, hop_row(): return lax.ppermute(value, 'row', pairs)  35.7 us
    ppermute x20, waiting for transfers between devices, hop_col(): return lax.ppermute(value, 'col', pairs)  23.5 us
    ppermute x20, starting transfers between devices, hop_col(): return lax.ppermute(value, 'col', pairs)  21.6 us
    ppermute x18, waiting for transfers between devices, hop_row(): return lax.ppermute(value, 'row', pairs)  17.1 us
    pallas_call x19, Pallas kernels, call(): pl.pallas_call(run, out_shape=outs, in_specs=[pl.BlockSpec(memory_space=p...  11.5 us
    pallas_call x1, Pallas kernels, shards(): pl.pallas_call(plan_body, out_shape=[VMEM((128, TILE, TILE), BF16), pltpu...  6.48 us
  transfers between devices with their start and end apart: 38, of which 16 were waited for; matrix products, arithmetic and copies ran while one was open for 0% of the time, Pallas kernels for 11%

profile of v9, /device:TPU:0, one launch (start us, length us, event | category | flops | bytes accessed | tf_op | source)
XLA Modules:
  0.0 118.1 jit_solution(406984457575074764)
XLA Ops:
  0.6 3.2 %collective-permute-start.3 = (bf16[1024,128]{1,0:T(8,128)(2,1)}, bf16[1024,128]{1,0:T(8,128)(2,1)S(1)}, u32[]{:S(2)}, u32[]{:S(2)}) collective-permute-start(bf16[1024,128]{1,0:T(8,128)(2,1)} %refs_1_.2), channel_id=1, source_target_pairs={{0,4},{1,5},{2,6},{3,7},{4,0},{5,1},{6,2},{7,3},{8,12},{9,13},{10,... | collective-permute-start | bytes 786440 | tf_op jit(solution)/shard_map/gather_features/ppermute | solution.py:31
  3.8 1.6 %collective-permute-start.2 = (bf16[1024,128]{1,0:T(8,128)(2,1)}, bf16[1024,128]{1,0:T(8,128)(2,1)S(1)}, u32[]{:S(2)}, u32[]{:S(2)}) collective-permute-start(bf16[1024,128]{1,0:T(8,128)(2,1)} %refs_1_.2), channel_id=1, source_target_pairs={{0,8},{1,9},{2,10},{3,11},{4,12},{5,13},{6,14},{7,15},{8,0},{9,1},... | collective-permute-start | bytes 786440 | tf_op jit(solution)/shard_map/gather_features/ppermute | solution.py:31
  8.8 6.5 %plan.1 = (bf16[128,256,256]{2,1,0:T(8,128)(2,1)S(1)}, s32[1152]{0:T(1024)S(4)}, s32[8]{0:T(128)S(4)}) custom-call(s32[2,128]{1,0:T(2,128)S(1)} %bitcast.7, s32[1]{0:T(128)} %bitcast.6.count, bf16[128,256,256]{2,1,0:T(8,128)(2,1)} %bitcast.9), custom_call_target="tpu_custom_call" | custom-call | bytes 16777216 | tf_op jit(solution)/shard_map/plan/pallas_call | solution.py:402
  16.5 1.7 %collective-permute-start.6 = (bf16[1024,128]{1,0:T(8,128)(2,1)S(1)}, bf16[1024,128]{1,0:T(8,128)(2,1)S(1)}, u32[]{:S(2)}, u32[]{:S(2)}) collective-permute-start(bf16[1024,128]{1,0:T(8,128)(2,1)S(1)} %collective-permute-done.3.refs_4_), channel_id=1, source_target_pairs={{0,8},{1,9},{2,10},{3,11},{4,12},{5,13},{6,14},{7,15},{8,0},{9,1},... | collective-permute-start | bytes 786440 | tf_op jit(solution)/shard_map/gather_features/ppermute | solution.py:31
  18.2 2.6 %collective-permute-start.5 = (bf16[1024,128]{1,0:T(8,128)(2,1)S(1)}, bf16[1024,128]{1,0:T(8,128)(2,1)S(1)}, u32[]{:S(2)}, u32[]{:S(2)}) collective-permute-start(bf16[1024,128]{1,0:T(8,128)(2,1)S(1)} %get-tuple-element.47), channel_id=1, source_target_pairs={{0,6},{1,7},{2,0},{3,1},{4,2},{5,3},{6,4},{7,5},{8,14},{9,15},{10,... | collective-permute-start | bytes 786440 | tf_op jit(solution)/shard_map/gather_features/ppermute | solution.py:31
  20.8 1.7 %forward_tiles.4.refs_3_.refs_4_ = f32[33,256,128]{2,1,0:T(8,128)S(1)} custom-call(s32[1152]{0:T(1024)S(4)} %get-tuple-element.44.refs_0_, s32[8]{0:T(128)S(4)} %get-tuple-element.45.refs_5_.refs_1_, bf16[128,256,256]{2,1,0:T(8,128)(2,1)S(1)} %get-tuple-element.46.refs_2_, bf16[20,256,128]{2,1,0:T(8,128)(2,1)S(1)} %get-tuple-element.48.refs_3_, ...), custom_call_target="tpu_custom_call" | custom-call | tf_op jit(solution)/shard_map/forward_tiles/pallas_call | solution.py:67
  22.5 2.7 %collective-permute-done.6.refs_2_ = bf16[1024,128]{1,0:T(8,128)(2,1)S(1)} collective-permute-done((bf16[1024,128]{1,0:T(8,128)(2,1)S(1)}, bf16[1024,128]{1,0:T(8,128)(2,1)S(1)}, u32[]{:S(2)}, u32[]{:S(2)}) %collective-permute-start.6) | collective-permute-done | bytes 262176 | tf_op jit(solution)/shard_map/gather_features/ppermute | solution.py:31
  26.7 3.4 %collective-permute-done.4.refs_0_ = bf16[1024,128]{1,0:T(8,128)(2,1)S(1)} collective-permute-done((bf16[1024,128]{1,0:T(8,128)(2,1)S(1)}, bf16[1024,128]{1,0:T(8,128)(2,1)S(1)}, u32[]{:S(2)}, u32[]{:S(2)}) %collective-permute-start.4) | collective-permute-done | bytes 262176 | tf_op jit(solution)/shard_map/gather_features/ppermute | solution.py:31
  31.0 1.5 %collective-permute-done.8.refs_3_ = bf16[12,256,128]{2,1,0:T(8,128)(2,1)S(1)} collective-permute-done((bf16[12,256,128]{2,1,0:T(8,128)(2,1)S(1)}, bf16[12,256,128]{2,1,0:T(8,128)(2,1)S(1)}, u32[]{:S(2)}, u32[]{:S(2)}) %collective-permute-start.8) | collective-permute-done | bytes 786464 | tf_op jit(solution)/shard_map/forward_tiles/ppermute | solution.py:31
  33.5 4.1 %collective-permute-start.11 = (bf16[1024,128]{1,0:T(8,128)(2,1)S(1)}, bf16[1024,128]{1,0:T(8,128)(2,1)S(1)}, u32[]{:S(2)}, u32[]{:S(2)}) collective-permute-start(bf16[1024,128]{1,0:T(8,128)(2,1)S(1)} %get-tuple-element.54), channel_id=1, source_target_pairs={{0,96},{16,112},{32,0},{48,16},{64,32},{80,48},{96,64},{112,80},{1... | collective-permute-start | bytes 786440 | tf_op jit(solution)/shard_map/sum_aggregates/ppermute | solution.py:39
  37.6 2.9 %collective-permute-start.13 = (bf16[1024,128]{1,0:T(8,128)(2,1)S(1)}, bf16[1024,128]{1,0:T(8,128)(2,1)S(1)}, u32[]{:S(2)}, u32[]{:S(2)}) collective-permute-start(bf16[1024,128]{1,0:T(8,128)(2,1)S(1)} %get-tuple-element.56), channel_id=1, source_target_pairs={{0,16},{16,0},{32,48},{48,32},{64,80},{80,64},{96,112},{112,96},{1... | collective-permute-start | bytes 786440 | tf_op jit(solution)/shard_map/sum_aggregates/ppermute | solution.py:39
  40.5 3.2 %collective-permute-start.9 = (bf16[1024,128]{1,0:T(8,128)(2,1)S(1)}, bf16[1024,128]{1,0:T(8,128)(2,1)S(1)}, u32[]{:S(2)}, u32[]{:S(2)}) collective-permute-start(bf16[1024,128]{1,0:T(8,128)(2,1)S(1)} %get-tuple-element.50), channel_id=1, source_target_pairs={{0,96},{16,112},{32,0},{48,16},{64,32},{80,48},{96,64},{112,80},{1... | collective-permute-start | bytes 786440 | tf_op jit(solution)/shard_map/sum_aggregates/ppermute | solution.py:39
  43.7 3.4 %collective-permute-done.12.refs_3_ = bf16[1024,128]{1,0:T(8,128)(2,1)S(1)} collective-permute-done((bf16[1024,128]{1,0:T(8,128)(2,1)S(1)}, bf16[1024,128]{1,0:T(8,128)(2,1)S(1)}, u32[]{:S(2)}, u32[]{:S(2)}) %collective-permute-start.12) | collective-permute-done | bytes 262176 | tf_op jit(solution)/shard_map/sum_aggregates/ppermute | solution.py:39
  47.3 1.7 %collective-permute-start.14 = (bf16[1024,128]{1,0:T(8,128)(2,1)S(1)}, bf16[1024,128]{1,0:T(8,128)(2,1)S(1)}, u32[]{:S(2)}, u32[]{:S(2)}) collective-permute-start(bf16[1024,128]{1,0:T(8,128)(2,1)S(1)} %get-tuple-element.57), channel_id=1, source_target_pairs={{0,64},{16,80},{32,96},{48,112},{64,0},{80,16},{96,32},{112,48},{1... | collective-permute-start | bytes 786440 | tf_op jit(solution)/shard_map/sum_aggregates/ppermute | solution.py:39
  48.9 2.9 %collective-permute-start.15 = (bf16[1024,128]{1,0:T(8,128)(2,1)S(1)}, bf16[1024,128]{1,0:T(8,128)(2,1)S(1)}, u32[]{:S(2)}, u32[]{:S(2)}) collective-permute-start(bf16[1024,128]{1,0:T(8,128)(2,1)S(1)} %get-tuple-element.58), channel_id=1, source_target_pairs={{0,16},{16,0},{32,48},{48,32},{64,80},{80,64},{96,112},{112,96},{1... | collective-permute-start | bytes 786440 | tf_op jit(solution)/shard_map/sum_aggregates/ppermute | solution.py:39
  51.8 6.2 %collective-permute-done.10.refs_7_ = bf16[1024,128]{1,0:T(8,128)(2,1)S(1)} collective-permute-done((bf16[1024,128]{1,0:T(8,128)(2,1)S(1)}, bf16[1024,128]{1,0:T(8,128)(2,1)S(1)}, u32[]{:S(2)}, u32[]{:S(2)}) %collective-permute-start.10) | collective-permute-done | bytes 262176 | tf_op jit(solution)/shard_map/sum_aggregates/ppermute | solution.py:39
  58.1 2.3 %dense.1 = (bf16[1024,256]{1,0:T(8,128)(2,1)}, bf16[1024,256]{1,0:T(8,128)(2,1)S(1)}, bf16[128,1024]{1,0:T(8,128)(2,1)S(1)}, bf16[144,1024]{1,0:T(8,128)(2,1)S(1...) custom-call(f32[1,256]{1,0:T(1,128)S(1)} %bitcast.8, ...), custom_call_target="tpu_custom_call" | custom-call | flops 335544320 | bytes 6291456 | tf_op jit(solution)/shard_map/dense/pallas_call | solution.py:67
  61.6 3.2 %collective-permute-start.16 = (bf16[128,1024]{1,0:T(8,128)(2,1)S(1)}, bf16[128,1024]{1,0:T(8,128)(2,1)S(1)}, u32[]{:S(2)}, u32[]{:S(2)}) collective-permute-start(bf16[128,1024]{1,0:T(8,128)(2,1)S(1)} %get-tuple-element.61.refs_3_), channel_id=1, source_target_pairs={{0,16},{16,0},{32,48},{48,32},{64,80},{80,64},{96,112},{112,96},{1... | collective-permute-start | bytes 786440 | tf_op jit(solution)/shard_map/gather_dz/ppermute | solution.py:39
  64.8 3.2 %collective-permute-start.22 = (bf16[144,1024]{1,0:T(8,128)(2,1)S(1)}, bf16[144,1024]{1,0:T(8,128)(2,1)S(1)}, u32[]{:S(2)}, u32[]{:S(2)}) collective-permute-start(bf16[144,1024]{1,0:T(8,128)(2,1)S(1)} %get-tuple-element.64), channel_id=1, source_target_pairs={{0,96},{16,112},{32,0},{48,16},{64,32},{80,48},{96,64},{112,80},{1... | collective-permute-start | bytes 884744 | tf_op jit(solution)/shard_map/gather_dz/ppermute | solution.py:39
  68.0 3.2 %collective-permute-done.19.refs_7_.refs_1_ = bf16[144,1024]{1,0:T(8,128)(2,1)S(1)} collective-permute-done((bf16[144,1024]{1,0:T(8,128)(2,1)S(1)}, bf16[144,1024]{1,0:T(8,128)(2,1)S(1)}, u32[]{:S(2)}, u32[]{:S(2)}) %collective-permute-start.19) | collective-permute-done | bytes 294944 | tf_op jit(solution)/shard_map/gather_dz/ppermute | solution.py:39
  71.2 3.6 %collective-permute-start.20 = (bf16[144,1024]{1,0:T(8,128)(2,1)S(1)}, bf16[144,1024]{1,0:T(8,128)(2,1)S(1)}, u32[]{:S(2)}, u32[]{:S(2)}) collective-permute-start(bf16[144,1024]{1,0:T(8,128)(2,1)S(1)} %collective-permute-done.19.refs_7_.refs_1_), channel_id=1, source_target_pairs={{0,16},{16,0},{32,48},{48,32},{64,80},{80,64},{96,112},{112,96},{1... | collective-permute-start | bytes 884744 | tf_op jit(solution)/shard_map/gather_dz/ppermute | solution.py:39
  77.1 2.1 %collective-permute-start.23 = (bf16[32,1024]{1,0:T(8,128)(2,1)S(1)}, bf16[32,1024]{1,0:T(8,128)(2,1)S(1)}, u32[]{:S(2)}, u32[]{:S(2)}) collective-permute-start(bf16[32,1024]{1,0:T(8,128)(2,1)S(1)} %gather_dz.1.refs_6_), channel_id=1, source_target_pairs={{0,16},{16,0},{32,48},{48,32},{64,80},{80,64},{96,112},{112,96},{1... | collective-permute-start | bytes 196616 | tf_op jit(solution)/shard_map/gather_dz/ppermute | solution.py:39
  79.2 1.6 %backward_tiles.3 = (f32[33,128,256]{2,1,0:T(8,128)S(1)}, f32[33,128,256]{2,1,0:T(8,128)S(1)}) custom-call(s32[1152]{0:T(1024)S(4)} %get-tuple-element.44.refs_0_, s32[8]{0:T(128)S(4)} %get-tuple-element.45.refs_5_.refs_1_, bf16[128,256,256]{2,1,0:T(8,128)(2,1)S(1)} %get-tuple-element.46.refs_2_, bf16[128,1024]{1,0:T(8,128)(2,1)S(1)} %get-tuple-element.61.refs_3_, ...), custom_call_target="tpu_custom_call" | custom-call | flops 1073741824 | bytes 8388608 | tf_op jit(solution)/shard_map/backward_tiles/pallas_call | solution.py:67
  80.9 2.1 %collective-permute-done.23.refs_7_ = bf16[32,1024]{1,0:T(8,128)(2,1)S(1)} collective-permute-done((bf16[32,1024]{1,0:T(8,128)(2,1)S(1)}, bf16[32,1024]{1,0:T(8,128)(2,1)S(1)}, u32[]{:S(2)}, u32[]{:S(2)}) %collective-permute-start.23) | collective-permute-done | bytes 65568 | tf_op jit(solution)/shard_map/gather_dz/ppermute | solution.py:39
  84.4 1.8 %collective-permute-done.24.refs_2_ = bf16[416,1024]{1,0:T(8,128)(2,1)S(1)} collective-permute-done((bf16[416,1024]{1,0:T(8,128)(2,1)S(1)}, bf16[416,1024]{1,0:T(8,128)(2,1)S(1)}, u32[]{:S(2)}, u32[]{:S(2)}) %collective-permute-start.24) | collective-permute-done | bytes 852000 | tf_op jit(solution)/shard_map/sum_grads/ppermute | solution.py:31
  90.2 2.7 %collective-permute-start.31 = (bf16[128,1024]{1,0:T(8,128)(2,1)S(1)}, bf16[128,1024]{1,0:T(8,128)(2,1)S(1)}, u32[]{:S(2)}, u32[]{:S(2)}) collective-permute-start(bf16[128,1024]{1,0:T(8,128)(2,1)S(1)} %get-tuple-element.77), channel_id=1, source_target_pairs={{0,6},{1,7},{2,0},{3,1},{4,2},{5,3},{6,4},{7,5},{8,14},{9,15},{10,... | collective-permute-start | bytes 786440 | tf_op jit(solution)/shard_map/sum_grads/ppermute | solution.py:31
  92.9 4.5 %collective-permute-done.29.refs_3_ = bf16[16,1024]{1,0:T(8,128)(2,1)S(1)} collective-permute-done((bf16[16,1024]{1,0:T(8,128)(2,1)S(1)}, bf16[16,1024]{1,0:T(8,128)(2,1)S(1)}, u32[]{:S(2)}, u32[]{:S(2)}) %collective-permute-start.29) | collective-permute-done | bytes 32800 | tf_op jit(solution)/shard_map/sum_grads/ppermute | solution.py:31
  99.4 3.4 %collective-permute-done.30.refs_5_.refs_1_ = bf16[32,1024]{1,0:T(8,128)(2,1)S(1)} collective-permute-done((bf16[32,1024]{1,0:T(8,128)(2,1)S(1)}, bf16[32,1024]{1,0:T(8,128)(2,1)S(1)}, u32[]{:S(2)}, u32[]{:S(2)}) %collective-permute-start.30) | collective-permute-done | bytes 65568 | tf_op jit(solution)/shard_map/sum_grads/ppermute | solution.py:31
  102.8 2.8 %collective-permute-done.32.refs_7_.refs_3_ = bf16[128,1024]{1,0:T(8,128)(2,1)S(1)} collective-permute-done((bf16[128,1024]{1,0:T(8,128)(2,1)S(1)}, bf16[128,1024]{1,0:T(8,128)(2,1)S(1)}, u32[]{:S(2)}, u32[]{:S(2)}) %collective-permute-start.32) | collective-permute-done | bytes 262176 | tf_op jit(solution)/shard_map/sum_grads/ppermute | solution.py:31
  105.9 1.5 %collective-permute-start.33 = (bf16[128,1024]{1,0:T(8,128)(2,1)S(1)}, bf16[128,1024]{1,0:T(8,128)(2,1)S(1)}, u32[]{:S(2)}, u32[]{:S(2)}) collective-permute-start(bf16[128,1024]{1,0:T(8,128)(2,1)S(1)} %get-tuple-element.80), channel_id=1, source_target_pairs={{0,4},{1,5},{2,6},{3,7},{4,0},{5,1},{6,2},{7,3},{8,12},{9,13},{10,... | collective-permute-start | bytes 786440 | tf_op jit(solution)/shard_map/sum_grads/ppermute | solution.py:31
  110.0 2.2 %collective-permute-start.36 = (f32[64,256]{1,0:T(8,128)S(1)}, f32[64,256]{1,0:T(8,128)S(1)}, u32[]{:S(2)}, u32[]{:S(2)}) collective-permute-start(f32[64,256]{1,0:T(8,128)S(1)} %sum_weights.2.refs_0_), channel_id=1, source_target_pairs={{0,64},{16,80},{32,96},{48,112},{64,0},{80,16},{96,32},{112,48},{1... | collective-permute-start | bytes 196616 | tf_op jit(solution)/shard_map/sum_weights/ppermute | solution.py:39
  112.1 2.2 %collective-permute-start.35 = (f32[64,256]{1,0:T(8,128)S(1)}, f32[64,256]{1,0:T(8,128)S(1)}, u32[]{:S(2)}, u32[]{:S(2)}) collective-permute-start(f32[64,256]{1,0:T(8,128)S(1)} %sum_weights.2.refs_0_), channel_id=1, source_target_pairs={{0,96},{16,112},{32,0},{48,16},{64,32},{80,48},{96,64},{112,80},{1... | collective-permute-start | bytes 196616 | tf_op jit(solution)/shard_map/sum_weights/ppermute | solution.py:39
  (76 shorter events, 24.9 us)
Async XLA Ops:
  0.6 14.6 %collective-permute-start.3 = (bf16[1024,128]{1,0:T(8,128)(2,1)}, bf16[1024,128]{1,0:T(8,128)(2,1)S(1)}, u32[]{:S(2)}, u32[]{:S(2)}) collective-permute-start(bf16[1024,128]{1,0:T(8,128)(2,1)} %refs_1_.2), channel_id=1, source_target_pairs={{0,4},{1,5},{2,6},{3,7},{4,0},{5,1},{6,2},{7,3},{8,12},{9,13},{10,... | collective-permute-start | bytes 786440 | tf_op jit(solution)/shard_map/gather_features/ppermute | solution.py:31
  3.8 11.4 %collective-permute-start.2 = (bf16[1024,128]{1,0:T(8,128)(2,1)}, bf16[1024,128]{1,0:T(8,128)(2,1)S(1)}, u32[]{:S(2)}, u32[]{:S(2)}) collective-permute-start(bf16[1024,128]{1,0:T(8,128)(2,1)} %refs_1_.2), channel_id=1, source_target_pairs={{0,8},{1,9},{2,10},{3,11},{4,12},{5,13},{6,14},{7,15},{8,0},{9,1},... | collective-permute-start | bytes 786440 | tf_op jit(solution)/shard_map/gather_features/ppermute | solution.py:31
  5.4 10.9 %collective-permute-start.1 = (bf16[1024,128]{1,0:T(8,128)(2,1)}, bf16[1024,128]{1,0:T(8,128)(2,1)S(1)}, u32[]{:S(2)}, u32[]{:S(2)}) collective-permute-start(bf16[1024,128]{1,0:T(8,128)(2,1)} %refs_1_.2), channel_id=1, source_target_pairs={{0,6},{1,7},{2,0},{3,1},{4,2},{5,3},{6,4},{7,5},{8,14},{9,15},{10,... | collective-permute-start | bytes 786440 | tf_op jit(solution)/shard_map/gather_features/ppermute | solution.py:31
  6.5 9.8 %collective-permute-start = (bf16[1024,128]{1,0:T(8,128)(2,1)}, bf16[1024,128]{1,0:T(8,128)(2,1)S(1)}, u32[]{:S(2)}, u32[]{:S(2)}) collective-permute-start(bf16[1024,128]{1,0:T(8,128)(2,1)} %refs_1_.2), channel_id=1, source_target_pairs={{0,2},{1,3},{2,4},{3,5},{4,6},{5,7},{6,0},{7,1},{8,10},{9,11},{10,... | collective-permute-start | bytes 786440 | tf_op jit(solution)/shard_map/gather_features/ppermute | solution.py:31
  16.5 8.7 %collective-permute-start.6 = (bf16[1024,128]{1,0:T(8,128)(2,1)S(1)}, bf16[1024,128]{1,0:T(8,128)(2,1)S(1)}, u32[]{:S(2)}, u32[]{:S(2)}) collective-permute-start(bf16[1024,128]{1,0:T(8,128)(2,1)S(1)} %collective-permute-done.3.refs_4_), channel_id=1, source_target_pairs={{0,8},{1,9},{2,10},{3,11},{4,12},{5,13},{6,14},{7,15},{8,0},{9,1},... | collective-permute-start | bytes 786440 | tf_op jit(solution)/shard_map/gather_features/ppermute | solution.py:31
  18.2 8.5 %collective-permute-start.5 = (bf16[1024,128]{1,0:T(8,128)(2,1)S(1)}, bf16[1024,128]{1,0:T(8,128)(2,1)S(1)}, u32[]{:S(2)}, u32[]{:S(2)}) collective-permute-start(bf16[1024,128]{1,0:T(8,128)(2,1)S(1)} %get-tuple-element.47), channel_id=1, source_target_pairs={{0,6},{1,7},{2,0},{3,1},{4,2},{5,3},{6,4},{7,5},{8,14},{9,15},{10,... | collective-permute-start | bytes 786440 | tf_op jit(solution)/shard_map/gather_features/ppermute | solution.py:31
  20.8 9.3 %collective-permute-start.4 = (bf16[1024,128]{1,0:T(8,128)(2,1)S(1)}, bf16[1024,128]{1,0:T(8,128)(2,1)S(1)}, u32[]{:S(2)}, u32[]{:S(2)}) collective-permute-start(bf16[1024,128]{1,0:T(8,128)(2,1)S(1)} %get-tuple-element.47), channel_id=1, source_target_pairs={{0,2},{1,3},{2,4},{3,5},{4,6},{5,7},{6,0},{7,1},{8,10},{9,11},{10,... | collective-permute-start | bytes 786440 | tf_op jit(solution)/shard_map/gather_features/ppermute | solution.py:31
  33.5 10.2 %collective-permute-start.11 = (bf16[1024,128]{1,0:T(8,128)(2,1)S(1)}, bf16[1024,128]{1,0:T(8,128)(2,1)S(1)}, u32[]{:S(2)}, u32[]{:S(2)}) collective-permute-start(bf16[1024,128]{1,0:T(8,128)(2,1)S(1)} %get-tuple-element.54), channel_id=1, source_target_pairs={{0,96},{16,112},{32,0},{48,16},{64,32},{80,48},{96,64},{112,80},{1... | collective-permute-start | bytes 786440 | tf_op jit(solution)/shard_map/sum_aggregates/ppermute | solution.py:39
  37.6 9.5 %collective-permute-start.12 = (bf16[1024,128]{1,0:T(8,128)(2,1)S(1)}, bf16[1024,128]{1,0:T(8,128)(2,1)S(1)}, u32[]{:S(2)}, u32[]{:S(2)}) collective-permute-start(bf16[1024,128]{1,0:T(8,128)(2,1)S(1)} %get-tuple-element.55), channel_id=1, source_target_pairs={{0,32},{16,48},{32,64},{48,80},{64,96},{80,112},{96,0},{112,16},{1... | collective-permute-start | bytes 786440 | tf_op jit(solution)/shard_map/sum_aggregates/ppermute | solution.py:39
  37.6 9.6 %collective-permute-start.13 = (bf16[1024,128]{1,0:T(8,128)(2,1)S(1)}, bf16[1024,128]{1,0:T(8,128)(2,1)S(1)}, u32[]{:S(2)}, u32[]{:S(2)}) collective-permute-start(bf16[1024,128]{1,0:T(8,128)(2,1)S(1)} %get-tuple-element.56), channel_id=1, source_target_pairs={{0,16},{16,0},{32,48},{48,32},{64,80},{80,64},{96,112},{112,96},{1... | collective-permute-start | bytes 786440 | tf_op jit(solution)/shard_map/sum_aggregates/ppermute | solution.py:39
  40.5 11.4 %collective-permute-start.9 = (bf16[1024,128]{1,0:T(8,128)(2,1)S(1)}, bf16[1024,128]{1,0:T(8,128)(2,1)S(1)}, u32[]{:S(2)}, u32[]{:S(2)}) collective-permute-start(bf16[1024,128]{1,0:T(8,128)(2,1)S(1)} %get-tuple-element.50), channel_id=1, source_target_pairs={{0,96},{16,112},{32,0},{48,16},{64,32},{80,48},{96,64},{112,80},{1... | collective-permute-start | bytes 786440 | tf_op jit(solution)/shard_map/sum_aggregates/ppermute | solution.py:39
  43.7 14.4 %collective-permute-start.10 = (bf16[1024,128]{1,0:T(8,128)(2,1)S(1)}, bf16[1024,128]{1,0:T(8,128)(2,1)S(1)}, u32[]{:S(2)}, u32[]{:S(2)}) collective-permute-start(bf16[1024,128]{1,0:T(8,128)(2,1)S(1)} %get-tuple-element.51), channel_id=1, source_target_pairs={{0,32},{16,48},{32,64},{48,80},{64,96},{80,112},{96,0},{112,16},{1... | collective-permute-start | bytes 786440 | tf_op jit(solution)/shard_map/sum_aggregates/ppermute | solution.py:39
  47.3 10.8 %collective-permute-start.14 = (bf16[1024,128]{1,0:T(8,128)(2,1)S(1)}, bf16[1024,128]{1,0:T(8,128)(2,1)S(1)}, u32[]{:S(2)}, u32[]{:S(2)}) collective-permute-start(bf16[1024,128]{1,0:T(8,128)(2,1)S(1)} %get-tuple-element.57), channel_id=1, source_target_pairs={{0,64},{16,80},{32,96},{48,112},{64,0},{80,16},{96,32},{112,48},{1... | collective-permute-start | bytes 786440 | tf_op jit(solution)/shard_map/sum_aggregates/ppermute | solution.py:39
  48.9 9.2 %collective-permute-start.15 = (bf16[1024,128]{1,0:T(8,128)(2,1)S(1)}, bf16[1024,128]{1,0:T(8,128)(2,1)S(1)}, u32[]{:S(2)}, u32[]{:S(2)}) collective-permute-start(bf16[1024,128]{1,0:T(8,128)(2,1)S(1)} %get-tuple-element.58), channel_id=1, source_target_pairs={{0,16},{16,0},{32,48},{48,32},{64,80},{80,64},{96,112},{112,96},{1... | collective-permute-start | bytes 786440 | tf_op jit(solution)/shard_map/sum_aggregates/ppermute | solution.py:39
  60.4 10.8 %collective-permute-start.19 = (bf16[144,1024]{1,0:T(8,128)(2,1)S(1)}, bf16[144,1024]{1,0:T(8,128)(2,1)S(1)}, u32[]{:S(2)}, u32[]{:S(2)}) collective-permute-start(bf16[144,1024]{1,0:T(8,128)(2,1)S(1)} %get-tuple-element.62), channel_id=1, source_target_pairs={{0,64},{16,80},{32,96},{48,112},{64,0},{80,16},{96,32},{112,48},{1... | collective-permute-start | bytes 884744 | tf_op jit(solution)/shard_map/gather_dz/ppermute | solution.py:39
  61.6 13.2 %collective-permute-start.16 = (bf16[128,1024]{1,0:T(8,128)(2,1)S(1)}, bf16[128,1024]{1,0:T(8,128)(2,1)S(1)}, u32[]{:S(2)}, u32[]{:S(2)}) collective-permute-start(bf16[128,1024]{1,0:T(8,128)(2,1)S(1)} %get-tuple-element.61.refs_3_), channel_id=1, source_target_pairs={{0,16},{16,0},{32,48},{48,32},{64,80},{80,64},{96,112},{112,96},{1... | collective-permute-start | bytes 786440 | tf_op jit(solution)/shard_map/gather_dz/ppermute | solution.py:39
  64.8 12.3 %collective-permute-start.21 = (bf16[144,1024]{1,0:T(8,128)(2,1)S(1)}, bf16[144,1024]{1,0:T(8,128)(2,1)S(1)}, u32[]{:S(2)}, u32[]{:S(2)}) collective-permute-start(bf16[144,1024]{1,0:T(8,128)(2,1)S(1)} %get-tuple-element.63), channel_id=1, source_target_pairs={{0,32},{16,48},{32,64},{48,80},{64,96},{80,112},{96,0},{112,16},{1... | collective-permute-start | bytes 884744 | tf_op jit(solution)/shard_map/gather_dz/ppermute | solution.py:39
  64.8 12.3 %collective-permute-start.22 = (bf16[144,1024]{1,0:T(8,128)(2,1)S(1)}, bf16[144,1024]{1,0:T(8,128)(2,1)S(1)}, u32[]{:S(2)}, u32[]{:S(2)}) collective-permute-start(bf16[144,1024]{1,0:T(8,128)(2,1)S(1)} %get-tuple-element.64), channel_id=1, source_target_pairs={{0,96},{16,112},{32,0},{48,16},{64,32},{80,48},{96,64},{112,80},{1... | collective-permute-start | bytes 884744 | tf_op jit(solution)/shard_map/gather_dz/ppermute | solution.py:39
  71.2 11.8 %collective-permute-start.20 = (bf16[144,1024]{1,0:T(8,128)(2,1)S(1)}, bf16[144,1024]{1,0:T(8,128)(2,1)S(1)}, u32[]{:S(2)}, u32[]{:S(2)}) collective-permute-start(bf16[144,1024]{1,0:T(8,128)(2,1)S(1)} %collective-permute-done.19.refs_7_.refs_1_), channel_id=1, source_target_pairs={{0,16},{16,0},{32,48},{48,32},{64,80},{80,64},{96,112},{112,96},{1... | collective-permute-start | bytes 884744 | tf_op jit(solution)/shard_map/gather_dz/ppermute | solution.py:39
  74.8 8.2 %collective-permute-start.18 = (bf16[128,1024]{1,0:T(8,128)(2,1)S(1)}, bf16[128,1024]{1,0:T(8,128)(2,1)S(1)}, u32[]{:S(2)}, u32[]{:S(2)}) collective-permute-start(bf16[128,1024]{1,0:T(8,128)(2,1)S(1)} %collective-permute-done.16.refs_6_), channel_id=1, source_target_pairs={{0,96},{16,112},{32,0},{48,16},{64,32},{80,48},{96,64},{112,80},{1... | collective-permute-start | bytes 786440 | tf_op jit(solution)/shard_map/gather_dz/ppermute | solution.py:39
  75.4 7.6 %collective-permute-start.17 = (bf16[128,1024]{1,0:T(8,128)(2,1)S(1)}, bf16[128,1024]{1,0:T(8,128)(2,1)S(1)}, u32[]{:S(2)}, u32[]{:S(2)}) collective-permute-start(bf16[128,1024]{1,0:T(8,128)(2,1)S(1)} %collective-permute-done.16.refs_6_), channel_id=1, source_target_pairs={{0,32},{16,48},{32,64},{48,80},{64,96},{80,112},{96,0},{112,16},{1... | collective-permute-start | bytes 786440 | tf_op jit(solution)/shard_map/gather_dz/ppermute | solution.py:39
  77.1 5.8 %collective-permute-start.23 = (bf16[32,1024]{1,0:T(8,128)(2,1)S(1)}, bf16[32,1024]{1,0:T(8,128)(2,1)S(1)}, u32[]{:S(2)}, u32[]{:S(2)}) collective-permute-start(bf16[32,1024]{1,0:T(8,128)(2,1)S(1)} %gather_dz.1.refs_6_), channel_id=1, source_target_pairs={{0,16},{16,0},{32,48},{48,32},{64,80},{80,64},{96,112},{112,96},{1... | collective-permute-start | bytes 196616 | tf_op jit(solution)/shard_map/gather_dz/ppermute | solution.py:39
  86.7 10.8 %collective-permute-start.26 = (bf16[144,1024]{1,0:T(8,128)(2,1)S(1)}, bf16[144,1024]{1,0:T(8,128)(2,1)S(1)}, u32[]{:S(2)}, u32[]{:S(2)}) collective-permute-start(bf16[144,1024]{1,0:T(8,128)(2,1)S(1)} %get-tuple-element.72), channel_id=1, source_target_pairs={{0,6},{1,7},{2,0},{3,1},{4,2},{5,3},{6,4},{7,5},{8,14},{9,15},{10,... | collective-permute-start | bytes 884744 | tf_op jit(solution)/shard_map/sum_grads/ppermute | solution.py:31
  87.5 10.9 %collective-permute-start.27 = (bf16[144,1024]{1,0:T(8,128)(2,1)S(1)}, bf16[144,1024]{1,0:T(8,128)(2,1)S(1)}, u32[]{:S(2)}, u32[]{:S(2)}) collective-permute-start(bf16[144,1024]{1,0:T(8,128)(2,1)S(1)} %get-tuple-element.73), channel_id=1, source_target_pairs={{0,2},{1,3},{2,4},{3,5},{4,6},{5,7},{6,0},{7,1},{8,10},{9,11},{10,... | collective-permute-start | bytes 884744 | tf_op jit(solution)/shard_map/sum_grads/ppermute | solution.py:31
  88.7 8.6 %collective-permute-start.29 = (bf16[16,1024]{1,0:T(8,128)(2,1)S(1)}, bf16[16,1024]{1,0:T(8,128)(2,1)S(1)}, u32[]{:S(2)}, u32[]{:S(2)}) collective-permute-start(bf16[16,1024]{1,0:T(8,128)(2,1)S(1)} %get-tuple-element.76), channel_id=1, source_target_pairs={{0,4},{1,5},{2,6},{3,7},{4,0},{5,1},{6,2},{7,3},{8,12},{9,13},{10,... | collective-permute-start | bytes 98312 | tf_op jit(solution)/shard_map/sum_grads/ppermute | solution.py:31
  89.6 9.8 %collective-permute-start.28 = (bf16[128,1024]{1,0:T(8,128)(2,1)S(1)}, bf16[128,1024]{1,0:T(8,128)(2,1)S(1)}, u32[]{:S(2)}, u32[]{:S(2)}) collective-permute-start(bf16[128,1024]{1,0:T(8,128)(2,1)S(1)} %get-tuple-element.74), channel_id=1, source_target_pairs={{0,8},{1,9},{2,10},{3,11},{4,12},{5,13},{6,14},{7,15},{8,0},{9,1},... | collective-permute-start | bytes 786440 | tf_op jit(solution)/shard_map/sum_grads/ppermute | solution.py:31
  90.2 12.6 %collective-permute-start.31 = (bf16[128,1024]{1,0:T(8,128)(2,1)S(1)}, bf16[128,1024]{1,0:T(8,128)(2,1)S(1)}, u32[]{:S(2)}, u32[]{:S(2)}) collective-permute-start(bf16[128,1024]{1,0:T(8,128)(2,1)S(1)} %get-tuple-element.77), channel_id=1, source_target_pairs={{0,6},{1,7},{2,0},{3,1},{4,2},{5,3},{6,4},{7,5},{8,14},{9,15},{10,... | collective-permute-start | bytes 786440 | tf_op jit(solution)/shard_map/sum_grads/ppermute | solution.py:31
  97.4 8.3 %collective-permute-start.32 = (bf16[128,1024]{1,0:T(8,128)(2,1)S(1)}, bf16[128,1024]{1,0:T(8,128)(2,1)S(1)}, u32[]{:S(2)}, u32[]{:S(2)}) collective-permute-start(bf16[128,1024]{1,0:T(8,128)(2,1)S(1)} %get-tuple-element.78), channel_id=1, source_target_pairs={{0,2},{1,3},{2,4},{3,5},{4,6},{5,7},{6,0},{7,1},{8,10},{9,11},{10,... | collective-permute-start | bytes 786440 | tf_op jit(solution)/shard_map/sum_grads/ppermute | solution.py:31
  105.9 11.3 %collective-permute-start.33 = (bf16[128,1024]{1,0:T(8,128)(2,1)S(1)}, bf16[128,1024]{1,0:T(8,128)(2,1)S(1)}, u32[]{:S(2)}, u32[]{:S(2)}) collective-permute-start(bf16[128,1024]{1,0:T(8,128)(2,1)S(1)} %get-tuple-element.80), channel_id=1, source_target_pairs={{0,4},{1,5},{2,6},{3,7},{4,0},{5,1},{6,2},{7,3},{8,12},{9,13},{10,... | collective-permute-start | bytes 786440 | tf_op jit(solution)/shard_map/sum_grads/ppermute | solution.py:31
  107.4 9.7 %collective-permute-start.34 = (bf16[128,1024]{1,0:T(8,128)(2,1)S(1)}, bf16[128,1024]{1,0:T(8,128)(2,1)S(1)}, u32[]{:S(2)}, u32[]{:S(2)}) collective-permute-start(bf16[128,1024]{1,0:T(8,128)(2,1)S(1)} %get-tuple-element.81), channel_id=1, source_target_pairs={{0,8},{1,9},{2,10},{3,11},{4,12},{5,13},{6,14},{7,15},{8,0},{9,1},... | collective-permute-start | bytes 786440 | tf_op jit(solution)/shard_map/sum_grads/ppermute | solution.py:31
  108.8 5.6 %collective-permute-start.37 = (f32[64,256]{1,0:T(8,128)S(1)}, f32[64,256]{1,0:T(8,128)S(1)}, u32[]{:S(2)}, u32[]{:S(2)}) collective-permute-start(f32[64,256]{1,0:T(8,128)S(1)} %sum_weights.2.refs_0_), channel_id=1, source_target_pairs={{0,32},{16,48},{32,64},{48,80},{64,96},{80,112},{96,0},{112,16},{1... | collective-permute-start | bytes 196616 | tf_op jit(solution)/shard_map/sum_weights/ppermute | solution.py:39
  110.0 5.8 %collective-permute-start.36 = (f32[64,256]{1,0:T(8,128)S(1)}, f32[64,256]{1,0:T(8,128)S(1)}, u32[]{:S(2)}, u32[]{:S(2)}) collective-permute-start(f32[64,256]{1,0:T(8,128)S(1)} %sum_weights.2.refs_0_), channel_id=1, source_target_pairs={{0,64},{16,80},{32,96},{48,112},{64,0},{80,16},{96,32},{112,48},{1... | collective-permute-start | bytes 196616 | tf_op jit(solution)/shard_map/sum_weights/ppermute | solution.py:39
  (12 other events, 138.1 us)
